TPU v7x, 512 devices: a whole 4x8x8 slice. The times are simulated.
512 devices in a mesh: dp: 32 (over z_hi, y), fsdp: 8 (over x, z_lo), section: 2 (over core).
Axes of the slice: x: 4, y: 8, z: 8 (z_hi: 4, z_lo: 2; z = z_hi * 2 + z_lo), core: 2. Of those that a mesh axis runs over, the one named last changes fastest.
Arguments:
- acts: bfloat16 [32768, 5120], P(('dp', 'section'), 'fsdp'), may hold values from -100 to 100
- output_gradient: bfloat16 [32768, 1024], P(('dp', 'section'), 'fsdp'), may hold values from -40 to 40
- lengths: int32 [128], P(('dp', 'section')), may hold values from 1 to 256
- buckets: int32 [128], P(('dp', 'section')), may hold values from 0 to 3
- frozen_key_weight: bfloat16 [5120, 1024], P('fsdp'), may hold values from -0.078125 to 0.078125
- adapter_down_weight: float32 [5120, 128], P('fsdp'), may hold values from -0.078125 to 0.078125
- adapter_up_weight: float32 [128, 1024], P(None, 'fsdp'), may hold values from -0.5 to 0.5
- prompts: bfloat16 [32768, 5120], P(('dp', 'section'), 'fsdp'), may hold values from -6 to 6
Outputs:
- input_gradient: bfloat16 [32768, 5120], P(('dp', 'section'), 'fsdp')
- next_down_weight: float32 [5120, 128], P('fsdp')
- next_up_weight: float32 [128, 1024], P(None, 'fsdp')
- keys: bfloat16 [32768, 1024], P(('dp', 'section'), 'fsdp')
All inputs are finite; a program needn't handle non-finite values.
Results may differ from a plain program's by a relative error of at most 0.0059.
Values may be sent and summed in bfloat16 or wider, within the bound.
No kernel may reach another device: no remote copies, remote signals or barrier semaphores. Data moves between devices by JAX's collectives and lax.ppermute only.
A program may use at most 64 MiB of HBM per device.

v0:
```python
import jax
import jax.numpy as jnp
from jax import lax
from jax.sharding import PartitionSpec as P

adapter_scale = 0.5
step_rate = 16.0
clip_norm = 1.0


def per_device(
    acts,
    output_gradient,
    lengths,
    buckets,
    frozen_key_weight,
    adapter_down_weight,
    adapter_up_weight,
    prompts,
):
    tok_rows = acts.shape[0]
    seq_count = lengths.shape[0]
    slot_len = tok_rows // seq_count
    alive_mask = jnp.arange(slot_len, dtype=jnp.int32)[None, :] < lengths[:, None]
    advantage = buckets.astype(jnp.float32)[:, None] - 1.5
    token_weight = jnp.where(alive_mask, advantage, jnp.float32(0.0)).reshape(tok_rows)
    key_gradient = (token_weight[:, None] * output_gradient.astype(jnp.float32)).astype(
        jnp.bfloat16
    )
    first_factor_half = adapter_down_weight.astype(jnp.bfloat16)
    second_factor_half = adapter_up_weight.astype(jnp.bfloat16)
    down_part = jnp.dot(acts, first_factor_half, preferred_element_type=jnp.float32)
    up_part = jnp.dot(key_gradient, second_factor_half.T, preferred_element_type=jnp.float32)
    down_acts, up_grads = lax.psum((down_part, up_part), "fsdp")
    down_weight_half = down_acts.astype(jnp.bfloat16)
    up_weight_half = up_grads.astype(jnp.bfloat16)
    up_gradient = adapter_scale * jnp.dot(
        down_weight_half.T, key_gradient, preferred_element_type=jnp.float32
    )
    down_gradient = adapter_scale * jnp.dot(
        acts.T, up_weight_half, preferred_element_type=jnp.float32
    )
    down_gradient, up_gradient = lax.psum((down_gradient, up_gradient), ("dp", "section"))
    squares = jnp.sum(down_gradient * down_gradient) + jnp.sum(up_gradient * up_gradient)
    squares = lax.psum(squares, "fsdp")
    scale_factor = step_rate * jnp.minimum(1.0, clip_norm / jnp.sqrt(squares + 1e-12))
    next_down_weight = adapter_down_weight - scale_factor * down_gradient
    next_up_weight = adapter_up_weight - scale_factor * up_gradient
    local_product = adapter_scale * jnp.dot(
        up_weight_half, first_factor_half.T, preferred_element_type=jnp.float32
    )
    input_gradient = local_product + jnp.dot(
        lax.all_gather(key_gradient, "fsdp", axis=1, tiled=True),
        frozen_key_weight.T,
        preferred_element_type=jnp.float32,
    )
    weight_column_count = lax.all_to_all(
        frozen_key_weight, "fsdp", split_axis=1, concat_axis=0, tiled=True
    )
    down_whole = lax.all_gather(next_down_weight, "fsdp", axis=0, tiled=True)
    weight_change = jnp.dot(down_whole, next_up_weight, precision=lax.Precision.HIGHEST)
    combined_weight = (
        weight_column_count.astype(jnp.float32) + adapter_scale * weight_change
    ).astype(jnp.bfloat16)
    keys = jnp.dot(
        lax.all_gather(prompts, "fsdp", axis=1, tiled=True),
        combined_weight,
        preferred_element_type=jnp.float32,
    )
    return (
        input_gradient.astype(jnp.bfloat16),
        next_down_weight,
        next_up_weight,
        keys.astype(jnp.bfloat16),
    )


def solution(mesh):
    placed = (
        P(("dp", "section"), "fsdp"),
        P(("dp", "section"), "fsdp"),
        P(("dp", "section")),
        P(("dp", "section")),
        P("fsdp", None),
        P("fsdp", None),
        P(None, "fsdp"),
        P(("dp", "section"), "fsdp"),
    )
    return jax.shard_map(
        per_device,
        mesh=mesh,
        in_specs=placed,
        out_specs=(
            P(("dp", "section"), "fsdp"),
            P("fsdp", None),
            P(None, "fsdp"),
            P(("dp", "section"), "fsdp"),
        ),
        check_vma=False,
    )
```

profile of v0, /device:TPU:1, one launch (start us, length us, event | category | flops | bytes accessed | tf_op | source)
XLA Modules:
  0.0 817.1 jit_solution(1927098920436080627)
XLA Ops:
  8.1 0.7 convert_add_fusion
  8.8 0.7 fusion.13
  9.5 1.0 multiply_convert_fusion
  10.6 1.1 fusion.11
  11.6 1.3 fusion.6
  13.0 39.4 %all-reduce.6 = (bf16[512,128]{1,0:T(8,128)(2,1)S(1)}, bf16[512,128]{1,0:T(8,128)(2,1)S(1)}) all-reduce(f32[512,128]{1,0:T(8,128)S(1)} %fusion.11, f32[512,128]{1,0:T(8,128)S(1)} %fusion.6), channel_id=1, replica_groups=mesh['dp'=32,'fsdp'=8,'section'=2] {'fsdp'}, use_global_device_ids=true, to_apply=%region_0.1 | all-reduce | flops 131072 | bytes 786432 | tf_op jit(solution)/shard_map/psum | solution.py:34
  52.3 1.0 fusion.3
  53.4 0.9 convolution_multiply_fusion.3
  54.2 0.0 all-gather.4.cloned.1.call-start
  54.3 0.5 all-gather.4.cloned.1.call-update
  54.8 0.0 all-gather.6.cloned.1.call-start
  54.9 538.7 %all-reduce.5.cloned.1.call-done = (f32[640,128]{0,1:T(8,128)}, f32[128,128]{1,0:T(8,128)}) async-done(((f32[640,128]{0,1:T(8,128)}, f32[128,128]{1,0:T(8,128)}), (f32[640,128]{0,1:T(8,128)}, f32[128,128]{1,0:T(8,128)})) %all-reduce.5.cloned.1.call-update) | async-done | bytes 393232 | tf_op jit(solution)/shard_map/psum | solution.py:43
  593.6 1.5 multiply_reduce_fusion.1
  595.0 1.7 multiply_reduce_fusion
  598.0 0.2 copy.18
  598.2 15.8 %psum.39 = f32[]{:T(128)} all-reduce(f32[]{:T(128)S(6)} %add.25), channel_id=1, replica_groups=mesh['dp'=32,'fsdp'=8,'section'=2] {'fsdp'}, use_global_device_ids=true, to_apply=%region_6.7 | all-reduce | flops 1 | bytes 8 | tf_op jit(solution)/shard_map/psum | solution.py:45
  614.7 1.7 multiply_subtract_fusion
  616.5 0.0 all-gather.8.cloned.1.call-start
  616.5 0.5 all-gather.8.cloned.1.call-update
  617.1 1.5 copy.19
  618.6 3.6 all-to-all-start
  622.2 1.4 convolution_multiply_fusion.1
  623.6 0.9 copy.21
  624.5 3.9 fusion.2
  628.4 8.6 %all-to-all-done = bf16[640,8,128]{0,2,1:T(8,128)(2,1)S(1)} async-done(((bf16[640,8,128]{0,2,1:T(8,128)(2,1)}), bf16[640,8,128]{0,2,1:T(8,128)(2,1)S(1)}, u32[]{:S(2)}, u32[]{:S(2)}) %all-to-all-start) | async-done | bytes 1310752 | tf_op jit(solution)/shard_map/all_to_all | solution.py:57
  636.9 1.7 convert_bitcast_fusion
  638.7 2.1 copy.20
  640.8 49.1 %all-gather.6.cloned.1.call-done = f32[5120,128]{0,1:T(8,128)} async-done(((f32[640,128]{0,1:T(8,128)}), f32[5120,128]{0,1:T(8,128)}) %all-gather.6.cloned.1.call-update) | async-done | bytes 2621456 | tf_op jit(solution)/shard_map/all_gather | solution.py:60
  690.0 7.1 fusion.1
  697.1 106.9 %all-gather.8.cloned.1.call-done = bf16[512,5120]{1,0:T(8,128)(2,1)} async-done(((bf16[512,640]{1,0:T(8,128)(2,1)}), bf16[512,5120]{1,0:T(8,128)(2,1)}) %all-gather.8.cloned.1.call-update) | async-done | bytes 5242896 | tf_op jit(solution)/shard_map/all_gather | solution.py:66
  804.0 4.8 fusion.4
  808.7 0.8 copy.22
  (22 shorter events, 0.2 us)
Async XLA Ops:
  8.0 3.6 copy-start
  8.0 585.6 %all-reduce.5.cloned.1.call-start = ((), (), s32[]{:S(2)}) async-start(), calls=%async_computation.4 | async-start | bytes 786432 | tf_op jit(solution)/shard_map/psum | solution.py:43
  10.5 42.8 %copy-start.3 = (bf16[512,128]{1,0:T(8,128)(2,1)}, bf16[512,128]{1,0:T(8,128)(2,1)S(1)}, u32[]{:S(2)}) copy-start(bf16[512,128]{1,0:T(8,128)(2,1)S(1)} %multiply_convert_fusion) | copy-start | bytes 393220
  52.3 545.7 %copy-start.2 = (f32[640,128]{1,0:T(8,128)S(1)}, f32[640,128]{1,0:T(8,128)}, u32[]{:S(2)}) copy-start(f32[640,128]{1,0:T(8,128)} %param.13) | copy-start | bytes 983044
  54.2 570.3 %all-gather.4.cloned.1.call-start = ((), (), s32[]{:S(2)}) async-start(), calls=%async_computation.1 | async-start | bytes 1179648 | tf_op jit(solution)/shard_map/all_gather | solution.py:53
  54.8 635.1 %all-gather.6.cloned.1.call-start = ((), (), s32[]{:S(2)}) async-start(), calls=%async_computation.2 | async-start | bytes 2949120 | tf_op jit(solution)/shard_map/all_gather | solution.py:60
  598.0 19.0 %copy-start.4 = (bf16[640,1024]{1,0:T(8,128)(2,1)S(1)}, bf16[640,1024]{1,0:T(8,128)(2,1)}, u32[]{:S(2)}) copy-start(bf16[640,1024]{1,0:T(8,128)(2,1)} %param.12) | copy-start | bytes 3932164
  616.5 187.5 %all-gather.8.cloned.1.call-start = ((), (), s32[]{:S(2)}) async-start(), calls=%async_computation.3 | async-start | bytes 5898240 | tf_op jit(solution)/shard_map/all_gather | solution.py:66
  618.6 18.4 %all-to-all-start = ((bf16[640,8,128]{0,2,1:T(8,128)(2,1)}), bf16[640,8,128]{0,2,1:T(8,128)(2,1)S(1)}, u32[]{:S(2)}, u32[]{:S(2)}) async-start(bf16[640,8,128]{0,2,1:T(8,128)(2,1)} %bitcast.1), calls=%async_computation | async-start | bytes 2621440 | tf_op jit(solution)/shard_map/all_to_all | solution.py:57
  622.1 1.4 copy-start.1
  622.2 2.3 copy-start.6
  622.2 2.3 copy-start.7
  624.5 65.5 %copy-start.5 = (f32[128,128]{1,0:T(8,128)}, f32[128,128]{1,0:T(8,128)S(1)}, u32[]{:S(2)}) copy-start(f32[128,128]{1,0:T(8,128)S(1)} %multiply_subtract_fusion.1) | copy-start | bytes 196612
Sparse Core Ops, SparseCore 0:
  54.4 539.1 all-reduce.4
Sparse Core Ops, SparseCore 1:
  57.3 50.0 all-gather.3
  616.6 73.4 all-gather.5
  692.1 111.8 all-gather.7
where the time goes:
time: 818 us; the launch traced here: 817 us
  waiting for transfers between devices  704 us (86%)
  blocking collectives  55.2 us (7%)
  matrix products  21.4 us (3%)
  between operations  17.8 us (2%)
  other arithmetic  9.05 us (1%)
    psum x1, waiting for transfers between devices, per_device(): lax.psum((down_gradient, up_gradient), ('dp', 'section'))  539 us
    all_gather x1, waiting for transfers between devices, per_device(): lax.all_gather(prompts, 'fsdp', axis=1, tiled=True)  107 us
    all_gather x1, waiting for transfers between devices, per_device(): down_whole = lax.all_gather(next_down_weight, 'fsdp', axis=0, tiled=True)  49.1 us
    psum x1, blocking collectives, per_device(): down_acts, up_grads = lax.psum((down_part, up_part), 'fsdp')  39.4 us
  transfers between devices with their start and end apart: 5, of which 4 were waited for; matrix products, arithmetic and copies ran while one was open for 3% of the time, Pallas kernels for 0%

commit v1 on v0

v1 whole, which is shorter than its diff:
```python
import jax
import jax.numpy as jnp
from jax import lax
from jax.experimental import pallas as pl
from jax.experimental.pallas import tpu as pltpu
from jax.sharding import Mesh
from jax.sharding import PartitionSpec as P

adapter_scale = 0.5
step_rate = 16.0
clip_norm = 1.0

AXES = ("zhi", "y", "x", "zlo", "core")
DP = ("zhi", "y")
FSDP = ("x", "zlo")
ROWS = ("zhi", "y", "core")
bf16 = jnp.bfloat16
f32 = jnp.float32


def swap(v, axis):
    return lax.all_to_all(v, axis, 0, 0, tiled=True)


def spread(v, axis, n):
    return swap(jnp.broadcast_to(v[None], (n,) + v.shape).reshape((n * v.shape[0],) + v.shape[1:]), axis)


def base_kernel(p_ref, w_ref, o_ref):
    o_ref[...] = jnp.dot(p_ref[...], w_ref[...], preferred_element_type=f32).astype(bf16)


def base_partials(prompts, weight, n):
    rows, width = prompts.shape
    cols = weight.shape[1] // n
    return pl.pallas_call(
        base_kernel,
        grid=(n,),
        in_specs=[
            pl.BlockSpec((rows, width), lambda k: (0, 0)),
            pl.BlockSpec((width, cols), lambda k: (0, k)),
        ],
        out_specs=pl.BlockSpec((rows, cols), lambda k: (k, 0)),
        out_shape=jax.ShapeDtypeStruct((n * rows, cols), bf16),
        compiler_params=pltpu.CompilerParams(vmem_limit_bytes=32 * 1024 * 1024),
        cost_estimate=pl.CostEstimate(
            flops=2 * rows * width * cols * n, bytes_accessed=4 * 1024 * 1024, transcendentals=0
        ),
    )(prompts, weight)


def per_device(acts, output_gradient, lengths, buckets, frozen, down_w, up_w, prompts):
    rows = acts.shape[0]
    slot = rows // lengths.shape[0]
    n_f = lax.axis_size(FSDP)
    n_d = lax.axis_size(DP)
    core = lax.axis_index("core")
    width, rank = down_w.shape

    alive = jnp.arange(slot, dtype=jnp.int32)[None, :] < lengths[:, None]
    adv = buckets.astype(f32)[:, None] - 1.5
    token_weight = jnp.where(alive, adv, f32(0.0)).reshape(rows)
    gk = (token_weight[:, None] * output_gradient.astype(f32)).astype(bf16)
    gk_full = lax.all_gather(gk, FSDP, axis=1, tiled=True)

    a_half = down_w.astype(bf16)
    b_half = up_w.astype(bf16)
    parts = jnp.concatenate(
        [
            jnp.dot(gk, b_half.T, preferred_element_type=f32),
            jnp.dot(acts, a_half, preferred_element_type=f32),
            jnp.dot(prompts, a_half, preferred_element_type=f32),
        ],
        axis=1,
    )
    base_parts = base_partials(prompts, frozen, n_f)
    keys_base = lax.psum_scatter(base_parts, FSDP, scatter_dimension=0, tiled=True)

    sums = swap(parts, FSDP).reshape(n_f, rows // n_f, 3 * rank).sum(0).astype(bf16)
    full = spread(sums, FSDP, n_f)
    up_half, down_half, p_a = full[:, :rank], full[:, rank : 2 * rank], full[:, 2 * rank :]

    g_down = adapter_scale * jnp.dot(acts.T, up_half, preferred_element_type=f32)
    g_up = adapter_scale * jnp.dot(down_half.T, gk, preferred_element_type=f32)
    g = jnp.concatenate([g_down, g_up], axis=0)
    half = g.shape[0] // 2
    g2 = g.reshape(2, half, g.shape[1])
    other = lax.ppermute(
        lax.dynamic_index_in_dim(g2, 1 - core, 0, keepdims=False), "core", [(0, 1), (1, 0)]
    )
    mine = lax.dynamic_index_in_dim(g2, core, 0, keepdims=False) + other
    part = swap(mine, DP).reshape(n_d, half // n_d, g.shape[1]).sum(0)
    mine = spread(part, DP, n_d)
    other = lax.ppermute(mine, "core", [(0, 1), (1, 0)])
    first = jnp.where(core == 0, mine, other)
    second = jnp.where(core == 0, other, mine)
    g = jnp.concatenate([first, second], axis=0)
    g_down, g_up = g[:width], g[width:]

    sq = jnp.sum(g * g)
    hi = sq.astype(bf16)
    mid = (sq - hi.astype(f32)).astype(bf16)
    low = (sq - hi.astype(f32) - mid.astype(f32)).astype(bf16)
    lanes = jnp.arange(rank)[None, :]
    tail = jnp.where(lanes == 0, hi, jnp.where(lanes == 1, mid, jnp.where(lanes == 2, low, bf16(0))))
    tail = jnp.broadcast_to(tail, (16, rank))
    p_g = jnp.dot(prompts, g_down.astype(bf16), preferred_element_type=f32).astype(bf16)
    got = spread(jnp.concatenate([p_g, tail], axis=0), FSDP, n_f).reshape(n_f, rows + 16, rank)
    p_g = got[:, :rows].astype(f32).sum(0)
    sq = got[:, rows, :3].astype(f32).sum()
    factor = step_rate * jnp.minimum(1.0, clip_norm / jnp.sqrt(sq + 1e-12))
    next_down = down_w - factor * g_down
    next_up = up_w - factor * g_up
    proj = p_a.astype(f32) - factor * p_g
    keys = keys_base.astype(f32) + adapter_scale * jnp.dot(
        proj.astype(bf16), next_up.astype(bf16), preferred_element_type=f32
    )

    input_gradient = adapter_scale * jnp.dot(
        up_half, a_half.T, preferred_element_type=f32
    ) + jnp.dot(gk_full, frozen.T, preferred_element_type=f32)
    return input_gradient.astype(bf16), next_down, next_up, keys.astype(bf16)


def solution(mesh):
    dp, fsdp, section = mesh.devices.shape
    fine = Mesh(mesh.devices.reshape(4, dp // 4, fsdp // 2, 2, section), AXES)
    rows_by_width = P(ROWS, FSDP)
    return jax.shard_map(
        per_device,
        mesh=fine,
        in_specs=(
            rows_by_width,
            rows_by_width,
            P(ROWS),
            P(ROWS),
            P(FSDP, None),
            P(FSDP, None),
            P(None, FSDP),
            rows_by_width,
        ),
        out_specs=(rows_by_width, P(FSDP, None), P(None, FSDP), rows_by_width),
        check_vma=False,
    )
```

time: 818 us -> 195 us (0.24)
  the two profiles are of different devices: /device:TPU:1 before, /device:TPU:8 now
where the time goes in v1:
time: 195 us; the launch traced here: 194 us
  waiting for transfers between devices  87.6 us (45%)
  blocking collectives  49 us (25%)
  between operations  16.4 us (8%)
  starting transfers between devices  15.9 us (8%)
  matrix products  10.6 us (5%)
  other arithmetic  5.31 us (3%)
  local copies, waits for them, and re-layouts  4.9 us (3%)
  Pallas kernels  4.56 us (2%)
    all_to_all x2, blocking collectives, swap(): return lax.all_to_all(v, axis, 0, 0, tiled=True)  49 us
    reduce_scatter x1, waiting for transfers between devices, per_device(): lax.psum_scatter(base_parts, FSDP, scatter_dimension=0, tiled=True)  40.7 us
    all_gather x1, waiting for transfers between devices, per_device(): gk_full = lax.all_gather(gk, FSDP, axis=1, tiled=True)  22 us
    all_to_all x3, waiting for transfers between devices, swap(): return lax.all_to_all(v, axis, 0, 0, tiled=True)  21.6 us
    all_to_all x3, starting transfers between devices, swap(): return lax.all_to_all(v, axis, 0, 0, tiled=True)  11.9 us
    pallas_call x1, Pallas kernels, base_partials(): pl.pallas_call(base_kernel, grid=(n,), in_specs=[pl.BlockSpec((rows, widt...  4.56 us
  transfers between devices with their start and end apart: 7, of which 6 were waited for; matrix products, arithmetic and copies ran while one was open for 6% of the time, Pallas kernels for 2%

profile of v1, /device:TPU:8, one launch (start us, length us, event | category | flops | bytes accessed | tf_op | source)
XLA Modules:
  0.0 194.2 jit_solution(2082781948360434106)
XLA Ops:
  7.2 0.7 convert_add_fusion
  7.9 0.7 fusion.19
  8.7 1.5 fusion.22
  10.3 0.4 fusion.24
  11.3 18.9 %all_to_all.42 = f32[8,64,384]{2,1,0:T(8,128)S(1)} all-to-all(f32[8,64,384]{2,1,0:T(8,128)S(1)} %bitcast.22), channel_id=1, replica_groups=mesh['zhi'=4,'y'=8,'x'=4,'zlo'=2,'core'=2] {'x','zlo'}, dimensions={0} | all-to-all | bytes 1572864 | tf_op jit(solution)/shard_map/all_to_all | solution.py:22
  30.2 0.8 broadcast_in_dim.56
  31.0 3.5 %all-to-all-start.1 = ((bf16[8,64,384]{2,1,0:T(8,128)(2,1)}), bf16[8,64,384]{2,1,0:T(8,128)(2,1)S(1)}, u32[]{:S(2)}, u32[]{:S(2)}) async-start(bf16[8,64,384]{2,1,0:T(8,128)(2,1)} %broadcast_in_dim.56), calls=%async_computation.1 | async-start | bytes 786432 | tf_op jit(solution)/shard_map/all_to_all | solution.py:22
  34.5 7.9 %all-to-all-done.1 = bf16[8,64,384]{2,1,0:T(8,128)(2,1)S(1)} async-done(((bf16[8,64,384]{2,1,0:T(8,128)(2,1)}), bf16[8,64,384]{2,1,0:T(8,128)(2,1)S(1)}, u32[]{:S(2)}, u32[]{:S(2)}) %all-to-all-start.1) | async-done | bytes 393248 | tf_op jit(solution)/shard_map/all_to_all | solution.py:22
  43.2 0.3 constant_dynamic-slice_fusion.1
  43.7 1.9 collective-permute-start
  45.8 1.2 collective-permute-done
  47.1 30.1 %all_to_all.43 = f32[32,12,128]{2,1,0:T(8,128)S(1)} all-to-all(f32[32,12,128]{2,1,0:T(8,128)S(1)} %all_to_all.32), channel_id=1, replica_groups=mesh['zhi'=4,'y'=8,'x'=4,'zlo'=2,'core'=2] {'zhi','y'}, dimensions={0} | all-to-all | bytes 393216 | tf_op jit(solution)/shard_map/all_to_all | solution.py:22
  77.3 0.7 broadcast_in_dim.57
  78.0 4.1 %all-to-all-start.3 = ((f32[32,12,128]{2,1,0:T(8,128)}), f32[32,12,128]{2,1,0:T(8,128)S(1)}, u32[]{:S(2)}, u32[]{:S(2)}) async-start(f32[32,12,128]{2,1,0:T(8,128)} %broadcast_in_dim.57), calls=%async_computation.3 | async-start | bytes 524288 | tf_op jit(solution)/shard_map/all_to_all | solution.py:22
  82.2 0.7 all-gather.2.cloned.1.call-update
  82.9 13.7 %all-to-all-done.3 = f32[32,12,128]{2,1,0:T(8,128)S(1)} async-done(((f32[32,12,128]{2,1,0:T(8,128)}), f32[32,12,128]{2,1,0:T(8,128)S(1)}, u32[]{:S(2)}, u32[]{:S(2)}) %all-to-all-start.3) | async-done | bytes 196640 | tf_op jit(solution)/shard_map/all_to_all | solution.py:22
  96.6 1.9 collective-permute-start.1
  98.5 1.4 collective-permute-done.1
  99.9 0.7 fusion.6
  102.0 0.4 fusion.4
  102.6 1.2 broadcast_in_dim.63
  103.7 4.4 %all-to-all-start.4 = ((bf16[8,528,128]{2,1,0:T(8,128)(2,1)}), bf16[8,528,128]{2,1,0:T(8,128)(2,1)}, u32[]{:S(2)}, u32[]{:S(2)}) async-start(bf16[8,528,128]{2,1,0:T(8,128)(2,1)} %broadcast_in_dim.63), calls=%async_computation.4 | async-start | bytes 2162688 | tf_op jit(solution)/shard_map/all_to_all | solution.py:22
  108.2 4.6 %shard_map.111 = bf16[4096,128]{1,0:T(8,128)(2,1)} custom-call(bf16[512,640]{1,0:T(8,128)(2,1)S(1)} %copy-done.1, bf16[640,1024]{1,0:T(8,128)(2,1)S(1)} %copy-done.2), custom_call_target="tpu_custom_call" | custom-call | flops 671088640 | bytes 4194304 | tf_op jit(solution)/shard_map/pallas_call | solution.py:36
  112.8 2.3 %convolution_multiply_fusion = f32[512,640]{1,0:T(8,128)} fusion(bf16[512,384]{1,0:T(8,128)(2,1)} %bitcast.25, f32[640,128]{1,0:T(8,128)S(1)} %copy-done.3), kind=kOutput, calls=%fused_computation.2 | convolution fusion | flops 84295680 | bytes 1769472 | tf_op jit(solution)/shard_map/dot_general | solution.py:119
  115.1 22.0 %all-gather.2.cloned.1.call-done = bf16[512,1024]{1,0:T(8,128)(2,1)} async-done(((bf16[512,128]{1,0:T(8,128)(2,1)}), bf16[512,1024]{1,0:T(8,128)(2,1)}) %all-gather.2.cloned.1.call-update) | async-done | bytes 1048592 | tf_op jit(solution)/shard_map/all_gather | solution.py:64
  137.0 3.5 %fusion = bf16[512,640]{1,0:T(8,128)(2,1)} fusion(f32[512,640]{1,0:T(8,128)} %convolution_multiply_fusion, bf16[512,1024]{1,0:T(8,128)(2,1)} %all-gather.2.cloned.1.call-done, bf16[640,1024]{1,0:T(8,128)(2,1)S(1)} %copy-done.2), kind=kOutput, calls=%fused_computation.3 | convolution fusion | flops 671744000 | bytes 4325376 | tf_op jit(solution)/shard_map/dot_general | solution.py:121
  140.5 0.7 slice.32
  141.4 0.6 convert_reduce_fusion.1
  142.7 1.4 convert_reduce_fusion
  144.1 0.8 multiply_subtract_fusion
  144.9 40.7 %reduce-scatter.2.cloned.1.call-done = bf16[512,128]{1,0:T(8,128)(2,1)} async-done(((bf16[4096,128]{1,0:T(8,128)(2,1)}), bf16[512,128]{1,0:T(8,128)(2,1)}) %reduce-scatter.2.cloned.1.call-update) | async-done | bytes 131088 | tf_op jit(solution)/shard_map/reduce_scatter | solution.py:77
  185.5 1.8 fusion.3
  (45 shorter events, 2.4 us)
Async XLA Ops:
  7.2 3.1 %copy-start = (bf16[512,640]{1,0:T(8,128)(2,1)S(1)}, bf16[512,640]{1,0:T(8,128)(2,1)}, u32[]{:S(2)}) copy-start(bf16[512,640]{1,0:T(8,128)(2,1)} %param.8) | copy-start | bytes 1966084
  7.2 3.1 %copy-start.3 = (f32[640,128]{1,0:T(8,128)S(1)}, f32[640,128]{1,0:T(8,128)}, u32[]{:S(2)}) copy-start(f32[640,128]{1,0:T(8,128)} %param.13) | copy-start | bytes 983044
  7.2 3.4 %copy-start.8 = (bf16[512,128]{1,0:T(8,128)(2,1)S(1)}, bf16[512,128]{1,0:T(8,128)(2,1)}, u32[]{:S(2)}) copy-start(bf16[512,128]{1,0:T(8,128)(2,1)} %param.9) | copy-start | bytes 393220
  8.7 2.1 %copy-start.6 = (f32[128,128]{1,0:T(8,128)S(1)}, f32[128,128]{1,0:T(8,128)}, u32[]{:S(2)}) copy-start(f32[128,128]{1,0:T(8,128)} %param.14) | copy-start | bytes 196612
  10.8 31.7 %copy-start.5 = (bf16[512,128]{1,0:T(8,128)(2,1)}, bf16[512,128]{1,0:T(8,128)(2,1)S(1)}, u32[]{:S(2)}) copy-start(bf16[512,128]{1,0:T(8,128)(2,1)S(1)} %multiply_convert_fusion) | copy-start | bytes 393220
  31.0 11.4 %all-to-all-start.1 = ((bf16[8,64,384]{2,1,0:T(8,128)(2,1)}), bf16[8,64,384]{2,1,0:T(8,128)(2,1)S(1)}, u32[]{:S(2)}, u32[]{:S(2)}) async-start(bf16[8,64,384]{2,1,0:T(8,128)(2,1)} %broadcast_in_dim.56), calls=%async_computation.1 | async-start | bytes 786432 | tf_op jit(solution)/shard_map/all_to_all | solution.py:22
  42.4 0.8 copy-start.4
  43.7 3.3 %collective-permute-start = (f32[384,128]{1,0:T(8,128)S(1)}, f32[384,128]{1,0:T(8,128)S(1)}, u32[]{:S(2)}, u32[]{:S(2)}) collective-permute-start(f32[384,128]{1,0:T(8,128)S(1)} %bitcast.27), channel_id=1, source_target_pairs={{0,1},{1,0},{2,3},{3,2},{4,5},{5,4},{6,7},{7,6},{8,9},{9,8},{10,11... | collective-permute-start | bytes 589832 | tf_op jit(solution)/shard_map/ppermute | solution.py:88
  77.3 24.7 %copy-start.1 = (bf16[512,640]{1,0:T(8,128)(2,1)S(1)}, bf16[512,640]{1,0:T(8,128)(2,1)}, u32[]{:S(2)}) copy-start(bf16[512,640]{1,0:T(8,128)(2,1)} %p_ref.1) | copy-start | bytes 1966084
  78.0 18.5 %all-to-all-start.3 = ((f32[32,12,128]{2,1,0:T(8,128)}), f32[32,12,128]{2,1,0:T(8,128)S(1)}, u32[]{:S(2)}, u32[]{:S(2)}) async-start(f32[32,12,128]{2,1,0:T(8,128)} %broadcast_in_dim.57), calls=%async_computation.3 | async-start | bytes 524288 | tf_op jit(solution)/shard_map/all_to_all | solution.py:22
  82.1 54.9 %all-gather.2.cloned.1.call-start = ((), (), s32[]{:S(2)}) async-start(), calls=%async_computation.6 | async-start | bytes 1179648 | tf_op jit(solution)/shard_map/all_gather | solution.py:64
  96.6 3.3 %collective-permute-start.1 = (f32[384,128]{1,0:T(8,128)S(1)}, f32[384,128]{1,0:T(8,128)S(1)}, u32[]{:S(2)}, u32[]{:S(2)}) collective-permute-start(f32[384,128]{1,0:T(8,128)S(1)} %all_to_all.35), channel_id=1, source_target_pairs={{0,1},{1,0},{2,3},{3,2},{4,5},{5,4},{6,7},{7,6},{8,9},{9,8},{10,11... | collective-permute-start | bytes 589832 | tf_op jit(solution)/shard_map/ppermute | solution.py:94
  103.7 4.4 %copy-start.2 = (bf16[640,1024]{1,0:T(8,128)(2,1)S(1)}, bf16[640,1024]{1,0:T(8,128)(2,1)}, u32[]{:S(2)}) copy-start(bf16[640,1024]{1,0:T(8,128)(2,1)} %w_ref.1) | copy-start | bytes 3932164
  103.7 36.8 %all-to-all-start.4 = ((bf16[8,528,128]{2,1,0:T(8,128)(2,1)}), bf16[8,528,128]{2,1,0:T(8,128)(2,1)}, u32[]{:S(2)}, u32[]{:S(2)}) async-start(bf16[8,528,128]{2,1,0:T(8,128)(2,1)} %broadcast_in_dim.63), calls=%async_computation.4 | async-start | bytes 2162688 | tf_op jit(solution)/shard_map/all_to_all | solution.py:22
  108.1 77.4 %reduce-scatter.2.cloned.1.call-start = ((), (), s32[]{:S(2)}) async-start(), calls=%async_computation.7 | async-start | bytes 1179648 | tf_op jit(solution)/shard_map/reduce_scatter | solution.py:77
  144.1 43.3 %copy-start.7 = (f32[128,128]{1,0:T(8,128)}, f32[128,128]{1,0:T(8,128)S(1)}, u32[]{:S(2)}) copy-start(f32[128,128]{1,0:T(8,128)S(1)} %fusion.14) | copy-start | bytes 196612
Sparse Core Ops, SparseCore 0:
  85.5 51.4 all-gather.1
  139.9 45.6 reduce-scatter.1

commit v2 on v1

v2 whole, which is shorter than its diff:
```python
import jax
import jax.numpy as jnp
from jax import lax
from jax.experimental import pallas as pl
from jax.experimental.pallas import tpu as pltpu
from jax.sharding import Mesh
from jax.sharding import PartitionSpec as P

adapter_scale = 0.5
step_rate = 16.0
clip_norm = 1.0

AXES = ("zhi", "y", "x", "zlo", "core")
FSDP = ("x", "zlo")
ROWS = ("zhi", "y", "core")
NEAR = ("y", "core")
FAR = "zhi"
TAIL = 16
bf16 = jnp.bfloat16
f32 = jnp.float32

NT = (((1,), (1,)), ((), ()))
TN = (((0,), (0,)), ((), ()))


def dot(a, b, dims=(((1,), (0,)), ((), ()))):
    return lax.dot_general(a, b, dims, preferred_element_type=f32)


def swap(v, axis):
    return lax.all_to_all(v, axis, 0, 0, tiled=True)


VMEM = None
SMEM = pl.BlockSpec(memory_space=pltpu.SMEM)
ANY = pl.BlockSpec(memory_space=pl.ANY)


def block(v):
    zeros = (0,) * len(v.shape)
    return pl.BlockSpec(v.shape, lambda i: zeros)


def call(kernel, outs, ins, args, flops=0, out_specs=None, **more):
    moved = sum(a.size * a.dtype.itemsize for a in args) + sum(
        o.size * o.dtype.itemsize for o in outs
    )
    return pl.pallas_call(
        kernel,
        grid=(1,),
        in_specs=[spec or block(a) for spec, a in zip(ins, args, strict=True)],
        out_specs=out_specs or tuple(block(o) for o in outs),
        out_shape=tuple(outs),
        compiler_params=pltpu.CompilerParams(vmem_limit_bytes=40 * 1024 * 1024),
        cost_estimate=pl.CostEstimate(flops=flops, bytes_accessed=moved, transcendentals=0),
        **more,
    )(*args)


def shape(dims, kind):
    return jax.ShapeDtypeStruct(dims, kind)


def parts_kernel(lens, buckets, acts, og, down_w, up_w, prompts, gk_ref, pay_ref):
    rows = acts.shape[0]
    seqs = lens.shape[0]
    slot = rows // seqs
    peers = pay_ref.shape[0]
    piece = rows // peers
    place = lax.broadcasted_iota(jnp.int32, (slot, 1), 0)
    for s in range(seqs):
        here = pl.ds(s * slot, slot)
        weight = jnp.where(place < lens[s], buckets[s].astype(f32) - 1.5, f32(0.0))
        gk_ref[here, :] = (weight * og[here, :].astype(f32)).astype(bf16)
    gk = gk_ref[...]
    a_half = down_w[...].astype(bf16)
    up = dot(gk, up_w[...].astype(bf16), NT).astype(bf16)
    down = dot(acts[...], a_half).astype(bf16)
    proj = dot(prompts[...], a_half).astype(bf16)
    for j in range(peers):
        here = slice(j * piece, (j + 1) * piece)
        pay_ref[j, 0:piece, :] = up[here]
        pay_ref[j, piece : 2 * piece, :] = down[here]
        pay_ref[j, 2 * piece : 3 * piece, :] = proj[here]
        pay_ref[j, 3 * piece :, :] = gk


def base_kernel(prompts, frozen, pay_ref):
    peers, long, cols = pay_ref.shape
    rows = prompts.shape[0]
    base = dot(prompts[...], frozen[...]).astype(bf16)
    for j in range(peers):
        pay_ref[j, long - rows :, :] = base[:, j * cols : (j + 1) * cols]


def sums_kernel(got_ref, pay_in, pay_ref, sums_ref, sems):
    del pay_in
    peers = got_ref.shape[0]
    part = sums_ref.shape[0]
    total = got_ref[0, :part, :].astype(f32)
    for j in range(1, peers):
        total += got_ref[j, :part, :].astype(f32)
    sums_ref[...] = total.astype(bf16)
    copies = [
        pltpu.make_async_copy(sums_ref, pay_ref.at[j, pl.ds(0, part), :], sems.at[j])
        for j in range(peers)
    ]
    for c in copies:
        c.start()
    for c in copies:
        c.wait()


def rejoin(got_ref, first, piece):
    return jnp.concatenate(
        [got_ref[j, first : first + piece, :] for j in range(got_ref.shape[0])], axis=0
    )


def grads_kernel(got_ref, acts, gk, pay_ref):
    rows = acts.shape[0]
    piece = rows // got_ref.shape[0]
    lanes = gk.shape[1]
    up = rejoin(got_ref, 0, piece)
    down = rejoin(got_ref, piece, piece)
    g = adapter_scale * jnp.concatenate([dot(up, acts[...], TN), dot(down, gk[...], TN)], axis=1)
    peers = pay_ref.shape[0]
    step = g.shape[0] // peers
    for j in range(peers):
        pay_ref[j] = jnp.concatenate(
            [
                g[j * step : (j + 1) * step, c * lanes : (c + 1) * lanes]
                for c in range(g.shape[1] // lanes)
            ],
            axis=0,
        ).astype(pay_ref.dtype)


def add_kernel(got_ref, pay_ref):
    total = got_ref[0].astype(f32)
    for j in range(1, got_ref.shape[0]):
        total += got_ref[j].astype(f32)
    total = total.astype(pay_ref.dtype)
    for j in range(pay_ref.shape[0]):
        pay_ref[j] = total


def whole_gradient(got_ref, rank):
    peers, long, _ = got_ref.shape
    step = rank // peers
    got = [got_ref[j].astype(f32) for j in range(peers)]
    return [
        jnp.concatenate([v[c * step : (c + 1) * step] for v in got], axis=0)
        for c in range(long // step)
    ]


def project_kernel(got_ref, prompts, pay_ref):
    rank = pay_ref.shape[2]
    rows = prompts.shape[0]
    blocks = whole_gradient(got_ref, rank)
    squares = sum(b * b for b in blocks)
    total = jnp.sum(squares, keepdims=True)
    high = total.astype(bf16)
    rest = total - high.astype(f32)
    middle = rest.astype(bf16)
    low = (rest - middle.astype(f32)).astype(bf16)
    lane = lax.broadcasted_iota(jnp.int32, (TAIL, rank), 1)
    tail = jnp.where(
        lane == 0,
        high.astype(f32),
        jnp.where(lane == 1, middle.astype(f32), jnp.where(lane == 2, low.astype(f32), 0.0)),
    ).astype(bf16)
    g_down = jnp.concatenate(blocks[:-1], axis=1).astype(bf16)
    proj = dot(prompts[...], g_down, NT).astype(bf16)
    for j in range(pay_ref.shape[0]):
        pay_ref[j, :rows, :] = proj
        pay_ref[j, rows:, :] = tail


def finish_kernel(got, got_base, got_g, down_w, up_w, next_down, next_up, keys):
    rows = keys.shape[0]
    rank = down_w.shape[1]
    peers = got.shape[0]
    piece = rows // peers
    lane = lax.broadcasted_iota(jnp.int32, (TAIL, rank), 1)
    place = lax.broadcasted_iota(jnp.int32, (TAIL, rank), 0)
    p_g = got[0, :rows, :].astype(f32)
    tail = got[0, rows:, :].astype(f32)
    base = got_base[0, 3 * piece :, :].astype(f32)
    for j in range(1, peers):
        p_g += got[j, :rows, :].astype(f32)
        tail += got[j, rows:, :].astype(f32)
        base += got_base[j, 3 * piece :, :].astype(f32)
    squares = jnp.sum(jnp.where((place == 0) & (lane < 3), tail, 0.0), keepdims=True)
    factor = step_rate * jnp.minimum(1.0, clip_norm / jnp.sqrt(squares + 1e-12))
    blocks = whole_gradient(got_g, rank)
    for c, block in enumerate(blocks[:-1]):
        here = pl.ds(c * rank, rank)
        next_down[here, :] = down_w[here, :] - factor * block.T
    new_up = up_w[...] - factor * blocks[-1]
    next_up[...] = new_up
    proj = rejoin(got_base, 2 * piece, piece).astype(f32) - factor * p_g
    keys[...] = (base + adapter_scale * dot(proj.astype(bf16), new_up.astype(bf16))).astype(bf16)


def input_kernel(got_gk, got_up, down_w, frozen, out):
    rows = out.shape[0]
    piece = rows // got_up.shape[0]
    gk = jnp.concatenate([got_gk[j, 3 * piece :, :] for j in range(got_gk.shape[0])], axis=1)
    up = rejoin(got_up, 0, piece)
    a_half = down_w[...].astype(bf16)
    out[...] = (dot(gk, frozen[...], NT) + adapter_scale * dot(up, a_half, NT)).astype(bf16)


def per_device(acts, output_gradient, lengths, buckets, frozen, down_w, up_w, prompts):
    rows = acts.shape[0]
    width, rank = down_w.shape
    cols = up_w.shape[1]
    n_f = lax.axis_size(FSDP)
    n_near = lax.axis_size(NEAR)
    n_far = lax.axis_size(FAR)
    piece = rows // n_f
    long = 3 * piece + rows
    slab = (width + cols) // n_near

    gk, pay = call(
        parts_kernel,
        [shape((rows, cols), bf16), shape((n_f, long, rank), bf16)],
        [SMEM, SMEM] + [VMEM] * 5,
        (lengths, buckets, acts, output_gradient, down_w, up_w, prompts),
        flops=2 * rows * rank * (2 * width + cols),
    )
    got_gk = swap(pay, FSDP)
    (pay,) = call(
        base_kernel,
        [shape((n_f, long, cols), bf16)],
        [VMEM, VMEM],
        (prompts, frozen),
        flops=2 * rows * width * cols * n_f,
    )
    (pay,) = call(
        sums_kernel,
        [shape((n_f, long, cols), bf16)],
        [VMEM, ANY],
        (got_gk, pay),
        input_output_aliases={1: 0},
        out_specs=(ANY,),
        scratch_shapes=[pltpu.VMEM((3 * piece, rank), bf16), pltpu.SemaphoreType.DMA((n_f,))],
    )
    got_base = swap(pay, FSDP)

    (pay,) = call(
        grads_kernel,
        [shape((n_near, slab, rank), bf16)],
        [VMEM] * 3,
        (got_base, acts, gk),
        flops=2 * rows * rank * (width + cols),
    )
    got = swap(pay, NEAR)
    (input_gradient,) = call(
        input_kernel,
        [shape((rows, width), bf16)],
        [VMEM] * 4,
        (got_gk, got_base, down_w, frozen),
        flops=2 * rows * width * (cols * n_f + rank),
    )
    (pay,) = call(add_kernel, [shape((n_far, slab, rank), bf16)], [VMEM], (got,))
    got = swap(pay, FAR)
    (pay,) = call(add_kernel, [shape((n_near, slab, rank), bf16)], [VMEM], (got,))
    got_g = swap(pay, NEAR)
    (pay,) = call(
        project_kernel,
        [shape((n_f, rows + TAIL, rank), bf16)],
        [VMEM] * 2,
        (got_g, prompts),
        flops=2 * rows * width * rank,
    )
    got = swap(pay, FSDP)
    next_down, next_up, keys = call(
        finish_kernel,
        [shape((width, rank), f32), shape((rank, cols), f32), shape((rows, cols), bf16)],
        [VMEM] * 5,
        (got, got_base, got_g, down_w, up_w),
        flops=2 * rows * rank * cols,
    )
    return input_gradient, next_down, next_up, keys


def solution(mesh):
    dp, fsdp, section = mesh.devices.shape
    fine = Mesh(mesh.devices.reshape(4, dp // 4, fsdp // 2, 2, section), AXES)
    rows_by_width = P(ROWS, FSDP)
    return jax.shard_map(
        per_device,
        mesh=fine,
        in_specs=(
            rows_by_width,
            rows_by_width,
            P(ROWS),
            P(ROWS),
            P(FSDP, None),
            P(FSDP, None),
            P(None, FSDP),
            rows_by_width,
        ),
        out_specs=(rows_by_width, P(FSDP, None), P(None, FSDP), rows_by_width),
        check_vma=False,
    )
```

time: 195 us -> 135 us (0.69)
  the two profiles are of different devices: /device:TPU:8 before, /device:TPU:1 now
where the time goes in v2:
time: 135 us
  blocking collectives  75 us (56%)
  waiting for transfers between devices  27.1 us (20%)
  local copies, waits for them, and re-layouts  11.6 us (9%)
  starting transfers between devices  11.2 us (8%)
  Pallas kernels  9.01 us (7%)
    all_to_all x4, blocking collectives, swap(): return lax.all_to_all(v, axis, 0, 0, tiled=True)  75 us
    all_to_all x2, waiting for transfers between devices, swap(): return lax.all_to_all(v, axis, 0, 0, tiled=True)  27.1 us
    unnamed x36, local copies, waits for them, and re-layouts  11.6 us
    all_to_all x2, starting transfers between devices, swap(): return lax.all_to_all(v, axis, 0, 0, tiled=True)  11.2 us
    pallas_call x9, Pallas kernels, call(): pl.pallas_call(kernel, grid=(1,), in_specs=[spec or block(a) for spec, a...  9.01 us
  transfers between devices with their start and end apart: 2, of which 2 were waited for; matrix products, arithmetic and copies ran while one was open for 0% of the time, Pallas kernels for 2%

profile of v2, /device:TPU:1, one launch (start us, length us, event | category | flops | bytes accessed | tf_op | source)
XLA Modules:
  0.0 134.6 jit_solution(8319734209881585545)
XLA Ops:
  0.6 0.0 copy-start.2
  0.6 1.1 copy-done.2
  1.7 1.0 copy-done.7
  2.7 1.1 copy-done.9
  3.8 0.8 copy-done.11
  4.6 0.9 copy-done.13
  5.5 0.7 copy-done.16
  6.2 0.7 copy-done.17
  6.8 2.3 %shard_map.111 = (bf16[512,128]{1,0:T(8,128)(2,1)S(1)}, bf16[8,704,128]{2,1,0:T(8,128)(2,1)}) custom-call(s32[2]{0:T(128)S(1)} %copy-done.16, s32[2]{0:T(128)S(1)} %copy-done.17, bf16[512,640]{1,0:T(8,128)(2,1)S(1)} %copy-done.9, bf16[512,128]{1,0:T(8,128)(2,1)S(1)} %copy-done.13, f32[640,128]{1,0:T(8,128)S(1)} %copy-done.7, f32[128,128]{1,0:T(8,128)S(1)} %copy-done.11, ...), custom_call_target="tpu_custom_call" | custom-call | flops 184549376 | bytes 3407888 | tf_op jit(solution)/shard_map/pallas_call | solution.py:48
  9.2 0.7 copy-done.14
  9.8 6.8 %all-to-all-start = ((bf16[8,704,128]{2,1,0:T(8,128)(2,1)}), bf16[8,704,128]{2,1,0:T(8,128)(2,1)S(1)}, u32[]{:S(2)}, u32[]{:S(2)}) async-start(bf16[8,704,128]{2,1,0:T(8,128)(2,1)} %get-tuple-element.9), calls=%async_computation | async-start | bytes 2883584 | tf_op jit(solution)/shard_map/all_to_all | solution.py:31
  16.6 0.0 copy-start.4
  16.6 1.3 copy-done.4
  17.9 1.0 shard_map.112.pay_in
  18.9 14.0 %all-to-all-done.got_ref.got_gk = bf16[8,704,128]{2,1,0:T(8,128)(2,1)S(1)} async-done(((bf16[8,704,128]{2,1,0:T(8,128)(2,1)}), bf16[8,704,128]{2,1,0:T(8,128)(2,1)S(1)}, u32[]{:S(2)}, u32[]{:S(2)}) %all-to-all-start) | async-done | bytes 1441824 | tf_op jit(solution)/shard_map/all_to_all | solution.py:31
  32.9 0.6 shard_map.113
  33.6 0.0 copy-start
  33.6 1.1 copy-done
  34.7 20.4 %all_to_all.30.got_up.got_ref.got_base = bf16[8,704,128]{2,1,0:T(8,128)(2,1)S(1)} all-to-all(bf16[8,704,128]{2,1,0:T(8,128)(2,1)S(1)} %shard_map.113), channel_id=1, replica_groups=mesh['zhi'=4,'y'=8,'x'=4,'zlo'=2,'core'=2] {'x','zlo'}, dimensions={0} | all-to-all | bytes 2883584 | tf_op jit(solution)/shard_map/all_to_all | solution.py:31
  55.1 0.0 copy-done.15
  55.1 0.3 shard_map.115
  55.4 24.3 %all_to_all.31.got_ref = bf16[16,48,128]{2,1,0:T(8,128)(2,1)S(1)} all-to-all(bf16[16,48,128]{2,1,0:T(8,128)(2,1)S(1)} %shard_map.115), channel_id=1, replica_groups=mesh['zhi'=4,'y'=8,'x'=4,'zlo'=2,'core'=2] {'y','core'}, dimensions={0} | all-to-all | bytes 393216 | tf_op jit(solution)/shard_map/all_to_all | solution.py:31
  79.8 15.7 %all_to_all.32.got_ref = bf16[4,48,128]{2,1,0:T(8,128)(2,1)S(1)} all-to-all(bf16[4,48,128]{2,1,0:T(8,128)(2,1)S(1)} %shard_map.116), channel_id=1, replica_groups=mesh['zhi'=4,'y'=8,'x'=4,'zlo'=2,'core'=2] {'zhi'}, dimensions={0} | all-to-all | bytes 98304 | tf_op jit(solution)/shard_map/all_to_all | solution.py:31
  95.5 14.5 %all_to_all.33.got_ref.got_g = bf16[16,48,128]{2,1,0:T(8,128)(2,1)S(1)} all-to-all(bf16[16,48,128]{2,1,0:T(8,128)(2,1)S(1)} %shard_map.117), channel_id=1, replica_groups=mesh['zhi'=4,'y'=8,'x'=4,'zlo'=2,'core'=2] {'y','core'}, dimensions={0} | all-to-all | bytes 393216 | tf_op jit(solution)/shard_map/all_to_all | solution.py:31
  110.1 0.3 shard_map.118
  110.4 1.0 copy-done.6
  111.4 4.4 %all-to-all-start.5 = ((bf16[8,528,128]{2,1,0:T(8,128)(2,1)}), bf16[8,528,128]{2,1,0:T(8,128)(2,1)}, u32[]{:S(2)}, u32[]{:S(2)}) async-start(bf16[8,528,128]{2,1,0:T(8,128)(2,1)} %copy-done.6), calls=%async_computation.5 | async-start | bytes 2162688 | tf_op jit(solution)/shard_map/all_to_all | solution.py:31
  115.8 0.0 copy-start.5
  115.8 1.3 copy-done.5
  117.1 2.0 %shard_map.114 = bf16[512,640]{1,0:T(8,128)(2,1)} custom-call(bf16[8,704,128]{2,1,0:T(8,128)(2,1)S(1)} %copy-done.1, bf16[8,704,128]{2,1,0:T(8,128)(2,1)S(1)} %all_to_all.30.got_up.got_ref.got_base, f32[640,128]{1,0:T(8,128)S(1)} %copy-done.8, bf16[640,1024]{1,0:T(8,128)(2,1)S(1)} %copy-done.5), custom_call_target="tpu_custom_call" | custom-call | flops 754974720 | bytes 5177344 | tf_op jit(solution)/shard_map/pallas_call | solution.py:48
  119.1 13.2 %all-to-all-done.5.got = bf16[8,528,128]{2,1,0:T(8,128)(2,1)} async-done(((bf16[8,528,128]{2,1,0:T(8,128)(2,1)}), bf16[8,528,128]{2,1,0:T(8,128)(2,1)}, u32[]{:S(2)}, u32[]{:S(2)}) %all-to-all-start.5) | async-done | bytes 1081376 | tf_op jit(solution)/shard_map/all_to_all | solution.py:31
  132.3 2.4 %shard_map.119 = (f32[640,128]{1,0:T(8,128)}, f32[128,128]{1,0:T(8,128)}, bf16[512,128]{1,0:T(8,128)(2,1)}) custom-call(bf16[8,528,128]{2,1,0:T(8,128)(2,1)} %all-to-all-done.5.got, bf16[8,704,128]{2,1,0:T(8,128)(2,1)S(1)} %all_to_all.30.got_up.got_ref.got_base, bf16[16,48,128]{2,1,0:T(8,128)(2,1)S(1)} %all_to_all.33.got_ref.got_g, ...), custom_call_target="tpu_custom_call" | custom-call | flops 16777216 | bytes 3637248 | tf_op jit(solution)/shard_map/pallas_call | solution.py:48
  (21 shorter events, 0.1 us)
Async XLA Ops:
  0.6 1.1 copy-start.2
  1.7 1.0 copy-start.7
  2.7 1.1 copy-start.9
  3.8 0.8 copy-start.11
  4.6 0.9 copy-start.13
  5.5 0.7 copy-start.16
  6.2 0.7 copy-start.17
  9.2 0.7 copy-start.14
  9.8 6.8 %copy-start.3 = (bf16[512,640]{1,0:T(8,128)(2,1)S(1)}, bf16[512,640]{1,0:T(8,128)(2,1)}, u32[]{:S(2)}) copy-start(bf16[512,640]{1,0:T(8,128)(2,1)} %prompts.5) | copy-start | bytes 1966084
  9.8 23.1 %all-to-all-start = ((bf16[8,704,128]{2,1,0:T(8,128)(2,1)}), bf16[8,704,128]{2,1,0:T(8,128)(2,1)S(1)}, u32[]{:S(2)}, u32[]{:S(2)}) async-start(bf16[8,704,128]{2,1,0:T(8,128)(2,1)} %get-tuple-element.9), calls=%async_computation | async-start | bytes 2883584 | tf_op jit(solution)/shard_map/all_to_all | solution.py:31
  16.6 1.3 copy-start.4
  33.6 1.1 copy-start
  34.7 20.4 %copy-start.10 = (bf16[512,640]{1,0:T(8,128)(2,1)S(1)}, bf16[512,640]{1,0:T(8,128)(2,1)}, u32[]{:S(2)}) copy-start(bf16[512,640]{1,0:T(8,128)(2,1)} %acts.3) | copy-start | bytes 1966084
  34.7 20.4 %copy-start.15 = (bf16[512,128]{1,0:T(8,128)(2,1)S(1)}, bf16[512,128]{1,0:T(8,128)(2,1)}, u32[]{:S(2)}) copy-start(bf16[512,128]{1,0:T(8,128)(2,1)} %copy-done.14) | copy-start | bytes 393220
  110.4 1.0 copy-start.6
  111.4 4.4 %copy-start.1 = (bf16[8,704,128]{2,1,0:T(8,128)(2,1)S(1)}, bf16[8,704,128]{2,1,0:T(8,128)(2,1)}, u32[]{:S(2)}) copy-start(bf16[8,704,128]{2,1,0:T(8,128)(2,1)} %copy-done) | copy-start | bytes 4325380
  111.4 4.4 %copy-start.8 = (f32[640,128]{1,0:T(8,128)S(1)}, f32[640,128]{1,0:T(8,128)}, u32[]{:S(2)}) copy-start(f32[640,128]{1,0:T(8,128)} %down_w.5) | copy-start | bytes 983044
  111.4 20.9 %all-to-all-start.5 = ((bf16[8,528,128]{2,1,0:T(8,128)(2,1)}), bf16[8,528,128]{2,1,0:T(8,128)(2,1)}, u32[]{:S(2)}, u32[]{:S(2)}) async-start(bf16[8,528,128]{2,1,0:T(8,128)(2,1)} %copy-done.6), calls=%async_computation.5 | async-start | bytes 2162688 | tf_op jit(solution)/shard_map/all_to_all | solution.py:31
  115.8 1.3 copy-start.5
  117.1 15.1 %copy-start.12 = (f32[128,128]{1,0:T(8,128)S(1)}, f32[128,128]{1,0:T(8,128)}, u32[]{:S(2)}) copy-start(f32[128,128]{1,0:T(8,128)} %up_w.3) | copy-start | bytes 196612

commit v3 on v2

--- a/solution.py
+++ b/solution.py
@@ -41,7 +41,7 @@
     return pl.BlockSpec(v.shape, lambda i: zeros)
 
 
-def call(kernel, outs, ins, args, flops=0, out_specs=None, **more):
+def call(kernel, outs, ins, args, flops=0, out_specs=None, limit=24, **more):
     moved = sum(a.size * a.dtype.itemsize for a in args) + sum(
         o.size * o.dtype.itemsize for o in outs
     )
@@ -51,7 +51,7 @@
         in_specs=[spec or block(a) for spec, a in zip(ins, args, strict=True)],
         out_specs=out_specs or tuple(block(o) for o in outs),
         out_shape=tuple(outs),
-        compiler_params=pltpu.CompilerParams(vmem_limit_bytes=40 * 1024 * 1024),
+        compiler_params=pltpu.CompilerParams(vmem_limit_bytes=limit * 1024 * 1024),
         cost_estimate=pl.CostEstimate(flops=flops, bytes_accessed=moved, transcendentals=0),
         **more,
     )(*args)
@@ -61,28 +61,53 @@
     return jax.ShapeDtypeStruct(dims, kind)
 
 
-def parts_kernel(lens, buckets, acts, og, down_w, up_w, prompts, gk_ref, pay_ref):
+def parts_kernel(
+    lens, buckets, acts, og, down_w, up_w, prompts, gk_out, pay,
+    acts_v, og_v, down_v, up_v, prompts_v, gk, parts, sems,
+):
     rows = acts.shape[0]
     seqs = lens.shape[0]
     slot = rows // seqs
-    peers = pay_ref.shape[0]
+    peers = pay.shape[0]
     piece = rows // peers
+    pairs = ((og, og_v), (up_w, up_v), (down_w, down_v), (acts, acts_v), (prompts, prompts_v))
+    loads = [pltpu.make_async_copy(a, b, sems.at[i]) for i, (a, b) in enumerate(pairs)]
+    for c in loads:
+        c.start()
+    loads[0].wait()
     place = lax.broadcasted_iota(jnp.int32, (slot, 1), 0)
     for s in range(seqs):
         here = pl.ds(s * slot, slot)
         weight = jnp.where(place < lens[s], buckets[s].astype(f32) - 1.5, f32(0.0))
-        gk_ref[here, :] = (weight * og[here, :].astype(f32)).astype(bf16)
-    gk = gk_ref[...]
-    a_half = down_w[...].astype(bf16)
-    up = dot(gk, up_w[...].astype(bf16), NT).astype(bf16)
-    down = dot(acts[...], a_half).astype(bf16)
-    proj = dot(prompts[...], a_half).astype(bf16)
-    for j in range(peers):
-        here = slice(j * piece, (j + 1) * piece)
-        pay_ref[j, 0:piece, :] = up[here]
-        pay_ref[j, piece : 2 * piece, :] = down[here]
-        pay_ref[j, 2 * piece : 3 * piece, :] = proj[here]
-        pay_ref[j, 3 * piece :, :] = gk
+        gk[here, :] = (weight * og_v[here, :].astype(f32)).astype(bf16)
+    first = len(pairs)
+    stores = [pltpu.make_async_copy(gk, gk_out, sems.at[first])] + [
+        pltpu.make_async_copy(gk, pay.at[j, pl.ds(3 * piece, rows), :], sems.at[first + 1 + j])
+        for j in range(peers)
+    ]
+    for c in stores:
+        c.start()
+
+    def put(k, v):
+        v = v.astype(bf16)
+        for j in range(peers):
+            parts[j, k * piece : (k + 1) * piece, :] = v[j * piece : (j + 1) * piece]
+
+    loads[1].wait()
+    put(0, dot(gk[...], up_v[...].astype(bf16), NT))
+    loads[2].wait()
+    a_half = down_v[...].astype(bf16)
+    loads[3].wait()
+    put(1, dot(acts_v[...], a_half))
+    loads[4].wait()
+    put(2, dot(prompts_v[...], a_half))
+    last = pltpu.make_async_copy(
+        parts, pay.at[:, pl.ds(0, 3 * piece), :], sems.at[first + 1 + peers]
+    )
+    last.start()
+    for c in stores:
+        c.wait()
+    last.wait()
 
 
 def base_kernel(prompts, frozen, pay_ref):
@@ -178,7 +203,7 @@
         pay_ref[j, rows:, :] = tail
 
 
-def finish_kernel(got, got_base, got_g, down_w, up_w, next_down, next_up, keys):
+def finish_kernel(got, got_base, base, got_g, down_w, up_w, next_down, next_up, keys):
     rows = keys.shape[0]
     rank = down_w.shape[1]
     peers = got.shape[0]
@@ -187,11 +212,9 @@
     place = lax.broadcasted_iota(jnp.int32, (TAIL, rank), 0)
     p_g = got[0, :rows, :].astype(f32)
     tail = got[0, rows:, :].astype(f32)
-    base = got_base[0, 3 * piece :, :].astype(f32)
     for j in range(1, peers):
         p_g += got[j, :rows, :].astype(f32)
         tail += got[j, rows:, :].astype(f32)
-        base += got_base[j, 3 * piece :, :].astype(f32)
     squares = jnp.sum(jnp.where((place == 0) & (lane < 3), tail, 0.0), keepdims=True)
     factor = step_rate * jnp.minimum(1.0, clip_norm / jnp.sqrt(squares + 1e-12))
     blocks = whole_gradient(got_g, rank)
@@ -201,11 +224,16 @@
     new_up = up_w[...] - factor * blocks[-1]
     next_up[...] = new_up
     proj = rejoin(got_base, 2 * piece, piece).astype(f32) - factor * p_g
-    keys[...] = (base + adapter_scale * dot(proj.astype(bf16), new_up.astype(bf16))).astype(bf16)
-
-
-def input_kernel(got_gk, got_up, down_w, frozen, out):
+    keys[...] = (base[...] + adapter_scale * dot(proj.astype(bf16), new_up.astype(bf16))).astype(bf16)
+
+
+def input_kernel(got_gk, got_up, down_w, frozen, out, base_out):
     rows = out.shape[0]
+    first = got_up.shape[1] - rows
+    base = got_up[0, first:, :].astype(f32)
+    for j in range(1, got_up.shape[0]):
+        base += got_up[j, first:, :].astype(f32)
+    base_out[...] = base
     piece = rows // got_up.shape[0]
     gk = jnp.concatenate([got_gk[j, 3 * piece :, :] for j in range(got_gk.shape[0])], axis=1)
     up = rejoin(got_up, 0, piece)
@@ -227,8 +255,20 @@
     gk, pay = call(
         parts_kernel,
         [shape((rows, cols), bf16), shape((n_f, long, rank), bf16)],
-        [SMEM, SMEM] + [VMEM] * 5,
+        [SMEM, SMEM] + [ANY] * 5,
         (lengths, buckets, acts, output_gradient, down_w, up_w, prompts),
+        out_specs=(ANY, ANY),
+        limit=60,
+        scratch_shapes=[
+            pltpu.VMEM((rows, width), bf16),
+            pltpu.VMEM((rows, cols), bf16),
+            pltpu.VMEM((width, rank), f32),
+            pltpu.VMEM((rank, cols), f32),
+            pltpu.VMEM((rows, width), bf16),
+            pltpu.VMEM((rows, cols), bf16),
+            pltpu.VMEM((n_f, 3 * piece, rank), bf16),
+            pltpu.SemaphoreType.DMA((7 + n_f,)),
+        ],
         flops=2 * rows * rank * (2 * width + cols),
     )
     got_gk = swap(pay, FSDP)
@@ -258,13 +298,14 @@
         flops=2 * rows * rank * (width + cols),
     )
     got = swap(pay, NEAR)
-    (input_gradient,) = call(
+    input_gradient, base = call(
         input_kernel,
-        [shape((rows, width), bf16)],
+        [shape((rows, width), bf16), shape((rows, cols), f32)],
         [VMEM] * 4,
         (got_gk, got_base, down_w, frozen),
         flops=2 * rows * width * (cols * n_f + rank),
     )
+    got, input_gradient, base = lax.optimization_barrier((got, input_gradient, base))
     (pay,) = call(add_kernel, [shape((n_far, slab, rank), bf16)], [VMEM], (got,))
     got = swap(pay, FAR)
     (pay,) = call(add_kernel, [shape((n_near, slab, rank), bf16)], [VMEM], (got,))
@@ -280,8 +321,8 @@
     next_down, next_up, keys = call(
         finish_kernel,
         [shape((width, rank), f32), shape((rank, cols), f32), shape((rows, cols), bf16)],
-        [VMEM] * 5,
-        (got, got_base, got_g, down_w, up_w),
+        [VMEM] * 6,
+        (got, got_base, base, got_g, down_w, up_w),
         flops=2 * rows * rank * cols,
     )
     return input_gradient, next_down, next_up, keys

time: 135 us -> 128 us (0.948)
  starting transfers between devices: 11.2 us -> 21 us
  waiting for transfers between devices: 27.1 us -> 19.3 us
  local copies, waits for them, and re-layouts: 11.6 us -> 6.1 us
  blocking collectives: 75 us -> 69.8 us
    all_to_all x2, starting transfers between devices: 11.2 us -> 21 us  [swap(): return lax.all_to_all(v, axis, 0, 0, tiled=True)]
    all_to_all x2, waiting for transfers between devices: 27.1 us -> 19.3 us  [swap(): return lax.all_to_all(v, axis, 0, 0, tiled=True)]
    unnamed x36 -> x26, local copies, waits for them, and re-layouts: 11.6 us -> 6.1 us
    all_to_all x4, blocking collectives: 75 us -> 69.8 us  [swap(): return lax.all_to_all(v, axis, 0, 0, tiled=True)]
where the time goes in v3:
time: 128 us; the launch traced here: 127 us
  blocking collectives  69.8 us (55%)
  starting transfers between devices  21 us (16%)
  waiting for transfers between devices  19.3 us (15%)
  Pallas kernels  10.3 us (8%)
  local copies, waits for them, and re-layouts  6.1 us (5%)
    all_to_all x4, blocking collectives, swap(): return lax.all_to_all(v, axis, 0, 0, tiled=True)  69.8 us
    all_to_all x2, starting transfers between devices, swap(): return lax.all_to_all(v, axis, 0, 0, tiled=True)  21 us
    all_to_all x2, waiting for transfers between devices, swap(): return lax.all_to_all(v, axis, 0, 0, tiled=True)  19.3 us
    pallas_call x9, Pallas kernels, call(): pl.pallas_call(kernel, grid=(1,), in_specs=[spec or block(a) for spec, a...  10.3 us
    unnamed x26, local copies, waits for them, and re-layouts  6.1 us
  transfers between devices with their start and end apart: 2, of which 2 were waited for; matrix products, arithmetic and copies ran while one was open for 0% of the time, Pallas kernels for 2%

profile of v3, /device:TPU:1, one launch (start us, length us, event | category | flops | bytes accessed | tf_op | source)
XLA Modules:
  0.0 127.1 jit_solution(7850859429294730241)
XLA Ops:
  0.6 3.7 %shard_map.111 = (bf16[512,128]{1,0:T(8,128)(2,1)}, bf16[8,704,128]{2,1,0:T(8,128)(2,1)}) custom-call(s32[2]{0:T(128)} %lens.1, s32[2]{0:T(128)} %buckets.1, bf16[512,640]{1,0:T(8,128)(2,1)} %acts.3, bf16[512,128]{1,0:T(8,128)(2,1)} %og.1, f32[640,128]{1,0:T(8,128)} %down_w.5, f32[128,128]{1,0:T(8,128)} %up_w.3, bf16[512,640]{1,0:T(8,128)(2,1)} %prompts.5), custom_call_target="tpu_custom_call" | custom-call | flops 184549376 | bytes 3407888 | tf_op jit(solution)/shard_map/pallas_call | solution.py:48
  4.4 0.0 copy-start.2
  4.4 6.8 %all-to-all-start = ((bf16[8,704,128]{2,1,0:T(8,128)(2,1)}), bf16[8,704,128]{2,1,0:T(8,128)(2,1)S(1)}, u32[]{:S(2)}, u32[]{:S(2)}) async-start(bf16[8,704,128]{2,1,0:T(8,128)(2,1)} %get-tuple-element.14), calls=%async_computation | async-start | bytes 2883584 | tf_op jit(solution)/shard_map/all_to_all | solution.py:31
  11.2 0.0 copy-start.3
  11.2 1.3 %copy-done.3 = bf16[640,1024]{1,0:T(8,128)(2,1)S(1)} copy-done((bf16[640,1024]{1,0:T(8,128)(2,1)S(1)}, bf16[640,1024]{1,0:T(8,128)(2,1)}, u32[]{:S(2)}) %copy-start.3) | copy-done | bytes 1310744
  12.5 1.0 shard_map.112.pay_in
  13.5 14.0 %all-to-all-done.got_ref.got_gk = bf16[8,704,128]{2,1,0:T(8,128)(2,1)S(1)} async-done(((bf16[8,704,128]{2,1,0:T(8,128)(2,1)}), bf16[8,704,128]{2,1,0:T(8,128)(2,1)S(1)}, u32[]{:S(2)}, u32[]{:S(2)}) %all-to-all-start) | async-done | bytes 1441824 | tf_op jit(solution)/shard_map/all_to_all | solution.py:31
  27.5 0.6 shard_map.113
  28.1 0.0 copy-start
  28.1 1.1 copy-done
  29.2 20.4 %all_to_all.30.got_ref.got_up.got_base = bf16[8,704,128]{2,1,0:T(8,128)(2,1)S(1)} all-to-all(bf16[8,704,128]{2,1,0:T(8,128)(2,1)S(1)} %shard_map.113), channel_id=1, replica_groups=mesh['zhi'=4,'y'=8,'x'=4,'zlo'=2,'core'=2] {'x','zlo'}, dimensions={0} | all-to-all | bytes 2883584 | tf_op jit(solution)/shard_map/all_to_all | solution.py:31
  49.7 0.0 copy-done.7
  49.7 0.3 shard_map.114
  50.0 0.7 copy-done.8
  50.7 14.2 %all-to-all-start.2 = ((bf16[16,48,128]{2,1,0:T(8,128)(2,1)}), bf16[16,48,128]{2,1,0:T(8,128)(2,1)}, u32[]{:S(2)}, u32[]{:S(2)}) async-start(bf16[16,48,128]{2,1,0:T(8,128)(2,1)} %copy-done.8), calls=%async_computation.2 | async-start | bytes 393216 | tf_op jit(solution)/shard_map/all_to_all | solution.py:31
  64.9 0.0 copy-start.4
  64.9 1.3 %copy-done.4 = bf16[640,1024]{1,0:T(8,128)(2,1)S(1)} copy-done((bf16[640,1024]{1,0:T(8,128)(2,1)S(1)}, bf16[640,1024]{1,0:T(8,128)(2,1)}, u32[]{:S(2)}) %copy-start.4) | copy-done | bytes 1310744
  66.2 1.0 copy-done.5
  67.2 2.2 %shard_map.115 = (bf16[512,640]{1,0:T(8,128)(2,1)}, f32[512,128]{1,0:T(8,128)S(1)}) custom-call(bf16[8,704,128]{2,1,0:T(8,128)(2,1)S(1)} %copy-done.1, bf16[8,704,128]{2,1,0:T(8,128)(2,1)S(1)} %all_to_all.30.got_ref.got_up.got_base, f32[640,128]{1,0:T(8,128)S(1)} %copy-done.5, bf16[640,1024]{1,0:T(8,128)(2,1)S(1)} %copy-done.4), custom_call_target="tpu_custom_call" | custom-call | flops 754974720 | bytes 5439488 | tf_op jit(solution)/shard_map/pallas_call | solution.py:48
  69.3 0.7 copy-done.9
  70.0 5.3 %all-to-all-done.2.got_ref = bf16[16,48,128]{2,1,0:T(8,128)(2,1)} async-done(((bf16[16,48,128]{2,1,0:T(8,128)(2,1)}), bf16[16,48,128]{2,1,0:T(8,128)(2,1)}, u32[]{:S(2)}, u32[]{:S(2)}) %all-to-all-start.2) | async-done | bytes 196640 | tf_op jit(solution)/shard_map/all_to_all | solution.py:31
  75.3 1.0 shard_map.116
  76.3 15.7 %all_to_all.31.got_ref = bf16[4,48,128]{2,1,0:T(8,128)(2,1)S(1)} all-to-all(bf16[4,48,128]{2,1,0:T(8,128)(2,1)S(1)} %shard_map.116), channel_id=1, replica_groups=mesh['zhi'=4,'y'=8,'x'=4,'zlo'=2,'core'=2] {'zhi'}, dimensions={0} | all-to-all | bytes 98304 | tf_op jit(solution)/shard_map/all_to_all | solution.py:31
  92.0 14.5 %all_to_all.32.got_ref.got_g = bf16[16,48,128]{2,1,0:T(8,128)(2,1)S(1)} all-to-all(bf16[16,48,128]{2,1,0:T(8,128)(2,1)S(1)} %shard_map.117), channel_id=1, replica_groups=mesh['zhi'=4,'y'=8,'x'=4,'zlo'=2,'core'=2] {'y','core'}, dimensions={0} | all-to-all | bytes 393216 | tf_op jit(solution)/shard_map/all_to_all | solution.py:31
  106.5 0.3 shard_map.118
  106.9 0.0 copy-start.6
  106.9 0.0 copy-start.10
  106.9 0.0 copy-start.11
  106.9 19.1 %all_to_all.33.got = bf16[8,528,128]{2,1,0:T(8,128)(2,1)S(1)} all-to-all(bf16[8,528,128]{2,1,0:T(8,128)(2,1)S(1)} %shard_map.118), channel_id=1, replica_groups=mesh['zhi'=4,'y'=8,'x'=4,'zlo'=2,'core'=2] {'x','zlo'}, dimensions={0} | all-to-all | bytes 2162688 | tf_op jit(solution)/shard_map/all_to_all | solution.py:31
  126.0 0.0 copy-done.6
  126.0 0.0 copy-done.11
  126.0 1.1 shard_map.119
  (11 shorter events, 0.0 us)
Async XLA Ops:
  4.4 6.8 %copy-start.2 = (bf16[512,640]{1,0:T(8,128)(2,1)S(1)}, bf16[512,640]{1,0:T(8,128)(2,1)}, u32[]{:S(2)}) copy-start(bf16[512,640]{1,0:T(8,128)(2,1)} %prompts.5) | copy-start | bytes 1966084
  4.4 23.1 %all-to-all-start = ((bf16[8,704,128]{2,1,0:T(8,128)(2,1)}), bf16[8,704,128]{2,1,0:T(8,128)(2,1)S(1)}, u32[]{:S(2)}, u32[]{:S(2)}) async-start(bf16[8,704,128]{2,1,0:T(8,128)(2,1)} %get-tuple-element.14), calls=%async_computation | async-start | bytes 2883584 | tf_op jit(solution)/shard_map/all_to_all | solution.py:31
  11.2 1.3 %copy-start.3 = (bf16[640,1024]{1,0:T(8,128)(2,1)S(1)}, bf16[640,1024]{1,0:T(8,128)(2,1)}, u32[]{:S(2)}) copy-start(bf16[640,1024]{1,0:T(8,128)(2,1)} %frozen.3) | copy-start | bytes 3932164
  28.1 1.1 copy-start
  29.2 20.4 %copy-start.7 = (bf16[512,640]{1,0:T(8,128)(2,1)S(1)}, bf16[512,640]{1,0:T(8,128)(2,1)}, u32[]{:S(2)}) copy-start(bf16[512,640]{1,0:T(8,128)(2,1)} %acts.3) | copy-start | bytes 1966084
  29.2 20.4 %copy-start.12 = (bf16[512,128]{1,0:T(8,128)(2,1)S(1)}, bf16[512,128]{1,0:T(8,128)(2,1)}, u32[]{:S(2)}) copy-start(bf16[512,128]{1,0:T(8,128)(2,1)} %get-tuple-element.15.gk) | copy-start | bytes 393220
  49.7 15.2 %copy-start.1 = (bf16[8,704,128]{2,1,0:T(8,128)(2,1)S(1)}, bf16[8,704,128]{2,1,0:T(8,128)(2,1)}, u32[]{:S(2)}) copy-start(bf16[8,704,128]{2,1,0:T(8,128)(2,1)} %copy-done) | copy-start | bytes 4325380
  50.0 0.7 copy-start.8
  50.7 24.6 %all-to-all-start.2 = ((bf16[16,48,128]{2,1,0:T(8,128)(2,1)}), bf16[16,48,128]{2,1,0:T(8,128)(2,1)}, u32[]{:S(2)}, u32[]{:S(2)}) async-start(bf16[16,48,128]{2,1,0:T(8,128)(2,1)} %copy-done.8), calls=%async_computation.2 | async-start | bytes 393216 | tf_op jit(solution)/shard_map/all_to_all | solution.py:31
  64.9 1.3 %copy-start.4 = (bf16[640,1024]{1,0:T(8,128)(2,1)S(1)}, bf16[640,1024]{1,0:T(8,128)(2,1)}, u32[]{:S(2)}) copy-start(bf16[640,1024]{1,0:T(8,128)(2,1)} %frozen.3) | copy-start | bytes 3932164
  66.2 1.0 copy-start.5
  69.3 0.7 copy-start.9
  106.9 19.1 %copy-start.6 = (f32[640,128]{1,0:T(8,128)S(1)}, f32[640,128]{1,0:T(8,128)}, u32[]{:S(2)}) copy-start(f32[640,128]{1,0:T(8,128)} %down_w.5) | copy-start | bytes 983044
  106.9 19.1 %copy-start.10 = (f32[512,128]{1,0:T(8,128)S(1)}, f32[512,128]{1,0:T(8,128)}, u32[]{:S(2)}) copy-start(f32[512,128]{1,0:T(8,128)} %copy-done.9) | copy-start | bytes 786436
  106.9 19.1 %copy-start.11 = (f32[128,128]{1,0:T(8,128)S(1)}, f32[128,128]{1,0:T(8,128)}, u32[]{:S(2)}) copy-start(f32[128,128]{1,0:T(8,128)} %up_w.3) | copy-start | bytes 196612

commit v4 on v3

--- a/solution.py
+++ b/solution.py
@@ -34,6 +34,7 @@
 VMEM = None
 SMEM = pl.BlockSpec(memory_space=pltpu.SMEM)
 ANY = pl.BlockSpec(memory_space=pl.ANY)
+HBM = pl.BlockSpec(memory_space=pltpu.HBM)
 
 
 def block(v):
@@ -62,15 +63,15 @@
 
 
 def parts_kernel(
-    lens, buckets, acts, og, down_w, up_w, prompts, gk_out, pay,
-    acts_v, og_v, down_v, up_v, prompts_v, gk, parts, sems,
+    lens, buckets, acts, og, down_w, up_w, gk_out, pay,
+    acts_v, og_v, down_v, up_v, gk, parts, sems,
 ):
     rows = acts.shape[0]
     seqs = lens.shape[0]
     slot = rows // seqs
     peers = pay.shape[0]
     piece = rows // peers
-    pairs = ((og, og_v), (up_w, up_v), (down_w, down_v), (acts, acts_v), (prompts, prompts_v))
+    pairs = ((og, og_v), (up_w, up_v), (down_w, down_v), (acts, acts_v))
     loads = [pltpu.make_async_copy(a, b, sems.at[i]) for i, (a, b) in enumerate(pairs)]
     for c in loads:
         c.start()
@@ -82,7 +83,7 @@
         gk[here, :] = (weight * og_v[here, :].astype(f32)).astype(bf16)
     first = len(pairs)
     stores = [pltpu.make_async_copy(gk, gk_out, sems.at[first])] + [
-        pltpu.make_async_copy(gk, pay.at[j, pl.ds(3 * piece, rows), :], sems.at[first + 1 + j])
+        pltpu.make_async_copy(gk, pay.at[j, pl.ds(2 * piece, rows), :], sems.at[first + 1 + j])
         for j in range(peers)
     ]
     for c in stores:
@@ -99,10 +100,8 @@
     a_half = down_v[...].astype(bf16)
     loads[3].wait()
     put(1, dot(acts_v[...], a_half))
-    loads[4].wait()
-    put(2, dot(prompts_v[...], a_half))
     last = pltpu.make_async_copy(
-        parts, pay.at[:, pl.ds(0, 3 * piece), :], sems.at[first + 1 + peers]
+        parts, pay.at[:, pl.ds(0, 2 * piece), :], sems.at[first + 1 + peers]
     )
     last.start()
     for c in stores:
@@ -110,12 +109,23 @@
     last.wait()
 
 
-def base_kernel(prompts, frozen, pay_ref):
-    peers, long, cols = pay_ref.shape
+def prompts_kernel(prompts, frozen, down_w, pay, base_v, proj_v, sems):
+    peers, long, cols = pay.shape
     rows = prompts.shape[0]
+    piece = rows // peers
+    proj = dot(prompts[...], down_w[...].astype(bf16)).astype(bf16)
     base = dot(prompts[...], frozen[...]).astype(bf16)
     for j in range(peers):
-        pay_ref[j, long - rows :, :] = base[:, j * cols : (j + 1) * cols]
+        proj_v[j] = proj[j * piece : (j + 1) * piece]
+        base_v[j] = base[:, j * cols : (j + 1) * cols]
+    copies = [
+        pltpu.make_async_copy(proj_v, pay.at[:, pl.ds(2 * piece, piece), :], sems.at[0]),
+        pltpu.make_async_copy(base_v, pay.at[:, pl.ds(3 * piece, rows), :], sems.at[1]),
+    ]
+    for c in copies:
+        c.start()
+    for c in copies:
+        c.wait()
 
 
 def sums_kernel(got_ref, pay_in, pay_ref, sums_ref, sems):
@@ -142,23 +152,26 @@
     )
 
 
-def grads_kernel(got_ref, acts, gk, pay_ref):
+def grads_kernel(got_ref, acts, gk, pay, pay_v, sem):
     rows = acts.shape[0]
     piece = rows // got_ref.shape[0]
     lanes = gk.shape[1]
     up = rejoin(got_ref, 0, piece)
     down = rejoin(got_ref, piece, piece)
     g = adapter_scale * jnp.concatenate([dot(up, acts[...], TN), dot(down, gk[...], TN)], axis=1)
-    peers = pay_ref.shape[0]
+    peers = pay.shape[0]
     step = g.shape[0] // peers
     for j in range(peers):
-        pay_ref[j] = jnp.concatenate(
+        pay_v[j] = jnp.concatenate(
             [
                 g[j * step : (j + 1) * step, c * lanes : (c + 1) * lanes]
                 for c in range(g.shape[1] // lanes)
             ],
             axis=0,
-        ).astype(pay_ref.dtype)
+        ).astype(pay.dtype)
+    copy = pltpu.make_async_copy(pay_v, pay, sem)
+    copy.start()
+    copy.wait()
 
 
 def add_kernel(got_ref, pay_ref):
@@ -180,7 +193,7 @@
     ]
 
 
-def project_kernel(got_ref, prompts, pay_ref):
+def project_kernel(got_ref, prompts, pa_rows, pay_ref):
     rank = pay_ref.shape[2]
     rows = prompts.shape[0]
     blocks = whole_gradient(got_ref, rank)
@@ -200,21 +213,21 @@
     proj = dot(prompts[...], g_down, NT).astype(bf16)
     for j in range(pay_ref.shape[0]):
         pay_ref[j, :rows, :] = proj
-        pay_ref[j, rows:, :] = tail
-
-
-def finish_kernel(got, got_base, base, got_g, down_w, up_w, next_down, next_up, keys):
+        pay_ref[j, rows : rows + TAIL, :] = tail
+        pay_ref[j, rows + TAIL :, :] = pa_rows[...]
+
+
+def finish_kernel(got, base, got_g, down_w, up_w, next_down, next_up, keys):
     rows = keys.shape[0]
     rank = down_w.shape[1]
     peers = got.shape[0]
-    piece = rows // peers
     lane = lax.broadcasted_iota(jnp.int32, (TAIL, rank), 1)
     place = lax.broadcasted_iota(jnp.int32, (TAIL, rank), 0)
     p_g = got[0, :rows, :].astype(f32)
-    tail = got[0, rows:, :].astype(f32)
+    tail = got[0, rows : rows + TAIL, :].astype(f32)
     for j in range(1, peers):
         p_g += got[j, :rows, :].astype(f32)
-        tail += got[j, rows:, :].astype(f32)
+        tail += got[j, rows : rows + TAIL, :].astype(f32)
     squares = jnp.sum(jnp.where((place == 0) & (lane < 3), tail, 0.0), keepdims=True)
     factor = step_rate * jnp.minimum(1.0, clip_norm / jnp.sqrt(squares + 1e-12))
     blocks = whole_gradient(got_g, rank)
@@ -223,22 +236,33 @@
         next_down[here, :] = down_w[here, :] - factor * block.T
     new_up = up_w[...] - factor * blocks[-1]
     next_up[...] = new_up
-    proj = rejoin(got_base, 2 * piece, piece).astype(f32) - factor * p_g
-    keys[...] = (base[...] + adapter_scale * dot(proj.astype(bf16), new_up.astype(bf16))).astype(bf16)
-
-
-def input_kernel(got_gk, got_up, down_w, frozen, out, base_out):
+    proj = rejoin(got, rows + TAIL, rows // peers).astype(f32) - factor * p_g
+    keys[...] = (
+        base[...] + adapter_scale * dot(proj.astype(bf16), new_up.astype(bf16))
+    ).astype(bf16)
+
+
+def frozen_kernel(got_gk, frozen, acts, out):
+    del acts
     rows = out.shape[0]
-    first = got_up.shape[1] - rows
-    base = got_up[0, first:, :].astype(f32)
-    for j in range(1, got_up.shape[0]):
-        base += got_up[j, first:, :].astype(f32)
-    base_out[...] = base
-    piece = rows // got_up.shape[0]
-    gk = jnp.concatenate([got_gk[j, 3 * piece :, :] for j in range(got_gk.shape[0])], axis=1)
-    up = rejoin(got_up, 0, piece)
+    peers, long, _ = got_gk.shape
+    gk = jnp.concatenate([got_gk[j, long - rows :, :] for j in range(peers)], axis=1)
+    out[...] = dot(gk, frozen[...], NT)
+
+
+def beside_kernel(got, down_w, part, out, base_out, pa_out):
+    rows = out.shape[0]
+    peers, long, _ = got.shape
+    piece = rows // peers
+    first = long - rows
     a_half = down_w[...].astype(bf16)
-    out[...] = (dot(gk, frozen[...], NT) + adapter_scale * dot(up, a_half, NT)).astype(bf16)
+    up = rejoin(got, 0, piece)
+    out[...] = (part[...] + adapter_scale * dot(up, a_half, NT)).astype(bf16)
+    total = got[0, first - piece :, :].astype(f32)
+    for j in range(1, peers):
+        total += got[j, first - piece :, :].astype(f32)
+    pa_out[...] = total[:piece].astype(bf16)
+    base_out[...] = total[piece:]
 
 
 def per_device(acts, output_gradient, lengths, buckets, frozen, down_w, up_w, prompts):
@@ -249,80 +273,97 @@
     n_near = lax.axis_size(NEAR)
     n_far = lax.axis_size(FAR)
     piece = rows // n_f
+    slab = (width + cols) // n_near
     long = 3 * piece + rows
-    slab = (width + cols) // n_near
 
     gk, pay = call(
         parts_kernel,
-        [shape((rows, cols), bf16), shape((n_f, long, rank), bf16)],
-        [SMEM, SMEM] + [ANY] * 5,
-        (lengths, buckets, acts, output_gradient, down_w, up_w, prompts),
-        out_specs=(ANY, ANY),
+        [shape((rows, cols), bf16), shape((n_f, 2 * piece + rows, rank), bf16)],
+        [SMEM, SMEM] + [ANY] * 4,
+        (lengths, buckets, acts, output_gradient, down_w, up_w),
+        flops=2 * rows * rank * (width + cols),
+        out_specs=(HBM, HBM),
         limit=60,
         scratch_shapes=[
             pltpu.VMEM((rows, width), bf16),
             pltpu.VMEM((rows, cols), bf16),
             pltpu.VMEM((width, rank), f32),
             pltpu.VMEM((rank, cols), f32),
-            pltpu.VMEM((rows, width), bf16),
             pltpu.VMEM((rows, cols), bf16),
-            pltpu.VMEM((n_f, 3 * piece, rank), bf16),
-            pltpu.SemaphoreType.DMA((7 + n_f,)),
+            pltpu.VMEM((n_f, 2 * piece, rank), bf16),
+            pltpu.SemaphoreType.DMA((6 + n_f,)),
         ],
-        flops=2 * rows * rank * (2 * width + cols),
     )
     got_gk = swap(pay, FSDP)
     (pay,) = call(
-        base_kernel,
+        prompts_kernel,
         [shape((n_f, long, cols), bf16)],
-        [VMEM, VMEM],
-        (prompts, frozen),
-        flops=2 * rows * width * cols * n_f,
+        [VMEM] * 3,
+        (prompts, frozen, down_w),
+        flops=2 * rows * width * (cols * n_f + rank),
+        out_specs=(HBM,),
+        scratch_shapes=[
+            pltpu.VMEM((n_f, rows, cols), bf16),
+            pltpu.VMEM((n_f, piece, rank), bf16),
+            pltpu.SemaphoreType.DMA((2,)),
+        ],
     )
     (pay,) = call(
         sums_kernel,
         [shape((n_f, long, cols), bf16)],
-        [VMEM, ANY],
+        [VMEM, HBM],
         (got_gk, pay),
         input_output_aliases={1: 0},
-        out_specs=(ANY,),
-        scratch_shapes=[pltpu.VMEM((3 * piece, rank), bf16), pltpu.SemaphoreType.DMA((n_f,))],
-    )
-    got_base = swap(pay, FSDP)
+        out_specs=(HBM,),
+        scratch_shapes=[pltpu.VMEM((2 * piece, rank), bf16), pltpu.SemaphoreType.DMA((n_f,))],
+    )
+    got = swap(pay, FSDP)
+    (input_part,) = call(
+        frozen_kernel,
+        [shape((rows, width), f32)],
+        [VMEM] * 3,
+        (got_gk, frozen, acts),
+        flops=2 * rows * width * cols * n_f,
+    )
+    got, input_part = lax.optimization_barrier((got, input_part))
 
     (pay,) = call(
         grads_kernel,
         [shape((n_near, slab, rank), bf16)],
         [VMEM] * 3,
-        (got_base, acts, gk),
+        (got, acts, gk),
         flops=2 * rows * rank * (width + cols),
-    )
-    got = swap(pay, NEAR)
-    input_gradient, base = call(
-        input_kernel,
-        [shape((rows, width), bf16), shape((rows, cols), f32)],
-        [VMEM] * 4,
-        (got_gk, got_base, down_w, frozen),
-        flops=2 * rows * width * (cols * n_f + rank),
-    )
-    got, input_gradient, base = lax.optimization_barrier((got, input_gradient, base))
-    (pay,) = call(add_kernel, [shape((n_far, slab, rank), bf16)], [VMEM], (got,))
+        out_specs=(HBM,),
+        scratch_shapes=[pltpu.VMEM((n_near, slab, rank), bf16), pltpu.SemaphoreType.DMA],
+    )
+    got_g = swap(pay, NEAR)
+    input_gradient, base, pa_rows = call(
+        beside_kernel,
+        [shape((rows, width), bf16), shape((rows, cols), f32), shape((piece, rank), bf16)],
+        [VMEM] * 3,
+        (got, down_w, input_part),
+        flops=2 * rows * width * rank,
+    )
+    got_g, input_gradient, base, pa_rows = lax.optimization_barrier(
+        (got_g, input_gradient, base, pa_rows)
+    )
+    (pay,) = call(add_kernel, [shape((n_far, slab, rank), bf16)], [VMEM], (got_g,))
     got = swap(pay, FAR)
     (pay,) = call(add_kernel, [shape((n_near, slab, rank), bf16)], [VMEM], (got,))
     got_g = swap(pay, NEAR)
     (pay,) = call(
         project_kernel,
-        [shape((n_f, rows + TAIL, rank), bf16)],
-        [VMEM] * 2,
-        (got_g, prompts),
+        [shape((n_f, rows + TAIL + piece, rank), bf16)],
+        [VMEM] * 3,
+        (got_g, prompts, pa_rows),
         flops=2 * rows * width * rank,
     )
     got = swap(pay, FSDP)
     next_down, next_up, keys = call(
         finish_kernel,
         [shape((width, rank), f32), shape((rank, cols), f32), shape((rows, cols), bf16)],
-        [VMEM] * 6,
-        (got, got_base, base, got_g, down_w, up_w),
+        [VMEM] * 5,
+        (got, base, got_g, down_w, up_w),
         flops=2 * rows * rank * cols,
     )
     return input_gradient, next_down, next_up, keys

time: 128 us -> 125 us (0.977)
  blocking collectives: 69.8 us -> 50.5 us
  waiting for transfers between devices: 19.3 us -> 31.8 us
  starting transfers between devices: 21 us -> 25.5 us
    all_to_all x4 -> x3, blocking collectives: 69.8 us -> 50.5 us  [swap(): return lax.all_to_all(v, axis, 0, 0, tiled=True)]
    all_to_all x2 -> x3, waiting for transfers between devices: 19.3 us -> 31.8 us  [swap(): return lax.all_to_all(v, axis, 0, 0, tiled=True)]
    all_to_all x2 -> x3, starting transfers between devices: 21 us -> 25.5 us  [swap(): return lax.all_to_all(v, axis, 0, 0, tiled=True)]
    unnamed x26 -> x22, local copies, waits for them, and re-layouts: 6.1 us -> 5.03 us
    pallas_call x9 -> x10, Pallas kernels: 10.3 us -> 10.9 us  [call(): pl.pallas_call(kernel, grid=(1,), in_specs=[spec or block(a) for spec, a...]
  transfers between devices with their start and end apart: 2 -> 3, of which waited for: 2 -> 3; matrix products, arithmetic and copies ran while one was open for 0% -> 0% of each run, Pallas kernels for 2% -> 3%
where the time goes in v4:
time: 125 us; the launch traced here: 124 us
  blocking collectives  50.5 us (40%)
  waiting for transfers between devices  31.8 us (25%)
  starting transfers between devices  25.5 us (20%)
  Pallas kernels  10.9 us (9%)
  local copies, waits for them, and re-layouts  5.03 us (4%)
    all_to_all x3, blocking collectives, swap(): return lax.all_to_all(v, axis, 0, 0, tiled=True)  50.5 us
    all_to_all x3, waiting for transfers between devices, swap(): return lax.all_to_all(v, axis, 0, 0, tiled=True)  31.8 us
    all_to_all x3, starting transfers between devices, swap(): return lax.all_to_all(v, axis, 0, 0, tiled=True)  25.5 us
    pallas_call x10, Pallas kernels, call(): pl.pallas_call(kernel, grid=(1,), in_specs=[spec or block(a) for spec, a...  10.9 us
    unnamed x22, local copies, waits for them, and re-layouts  5.03 us
  transfers between devices with their start and end apart: 3, of which 3 were waited for; matrix products, arithmetic and copies ran while one was open for 0% of the time, Pallas kernels for 3%

profile of v4, /device:TPU:1, one launch (start us, length us, event | category | flops | bytes accessed | tf_op | source)
XLA Modules:
  0.0 124.5 jit_solution(3577087078729545903)
XLA Ops:
  0.6 3.2 %shard_map.111 = (bf16[512,128]{1,0:T(8,128)(2,1)}, bf16[8,640,128]{2,1,0:T(8,128)(2,1)}) custom-call(s32[2]{0:T(128)} %lens.1, s32[2]{0:T(128)} %buckets.1, bf16[512,640]{1,0:T(8,128)(2,1)} %acts.5, bf16[512,128]{1,0:T(8,128)(2,1)} %og.1, f32[640,128]{1,0:T(8,128)} %down_w.7, f32[128,128]{1,0:T(8,128)} %up_w.3), custom_call_target="tpu_custom_call" | custom-call | flops 100663296 | bytes 2621456 | tf_op jit(solution)/shard_map/pallas_call | solution.py:49
  3.8 0.0 copy-start.1
  3.8 0.0 copy-start.7
  3.8 6.8 %all-to-all-start = ((bf16[8,640,128]{2,1,0:T(8,128)(2,1)}), bf16[8,640,128]{2,1,0:T(8,128)(2,1)S(1)}, u32[]{:S(2)}, u32[]{:S(2)}) async-start(bf16[8,640,128]{2,1,0:T(8,128)(2,1)} %get-tuple-element.18), calls=%async_computation | async-start | bytes 2621440 | tf_op jit(solution)/shard_map/all_to_all | solution.py:31
  10.6 0.0 copy-done.1
  10.6 0.0 copy-done.7
  10.7 0.0 copy-start.3
  10.7 1.3 %copy-done.3 = bf16[640,1024]{1,0:T(8,128)(2,1)S(1)} copy-done((bf16[640,1024]{1,0:T(8,128)(2,1)S(1)}, bf16[640,1024]{1,0:T(8,128)(2,1)}, u32[]{:S(2)}) %copy-start.3) | copy-done | bytes 1310744
  12.0 2.1 %shard_map.112.pay_in = bf16[8,704,128]{2,1,0:T(8,128)(2,1)} custom-call(bf16[512,640]{1,0:T(8,128)(2,1)S(1)} %copy-done.7, bf16[640,1024]{1,0:T(8,128)(2,1)S(1)} %copy-done.3, f32[640,128]{1,0:T(8,128)S(1)} %copy-done.1), custom_call_target="tpu_custom_call" | custom-call | flops 754974720 | bytes 3735552 | tf_op jit(solution)/shard_map/pallas_call | solution.py:49
  14.1 11.4 %all-to-all-done.got_ref.got_gk = bf16[8,640,128]{2,1,0:T(8,128)(2,1)S(1)} async-done(((bf16[8,640,128]{2,1,0:T(8,128)(2,1)}), bf16[8,640,128]{2,1,0:T(8,128)(2,1)S(1)}, u32[]{:S(2)}, u32[]{:S(2)}) %all-to-all-start) | async-done | bytes 1310752 | tf_op jit(solution)/shard_map/all_to_all | solution.py:31
  25.5 0.8 shard_map.113
  26.4 0.0 copy-start
  26.4 4.3 %all-to-all-start.1 = ((bf16[8,704,128]{2,1,0:T(8,128)(2,1)}), bf16[8,704,128]{2,1,0:T(8,128)(2,1)S(1)}, u32[]{:S(2)}, u32[]{:S(2)}) async-start(bf16[8,704,128]{2,1,0:T(8,128)(2,1)} %shard_map.113), calls=%async_computation.1 | async-start | bytes 2883584 | tf_op jit(solution)/shard_map/all_to_all | solution.py:31
  30.7 0.0 copy-done
  30.7 0.0 copy-start.4
  30.7 1.3 %copy-done.4 = bf16[640,1024]{1,0:T(8,128)(2,1)S(1)} copy-done((bf16[640,1024]{1,0:T(8,128)(2,1)S(1)}, bf16[640,1024]{1,0:T(8,128)(2,1)}, u32[]{:S(2)}) %copy-start.4) | copy-done | bytes 1310744
  32.0 1.0 shard_map.114.part
  33.0 1.1 copy-done.5
  34.1 12.6 %all-to-all-done.1.got_ref.got = bf16[8,704,128]{2,1,0:T(8,128)(2,1)S(1)} async-done(((bf16[8,704,128]{2,1,0:T(8,128)(2,1)}), bf16[8,704,128]{2,1,0:T(8,128)(2,1)S(1)}, u32[]{:S(2)}, u32[]{:S(2)}) %all-to-all-start.1) | async-done | bytes 1441824 | tf_op jit(solution)/shard_map/all_to_all | solution.py:31
  46.6 1.0 shard_map.115
  47.7 14.4 %all-to-all-start.2 = ((bf16[16,48,128]{2,1,0:T(8,128)(2,1)}), bf16[16,48,128]{2,1,0:T(8,128)(2,1)S(1)}, u32[]{:S(2)}, u32[]{:S(2)}) async-start(bf16[16,48,128]{2,1,0:T(8,128)(2,1)} %shard_map.115), calls=%async_computation.2 | async-start | bytes 393216 | tf_op jit(solution)/shard_map/all_to_all | solution.py:31
  62.1 0.0 copy-done.2
  62.1 1.3 %copy-done.6 = f32[512,640]{1,0:T(8,128)S(1)} copy-done((f32[512,640]{1,0:T(8,128)S(1)}, f32[512,640]{1,0:T(8,128)}, u32[]{:S(2)}) %copy-start.6) | copy-done | bytes 1310744
  63.4 1.2 shard_map.116
  64.6 7.8 %all-to-all-done.2.got_ref = bf16[16,48,128]{2,1,0:T(8,128)(2,1)S(1)} async-done(((bf16[16,48,128]{2,1,0:T(8,128)(2,1)}), bf16[16,48,128]{2,1,0:T(8,128)(2,1)S(1)}, u32[]{:S(2)}, u32[]{:S(2)}) %all-to-all-start.2) | async-done | bytes 196640 | tf_op jit(solution)/shard_map/all_to_all | solution.py:31
  72.4 15.7 %all_to_all.30.got_ref = bf16[4,48,128]{2,1,0:T(8,128)(2,1)S(1)} all-to-all(bf16[4,48,128]{2,1,0:T(8,128)(2,1)S(1)} %shard_map.117), channel_id=1, replica_groups=mesh['zhi'=4,'y'=8,'x'=4,'zlo'=2,'core'=2] {'zhi'}, dimensions={0} | all-to-all | bytes 98304 | tf_op jit(solution)/shard_map/all_to_all | solution.py:31
  88.2 14.5 %all_to_all.31.got_ref.got_g = bf16[16,48,128]{2,1,0:T(8,128)(2,1)S(1)} all-to-all(bf16[16,48,128]{2,1,0:T(8,128)(2,1)S(1)} %shard_map.118), channel_id=1, replica_groups=mesh['zhi'=4,'y'=8,'x'=4,'zlo'=2,'core'=2] {'y','core'}, dimensions={0} | all-to-all | bytes 393216 | tf_op jit(solution)/shard_map/all_to_all | solution.py:31
  102.7 0.3 shard_map.119
  103.1 0.0 copy-start.9
  103.1 20.2 %all_to_all.32.got = bf16[8,592,128]{2,1,0:T(8,128)(2,1)S(1)} all-to-all(bf16[8,592,128]{2,1,0:T(8,128)(2,1)S(1)} %shard_map.119), channel_id=1, replica_groups=mesh['zhi'=4,'y'=8,'x'=4,'zlo'=2,'core'=2] {'x','zlo'}, dimensions={0} | all-to-all | bytes 2424832 | tf_op jit(solution)/shard_map/all_to_all | solution.py:31
  123.3 0.0 copy-done.9
  123.3 1.1 shard_map.120
  (9 shorter events, 0.1 us)
Async XLA Ops:
  3.8 6.8 %copy-start.1 = (f32[640,128]{1,0:T(8,128)S(1)}, f32[640,128]{1,0:T(8,128)}, u32[]{:S(2)}) copy-start(f32[640,128]{1,0:T(8,128)} %down_w.7) | copy-start | bytes 983044
  3.8 6.8 %copy-start.7 = (bf16[512,640]{1,0:T(8,128)(2,1)S(1)}, bf16[512,640]{1,0:T(8,128)(2,1)}, u32[]{:S(2)}) copy-start(bf16[512,640]{1,0:T(8,128)(2,1)} %prompts.3) | copy-start | bytes 1966084
  3.8 21.7 %all-to-all-start = ((bf16[8,640,128]{2,1,0:T(8,128)(2,1)}), bf16[8,640,128]{2,1,0:T(8,128)(2,1)S(1)}, u32[]{:S(2)}, u32[]{:S(2)}) async-start(bf16[8,640,128]{2,1,0:T(8,128)(2,1)} %get-tuple-element.18), calls=%async_computation | async-start | bytes 2621440 | tf_op jit(solution)/shard_map/all_to_all | solution.py:31
  10.7 1.3 %copy-start.3 = (bf16[640,1024]{1,0:T(8,128)(2,1)S(1)}, bf16[640,1024]{1,0:T(8,128)(2,1)}, u32[]{:S(2)}) copy-start(bf16[640,1024]{1,0:T(8,128)(2,1)} %frozen.3) | copy-start | bytes 3932164
  26.4 4.3 %copy-start = (bf16[512,640]{1,0:T(8,128)(2,1)S(1)}, bf16[512,640]{1,0:T(8,128)(2,1)}, u32[]{:S(2)}) copy-start(bf16[512,640]{1,0:T(8,128)(2,1)} %acts.5) | copy-start | bytes 1966084
  26.4 20.2 %all-to-all-start.1 = ((bf16[8,704,128]{2,1,0:T(8,128)(2,1)}), bf16[8,704,128]{2,1,0:T(8,128)(2,1)S(1)}, u32[]{:S(2)}, u32[]{:S(2)}) async-start(bf16[8,704,128]{2,1,0:T(8,128)(2,1)} %shard_map.113), calls=%async_computation.1 | async-start | bytes 2883584 | tf_op jit(solution)/shard_map/all_to_all | solution.py:31
  30.7 1.3 %copy-start.4 = (bf16[640,1024]{1,0:T(8,128)(2,1)S(1)}, bf16[640,1024]{1,0:T(8,128)(2,1)}, u32[]{:S(2)}) copy-start(bf16[640,1024]{1,0:T(8,128)(2,1)} %frozen.3) | copy-start | bytes 3932164
  32.0 14.7 %copy-start.10 = (bf16[512,128]{1,0:T(8,128)(2,1)S(1)}, bf16[512,128]{1,0:T(8,128)(2,1)}, u32[]{:S(2)}) copy-start(bf16[512,128]{1,0:T(8,128)(2,1)} %get-tuple-element.20.gk) | copy-start | bytes 393220
  33.0 1.1 copy-start.5
  46.6 15.5 %copy-start.2 = (f32[640,128]{1,0:T(8,128)S(1)}, f32[640,128]{1,0:T(8,128)}, u32[]{:S(2)}) copy-start(f32[640,128]{1,0:T(8,128)} %down_w.7) | copy-start | bytes 983044
  47.7 24.8 %all-to-all-start.2 = ((bf16[16,48,128]{2,1,0:T(8,128)(2,1)}), bf16[16,48,128]{2,1,0:T(8,128)(2,1)S(1)}, u32[]{:S(2)}, u32[]{:S(2)}) async-start(bf16[16,48,128]{2,1,0:T(8,128)(2,1)} %shard_map.115), calls=%async_computation.2 | async-start | bytes 393216 | tf_op jit(solution)/shard_map/all_to_all | solution.py:31
  62.1 1.3 %copy-start.6 = (f32[512,640]{1,0:T(8,128)S(1)}, f32[512,640]{1,0:T(8,128)}, u32[]{:S(2)}) copy-start(f32[512,640]{1,0:T(8,128)} %copy-done.5) | copy-start | bytes 3932164
  63.4 39.3 %copy-start.8 = (bf16[512,640]{1,0:T(8,128)(2,1)S(1)}, bf16[512,640]{1,0:T(8,128)(2,1)}, u32[]{:S(2)}) copy-start(bf16[512,640]{1,0:T(8,128)(2,1)} %prompts.3) | copy-start | bytes 1966084
  103.1 20.3 %copy-start.9 = (f32[128,128]{1,0:T(8,128)S(1)}, f32[128,128]{1,0:T(8,128)}, u32[]{:S(2)}) copy-start(f32[128,128]{1,0:T(8,128)} %up_w.3) | copy-start | bytes 196612

commit v5 on v4

--- a/solution.py
+++ b/solution.py
@@ -25,6 +25,15 @@
 
 def dot(a, b, dims=(((1,), (0,)), ((), ()))):
     return lax.dot_general(a, b, dims, preferred_element_type=f32)
+
+
+Z_PAIRS = ((0, 1), (1, 0))
+X_NEAR = ((0, 1), (1, 0), (2, 3), (3, 2))
+X_FAR = ((0, 3), (3, 0), (1, 2), (2, 1))
+
+
+def owner_mask(i):
+    return (i & 1) ^ (2 if i & 2 else 0) ^ (6 if i & 4 else 0)
 
 
 def swap(v, axis):
@@ -82,12 +91,8 @@
         weight = jnp.where(place < lens[s], buckets[s].astype(f32) - 1.5, f32(0.0))
         gk[here, :] = (weight * og_v[here, :].astype(f32)).astype(bf16)
     first = len(pairs)
-    stores = [pltpu.make_async_copy(gk, gk_out, sems.at[first])] + [
-        pltpu.make_async_copy(gk, pay.at[j, pl.ds(2 * piece, rows), :], sems.at[first + 1 + j])
-        for j in range(peers)
-    ]
-    for c in stores:
-        c.start()
+    store = pltpu.make_async_copy(gk, gk_out, sems.at[first])
+    store.start()
 
     def put(k, v):
         v = v.astype(bf16)
@@ -100,16 +105,14 @@
     a_half = down_v[...].astype(bf16)
     loads[3].wait()
     put(1, dot(acts_v[...], a_half))
-    last = pltpu.make_async_copy(
-        parts, pay.at[:, pl.ds(0, 2 * piece), :], sems.at[first + 1 + peers]
-    )
+    last = pltpu.make_async_copy(parts, pay, sems.at[first + 1])
     last.start()
-    for c in stores:
-        c.wait()
+    store.wait()
     last.wait()
 
 
-def prompts_kernel(prompts, frozen, down_w, pay, base_v, proj_v, sems):
+def prompts_kernel(prompts, frozen, down_w, acts, pay, base_v, proj_v, sems):
+    del acts
     peers, long, cols = pay.shape
     rows = prompts.shape[0]
     piece = rows // peers
@@ -174,13 +177,31 @@
     copy.wait()
 
 
-def add_kernel(got_ref, pay_ref):
+def add_kernel(got_ref, pay, total_v, sems):
     total = got_ref[0].astype(f32)
     for j in range(1, got_ref.shape[0]):
         total += got_ref[j].astype(f32)
-    total = total.astype(pay_ref.dtype)
-    for j in range(pay_ref.shape[0]):
-        pay_ref[j] = total
+    total_v[...] = total.astype(pay.dtype)
+    copies = [
+        pltpu.make_async_copy(total_v, pay.at[j], sems.at[j]) for j in range(pay.shape[0])
+    ]
+    for c in copies:
+        c.start()
+    for c in copies:
+        c.wait()
+
+
+def add(got, peers):
+    dims = got.shape[1:]
+    (pay,) = call(
+        add_kernel,
+        [shape((peers,) + dims, bf16)],
+        [VMEM],
+        (got,),
+        out_specs=(HBM,),
+        scratch_shapes=[pltpu.VMEM(dims, bf16), pltpu.SemaphoreType.DMA((peers,))],
+    )
+    return pay
 
 
 def whole_gradient(got_ref, rank):
@@ -242,22 +263,30 @@
     ).astype(bf16)
 
 
-def frozen_kernel(got_gk, frozen, acts, out):
-    del acts
+def input_kernel(place, near, far, up, down_w, frozen, out, gk):
     rows = out.shape[0]
-    peers, long, _ = got_gk.shape
-    gk = jnp.concatenate([got_gk[j, long - rows :, :] for j in range(peers)], axis=1)
-    out[...] = dot(gk, frozen[...], NT)
-
-
-def beside_kernel(got, down_w, part, out, base_out, pa_out):
-    rows = out.shape[0]
+    lanes = near.shape[1]
+    count = near.shape[0] // rows
+    for i in range(2 * count):
+        ref = near if i < count else far
+        block = ref[(i % count) * rows : (i % count + 1) * rows, :]
+        owner = place[0] ^ owner_mask(i)
+        gk[:, pl.ds(pl.multiple_of(owner * lanes, lanes), lanes)] = block
+    a_half = down_w[...].astype(bf16)
+    out[...] = (
+        dot(gk[...], frozen[...], NT) + adapter_scale * dot(up[...], a_half, NT)
+    ).astype(bf16)
+
+
+def beside_kernel(got, two, other, base_out, pa_out, up_out, four):
+    count = two.shape[0]
+    four[:count, :] = two[...]
+    four[count:, :] = other[...]
+    rows = base_out.shape[0]
     peers, long, _ = got.shape
     piece = rows // peers
     first = long - rows
-    a_half = down_w[...].astype(bf16)
-    up = rejoin(got, 0, piece)
-    out[...] = (part[...] + adapter_scale * dot(up, a_half, NT)).astype(bf16)
+    up_out[...] = rejoin(got, 0, piece)
     total = got[0, first - piece :, :].astype(f32)
     for j in range(1, peers):
         total += got[j, first - piece :, :].astype(f32)
@@ -278,7 +307,7 @@
 
     gk, pay = call(
         parts_kernel,
-        [shape((rows, cols), bf16), shape((n_f, 2 * piece + rows, rank), bf16)],
+        [shape((rows, cols), bf16), shape((n_f, 2 * piece, rank), bf16)],
         [SMEM, SMEM] + [ANY] * 4,
         (lengths, buckets, acts, output_gradient, down_w, up_w),
         flops=2 * rows * rank * (width + cols),
@@ -291,15 +320,16 @@
             pltpu.VMEM((rank, cols), f32),
             pltpu.VMEM((rows, cols), bf16),
             pltpu.VMEM((n_f, 2 * piece, rank), bf16),
-            pltpu.SemaphoreType.DMA((6 + n_f,)),
+            pltpu.SemaphoreType.DMA((6,)),
         ],
     )
-    got_gk = swap(pay, FSDP)
+    got = swap(pay, FSDP)
+    other = lax.ppermute(gk, "zlo", Z_PAIRS)
     (pay,) = call(
         prompts_kernel,
         [shape((n_f, long, cols), bf16)],
-        [VMEM] * 3,
-        (prompts, frozen, down_w),
+        [VMEM] * 4,
+        (prompts, frozen, down_w, acts),
         flops=2 * rows * width * (cols * n_f + rank),
         out_specs=(HBM,),
         scratch_shapes=[
@@ -308,24 +338,20 @@
             pltpu.SemaphoreType.DMA((2,)),
         ],
     )
+    got, pay, other = lax.optimization_barrier((got, pay, other))
     (pay,) = call(
         sums_kernel,
         [shape((n_f, long, cols), bf16)],
         [VMEM, HBM],
-        (got_gk, pay),
+        (got, pay),
         input_output_aliases={1: 0},
         out_specs=(HBM,),
         scratch_shapes=[pltpu.VMEM((2 * piece, rank), bf16), pltpu.SemaphoreType.DMA((n_f,))],
     )
     got = swap(pay, FSDP)
-    (input_part,) = call(
-        frozen_kernel,
-        [shape((rows, width), f32)],
-        [VMEM] * 3,
-        (got_gk, frozen, acts),
-        flops=2 * rows * width * cols * n_f,
-    )
-    got, input_part = lax.optimization_barrier((got, input_part))
+    two = jnp.concatenate([gk, other], axis=0)
+    other = lax.ppermute(two, "x", X_NEAR)
+    got, two, other = lax.optimization_barrier((got, two, other))
 
     (pay,) = call(
         grads_kernel,
@@ -337,20 +363,30 @@
         scratch_shapes=[pltpu.VMEM((n_near, slab, rank), bf16), pltpu.SemaphoreType.DMA],
     )
     got_g = swap(pay, NEAR)
-    input_gradient, base, pa_rows = call(
+    base, pa_rows, up, four = call(
         beside_kernel,
-        [shape((rows, width), bf16), shape((rows, cols), f32), shape((piece, rank), bf16)],
+        [
+            shape((rows, cols), f32),
+            shape((piece, rank), bf16),
+            shape((rows, rank), bf16),
+            shape((4 * rows, cols), bf16),
+        ],
         [VMEM] * 3,
-        (got, down_w, input_part),
-        flops=2 * rows * width * rank,
-    )
-    got_g, input_gradient, base, pa_rows = lax.optimization_barrier(
-        (got_g, input_gradient, base, pa_rows)
-    )
-    (pay,) = call(add_kernel, [shape((n_far, slab, rank), bf16)], [VMEM], (got_g,))
-    got = swap(pay, FAR)
-    (pay,) = call(add_kernel, [shape((n_near, slab, rank), bf16)], [VMEM], (got,))
-    got_g = swap(pay, NEAR)
+        (got, two, other),
+    )
+    other = lax.ppermute(four, "x", X_FAR)
+    got_g, base, pa_rows, up = lax.optimization_barrier((got_g, base, pa_rows, up))
+    got = swap(add(got_g, n_far), FAR)
+    got_g = swap(add(got, n_near), NEAR)
+    (input_gradient,) = call(
+        input_kernel,
+        [shape((rows, width), bf16)],
+        [SMEM] + [VMEM] * 5,
+        (lax.axis_index(FSDP).reshape(1), four, other, up, down_w, frozen),
+        flops=2 * rows * width * (cols * n_f + rank),
+        scratch_shapes=[pltpu.VMEM((rows, cols * n_f), bf16)],
+    )
+    got_g, input_gradient = lax.optimization_barrier((got_g, input_gradient))
     (pay,) = call(
         project_kernel,
         [shape((n_f, rows + TAIL + piece, rank), bf16)],

time: 125 us -> 123 us (0.984)
  blocking collectives: 50.5 us -> 37.5 us
  starting transfers between devices: 25.5 us -> 37.4 us
  waiting for transfers between devices: 31.8 us -> 26.5 us
  Pallas kernels: 10.9 us -> 13.8 us
    all_to_all x3 -> x4, waiting for transfers between devices: 31.8 us -> 9.8 us  [swap(): return lax.all_to_all(v, axis, 0, 0, tiled=True)]
    ppermute x0 -> x3, waiting for transfers between devices: none -> 16.7 us  [the longest x1 16.7 us: per_device(): other = lax.ppermute(two, 'x', X_NEAR)]
    all_to_all x3 -> x2, blocking collectives: 50.5 us -> 37.5 us  [swap(): return lax.all_to_all(v, axis, 0, 0, tiled=True)]
    ppermute x0 -> x3, starting transfers between devices: none -> 10.4 us  [the longest x1 3.69 us: per_device(): other = lax.ppermute(four, 'x', X_FAR)]
    pallas_call x10, Pallas kernels: 10.9 us -> 13.8 us  [call(): pl.pallas_call(kernel, grid=(1,), in_specs=[spec or block(a) for spec, a...]
    all_to_all x3 -> x4, starting transfers between devices: 25.5 us -> 26.9 us  [swap(): return lax.all_to_all(v, axis, 0, 0, tiled=True)]
    unnamed x22 -> x23, local copies, waits for them, and re-layouts: 5.03 us -> 5.01 us
  transfers between devices with their start and end apart: 3 -> 7, of which waited for: 3 -> 3; matrix products, arithmetic and copies ran while one was open for 0% -> 1% of each run, Pallas kernels for 3% -> 6%
where the time goes in v5:
time: 123 us; the launch traced here: 122 us
  blocking collectives  37.5 us (30%)
  starting transfers between devices  37.4 us (30%)
  waiting for transfers between devices  26.5 us (22%)
  Pallas kernels  13.8 us (11%)
  local copies, waits for them, and re-layouts  5.94 us (5%)
    all_to_all x2, blocking collectives, swap(): return lax.all_to_all(v, axis, 0, 0, tiled=True)  37.5 us
    all_to_all x4, starting transfers between devices, swap(): return lax.all_to_all(v, axis, 0, 0, tiled=True)  26.9 us
    ppermute x1, waiting for transfers between devices, per_device(): other = lax.ppermute(two, 'x', X_NEAR)  16.7 us
    pallas_call x10, Pallas kernels, call(): pl.pallas_call(kernel, grid=(1,), in_specs=[spec or block(a) for spec, a...  13.8 us
    all_to_all x4, waiting for transfers between devices, swap(): return lax.all_to_all(v, axis, 0, 0, tiled=True)  9.8 us
    unnamed x23, local copies, waits for them, and re-layouts  5.01 us
    ppermute x1, starting transfers between devices, per_device(): other = lax.ppermute(four, 'x', X_FAR)  3.69 us
    ppermute x1, starting transfers between devices, per_device(): other = lax.ppermute(two, 'x', X_NEAR)  3.36 us
  transfers between devices with their start and end apart: 7, of which 3 were waited for; matrix products, arithmetic and copies ran while one was open for 1% of the time, Pallas kernels for 6%

profile of v5, /device:TPU:1, one launch (start us, length us, event | category | flops | bytes accessed | tf_op | source)
XLA Modules:
  0.0 121.9 jit_solution(8932572253081150973)
XLA Ops:
  0.7 3.2 %shard_map.111 = (bf16[512,128]{1,0:T(8,128)(2,1)}, bf16[8,128,128]{2,1,0:T(8,128)(2,1)}) custom-call(s32[2]{0:T(128)} %lens.1, s32[2]{0:T(128)} %buckets.1, bf16[512,640]{1,0:T(8,128)(2,1)} %acts.5, bf16[512,128]{1,0:T(8,128)(2,1)} %og.1, f32[640,128]{1,0:T(8,128)} %down_w.7, f32[128,128]{1,0:T(8,128)} %up_w.3), custom_call_target="tpu_custom_call" | custom-call | flops 100663296 | bytes 1572880 | tf_op jit(solution)/shard_map/pallas_call | solution.py:58
  3.9 6.7 %all-to-all-start = ((bf16[8,128,128]{2,1,0:T(8,128)(2,1)}), bf16[8,128,128]{2,1,0:T(8,128)(2,1)S(1)}, u32[]{:S(2)}, u32[]{:S(2)}) async-start(bf16[8,128,128]{2,1,0:T(8,128)(2,1)} %get-tuple-element.25), calls=%async_computation | async-start | bytes 524288 | tf_op jit(solution)/shard_map/all_to_all | solution.py:40
  10.6 3.4 %collective-permute-start = (bf16[512,128]{1,0:T(8,128)(2,1)}, bf16[512,128]{1,0:T(8,128)(2,1)}, u32[]{:S(2)}, u32[]{:S(2)}) collective-permute-start(bf16[512,128]{1,0:T(8,128)(2,1)} %get-tuple-element.26.gk), channel_id=1, source_target_pairs={{0,2},{2,0},{1,3},{3,1},{4,6},{6,4},{5,7},{7,5},{8,10},{10,8},{9,1... | collective-permute-start | bytes 393224 | tf_op jit(solution)/shard_map/ppermute | solution.py:327
  14.0 0.0 copy-start.2
  14.0 1.3 %copy-done.2 = bf16[640,1024]{1,0:T(8,128)(2,1)S(1)} copy-done((bf16[640,1024]{1,0:T(8,128)(2,1)S(1)}, bf16[640,1024]{1,0:T(8,128)(2,1)}, u32[]{:S(2)}) %copy-start.2) | copy-done | bytes 1310744
  15.3 2.2 %shard_map.112.pay_in = bf16[8,704,128]{2,1,0:T(8,128)(2,1)} custom-call(bf16[512,640]{1,0:T(8,128)(2,1)S(1)} %copy-done.4, bf16[640,1024]{1,0:T(8,128)(2,1)S(1)} %copy-done.2, f32[640,128]{1,0:T(8,128)S(1)} %copy-done.1, bf16[512,640]{1,0:T(8,128)(2,1)S(1)} %copy-done), custom_call_target="tpu_custom_call" | custom-call | flops 754974720 | bytes 4390912 | tf_op jit(solution)/shard_map/pallas_call | solution.py:58
  17.5 0.8 shard_map.113
  18.3 0.0 copy-start.5
  18.3 5.0 %all-to-all-start.1 = ((bf16[8,704,128]{2,1,0:T(8,128)(2,1)}), bf16[8,704,128]{2,1,0:T(8,128)(2,1)S(1)}, u32[]{:S(2)}, u32[]{:S(2)}) async-start(bf16[8,704,128]{2,1,0:T(8,128)(2,1)} %shard_map.113), calls=%async_computation.1 | async-start | bytes 2883584 | tf_op jit(solution)/shard_map/all_to_all | solution.py:40
  23.4 0.9 constant_dynamic-update-slice_fusion.two
  24.3 3.4 %collective-permute-start.1 = (bf16[1024,128]{1,0:T(8,128)(2,1)S(1)}, bf16[1024,128]{1,0:T(8,128)(2,1)S(1)}, u32[]{:S(2)}, u32[]{:S(2)}) collective-permute-start(bf16[1024,128]{1,0:T(8,128)(2,1)S(1)} %constant_dynamic-update-slice_fusion.two), channel_id=1, source_target_pairs={{0,4},{4,0},{8,12},{12,8},{1,5},{5,1},{9,13},{13,9},{2,6},{6,2},{1... | collective-permute-start | bytes 786440 | tf_op jit(solution)/shard_map/ppermute | solution.py:353
  27.7 16.7 %collective-permute-done.1.other = bf16[1024,128]{1,0:T(8,128)(2,1)S(1)} collective-permute-done((bf16[1024,128]{1,0:T(8,128)(2,1)S(1)}, bf16[1024,128]{1,0:T(8,128)(2,1)S(1)}, u32[]{:S(2)}, u32[]{:S(2)}) %collective-permute-start.1) | collective-permute-done | bytes 262176 | tf_op jit(solution)/shard_map/ppermute | solution.py:353
  44.3 0.7 copy-done.6
  45.0 1.0 shard_map.114
  46.1 10.2 %all-to-all-start.2 = ((bf16[16,48,128]{2,1,0:T(8,128)(2,1)}), bf16[16,48,128]{2,1,0:T(8,128)(2,1)S(1)}, u32[]{:S(2)}, u32[]{:S(2)}) async-start(bf16[16,48,128]{2,1,0:T(8,128)(2,1)} %shard_map.114), calls=%async_computation.2 | async-start | bytes 393216 | tf_op jit(solution)/shard_map/all_to_all | solution.py:40
  56.3 0.9 copy-done.7
  57.2 0.9 shard_map.115
  58.1 0.7 copy-done.8
  58.8 3.7 %collective-permute-start.2 = (bf16[2048,128]{1,0:T(8,128)(2,1)}, bf16[2048,128]{1,0:T(8,128)(2,1)S(1)}, u32[]{:S(2)}, u32[]{:S(2)}) collective-permute-start(bf16[2048,128]{1,0:T(8,128)(2,1)} %get-tuple-element.37.near), channel_id=1, source_target_pairs={{0,12},{12,0},{4,8},{8,4},{1,13},{13,1},{5,9},{9,5},{2,14},{14,2},... | collective-permute-start | bytes 1572872 | tf_op jit(solution)/shard_map/ppermute | solution.py:377
  62.5 4.1 %all-to-all-done.2.got_ref = bf16[16,48,128]{2,1,0:T(8,128)(2,1)S(1)} async-done(((bf16[16,48,128]{2,1,0:T(8,128)(2,1)}), bf16[16,48,128]{2,1,0:T(8,128)(2,1)S(1)}, u32[]{:S(2)}, u32[]{:S(2)}) %all-to-all-start.2) | async-done | bytes 196640 | tf_op jit(solution)/shard_map/all_to_all | solution.py:40
  66.6 0.1 shard_map.116
  66.7 15.8 %all_to_all.30.got_ref = bf16[4,48,128]{2,1,0:T(8,128)(2,1)S(1)} all-to-all(bf16[4,48,128]{2,1,0:T(8,128)(2,1)S(1)} %shard_map.116), channel_id=1, replica_groups=mesh['zhi'=4,'y'=8,'x'=4,'zlo'=2,'core'=2] {'zhi'}, dimensions={0} | all-to-all | bytes 98304 | tf_op jit(solution)/shard_map/all_to_all | solution.py:40
  82.6 0.8 shard_map.117
  83.4 5.0 %all-to-all-start.4 = ((bf16[16,48,128]{2,1,0:T(8,128)(2,1)}), bf16[16,48,128]{2,1,0:T(8,128)(2,1)S(1)}, u32[]{:S(2)}, u32[]{:S(2)}) async-start(bf16[16,48,128]{2,1,0:T(8,128)(2,1)} %shard_map.117), calls=%async_computation.4 | async-start | bytes 393216 | tf_op jit(solution)/shard_map/all_to_all | solution.py:40
  88.4 0.0 copy-start.3
  88.5 1.3 %copy-done.3 = bf16[640,1024]{1,0:T(8,128)(2,1)S(1)} copy-done((bf16[640,1024]{1,0:T(8,128)(2,1)S(1)}, bf16[640,1024]{1,0:T(8,128)(2,1)}, u32[]{:S(2)}) %copy-start.3) | copy-done | bytes 1310744
  89.8 3.3 %shard_map.118 = bf16[512,640]{1,0:T(8,128)(2,1)} custom-call(s32[1]{0:T(128)} %bitcast.place, bf16[2048,128]{1,0:T(8,128)(2,1)} %get-tuple-element.37.near, bf16[2048,128]{1,0:T(8,128)(2,1)S(1)} %collective-permute-done.2.far, bf16[512,128]{1,0:T(8,128)(2,1)S(1)} %get-tuple-element.38.up, f32[640,128]{1,0:T(8,128)S(1)} %copy-done.1, ...), custom_call_target="tpu_custom_call" | custom-call | flops 754974720 | bytes 3473412 | tf_op jit(solution)/shard_map/pallas_call | solution.py:58
  93.0 5.7 %all-to-all-done.4.got_ref.got_g = bf16[16,48,128]{2,1,0:T(8,128)(2,1)S(1)} async-done(((bf16[16,48,128]{2,1,0:T(8,128)(2,1)}), bf16[16,48,128]{2,1,0:T(8,128)(2,1)S(1)}, u32[]{:S(2)}, u32[]{:S(2)}) %all-to-all-start.4) | async-done | bytes 196640 | tf_op jit(solution)/shard_map/all_to_all | solution.py:40
  98.8 0.4 shard_map.119
  99.1 0.0 copy-start.9
  99.1 21.7 %all_to_all.31.got = bf16[8,592,128]{2,1,0:T(8,128)(2,1)S(1)} all-to-all(bf16[8,592,128]{2,1,0:T(8,128)(2,1)S(1)} %shard_map.119), channel_id=1, replica_groups=mesh['zhi'=4,'y'=8,'x'=4,'zlo'=2,'core'=2] {'x','zlo'}, dimensions={0} | all-to-all | bytes 2424832 | tf_op jit(solution)/shard_map/all_to_all | solution.py:40
  120.8 1.1 shard_map.120
  (18 shorter events, 0.0 us)
Async XLA Ops:
  0.6 13.3 %copy-start.1 = (f32[640,128]{1,0:T(8,128)S(1)}, f32[640,128]{1,0:T(8,128)}, u32[]{:S(2)}) copy-start(f32[640,128]{1,0:T(8,128)} %down_w.7) | copy-start | bytes 983044
  0.6 13.3 %copy-start = (bf16[512,640]{1,0:T(8,128)(2,1)S(1)}, bf16[512,640]{1,0:T(8,128)(2,1)}, u32[]{:S(2)}) copy-start(bf16[512,640]{1,0:T(8,128)(2,1)} %acts.5) | copy-start | bytes 1966084
  0.7 13.3 %copy-start.4 = (bf16[512,640]{1,0:T(8,128)(2,1)S(1)}, bf16[512,640]{1,0:T(8,128)(2,1)}, u32[]{:S(2)}) copy-start(bf16[512,640]{1,0:T(8,128)(2,1)} %prompts.3) | copy-start | bytes 1966084
  3.9 13.6 %all-to-all-start = ((bf16[8,128,128]{2,1,0:T(8,128)(2,1)}), bf16[8,128,128]{2,1,0:T(8,128)(2,1)S(1)}, u32[]{:S(2)}, u32[]{:S(2)}) async-start(bf16[8,128,128]{2,1,0:T(8,128)(2,1)} %get-tuple-element.25), calls=%async_computation | async-start | bytes 524288 | tf_op jit(solution)/shard_map/all_to_all | solution.py:40
  10.6 6.9 %collective-permute-start = (bf16[512,128]{1,0:T(8,128)(2,1)}, bf16[512,128]{1,0:T(8,128)(2,1)}, u32[]{:S(2)}, u32[]{:S(2)}) collective-permute-start(bf16[512,128]{1,0:T(8,128)(2,1)} %get-tuple-element.26.gk), channel_id=1, source_target_pairs={{0,2},{2,0},{1,3},{3,1},{4,6},{6,4},{5,7},{7,5},{8,10},{10,8},{9,1... | collective-permute-start | bytes 393224 | tf_op jit(solution)/shard_map/ppermute | solution.py:327
  14.0 1.3 %copy-start.2 = (bf16[640,1024]{1,0:T(8,128)(2,1)S(1)}, bf16[640,1024]{1,0:T(8,128)(2,1)}, u32[]{:S(2)}) copy-start(bf16[640,1024]{1,0:T(8,128)(2,1)} %frozen.3) | copy-start | bytes 3932164
  18.3 5.0 %copy-start.5 = (bf16[512,128]{1,0:T(8,128)(2,1)S(1)}, bf16[512,128]{1,0:T(8,128)(2,1)}, u32[]{:S(2)}) copy-start(bf16[512,128]{1,0:T(8,128)(2,1)} %get-tuple-element.26.gk) | copy-start | bytes 393220
  18.3 26.7 %all-to-all-start.1 = ((bf16[8,704,128]{2,1,0:T(8,128)(2,1)}), bf16[8,704,128]{2,1,0:T(8,128)(2,1)S(1)}, u32[]{:S(2)}, u32[]{:S(2)}) async-start(bf16[8,704,128]{2,1,0:T(8,128)(2,1)} %shard_map.113), calls=%async_computation.1 | async-start | bytes 2883584 | tf_op jit(solution)/shard_map/all_to_all | solution.py:40
  24.3 20.0 %collective-permute-start.1 = (bf16[1024,128]{1,0:T(8,128)(2,1)S(1)}, bf16[1024,128]{1,0:T(8,128)(2,1)S(1)}, u32[]{:S(2)}, u32[]{:S(2)}) collective-permute-start(bf16[1024,128]{1,0:T(8,128)(2,1)S(1)} %constant_dynamic-update-slice_fusion.two), channel_id=1, source_target_pairs={{0,4},{4,0},{8,12},{12,8},{1,5},{5,1},{9,13},{13,9},{2,6},{6,2},{1... | collective-permute-start | bytes 786440 | tf_op jit(solution)/shard_map/ppermute | solution.py:353
  44.3 0.7 copy-start.6
  46.1 20.5 %all-to-all-start.2 = ((bf16[16,48,128]{2,1,0:T(8,128)(2,1)}), bf16[16,48,128]{2,1,0:T(8,128)(2,1)S(1)}, u32[]{:S(2)}, u32[]{:S(2)}) async-start(bf16[16,48,128]{2,1,0:T(8,128)(2,1)} %shard_map.114), calls=%async_computation.2 | async-start | bytes 393216 | tf_op jit(solution)/shard_map/all_to_all | solution.py:40
  56.3 0.9 copy-start.7
  58.1 0.7 copy-start.8
  58.8 29.6 %collective-permute-start.2 = (bf16[2048,128]{1,0:T(8,128)(2,1)}, bf16[2048,128]{1,0:T(8,128)(2,1)S(1)}, u32[]{:S(2)}, u32[]{:S(2)}) collective-permute-start(bf16[2048,128]{1,0:T(8,128)(2,1)} %get-tuple-element.37.near), channel_id=1, source_target_pairs={{0,12},{12,0},{4,8},{8,4},{1,13},{13,1},{5,9},{9,5},{2,14},{14,2},... | collective-permute-start | bytes 1572872 | tf_op jit(solution)/shard_map/ppermute | solution.py:377
  83.4 15.4 %all-to-all-start.4 = ((bf16[16,48,128]{2,1,0:T(8,128)(2,1)}), bf16[16,48,128]{2,1,0:T(8,128)(2,1)S(1)}, u32[]{:S(2)}, u32[]{:S(2)}) async-start(bf16[16,48,128]{2,1,0:T(8,128)(2,1)} %shard_map.117), calls=%async_computation.4 | async-start | bytes 393216 | tf_op jit(solution)/shard_map/all_to_all | solution.py:40
  88.4 1.3 %copy-start.3 = (bf16[640,1024]{1,0:T(8,128)(2,1)S(1)}, bf16[640,1024]{1,0:T(8,128)(2,1)}, u32[]{:S(2)}) copy-start(bf16[640,1024]{1,0:T(8,128)(2,1)} %frozen.3) | copy-start | bytes 3932164
  99.1 21.7 %copy-start.9 = (f32[512,128]{1,0:T(8,128)S(1)}, f32[512,128]{1,0:T(8,128)}, u32[]{:S(2)}) copy-start(f32[512,128]{1,0:T(8,128)} %copy-done.8) | copy-start | bytes 786436
  99.1 21.7 %copy-start.10 = (f32[128,128]{1,0:T(8,128)S(1)}, f32[128,128]{1,0:T(8,128)}, u32[]{:S(2)}) copy-start(f32[128,128]{1,0:T(8,128)} %up_w.3) | copy-start | bytes 196612

commit v6 on v5

--- a/solution.py
+++ b/solution.py
@@ -111,42 +111,49 @@
     last.wait()
 
 
-def prompts_kernel(prompts, frozen, down_w, acts, pay, base_v, proj_v, sems):
+def prompts_kernel(place, prompts, frozen, down_w, acts, proj_out, keep, send, base):
     del acts
-    peers, long, cols = pay.shape
     rows = prompts.shape[0]
-    piece = rows // peers
-    proj = dot(prompts[...], down_w[...].astype(bf16)).astype(bf16)
-    base = dot(prompts[...], frozen[...]).astype(bf16)
+    cols = keep.shape[1]
+    count = keep.shape[0] // rows
+    proj_out[...] = dot(prompts[...], down_w[...].astype(bf16)).astype(bf16)
+    base[...] = dot(prompts[...], frozen[...])
+    for i in range(2 * count):
+        owner = place[0] ^ owner_mask(i)
+        part = base[:, pl.ds(pl.multiple_of(owner * cols, cols), cols)]
+        here = pl.ds((i % count) * rows, rows)
+        if i < count:
+            keep[here, :] = part
+        else:
+            send[here, :] = part.astype(bf16)
+
+
+def halve_kernel(held, got, keep, send):
+    half = keep.shape[0]
+    keep[...] = held[:half, :] + got[:half, :].astype(f32)
+    send[...] = (held[half:, :] + got[half:, :].astype(f32)).astype(bf16)
+
+
+def halve(held, got):
+    half = held.shape[0] // 2
+    dims = (half, held.shape[1])
+    return call(halve_kernel, [shape(dims, f32), shape(dims, bf16)], [VMEM] * 2, (held, got))
+
+
+def sums_kernel(got_ref, proj, pay, pay_v, sem):
+    peers, long, _ = pay.shape
+    part = got_ref.shape[1]
+    piece = long - part
+    total = got_ref[0].astype(f32)
+    for j in range(1, peers):
+        total += got_ref[j].astype(f32)
+    total = total.astype(bf16)
     for j in range(peers):
-        proj_v[j] = proj[j * piece : (j + 1) * piece]
-        base_v[j] = base[:, j * cols : (j + 1) * cols]
-    copies = [
-        pltpu.make_async_copy(proj_v, pay.at[:, pl.ds(2 * piece, piece), :], sems.at[0]),
-        pltpu.make_async_copy(base_v, pay.at[:, pl.ds(3 * piece, rows), :], sems.at[1]),
-    ]
-    for c in copies:
-        c.start()
-    for c in copies:
-        c.wait()
-
-
-def sums_kernel(got_ref, pay_in, pay_ref, sums_ref, sems):
-    del pay_in
-    peers = got_ref.shape[0]
-    part = sums_ref.shape[0]
-    total = got_ref[0, :part, :].astype(f32)
-    for j in range(1, peers):
-        total += got_ref[j, :part, :].astype(f32)
-    sums_ref[...] = total.astype(bf16)
-    copies = [
-        pltpu.make_async_copy(sums_ref, pay_ref.at[j, pl.ds(0, part), :], sems.at[j])
-        for j in range(peers)
-    ]
-    for c in copies:
-        c.start()
-    for c in copies:
-        c.wait()
+        pay_v[j, :part, :] = total
+        pay_v[j, part:, :] = proj[j * piece : (j + 1) * piece, :]
+    copy = pltpu.make_async_copy(pay_v, pay, sem)
+    copy.start()
+    copy.wait()
 
 
 def rejoin(got_ref, first, piece):
@@ -238,7 +245,7 @@
         pay_ref[j, rows + TAIL :, :] = pa_rows[...]
 
 
-def finish_kernel(got, base, got_g, down_w, up_w, next_down, next_up, keys):
+def finish_kernel(got, base, base_got, got_g, down_w, up_w, next_down, next_up, keys):
     rows = keys.shape[0]
     rank = down_w.shape[1]
     peers = got.shape[0]
@@ -259,7 +266,7 @@
     next_up[...] = new_up
     proj = rejoin(got, rows + TAIL, rows // peers).astype(f32) - factor * p_g
     keys[...] = (
-        base[...] + adapter_scale * dot(proj.astype(bf16), new_up.astype(bf16))
+        base[...] + base_got[...].astype(f32) + adapter_scale * dot(proj.astype(bf16), new_up.astype(bf16))
     ).astype(bf16)
 
 
@@ -278,20 +285,17 @@
     ).astype(bf16)
 
 
-def beside_kernel(got, two, other, base_out, pa_out, up_out, four):
+def beside_kernel(got, two, other, pa_out, up_out, four):
     count = two.shape[0]
     four[:count, :] = two[...]
     four[count:, :] = other[...]
-    rows = base_out.shape[0]
-    peers, long, _ = got.shape
-    piece = rows // peers
-    first = long - rows
+    peers = got.shape[0]
+    piece = pa_out.shape[0]
     up_out[...] = rejoin(got, 0, piece)
-    total = got[0, first - piece :, :].astype(f32)
+    total = got[0, 2 * piece :, :].astype(f32)
     for j in range(1, peers):
-        total += got[j, first - piece :, :].astype(f32)
-    pa_out[...] = total[:piece].astype(bf16)
-    base_out[...] = total[piece:]
+        total += got[j, 2 * piece :, :].astype(f32)
+    pa_out[...] = total.astype(bf16)
 
 
 def per_device(acts, output_gradient, lengths, buckets, frozen, down_w, up_w, prompts):
@@ -303,7 +307,6 @@
     n_far = lax.axis_size(FAR)
     piece = rows // n_f
     slab = (width + cols) // n_near
-    long = 3 * piece + rows
 
     gk, pay = call(
         parts_kernel,
@@ -325,33 +328,33 @@
     )
     got = swap(pay, FSDP)
     other = lax.ppermute(gk, "zlo", Z_PAIRS)
-    (pay,) = call(
+    place = lax.axis_index(FSDP).reshape(1)
+    proj, held, send = call(
         prompts_kernel,
-        [shape((n_f, long, cols), bf16)],
-        [VMEM] * 4,
-        (prompts, frozen, down_w, acts),
+        [
+            shape((rows, rank), bf16),
+            shape((n_f // 2 * rows, cols), f32),
+            shape((n_f // 2 * rows, cols), bf16),
+        ],
+        [SMEM] + [VMEM] * 4,
+        (place, prompts, frozen, down_w, acts),
         flops=2 * rows * width * (cols * n_f + rank),
-        out_specs=(HBM,),
-        scratch_shapes=[
-            pltpu.VMEM((n_f, rows, cols), bf16),
-            pltpu.VMEM((n_f, piece, rank), bf16),
-            pltpu.SemaphoreType.DMA((2,)),
-        ],
-    )
-    got, pay, other = lax.optimization_barrier((got, pay, other))
+        scratch_shapes=[pltpu.VMEM((rows, cols * n_f), f32)],
+    )
+    got, proj, held, send, other = lax.optimization_barrier((got, proj, held, send, other))
     (pay,) = call(
         sums_kernel,
-        [shape((n_f, long, cols), bf16)],
-        [VMEM, HBM],
-        (got, pay),
-        input_output_aliases={1: 0},
+        [shape((n_f, 3 * piece, rank), bf16)],
+        [VMEM] * 2,
+        (got, proj),
         out_specs=(HBM,),
-        scratch_shapes=[pltpu.VMEM((2 * piece, rank), bf16), pltpu.SemaphoreType.DMA((n_f,))],
+        scratch_shapes=[pltpu.VMEM((n_f, 3 * piece, rank), bf16), pltpu.SemaphoreType.DMA],
     )
     got = swap(pay, FSDP)
     two = jnp.concatenate([gk, other], axis=0)
     other = lax.ppermute(two, "x", X_NEAR)
-    got, two, other = lax.optimization_barrier((got, two, other))
+    base_got = lax.ppermute(send, "x", X_FAR)
+    got, two = lax.optimization_barrier((got, two))
 
     (pay,) = call(
         grads_kernel,
@@ -363,30 +366,35 @@
         scratch_shapes=[pltpu.VMEM((n_near, slab, rank), bf16), pltpu.SemaphoreType.DMA],
     )
     got_g = swap(pay, NEAR)
-    base, pa_rows, up, four = call(
+    pa_rows, up, four = call(
         beside_kernel,
         [
-            shape((rows, cols), f32),
             shape((piece, rank), bf16),
             shape((rows, rank), bf16),
-            shape((4 * rows, cols), bf16),
+            shape((n_f // 2 * rows, cols), bf16),
         ],
         [VMEM] * 3,
         (got, two, other),
     )
     other = lax.ppermute(four, "x", X_FAR)
-    got_g, base, pa_rows, up = lax.optimization_barrier((got_g, base, pa_rows, up))
+    held, send = halve(held, base_got)
+    got_g, pa_rows, up, held, send = lax.optimization_barrier((got_g, pa_rows, up, held, send))
+    base_got = lax.ppermute(send, "x", X_NEAR)
     got = swap(add(got_g, n_far), FAR)
     got_g = swap(add(got, n_near), NEAR)
     (input_gradient,) = call(
         input_kernel,
         [shape((rows, width), bf16)],
         [SMEM] + [VMEM] * 5,
-        (lax.axis_index(FSDP).reshape(1), four, other, up, down_w, frozen),
+        (place, four, other, up, down_w, frozen),
         flops=2 * rows * width * (cols * n_f + rank),
         scratch_shapes=[pltpu.VMEM((rows, cols * n_f), bf16)],
     )
-    got_g, input_gradient = lax.optimization_barrier((got_g, input_gradient))
+    base, send = halve(held, base_got)
+    base_got = lax.ppermute(send, "zlo", Z_PAIRS)
+    got_g, input_gradient, base, base_got = lax.optimization_barrier(
+        (got_g, input_gradient, base, base_got)
+    )
     (pay,) = call(
         project_kernel,
         [shape((n_f, rows + TAIL + piece, rank), bf16)],
@@ -398,8 +406,8 @@
     next_down, next_up, keys = call(
         finish_kernel,
         [shape((width, rank), f32), shape((rank, cols), f32), shape((rows, cols), bf16)],
-        [VMEM] * 5,
-        (got, base, got_g, down_w, up_w),
+        [VMEM] * 6,
+        (got, base, base_got, got_g, down_w, up_w),
         flops=2 * rows * rank * cols,
     )
     return input_gradient, next_down, next_up, keys

time: 123 us -> 111 us (0.902)
  starting transfers between devices: 37.4 us -> 56.2 us
  waiting for transfers between devices: 26.5 us -> 7.78 us
  blocking collectives: 37.5 us -> 22 us
  Pallas kernels: 13.8 us -> 15.9 us
    ppermute x1, waiting for transfers between devices: 16.7 us -> 0.01 us  [per_device(): other = lax.ppermute(two, 'x', X_NEAR)]
    all_to_all x2 -> x1, blocking collectives: 37.5 us -> 22 us  [swap(): return lax.all_to_all(v, axis, 0, 0, tiled=True)]
    ppermute x0 -> x3, starting transfers between devices: none -> 11 us  [the longest x1 4.58 us: per_device(): base_got = lax.ppermute(send, 'x', X_FAR)]
    all_to_all x4 -> x5, starting transfers between devices: 26.9 us -> 37.2 us  [swap(): return lax.all_to_all(v, axis, 0, 0, tiled=True)]
    all_to_all x4 -> x5, waiting for transfers between devices: 9.8 us -> 7.76 us  [swap(): return lax.all_to_all(v, axis, 0, 0, tiled=True)]
    pallas_call x10 -> x12, Pallas kernels: 13.8 us -> 15.9 us  [call(): pl.pallas_call(kernel, grid=(1,), in_specs=[spec or block(a) for spec, a...]
    ppermute x1, starting transfers between devices: 3.36 us -> 1.92 us  [per_device(): other = lax.ppermute(two, 'x', X_NEAR)]
    unnamed x23 -> x29, local copies, waits for them, and re-layouts: 5.01 us -> 6.22 us
  transfers between devices with their start and end apart: 7 -> 11, of which waited for: 3 -> 3; matrix products, arithmetic and copies ran while one was open for 1% -> 1% of each run, Pallas kernels for 6% -> 9%
where the time goes in v6:
time: 111 us; the launch traced here: 110 us
  starting transfers between devices  56.2 us (51%)
  blocking collectives  22 us (20%)
  Pallas kernels  15.9 us (14%)
  waiting for transfers between devices  7.78 us (7%)
  local copies, waits for them, and re-layouts  7.14 us (6%)
    all_to_all x5, starting transfers between devices, swap(): return lax.all_to_all(v, axis, 0, 0, tiled=True)  37.2 us
    all_to_all x1, blocking collectives, swap(): return lax.all_to_all(v, axis, 0, 0, tiled=True)  22 us
    pallas_call x12, Pallas kernels, call(): pl.pallas_call(kernel, grid=(1,), in_specs=[spec or block(a) for spec, a...  15.9 us
    all_to_all x5, waiting for transfers between devices, swap(): return lax.all_to_all(v, axis, 0, 0, tiled=True)  7.76 us
    unnamed x29, local copies, waits for them, and re-layouts  6.22 us
    ppermute x1, starting transfers between devices, per_device(): base_got = lax.ppermute(send, 'x', X_FAR)  4.58 us
    ppermute x1, starting transfers between devices, per_device(): base_got = lax.ppermute(send, 'x', X_NEAR)  3.39 us
    ppermute x1, starting transfers between devices, per_device(): other = lax.ppermute(gk, 'zlo', Z_PAIRS)  3.36 us
  transfers between devices with their start and end apart: 11, of which 3 were waited for; matrix products, arithmetic and copies ran while one was open for 1% of the time, Pallas kernels for 9%

profile of v6, /device:TPU:1, one launch (start us, length us, event | category | flops | bytes accessed | tf_op | source)
XLA Modules:
  0.0 109.9 jit_solution(11378268507665885104)
XLA Ops:
  0.7 3.2 %shard_map.111 = (bf16[512,128]{1,0:T(8,128)(2,1)}, bf16[8,128,128]{2,1,0:T(8,128)(2,1)}) custom-call(s32[2]{0:T(128)} %lens.1, s32[2]{0:T(128)} %buckets.1, bf16[512,640]{1,0:T(8,128)(2,1)} %acts.5, bf16[512,128]{1,0:T(8,128)(2,1)} %og.1, f32[640,128]{1,0:T(8,128)} %down_w.7, f32[128,128]{1,0:T(8,128)} %up_w.3), custom_call_target="tpu_custom_call" | custom-call | flops 100663296 | bytes 1572880 | tf_op jit(solution)/shard_map/pallas_call | solution.py:58
  3.9 6.7 %all-to-all-start = ((bf16[8,128,128]{2,1,0:T(8,128)(2,1)}), bf16[8,128,128]{2,1,0:T(8,128)(2,1)S(1)}, u32[]{:S(2)}, u32[]{:S(2)}) async-start(bf16[8,128,128]{2,1,0:T(8,128)(2,1)} %get-tuple-element.35), calls=%async_computation | async-start | bytes 524288 | tf_op jit(solution)/shard_map/all_to_all | solution.py:40
  10.6 3.4 %collective-permute-start = (bf16[512,128]{1,0:T(8,128)(2,1)}, bf16[512,128]{1,0:T(8,128)(2,1)S(1)}, u32[]{:S(2)}, u32[]{:S(2)}) collective-permute-start(bf16[512,128]{1,0:T(8,128)(2,1)} %get-tuple-element.39.gk), channel_id=1, source_target_pairs={{0,2},{2,0},{1,3},{3,1},{4,6},{6,4},{5,7},{7,5},{8,10},{10,8},{9,1... | collective-permute-start | bytes 393224 | tf_op jit(solution)/shard_map/ppermute | solution.py:330
  14.0 1.3 %copy-done.1 = bf16[640,1024]{1,0:T(8,128)(2,1)S(1)} copy-done((bf16[640,1024]{1,0:T(8,128)(2,1)S(1)}, bf16[640,1024]{1,0:T(8,128)(2,1)}, u32[]{:S(2)}) %copy-start.1) | copy-done | bytes 1310744
  15.3 1.4 %shard_map.112 = (bf16[512,128]{1,0:T(8,128)(2,1)S(1)}, f32[2048,128]{1,0:T(8,128)S(1)}, bf16[2048,128]{1,0:T(8,128)(2,1)S(1)}) custom-call(s32[1]{0:T(128)} %bitcast.place, bf16[512,640]{1,0:T(8,128)(2,1)S(1)} %copy-done.4, bf16[640,1024]{1,0:T(8,128)(2,1)S(1)} %copy-done.1, f32[640,128]{1,0:T(8,128)S(1)} %copy-done.3, bf16[512,640]{1,0:T(8,128)(2,1)S(1)} %copy-done), custom_call_target="tpu_custom_call" | custom-call | flops 754974720 | bytes 4653060 | tf_op jit(solution)/shard_map/pallas_call | solution.py:58
  16.7 0.8 copy-done.11
  17.5 0.8 shard_map.113
  18.4 4.9 %all-to-all-start.1 = ((bf16[8,192,128]{2,1,0:T(8,128)(2,1)}), bf16[8,192,128]{2,1,0:T(8,128)(2,1)S(1)}, u32[]{:S(2)}, u32[]{:S(2)}) async-start(bf16[8,192,128]{2,1,0:T(8,128)(2,1)} %shard_map.113), calls=%async_computation.1 | async-start | bytes 786432 | tf_op jit(solution)/shard_map/all_to_all | solution.py:40
  23.2 4.6 %collective-permute-start.2 = (bf16[2048,128]{1,0:T(8,128)(2,1)}, bf16[2048,128]{1,0:T(8,128)(2,1)}, u32[]{:S(2)}, u32[]{:S(2)}) collective-permute-start(bf16[2048,128]{1,0:T(8,128)(2,1)} %copy-done.11), channel_id=1, source_target_pairs={{0,12},{12,0},{4,8},{8,4},{1,13},{13,1},{5,9},{9,5},{2,14},{14,2},... | collective-permute-start | bytes 1572872 | tf_op jit(solution)/shard_map/ppermute | solution.py:356
  27.8 0.9 constant_dynamic-update-slice_fusion.two
  28.8 1.9 %collective-permute-start.1 = (bf16[1024,128]{1,0:T(8,128)(2,1)S(1)}, bf16[1024,128]{1,0:T(8,128)(2,1)}, u32[]{:S(2)}, u32[]{:S(2)}) collective-permute-start(bf16[1024,128]{1,0:T(8,128)(2,1)S(1)} %constant_dynamic-update-slice_fusion.two), channel_id=1, source_target_pairs={{0,4},{4,0},{8,12},{12,8},{1,5},{5,1},{9,13},{13,9},{2,6},{6,2},{1... | collective-permute-start | bytes 786440 | tf_op jit(solution)/shard_map/ppermute | solution.py:355
  30.7 1.0 shard_map.114
  31.7 9.8 %all-to-all-start.2 = ((bf16[16,48,128]{2,1,0:T(8,128)(2,1)}), bf16[16,48,128]{2,1,0:T(8,128)(2,1)S(1)}, u32[]{:S(2)}, u32[]{:S(2)}) async-start(bf16[16,48,128]{2,1,0:T(8,128)(2,1)} %shard_map.114), calls=%async_computation.2 | async-start | bytes 393216 | tf_op jit(solution)/shard_map/all_to_all | solution.py:40
  41.6 1.8 %shard_map.115 = (bf16[64,128]{1,0:T(8,128)(2,1)S(1)}, bf16[512,128]{1,0:T(8,128)(2,1)S(1)}, bf16[2048,128]{1,0:T(8,128)(2,1)}) custom-call(bf16[8,192,128]{2,1,0:T(8,128)(2,1)S(1)} %all-to-all-done.1.got_ref.got, bf16[1024,128]{1,0:T(8,128)(2,1)S(1)} %constant_dynamic-update-slice_fusion.two, bf16[1024,128]{1,0:T(8,128)(2,1)} %collective-permute-done.1.other), custom_call_target="tpu_custom_call" | custom-call | bytes 1589248 | tf_op jit(solution)/shard_map/pallas_call | solution.py:58
  44.0 2.8 %collective-permute-start.3 = (bf16[2048,128]{1,0:T(8,128)(2,1)}, bf16[2048,128]{1,0:T(8,128)(2,1)}, u32[]{:S(2)}, u32[]{:S(2)}) collective-permute-start(bf16[2048,128]{1,0:T(8,128)(2,1)} %get-tuple-element.52.near), channel_id=1, source_target_pairs={{0,12},{12,0},{4,8},{8,4},{1,13},{13,1},{5,9},{9,5},{2,14},{14,2},... | collective-permute-start | bytes 1572872 | tf_op jit(solution)/shard_map/ppermute | solution.py:379
  46.9 1.1 %shard_map.116 = (f32[1024,128]{1,0:T(8,128)S(1)}, bf16[1024,128]{1,0:T(8,128)(2,1)S(1)}) custom-call(f32[2048,128]{1,0:T(8,128)S(1)} %get-tuple-element.47.held, bf16[2048,128]{1,0:T(8,128)(2,1)} %collective-permute-done.2.got), custom_call_target="tpu_custom_call" | custom-call | bytes 2359296 | tf_op jit(solution)/shard_map/pallas_call | solution.py:58
  48.0 0.8 copy-done.5
  48.8 0.7 copy-done.12
  49.5 2.4 %all-to-all-done.2.got_ref = bf16[16,48,128]{2,1,0:T(8,128)(2,1)S(1)} async-done(((bf16[16,48,128]{2,1,0:T(8,128)(2,1)}), bf16[16,48,128]{2,1,0:T(8,128)(2,1)S(1)}, u32[]{:S(2)}, u32[]{:S(2)}) %all-to-all-start.2) | async-done | bytes 196640 | tf_op jit(solution)/shard_map/all_to_all | solution.py:40
  51.9 0.7 shard_map.117
  52.6 9.1 %all-to-all-start.3 = ((bf16[4,48,128]{2,1,0:T(8,128)(2,1)}), bf16[4,48,128]{2,1,0:T(8,128)(2,1)S(1)}, u32[]{:S(2)}, u32[]{:S(2)}) async-start(bf16[4,48,128]{2,1,0:T(8,128)(2,1)} %shard_map.117), calls=%async_computation.3 | async-start | bytes 98304 | tf_op jit(solution)/shard_map/all_to_all | solution.py:40
  61.7 3.4 %collective-permute-start.4 = (bf16[1024,128]{1,0:T(8,128)(2,1)}, bf16[1024,128]{1,0:T(8,128)(2,1)S(1)}, u32[]{:S(2)}, u32[]{:S(2)}) collective-permute-start(bf16[1024,128]{1,0:T(8,128)(2,1)} %copy-done.12), channel_id=1, source_target_pairs={{0,4},{4,0},{8,12},{12,8},{1,5},{5,1},{9,13},{13,9},{2,6},{6,2},{1... | collective-permute-start | bytes 786440 | tf_op jit(solution)/shard_map/ppermute | solution.py:382
  65.1 3.5 %all-to-all-done.3.got_ref = bf16[4,48,128]{2,1,0:T(8,128)(2,1)S(1)} async-done(((bf16[4,48,128]{2,1,0:T(8,128)(2,1)}), bf16[4,48,128]{2,1,0:T(8,128)(2,1)S(1)}, u32[]{:S(2)}, u32[]{:S(2)}) %all-to-all-start.3) | async-done | bytes 49184 | tf_op jit(solution)/shard_map/all_to_all | solution.py:40
  68.6 0.8 shard_map.118
  69.4 6.7 %all-to-all-start.4 = ((bf16[16,48,128]{2,1,0:T(8,128)(2,1)}), bf16[16,48,128]{2,1,0:T(8,128)(2,1)S(1)}, u32[]{:S(2)}, u32[]{:S(2)}) async-start(bf16[16,48,128]{2,1,0:T(8,128)(2,1)} %shard_map.118), calls=%async_computation.4 | async-start | bytes 393216 | tf_op jit(solution)/shard_map/all_to_all | solution.py:40
  76.2 1.0 copy-done.6
  77.2 3.0 %collective-permute-start.5 = (bf16[512,128]{1,0:T(8,128)(2,1)S(1)}, bf16[512,128]{1,0:T(8,128)(2,1)S(1)}, u32[]{:S(2)}, u32[]{:S(2)}) collective-permute-start(bf16[512,128]{1,0:T(8,128)(2,1)S(1)} %get-tuple-element.57), channel_id=1, source_target_pairs={{0,2},{2,0},{1,3},{3,1},{4,6},{6,4},{5,7},{7,5},{8,10},{10,8},{9,1... | collective-permute-start | bytes 393224 | tf_op jit(solution)/shard_map/ppermute | solution.py:394
  80.3 0.9 copy-done.10
  81.2 3.4 %shard_map.119 = bf16[512,640]{1,0:T(8,128)(2,1)} custom-call(s32[1]{0:T(128)} %bitcast.place, bf16[2048,128]{1,0:T(8,128)(2,1)} %get-tuple-element.52.near, bf16[2048,128]{1,0:T(8,128)(2,1)} %collective-permute-done.3.far, bf16[512,128]{1,0:T(8,128)(2,1)S(1)} %copy-done.10, f32[640,128]{1,0:T(8,128)S(1)} %copy-done.3, bf16[640,1024]{1,0:T(8,128)(2,1)S(1)} %copy-done.2), custom_call_target="tpu_custom_call" | custom-call | flops 754974720 | bytes 3473412 | tf_op jit(solution)/shard_map/pallas_call | solution.py:58
  84.6 1.9 %all-to-all-done.4.got_ref.got_g = bf16[16,48,128]{2,1,0:T(8,128)(2,1)S(1)} async-done(((bf16[16,48,128]{2,1,0:T(8,128)(2,1)}), bf16[16,48,128]{2,1,0:T(8,128)(2,1)S(1)}, u32[]{:S(2)}, u32[]{:S(2)}) %all-to-all-start.4) | async-done | bytes 196640 | tf_op jit(solution)/shard_map/all_to_all | solution.py:40
  86.8 22.0 %all_to_all.30.got = bf16[8,592,128]{2,1,0:T(8,128)(2,1)S(1)} all-to-all(bf16[8,592,128]{2,1,0:T(8,128)(2,1)S(1)} %shard_map.121), channel_id=1, replica_groups=mesh['zhi'=4,'y'=8,'x'=4,'zlo'=2,'core'=2] {'x','zlo'}, dimensions={0} | all-to-all | bytes 2424832 | tf_op jit(solution)/shard_map/all_to_all | solution.py:40
  108.8 1.1 %shard_map.122 = (f32[640,128]{1,0:T(8,128)}, f32[128,128]{1,0:T(8,128)}, bf16[512,128]{1,0:T(8,128)(2,1)}) custom-call(bf16[8,592,128]{2,1,0:T(8,128)(2,1)S(1)} %all_to_all.30.got, f32[512,128]{1,0:T(8,128)S(1)} %get-tuple-element.61.base, bf16[512,128]{1,0:T(8,128)(2,1)S(1)} %collective-permute-done.5.base_got, ...), custom_call_target="tpu_custom_call" | custom-call | flops 16777216 | bytes 2719744 | tf_op jit(solution)/shard_map/pallas_call | solution.py:58
  (33 shorter events, 1.1 us)
Async XLA Ops:
  0.6 13.3 %copy-start.3 = (f32[640,128]{1,0:T(8,128)S(1)}, f32[640,128]{1,0:T(8,128)}, u32[]{:S(2)}) copy-start(f32[640,128]{1,0:T(8,128)} %down_w.7) | copy-start | bytes 983044
  0.6 13.3 %copy-start = (bf16[512,640]{1,0:T(8,128)(2,1)S(1)}, bf16[512,640]{1,0:T(8,128)(2,1)}, u32[]{:S(2)}) copy-start(bf16[512,640]{1,0:T(8,128)(2,1)} %acts.5) | copy-start | bytes 1966084
  0.7 13.3 %copy-start.4 = (bf16[512,640]{1,0:T(8,128)(2,1)S(1)}, bf16[512,640]{1,0:T(8,128)(2,1)}, u32[]{:S(2)}) copy-start(bf16[512,640]{1,0:T(8,128)(2,1)} %prompts.3) | copy-start | bytes 1966084
  3.9 13.6 %all-to-all-start = ((bf16[8,128,128]{2,1,0:T(8,128)(2,1)}), bf16[8,128,128]{2,1,0:T(8,128)(2,1)S(1)}, u32[]{:S(2)}, u32[]{:S(2)}) async-start(bf16[8,128,128]{2,1,0:T(8,128)(2,1)} %get-tuple-element.35), calls=%async_computation | async-start | bytes 524288 | tf_op jit(solution)/shard_map/all_to_all | solution.py:40
  10.6 7.0 %collective-permute-start = (bf16[512,128]{1,0:T(8,128)(2,1)}, bf16[512,128]{1,0:T(8,128)(2,1)S(1)}, u32[]{:S(2)}, u32[]{:S(2)}) collective-permute-start(bf16[512,128]{1,0:T(8,128)(2,1)} %get-tuple-element.39.gk), channel_id=1, source_target_pairs={{0,2},{2,0},{1,3},{3,1},{4,6},{6,4},{5,7},{7,5},{8,10},{10,8},{9,1... | collective-permute-start | bytes 393224 | tf_op jit(solution)/shard_map/ppermute | solution.py:330
  14.0 1.3 %copy-start.1 = (bf16[640,1024]{1,0:T(8,128)(2,1)S(1)}, bf16[640,1024]{1,0:T(8,128)(2,1)}, u32[]{:S(2)}) copy-start(bf16[640,1024]{1,0:T(8,128)(2,1)} %frozen.3) | copy-start | bytes 3932164
  16.7 0.8 copy-start.11
  17.5 5.7 %copy-start.7 = (bf16[512,128]{1,0:T(8,128)(2,1)S(1)}, bf16[512,128]{1,0:T(8,128)(2,1)}, u32[]{:S(2)}) copy-start(bf16[512,128]{1,0:T(8,128)(2,1)} %get-tuple-element.39.gk) | copy-start | bytes 393220
  17.5 0.8 copy-start.13
  18.4 12.3 %all-to-all-start.1 = ((bf16[8,192,128]{2,1,0:T(8,128)(2,1)}), bf16[8,192,128]{2,1,0:T(8,128)(2,1)S(1)}, u32[]{:S(2)}, u32[]{:S(2)}) async-start(bf16[8,192,128]{2,1,0:T(8,128)(2,1)} %shard_map.113), calls=%async_computation.1 | async-start | bytes 786432 | tf_op jit(solution)/shard_map/all_to_all | solution.py:40
  23.2 23.6 %collective-permute-start.2 = (bf16[2048,128]{1,0:T(8,128)(2,1)}, bf16[2048,128]{1,0:T(8,128)(2,1)}, u32[]{:S(2)}, u32[]{:S(2)}) collective-permute-start(bf16[2048,128]{1,0:T(8,128)(2,1)} %copy-done.11), channel_id=1, source_target_pairs={{0,12},{12,0},{4,8},{8,4},{1,13},{13,1},{5,9},{9,5},{2,14},{14,2},... | collective-permute-start | bytes 1572872 | tf_op jit(solution)/shard_map/ppermute | solution.py:356
  28.8 12.8 %collective-permute-start.1 = (bf16[1024,128]{1,0:T(8,128)(2,1)S(1)}, bf16[1024,128]{1,0:T(8,128)(2,1)}, u32[]{:S(2)}, u32[]{:S(2)}) collective-permute-start(bf16[1024,128]{1,0:T(8,128)(2,1)S(1)} %constant_dynamic-update-slice_fusion.two), channel_id=1, source_target_pairs={{0,4},{4,0},{8,12},{12,8},{1,5},{5,1},{9,13},{13,9},{2,6},{6,2},{1... | collective-permute-start | bytes 786440 | tf_op jit(solution)/shard_map/ppermute | solution.py:355
  31.7 20.2 %all-to-all-start.2 = ((bf16[16,48,128]{2,1,0:T(8,128)(2,1)}), bf16[16,48,128]{2,1,0:T(8,128)(2,1)S(1)}, u32[]{:S(2)}, u32[]{:S(2)}) async-start(bf16[16,48,128]{2,1,0:T(8,128)(2,1)} %shard_map.114), calls=%async_computation.2 | async-start | bytes 393216 | tf_op jit(solution)/shard_map/all_to_all | solution.py:40
  43.4 0.7 copy-start.9
  44.0 36.2 %collective-permute-start.3 = (bf16[2048,128]{1,0:T(8,128)(2,1)}, bf16[2048,128]{1,0:T(8,128)(2,1)}, u32[]{:S(2)}, u32[]{:S(2)}) collective-permute-start(bf16[2048,128]{1,0:T(8,128)(2,1)} %get-tuple-element.52.near), channel_id=1, source_target_pairs={{0,12},{12,0},{4,8},{8,4},{1,13},{13,1},{5,9},{9,5},{2,14},{14,2},... | collective-permute-start | bytes 1572872 | tf_op jit(solution)/shard_map/ppermute | solution.py:379
  48.0 0.8 copy-start.5
  48.8 0.7 copy-start.12
  49.5 30.7 %copy-start.2 = (bf16[640,1024]{1,0:T(8,128)(2,1)S(1)}, bf16[640,1024]{1,0:T(8,128)(2,1)}, u32[]{:S(2)}) copy-start(bf16[640,1024]{1,0:T(8,128)(2,1)} %frozen.3) | copy-start | bytes 3932164
  52.6 16.0 %all-to-all-start.3 = ((bf16[4,48,128]{2,1,0:T(8,128)(2,1)}), bf16[4,48,128]{2,1,0:T(8,128)(2,1)S(1)}, u32[]{:S(2)}, u32[]{:S(2)}) async-start(bf16[4,48,128]{2,1,0:T(8,128)(2,1)} %shard_map.117), calls=%async_computation.3 | async-start | bytes 98304 | tf_op jit(solution)/shard_map/all_to_all | solution.py:40
  61.7 14.4 %collective-permute-start.4 = (bf16[1024,128]{1,0:T(8,128)(2,1)}, bf16[1024,128]{1,0:T(8,128)(2,1)S(1)}, u32[]{:S(2)}, u32[]{:S(2)}) collective-permute-start(bf16[1024,128]{1,0:T(8,128)(2,1)} %copy-done.12), channel_id=1, source_target_pairs={{0,4},{4,0},{8,12},{12,8},{1,5},{5,1},{9,13},{13,9},{2,6},{6,2},{1... | collective-permute-start | bytes 786440 | tf_op jit(solution)/shard_map/ppermute | solution.py:382
  69.4 17.0 %all-to-all-start.4 = ((bf16[16,48,128]{2,1,0:T(8,128)(2,1)}), bf16[16,48,128]{2,1,0:T(8,128)(2,1)S(1)}, u32[]{:S(2)}, u32[]{:S(2)}) async-start(bf16[16,48,128]{2,1,0:T(8,128)(2,1)} %shard_map.118), calls=%async_computation.4 | async-start | bytes 393216 | tf_op jit(solution)/shard_map/all_to_all | solution.py:40
  76.1 1.0 copy-start.6
  77.2 7.3 %collective-permute-start.5 = (bf16[512,128]{1,0:T(8,128)(2,1)S(1)}, bf16[512,128]{1,0:T(8,128)(2,1)S(1)}, u32[]{:S(2)}, u32[]{:S(2)}) collective-permute-start(bf16[512,128]{1,0:T(8,128)(2,1)S(1)} %get-tuple-element.57), channel_id=1, source_target_pairs={{0,2},{2,0},{1,3},{3,1},{4,6},{6,4},{5,7},{7,5},{8,10},{10,8},{9,1... | collective-permute-start | bytes 393224 | tf_op jit(solution)/shard_map/ppermute | solution.py:394
  80.3 0.9 copy-start.10
  86.8 22.0 %copy-start.8 = (f32[128,128]{1,0:T(8,128)S(1)}, f32[128,128]{1,0:T(8,128)}, u32[]{:S(2)}) copy-start(f32[128,128]{1,0:T(8,128)} %up_w.3) | copy-start | bytes 196612

commit v7 on v6

--- a/solution.py
+++ b/solution.py
@@ -111,49 +111,86 @@
     last.wait()
 
 
-def prompts_kernel(place, prompts, frozen, down_w, acts, proj_out, keep, send, base):
+def prompts_kernel(
+    place, prompts, frozen, down_w, acts, pay, keep, send, base, proj_v, keep_v, send_v, sems
+):
     del acts
     rows = prompts.shape[0]
-    cols = keep.shape[1]
+    peers, long, cols = pay.shape
+    piece = rows // peers
     count = keep.shape[0] // rows
-    proj_out[...] = dot(prompts[...], down_w[...].astype(bf16)).astype(bf16)
     base[...] = dot(prompts[...], frozen[...])
-    for i in range(2 * count):
+
+    def part(i):
         owner = place[0] ^ owner_mask(i)
-        part = base[:, pl.ds(pl.multiple_of(owner * cols, cols), cols)]
-        here = pl.ds((i % count) * rows, rows)
-        if i < count:
-            keep[here, :] = part
-        else:
-            send[here, :] = part.astype(bf16)
-
-
-def halve_kernel(held, got, keep, send):
+        return base[:, pl.ds(pl.multiple_of(owner * cols, cols), cols)]
+
+    for i in range(count):
+        send_v[i * rows : (i + 1) * rows, :] = part(count + i).astype(bf16)
+    copies = [pltpu.make_async_copy(send_v, send, sems.at[0])]
+    copies[0].start()
+    for i in range(count):
+        keep_v[i * rows : (i + 1) * rows, :] = part(i)
+    copies.append(pltpu.make_async_copy(keep_v, keep, sems.at[1]))
+    copies[1].start()
+    proj = dot(prompts[...], down_w[...].astype(bf16)).astype(bf16)
+    for j in range(peers):
+        proj_v[j] = proj[j * piece : (j + 1) * piece]
+    copies.append(
+        pltpu.make_async_copy(proj_v, pay.at[:, pl.ds(long - piece, piece), :], sems.at[2])
+    )
+    copies[2].start()
+    for c in copies:
+        c.wait()
+
+
+def halve_kernel(held, got, keep, send, keep_v, send_v, sems):
     half = keep.shape[0]
-    keep[...] = held[:half, :] + got[:half, :].astype(f32)
-    send[...] = (held[half:, :] + got[half:, :].astype(f32)).astype(bf16)
+    send_v[...] = (held[half:, :] + got[half:, :].astype(f32)).astype(bf16)
+    copies = [pltpu.make_async_copy(send_v, send, sems.at[0])]
+    copies[0].start()
+    keep_v[...] = held[:half, :] + got[:half, :].astype(f32)
+    copies.append(pltpu.make_async_copy(keep_v, keep, sems.at[1]))
+    copies[1].start()
+    for c in copies:
+        c.wait()
 
 
 def halve(held, got):
-    half = held.shape[0] // 2
-    dims = (half, held.shape[1])
-    return call(halve_kernel, [shape(dims, f32), shape(dims, bf16)], [VMEM] * 2, (held, got))
-
-
-def sums_kernel(got_ref, proj, pay, pay_v, sem):
-    peers, long, _ = pay.shape
-    part = got_ref.shape[1]
-    piece = long - part
+    dims = (held.shape[0] // 2, held.shape[1])
+    return call(
+        halve_kernel,
+        [shape(dims, f32), shape(dims, bf16)],
+        [VMEM] * 2,
+        (held, got),
+        out_specs=(HBM, HBM),
+        limit=60,
+        scratch_shapes=[
+            pltpu.VMEM(dims, f32),
+            pltpu.VMEM(dims, bf16),
+            pltpu.SemaphoreType.DMA((2,)),
+        ],
+    )
+
+
+def send_copies(value, pay, sems, first=0):
+    copies = [
+        pltpu.make_async_copy(value, pay.at[j, pl.ds(first, value.shape[0]), :], sems.at[j])
+        for j in range(pay.shape[0])
+    ]
+    for c in copies:
+        c.start()
+    for c in copies:
+        c.wait()
+
+
+def sums_kernel(got_ref, pay_in, pay, sums_v, sems):
+    del pay_in
     total = got_ref[0].astype(f32)
-    for j in range(1, peers):
+    for j in range(1, got_ref.shape[0]):
         total += got_ref[j].astype(f32)
-    total = total.astype(bf16)
-    for j in range(peers):
-        pay_v[j, :part, :] = total
-        pay_v[j, part:, :] = proj[j * piece : (j + 1) * piece, :]
-    copy = pltpu.make_async_copy(pay_v, pay, sem)
-    copy.start()
-    copy.wait()
+    sums_v[...] = total.astype(bf16)
+    send_copies(sums_v, pay, sems)
 
 
 def rejoin(got_ref, first, piece):
@@ -221,9 +258,9 @@
     ]
 
 
-def project_kernel(got_ref, prompts, pa_rows, pay_ref):
-    rank = pay_ref.shape[2]
-    rows = prompts.shape[0]
+def project_kernel(got_ref, prompts, pay):
+    peers, long, rank = pay.shape
+    piece = long - TAIL
     blocks = whole_gradient(got_ref, rank)
     squares = sum(b * b for b in blocks)
     total = jnp.sum(squares, keepdims=True)
@@ -239,34 +276,51 @@
     ).astype(bf16)
     g_down = jnp.concatenate(blocks[:-1], axis=1).astype(bf16)
     proj = dot(prompts[...], g_down, NT).astype(bf16)
-    for j in range(pay_ref.shape[0]):
-        pay_ref[j, :rows, :] = proj
-        pay_ref[j, rows : rows + TAIL, :] = tail
-        pay_ref[j, rows + TAIL :, :] = pa_rows[...]
-
-
-def finish_kernel(got, base, base_got, got_g, down_w, up_w, next_down, next_up, keys):
-    rows = keys.shape[0]
+    for j in range(peers):
+        pay[j, :piece, :] = proj[j * piece : (j + 1) * piece]
+        pay[j, piece:, :] = tail
+
+
+def step_factor(got):
+    peers, long, rank = got.shape
+    piece = long - TAIL
+    lane = lax.broadcasted_iota(jnp.int32, (TAIL, rank), 1)
+    row = lax.broadcasted_iota(jnp.int32, (TAIL, rank), 0)
+    tail = got[0, piece:, :].astype(f32)
+    for j in range(1, peers):
+        tail += got[j, piece:, :].astype(f32)
+    squares = jnp.sum(jnp.where((row == 0) & (lane < 3), tail, 0.0), keepdims=True)
+    return step_rate * jnp.minimum(1.0, clip_norm / jnp.sqrt(squares + 1e-12))
+
+
+def rows_kernel(got, pa_rows, pay, rows_v, sems):
+    peers, long, _ = got.shape
+    piece = long - TAIL
+    p_g = got[0, :piece, :].astype(f32)
+    for j in range(1, peers):
+        p_g += got[j, :piece, :].astype(f32)
+    rows_v[...] = (pa_rows[...] - step_factor(got) * p_g).astype(bf16)
+    send_copies(rows_v, pay, sems)
+
+
+def weights_kernel(got, got_g, down_w, up_w, base, base_got, next_down, next_up):
+    del base, base_got
     rank = down_w.shape[1]
-    peers = got.shape[0]
-    lane = lax.broadcasted_iota(jnp.int32, (TAIL, rank), 1)
-    place = lax.broadcasted_iota(jnp.int32, (TAIL, rank), 0)
-    p_g = got[0, :rows, :].astype(f32)
-    tail = got[0, rows : rows + TAIL, :].astype(f32)
-    for j in range(1, peers):
-        p_g += got[j, :rows, :].astype(f32)
-        tail += got[j, rows : rows + TAIL, :].astype(f32)
-    squares = jnp.sum(jnp.where((place == 0) & (lane < 3), tail, 0.0), keepdims=True)
-    factor = step_rate * jnp.minimum(1.0, clip_norm / jnp.sqrt(squares + 1e-12))
+    factor = step_factor(got)
     blocks = whole_gradient(got_g, rank)
-    for c, block in enumerate(blocks[:-1]):
+    for c, part in enumerate(blocks[:-1]):
         here = pl.ds(c * rank, rank)
-        next_down[here, :] = down_w[here, :] - factor * block.T
-    new_up = up_w[...] - factor * blocks[-1]
-    next_up[...] = new_up
-    proj = rejoin(got, rows + TAIL, rows // peers).astype(f32) - factor * p_g
+        next_down[here, :] = down_w[here, :] - factor * part.T
+    next_up[...] = up_w[...] - factor * blocks[-1]
+
+
+def keys_kernel(got, base, base_got, sums, got_g, up_w, keys):
+    proj = rejoin(got, 0, got.shape[1])
+    new_up = up_w[...] - step_factor(sums) * whole_gradient(got_g, up_w.shape[0])[-1]
     keys[...] = (
-        base[...] + base_got[...].astype(f32) + adapter_scale * dot(proj.astype(bf16), new_up.astype(bf16))
+        base[...]
+        + base_got[...].astype(f32)
+        + adapter_scale * dot(proj, new_up.astype(bf16))
     ).astype(bf16)
 
 
@@ -295,7 +349,7 @@
     total = got[0, 2 * piece :, :].astype(f32)
     for j in range(1, peers):
         total += got[j, 2 * piece :, :].astype(f32)
-    pa_out[...] = total.astype(bf16)
+    pa_out[...] = total
 
 
 def per_device(acts, output_gradient, lengths, buckets, frozen, down_w, up_w, prompts):
@@ -329,26 +383,33 @@
     got = swap(pay, FSDP)
     other = lax.ppermute(gk, "zlo", Z_PAIRS)
     place = lax.axis_index(FSDP).reshape(1)
-    proj, held, send = call(
+    half = n_f // 2 * rows
+    pay, held, send = call(
         prompts_kernel,
-        [
-            shape((rows, rank), bf16),
-            shape((n_f // 2 * rows, cols), f32),
-            shape((n_f // 2 * rows, cols), bf16),
-        ],
+        [shape((n_f, 3 * piece, rank), bf16), shape((half, cols), f32), shape((half, cols), bf16)],
         [SMEM] + [VMEM] * 4,
         (place, prompts, frozen, down_w, acts),
         flops=2 * rows * width * (cols * n_f + rank),
-        scratch_shapes=[pltpu.VMEM((rows, cols * n_f), f32)],
-    )
-    got, proj, held, send, other = lax.optimization_barrier((got, proj, held, send, other))
+        out_specs=(HBM, HBM, HBM),
+        limit=60,
+        scratch_shapes=[
+            pltpu.VMEM((rows, cols * n_f), f32),
+            pltpu.VMEM((n_f, piece, rank), bf16),
+            pltpu.VMEM((half, cols), f32),
+            pltpu.VMEM((half, cols), bf16),
+            pltpu.SemaphoreType.DMA((3,)),
+        ],
+    )
+    got, pay, held, send, other = lax.optimization_barrier((got, pay, held, send, other))
     (pay,) = call(
         sums_kernel,
-        [shape((n_f, 3 * piece, rank), bf16)],
-        [VMEM] * 2,
-        (got, proj),
+        [shape(pay.shape, bf16)],
+        [VMEM, HBM],
+        (got, pay),
+        input_output_aliases={1: 0},
         out_specs=(HBM,),
-        scratch_shapes=[pltpu.VMEM((n_f, 3 * piece, rank), bf16), pltpu.SemaphoreType.DMA],
+        limit=60,
+        scratch_shapes=[pltpu.VMEM((2 * piece, rank), bf16), pltpu.SemaphoreType.DMA((n_f,))],
     )
     got = swap(pay, FSDP)
     two = jnp.concatenate([gk, other], axis=0)
@@ -369,12 +430,13 @@
     pa_rows, up, four = call(
         beside_kernel,
         [
-            shape((piece, rank), bf16),
+            shape((piece, rank), f32),
             shape((rows, rank), bf16),
             shape((n_f // 2 * rows, cols), bf16),
         ],
         [VMEM] * 3,
         (got, two, other),
+        limit=60,
     )
     other = lax.ppermute(four, "x", X_FAR)
     held, send = halve(held, base_got)
@@ -382,6 +444,33 @@
     base_got = lax.ppermute(send, "x", X_NEAR)
     got = swap(add(got_g, n_far), FAR)
     got_g = swap(add(got, n_near), NEAR)
+    base, send = halve(held, base_got)
+    base_got = lax.ppermute(send, "zlo", Z_PAIRS)
+    got_g, base, base_got = lax.optimization_barrier((got_g, base, base_got))
+
+    (pay,) = call(
+        project_kernel,
+        [shape((n_f, piece + TAIL, rank), bf16)],
+        [VMEM] * 2,
+        (got_g, prompts),
+        flops=2 * rows * width * rank,
+    )
+    sums = swap(pay, FSDP)
+    (pay,) = call(
+        rows_kernel,
+        [shape((n_f, piece, rank), bf16)],
+        [VMEM] * 2,
+        (sums, pa_rows),
+        out_specs=(HBM,),
+        scratch_shapes=[pltpu.VMEM((piece, rank), bf16), pltpu.SemaphoreType.DMA((n_f,))],
+    )
+    got = swap(pay, FSDP)
+    next_down, next_up = call(
+        weights_kernel,
+        [shape((width, rank), f32), shape((rank, cols), f32)],
+        [VMEM] * 6,
+        (sums, got_g, down_w, up_w, base, base_got),
+    )
     (input_gradient,) = call(
         input_kernel,
         [shape((rows, width), bf16)],
@@ -390,24 +479,14 @@
         flops=2 * rows * width * (cols * n_f + rank),
         scratch_shapes=[pltpu.VMEM((rows, cols * n_f), bf16)],
     )
-    base, send = halve(held, base_got)
-    base_got = lax.ppermute(send, "zlo", Z_PAIRS)
-    got_g, input_gradient, base, base_got = lax.optimization_barrier(
-        (got_g, input_gradient, base, base_got)
-    )
-    (pay,) = call(
-        project_kernel,
-        [shape((n_f, rows + TAIL + piece, rank), bf16)],
-        [VMEM] * 3,
-        (got_g, prompts, pa_rows),
-        flops=2 * rows * width * rank,
-    )
-    got = swap(pay, FSDP)
-    next_down, next_up, keys = call(
-        finish_kernel,
-        [shape((width, rank), f32), shape((rank, cols), f32), shape((rows, cols), bf16)],
+    got, next_down, next_up, input_gradient = lax.optimization_barrier(
+        (got, next_down, next_up, input_gradient)
+    )
+    (keys,) = call(
+        keys_kernel,
+        [shape((rows, cols), bf16)],
         [VMEM] * 6,
-        (got, base, base_got, got_g, down_w, up_w),
+        (got, base, base_got, sums, got_g, up_w),
         flops=2 * rows * rank * cols,
     )
     return input_gradient, next_down, next_up, keys

time: 111 us -> 118 us (1.063); the launches traced: 110 us -> 116 us
  blocking collectives: 22 us -> 12.2 us
  Pallas kernels: 15.9 us -> 24.4 us
  waiting for transfers between devices: 7.78 us -> 16.1 us
  local copies, waits for them, and re-layouts: 7.14 us -> 2.28 us
  starting transfers between devices: 56.2 us -> 59.8 us
    all_to_all x1, blocking collectives: 22 us -> 12.2 us  [swap(): return lax.all_to_all(v, axis, 0, 0, tiled=True)]
    pallas_call x12 -> x14, Pallas kernels: 15.9 us -> 24.4 us  [call(): pl.pallas_call(kernel, grid=(1,), in_specs=[spec or block(a) for spec, a...]
    all_to_all x5 -> x6, starting transfers between devices: 37.2 us -> 42.7 us  [swap(): return lax.all_to_all(v, axis, 0, 0, tiled=True)]
    ppermute x1, waiting for transfers between devices: 0.01 us -> 4.67 us  [per_device(): other = lax.ppermute(two, 'x', X_NEAR)]
    unnamed x29 -> x33, local copies, waits for them, and re-layouts: 6.22 us -> 2.26 us
    ppermute x1, waiting for transfers between devices: 0.01 us -> 1.86 us  [per_device(): base_got = lax.ppermute(send, 'zlo', Z_PAIRS)]
    all_to_all x5 -> x6, waiting for transfers between devices: 7.76 us -> 9.52 us  [swap(): return lax.all_to_all(v, axis, 0, 0, tiled=True)]
    ppermute x1, starting transfers between devices: 3.39 us -> 1.91 us  [per_device(): base_got = lax.ppermute(send, 'x', X_NEAR)]
  transfers between devices with their start and end apart: 11 -> 12, of which waited for: 3 -> 6; matrix products, arithmetic and copies ran while one was open for 1% -> 0% of each run, Pallas kernels for 9% -> 15%
where the time goes in v7:
time: 118 us; the launch traced here: 116 us
  starting transfers between devices  59.8 us (51%)
  Pallas kernels  24.4 us (21%)
  waiting for transfers between devices  16.1 us (14%)
  blocking collectives  12.2 us (10%)
  local copies, waits for them, and re-layouts  2.28 us (2%)
    all_to_all x6, starting transfers between devices, swap(): return lax.all_to_all(v, axis, 0, 0, tiled=True)  42.7 us
    pallas_call x14, Pallas kernels, call(): pl.pallas_call(kernel, grid=(1,), in_specs=[spec or block(a) for spec, a...  24.4 us
    all_to_all x1, blocking collectives, swap(): return lax.all_to_all(v, axis, 0, 0, tiled=True)  12.2 us
    all_to_all x6, waiting for transfers between devices, swap(): return lax.all_to_all(v, axis, 0, 0, tiled=True)  9.52 us
    ppermute x1, waiting for transfers between devices, per_device(): other = lax.ppermute(two, 'x', X_NEAR)  4.67 us
    ppermute x1, starting transfers between devices, per_device(): base_got = lax.ppermute(send, 'x', X_FAR)  4.57 us
    ppermute x1, starting transfers between devices, per_device(): other = lax.ppermute(gk, 'zlo', Z_PAIRS)  3.36 us
    ppermute x1, starting transfers between devices, per_device(): base_got = lax.ppermute(send, 'zlo', Z_PAIRS)  2.66 us
  transfers between devices with their start and end apart: 12, of which 6 were waited for; matrix products, arithmetic and copies ran while one was open for 0% of the time, Pallas kernels for 15%

profile of v7, /device:TPU:1, one launch (start us, length us, event | category | flops | bytes accessed | tf_op | source)
XLA Modules:
  0.0 115.6 jit_solution(12623539570651672038)
XLA Ops:
  0.6 3.1 %shard_map.111 = (bf16[512,128]{1,0:T(8,128)(2,1)}, bf16[8,128,128]{2,1,0:T(8,128)(2,1)}) custom-call(s32[2]{0:T(128)} %lens.1, s32[2]{0:T(128)} %buckets.1, bf16[512,640]{1,0:T(8,128)(2,1)} %acts.5, bf16[512,128]{1,0:T(8,128)(2,1)} %og.1, f32[640,128]{1,0:T(8,128)} %down_w.7, f32[128,128]{1,0:T(8,128)} %up_w.5), custom_call_target="tpu_custom_call" | custom-call | flops 100663296 | bytes 1572880 | tf_op jit(solution)/shard_map/pallas_call | solution.py:58
  3.7 6.7 %all-to-all-start = ((bf16[8,128,128]{2,1,0:T(8,128)(2,1)}), bf16[8,128,128]{2,1,0:T(8,128)(2,1)S(1)}, u32[]{:S(2)}, u32[]{:S(2)}) async-start(bf16[8,128,128]{2,1,0:T(8,128)(2,1)} %get-tuple-element.37), calls=%async_computation | async-start | bytes 524288 | tf_op jit(solution)/shard_map/all_to_all | solution.py:40
  10.4 3.4 %collective-permute-start = (bf16[512,128]{1,0:T(8,128)(2,1)}, bf16[512,128]{1,0:T(8,128)(2,1)S(1)}, u32[]{:S(2)}, u32[]{:S(2)}) collective-permute-start(bf16[512,128]{1,0:T(8,128)(2,1)} %get-tuple-element.41.gk), channel_id=1, source_target_pairs={{0,2},{2,0},{1,3},{3,1},{4,6},{6,4},{5,7},{7,5},{8,10},{10,8},{9,1... | collective-permute-start | bytes 393224 | tf_op jit(solution)/shard_map/ppermute | solution.py:384
  13.8 4.2 %shard_map.112 = (bf16[8,192,128]{2,1,0:T(8,128)(2,1)}, f32[2048,128]{1,0:T(8,128)}, bf16[2048,128]{1,0:T(8,128)(2,1)}) custom-call(s32[1]{0:T(128)} %bitcast.place, bf16[512,640]{1,0:T(8,128)(2,1)} %prompts.3, bf16[640,1024]{1,0:T(8,128)(2,1)} %frozen.3, f32[640,128]{1,0:T(8,128)} %down_w.7, bf16[512,640]{1,0:T(8,128)(2,1)} %acts.5), custom_call_target="tpu_custom_call" | custom-call | flops 754974720 | bytes 4915204 | tf_op jit(solution)/shard_map/pallas_call | solution.py:58
  18.8 1.8 %shard_map.113 = bf16[8,192,128]{2,1,0:T(8,128)(2,1)} custom-call(bf16[8,128,128]{2,1,0:T(8,128)(2,1)} %copy-done.11, bf16[8,192,128]{2,1,0:T(8,128)(2,1)} %get-tuple-element.43.pay_in), custom_call_target="tpu_custom_call", output_to_operand_aliasing={{}: (1, {})} | custom-call | bytes 1048576 | tf_op jit(solution)/shard_map/pallas_call | solution.py:58
  20.5 4.2 %all-to-all-start.1 = ((bf16[8,192,128]{2,1,0:T(8,128)(2,1)}), bf16[8,192,128]{2,1,0:T(8,128)(2,1)S(1)}, u32[]{:S(2)}, u32[]{:S(2)}) async-start(bf16[8,192,128]{2,1,0:T(8,128)(2,1)} %shard_map.113), calls=%async_computation.1 | async-start | bytes 786432 | tf_op jit(solution)/shard_map/all_to_all | solution.py:40
  24.7 4.6 %collective-permute-start.2 = (bf16[2048,128]{1,0:T(8,128)(2,1)S(1)}, bf16[2048,128]{1,0:T(8,128)(2,1)S(1)}, u32[]{:S(2)}, u32[]{:S(2)}) collective-permute-start(bf16[2048,128]{1,0:T(8,128)(2,1)S(1)} %copy-done.15), channel_id=1, source_target_pairs={{0,12},{12,0},{4,8},{8,4},{1,13},{13,1},{5,9},{9,5},{2,14},{14,2},... | collective-permute-start | bytes 1572872 | tf_op jit(solution)/shard_map/ppermute | solution.py:417
  29.4 2.2 %all-to-all-done.1.got_ref.got = bf16[8,192,128]{2,1,0:T(8,128)(2,1)S(1)} async-done(((bf16[8,192,128]{2,1,0:T(8,128)(2,1)}), bf16[8,192,128]{2,1,0:T(8,128)(2,1)S(1)}, u32[]{:S(2)}, u32[]{:S(2)}) %all-to-all-start.1) | async-done | bytes 393248 | tf_op jit(solution)/shard_map/all_to_all | solution.py:40
  31.6 1.0 shard_map.114
  32.6 10.2 %all-to-all-start.2 = ((bf16[16,48,128]{2,1,0:T(8,128)(2,1)}), bf16[16,48,128]{2,1,0:T(8,128)(2,1)S(1)}, u32[]{:S(2)}, u32[]{:S(2)}) async-start(bf16[16,48,128]{2,1,0:T(8,128)(2,1)} %shard_map.114), calls=%async_computation.2 | async-start | bytes 393216 | tf_op jit(solution)/shard_map/all_to_all | solution.py:40
  42.8 1.9 %collective-permute-start.1 = (bf16[1024,128]{1,0:T(8,128)(2,1)S(1)}, bf16[1024,128]{1,0:T(8,128)(2,1)S(1)}, u32[]{:S(2)}, u32[]{:S(2)}) collective-permute-start(bf16[1024,128]{1,0:T(8,128)(2,1)S(1)} %constant_dynamic-update-slice_fusion.two), channel_id=1, source_target_pairs={{0,4},{4,0},{8,12},{12,8},{1,5},{5,1},{9,13},{13,9},{2,6},{6,2},{1... | collective-permute-start | bytes 786440 | tf_op jit(solution)/shard_map/ppermute | solution.py:416
  44.8 0.8 copy-done.13
  45.6 2.3 %shard_map.116 = (f32[1024,128]{1,0:T(8,128)}, bf16[1024,128]{1,0:T(8,128)(2,1)}) custom-call(f32[2048,128]{1,0:T(8,128)} %get-tuple-element.49.held, bf16[2048,128]{1,0:T(8,128)(2,1)} %copy-done.13), custom_call_target="tpu_custom_call" | custom-call | bytes 2359296 | tf_op jit(solution)/shard_map/pallas_call | solution.py:58
  47.9 4.7 %collective-permute-done.1.other = bf16[1024,128]{1,0:T(8,128)(2,1)S(1)} collective-permute-done((bf16[1024,128]{1,0:T(8,128)(2,1)S(1)}, bf16[1024,128]{1,0:T(8,128)(2,1)S(1)}, u32[]{:S(2)}, u32[]{:S(2)}) %collective-permute-start.1) | collective-permute-done | bytes 262176 | tf_op jit(solution)/shard_map/ppermute | solution.py:416
  53.3 2.0 %shard_map.115 = (f32[64,128]{1,0:T(8,128)}, bf16[512,128]{1,0:T(8,128)(2,1)}, bf16[2048,128]{1,0:T(8,128)(2,1)}) custom-call(bf16[8,192,128]{2,1,0:T(8,128)(2,1)} %copy-done.3, bf16[1024,128]{1,0:T(8,128)(2,1)} %copy-done.12, bf16[1024,128]{1,0:T(8,128)(2,1)} %copy-done.14), custom_call_target="tpu_custom_call" | custom-call | bytes 1605632 | tf_op jit(solution)/shard_map/pallas_call | solution.py:58
  56.0 9.1 %all-to-all-start.3 = ((bf16[4,48,128]{2,1,0:T(8,128)(2,1)}), bf16[4,48,128]{2,1,0:T(8,128)(2,1)S(1)}, u32[]{:S(2)}, u32[]{:S(2)}) async-start(bf16[4,48,128]{2,1,0:T(8,128)(2,1)} %shard_map.117), calls=%async_computation.3 | async-start | bytes 98304 | tf_op jit(solution)/shard_map/all_to_all | solution.py:40
  65.1 1.9 %collective-permute-start.3 = (bf16[1024,128]{1,0:T(8,128)(2,1)}, bf16[1024,128]{1,0:T(8,128)(2,1)}, u32[]{:S(2)}, u32[]{:S(2)}) collective-permute-start(bf16[1024,128]{1,0:T(8,128)(2,1)} %get-tuple-element.55), channel_id=1, source_target_pairs={{0,4},{4,0},{8,12},{12,8},{1,5},{5,1},{9,13},{13,9},{2,6},{6,2},{1... | collective-permute-start | bytes 786440 | tf_op jit(solution)/shard_map/ppermute | solution.py:444
  67.0 5.0 %all-to-all-done.3.got_ref = bf16[4,48,128]{2,1,0:T(8,128)(2,1)S(1)} async-done(((bf16[4,48,128]{2,1,0:T(8,128)(2,1)}), bf16[4,48,128]{2,1,0:T(8,128)(2,1)S(1)}, u32[]{:S(2)}, u32[]{:S(2)}) %all-to-all-start.3) | async-done | bytes 49184 | tf_op jit(solution)/shard_map/all_to_all | solution.py:40
  72.1 0.8 shard_map.118
  72.9 9.1 %all-to-all-start.4 = ((bf16[16,48,128]{2,1,0:T(8,128)(2,1)}), bf16[16,48,128]{2,1,0:T(8,128)(2,1)S(1)}, u32[]{:S(2)}, u32[]{:S(2)}) async-start(bf16[16,48,128]{2,1,0:T(8,128)(2,1)} %shard_map.118), calls=%async_computation.4 | async-start | bytes 393216 | tf_op jit(solution)/shard_map/all_to_all | solution.py:40
  82.1 2.0 %shard_map.119 = (f32[512,128]{1,0:T(8,128)}, bf16[512,128]{1,0:T(8,128)(2,1)}) custom-call(f32[1024,128]{1,0:T(8,128)} %get-tuple-element.54.held, bf16[1024,128]{1,0:T(8,128)(2,1)} %collective-permute-done.3.got), custom_call_target="tpu_custom_call" | custom-call | bytes 1179648 | tf_op jit(solution)/shard_map/pallas_call | solution.py:58
  84.1 2.7 %collective-permute-start.4 = (bf16[512,128]{1,0:T(8,128)(2,1)}, bf16[512,128]{1,0:T(8,128)(2,1)S(1)}, u32[]{:S(2)}, u32[]{:S(2)}) collective-permute-start(bf16[512,128]{1,0:T(8,128)(2,1)} %get-tuple-element.57), channel_id=1, source_target_pairs={{0,2},{2,0},{1,3},{3,1},{4,6},{6,4},{5,7},{7,5},{8,10},{10,8},{9,1... | collective-permute-start | bytes 393224 | tf_op jit(solution)/shard_map/ppermute | solution.py:448
  86.8 2.6 %collective-permute-start.5 = (bf16[2048,128]{1,0:T(8,128)(2,1)S(1)}, bf16[2048,128]{1,0:T(8,128)(2,1)}, u32[]{:S(2)}, u32[]{:S(2)}) collective-permute-start(bf16[2048,128]{1,0:T(8,128)(2,1)S(1)} %copy-done.7), channel_id=1, source_target_pairs={{0,12},{12,0},{4,8},{8,4},{1,13},{13,1},{5,9},{9,5},{2,14},{14,2},... | collective-permute-start | bytes 1572872 | tf_op jit(solution)/shard_map/ppermute | solution.py:441
  89.4 1.9 %collective-permute-done.4.base_got = bf16[512,128]{1,0:T(8,128)(2,1)S(1)} collective-permute-done((bf16[512,128]{1,0:T(8,128)(2,1)}, bf16[512,128]{1,0:T(8,128)(2,1)S(1)}, u32[]{:S(2)}, u32[]{:S(2)}) %collective-permute-start.4) | collective-permute-done | bytes 131104 | tf_op jit(solution)/shard_map/ppermute | solution.py:448
  91.3 1.1 all-to-all-done.4.got_ref.got_g
  92.7 12.2 %all_to_all.35.got.sums = bf16[8,80,128]{2,1,0:T(8,128)(2,1)S(1)} all-to-all(bf16[8,80,128]{2,1,0:T(8,128)(2,1)S(1)} %shard_map.120), channel_id=1, replica_groups=mesh['zhi'=4,'y'=8,'x'=4,'zlo'=2,'core'=2] {'x','zlo'}, dimensions={0} | all-to-all | bytes 327680 | tf_op jit(solution)/shard_map/all_to_all | solution.py:40
  104.9 0.9 shard_map.121
  105.8 3.4 %all-to-all-start.6 = ((bf16[8,64,128]{2,1,0:T(8,128)(2,1)}), bf16[8,64,128]{2,1,0:T(8,128)(2,1)S(1)}, u32[]{:S(2)}, u32[]{:S(2)}) async-start(bf16[8,64,128]{2,1,0:T(8,128)(2,1)} %shard_map.121), calls=%async_computation.6 | async-start | bytes 262144 | tf_op jit(solution)/shard_map/all_to_all | solution.py:40
  109.2 3.3 %shard_map.123 = bf16[512,640]{1,0:T(8,128)(2,1)} custom-call(s32[1]{0:T(128)} %bitcast.place, bf16[2048,128]{1,0:T(8,128)(2,1)S(1)} %copy-done.7, bf16[2048,128]{1,0:T(8,128)(2,1)} %collective-permute-done.5.far, bf16[512,128]{1,0:T(8,128)(2,1)S(1)} %copy-done.9, f32[640,128]{1,0:T(8,128)S(1)} %copy-done.2, bf16[640,1024]{1,0:T(8,128)(2,1)S(1)} %copy-done.1), custom_call_target="tpu_custom_call" | custom-call | flops 754974720 | bytes 3473412 | tf_op jit(solution)/shard_map/pallas_call | solution.py:58
  112.6 0.9 shard_map.122
  113.5 1.2 %all-to-all-done.6.got = bf16[8,64,128]{2,1,0:T(8,128)(2,1)S(1)} async-done(((bf16[8,64,128]{2,1,0:T(8,128)(2,1)}), bf16[8,64,128]{2,1,0:T(8,128)(2,1)S(1)}, u32[]{:S(2)}, u32[]{:S(2)}) %all-to-all-start.6) | async-done | bytes 131104 | tf_op jit(solution)/shard_map/all_to_all | solution.py:40
  114.7 1.0 shard_map.124
  (41 shorter events, 2.5 us)
Async XLA Ops:
  3.7 14.3 %all-to-all-start = ((bf16[8,128,128]{2,1,0:T(8,128)(2,1)}), bf16[8,128,128]{2,1,0:T(8,128)(2,1)S(1)}, u32[]{:S(2)}, u32[]{:S(2)}) async-start(bf16[8,128,128]{2,1,0:T(8,128)(2,1)} %get-tuple-element.37), calls=%async_computation | async-start | bytes 524288 | tf_op jit(solution)/shard_map/all_to_all | solution.py:40
  10.4 7.6 %collective-permute-start = (bf16[512,128]{1,0:T(8,128)(2,1)}, bf16[512,128]{1,0:T(8,128)(2,1)S(1)}, u32[]{:S(2)}, u32[]{:S(2)}) collective-permute-start(bf16[512,128]{1,0:T(8,128)(2,1)} %get-tuple-element.41.gk), channel_id=1, source_target_pairs={{0,2},{2,0},{1,3},{3,1},{4,6},{6,4},{5,7},{7,5},{8,10},{10,8},{9,1... | collective-permute-start | bytes 393224 | tf_op jit(solution)/shard_map/ppermute | solution.py:384
  18.0 6.7 %copy-start.15 = (bf16[2048,128]{1,0:T(8,128)(2,1)S(1)}, bf16[2048,128]{1,0:T(8,128)(2,1)}, u32[]{:S(2)}) copy-start(bf16[2048,128]{1,0:T(8,128)(2,1)} %get-tuple-element.50) | copy-start | bytes 1572868
  18.0 11.3 %copy-start.8 = (bf16[512,128]{1,0:T(8,128)(2,1)S(1)}, bf16[512,128]{1,0:T(8,128)(2,1)}, u32[]{:S(2)}) copy-start(bf16[512,128]{1,0:T(8,128)(2,1)} %get-tuple-element.41.gk) | copy-start | bytes 393220
  18.0 13.6 %copy-start = (bf16[512,640]{1,0:T(8,128)(2,1)S(1)}, bf16[512,640]{1,0:T(8,128)(2,1)}, u32[]{:S(2)}) copy-start(bf16[512,640]{1,0:T(8,128)(2,1)} %acts.5) | copy-start | bytes 1966084
  18.1 0.7 copy-start.11
  20.5 11.1 %all-to-all-start.1 = ((bf16[8,192,128]{2,1,0:T(8,128)(2,1)}), bf16[8,192,128]{2,1,0:T(8,128)(2,1)S(1)}, u32[]{:S(2)}, u32[]{:S(2)}) async-start(bf16[8,192,128]{2,1,0:T(8,128)(2,1)} %shard_map.113), calls=%async_computation.1 | async-start | bytes 786432 | tf_op jit(solution)/shard_map/all_to_all | solution.py:40
  24.7 20.1 %collective-permute-start.2 = (bf16[2048,128]{1,0:T(8,128)(2,1)S(1)}, bf16[2048,128]{1,0:T(8,128)(2,1)S(1)}, u32[]{:S(2)}, u32[]{:S(2)}) collective-permute-start(bf16[2048,128]{1,0:T(8,128)(2,1)S(1)} %copy-done.15), channel_id=1, source_target_pairs={{0,12},{12,0},{4,8},{8,4},{1,13},{13,1},{5,9},{9,5},{2,14},{14,2},... | collective-permute-start | bytes 1572872 | tf_op jit(solution)/shard_map/ppermute | solution.py:417
  29.3 18.6 %copy-start.12 = (bf16[1024,128]{1,0:T(8,128)(2,1)}, bf16[1024,128]{1,0:T(8,128)(2,1)S(1)}, u32[]{:S(2)}) copy-start(bf16[1024,128]{1,0:T(8,128)(2,1)S(1)} %constant_dynamic-update-slice_fusion.two) | copy-start | bytes 786436
  31.6 16.3 %copy-start.3 = (bf16[8,192,128]{2,1,0:T(8,128)(2,1)}, bf16[8,192,128]{2,1,0:T(8,128)(2,1)S(1)}, u32[]{:S(2)}) copy-start(bf16[8,192,128]{2,1,0:T(8,128)(2,1)S(1)} %all-to-all-done.1.got_ref.got) | copy-start | bytes 1179652
  32.6 22.7 %all-to-all-start.2 = ((bf16[16,48,128]{2,1,0:T(8,128)(2,1)}), bf16[16,48,128]{2,1,0:T(8,128)(2,1)S(1)}, u32[]{:S(2)}, u32[]{:S(2)}) async-start(bf16[16,48,128]{2,1,0:T(8,128)(2,1)} %shard_map.114), calls=%async_computation.2 | async-start | bytes 393216 | tf_op jit(solution)/shard_map/all_to_all | solution.py:40
  42.8 9.8 %collective-permute-start.1 = (bf16[1024,128]{1,0:T(8,128)(2,1)S(1)}, bf16[1024,128]{1,0:T(8,128)(2,1)S(1)}, u32[]{:S(2)}, u32[]{:S(2)}) collective-permute-start(bf16[1024,128]{1,0:T(8,128)(2,1)S(1)} %constant_dynamic-update-slice_fusion.two), channel_id=1, source_target_pairs={{0,4},{4,0},{8,12},{12,8},{1,5},{5,1},{9,13},{13,9},{2,6},{6,2},{1... | collective-permute-start | bytes 786440 | tf_op jit(solution)/shard_map/ppermute | solution.py:416
  44.8 0.8 copy-start.13
  47.9 44.5 %copy-start.4 = (bf16[512,640]{1,0:T(8,128)(2,1)S(1)}, bf16[512,640]{1,0:T(8,128)(2,1)}, u32[]{:S(2)}) copy-start(bf16[512,640]{1,0:T(8,128)(2,1)} %prompts.3) | copy-start | bytes 1966084
  52.6 0.7 copy-start.14
  55.3 31.5 %copy-start.7 = (bf16[2048,128]{1,0:T(8,128)(2,1)S(1)}, bf16[2048,128]{1,0:T(8,128)(2,1)}, u32[]{:S(2)}) copy-start(bf16[2048,128]{1,0:T(8,128)(2,1)} %get-tuple-element.64.near) | copy-start | bytes 1572868
  56.0 16.1 %all-to-all-start.3 = ((bf16[4,48,128]{2,1,0:T(8,128)(2,1)}), bf16[4,48,128]{2,1,0:T(8,128)(2,1)S(1)}, u32[]{:S(2)}, u32[]{:S(2)}) async-start(bf16[4,48,128]{2,1,0:T(8,128)(2,1)} %shard_map.117), calls=%async_computation.3 | async-start | bytes 98304 | tf_op jit(solution)/shard_map/all_to_all | solution.py:40
  65.1 17.0 %collective-permute-start.3 = (bf16[1024,128]{1,0:T(8,128)(2,1)}, bf16[1024,128]{1,0:T(8,128)(2,1)}, u32[]{:S(2)}, u32[]{:S(2)}) collective-permute-start(bf16[1024,128]{1,0:T(8,128)(2,1)} %get-tuple-element.55), channel_id=1, source_target_pairs={{0,4},{4,0},{8,12},{12,8},{1,5},{5,1},{9,13},{13,9},{2,6},{6,2},{1... | collective-permute-start | bytes 786440 | tf_op jit(solution)/shard_map/ppermute | solution.py:444
  72.9 32.0 %copy-start.10 = (f32[64,128]{1,0:T(8,128)S(1)}, f32[64,128]{1,0:T(8,128)}, u32[]{:S(2)}) copy-start(f32[64,128]{1,0:T(8,128)} %get-tuple-element.59.pa_rows) | copy-start | bytes 98308
  72.9 19.5 %all-to-all-start.4 = ((bf16[16,48,128]{2,1,0:T(8,128)(2,1)}), bf16[16,48,128]{2,1,0:T(8,128)(2,1)S(1)}, u32[]{:S(2)}, u32[]{:S(2)}) async-start(bf16[16,48,128]{2,1,0:T(8,128)(2,1)} %shard_map.118), calls=%async_computation.4 | async-start | bytes 393216 | tf_op jit(solution)/shard_map/all_to_all | solution.py:40
  82.0 27.2 %copy-start.1 = (bf16[640,1024]{1,0:T(8,128)(2,1)S(1)}, bf16[640,1024]{1,0:T(8,128)(2,1)}, u32[]{:S(2)}) copy-start(bf16[640,1024]{1,0:T(8,128)(2,1)} %frozen.3) | copy-start | bytes 3932164
  82.1 27.2 %copy-start.2 = (f32[640,128]{1,0:T(8,128)S(1)}, f32[640,128]{1,0:T(8,128)}, u32[]{:S(2)}) copy-start(f32[640,128]{1,0:T(8,128)} %down_w.7) | copy-start | bytes 983044
  82.1 27.2 %copy-start.9 = (bf16[512,128]{1,0:T(8,128)(2,1)S(1)}, bf16[512,128]{1,0:T(8,128)(2,1)}, u32[]{:S(2)}) copy-start(bf16[512,128]{1,0:T(8,128)(2,1)} %get-tuple-element.65.up) | copy-start | bytes 393220
  84.1 7.2 %collective-permute-start.4 = (bf16[512,128]{1,0:T(8,128)(2,1)}, bf16[512,128]{1,0:T(8,128)(2,1)S(1)}, u32[]{:S(2)}, u32[]{:S(2)}) collective-permute-start(bf16[512,128]{1,0:T(8,128)(2,1)} %get-tuple-element.57), channel_id=1, source_target_pairs={{0,2},{2,0},{1,3},{3,1},{4,6},{6,4},{5,7},{7,5},{8,10},{10,8},{9,1... | collective-permute-start | bytes 393224 | tf_op jit(solution)/shard_map/ppermute | solution.py:448
  86.8 22.4 %collective-permute-start.5 = (bf16[2048,128]{1,0:T(8,128)(2,1)S(1)}, bf16[2048,128]{1,0:T(8,128)(2,1)}, u32[]{:S(2)}, u32[]{:S(2)}) collective-permute-start(bf16[2048,128]{1,0:T(8,128)(2,1)S(1)} %copy-done.7), channel_id=1, source_target_pairs={{0,12},{12,0},{4,8},{8,4},{1,13},{13,1},{5,9},{9,5},{2,14},{14,2},... | collective-permute-start | bytes 1572872 | tf_op jit(solution)/shard_map/ppermute | solution.py:441
  105.8 8.9 %all-to-all-start.6 = ((bf16[8,64,128]{2,1,0:T(8,128)(2,1)}), bf16[8,64,128]{2,1,0:T(8,128)(2,1)S(1)}, u32[]{:S(2)}, u32[]{:S(2)}) async-start(bf16[8,64,128]{2,1,0:T(8,128)(2,1)} %shard_map.121), calls=%async_computation.6 | async-start | bytes 262144 | tf_op jit(solution)/shard_map/all_to_all | solution.py:40
  109.2 3.4 %copy-start.5 = (f32[512,128]{1,0:T(8,128)S(1)}, f32[512,128]{1,0:T(8,128)}, u32[]{:S(2)}) copy-start(f32[512,128]{1,0:T(8,128)} %get-tuple-element.60.base) | copy-start | bytes 786436
  109.2 3.4 %copy-start.6 = (f32[128,128]{1,0:T(8,128)S(1)}, f32[128,128]{1,0:T(8,128)}, u32[]{:S(2)}) copy-start(f32[128,128]{1,0:T(8,128)} %up_w.5) | copy-start | bytes 196612

commit v8 on v6

--- a/solution.py
+++ b/solution.py
@@ -72,7 +72,7 @@
 
 
 def parts_kernel(
-    lens, buckets, acts, og, down_w, up_w, gk_out, pay,
+    lens, buckets, acts, og, down_w, up_w, gk_out, two_out, pay,
     acts_v, og_v, down_v, up_v, gk, parts, sems,
 ):
     rows = acts.shape[0]
@@ -91,8 +91,12 @@
         weight = jnp.where(place < lens[s], buckets[s].astype(f32) - 1.5, f32(0.0))
         gk[here, :] = (weight * og_v[here, :].astype(f32)).astype(bf16)
     first = len(pairs)
-    store = pltpu.make_async_copy(gk, gk_out, sems.at[first])
-    store.start()
+    stores = [
+        pltpu.make_async_copy(gk, gk_out, sems.at[first]),
+        pltpu.make_async_copy(gk, two_out.at[pl.ds(0, rows), :], sems.at[first + 1]),
+    ]
+    for c in stores:
+        c.start()
 
     def put(k, v):
         v = v.astype(bf16)
@@ -105,27 +109,40 @@
     a_half = down_v[...].astype(bf16)
     loads[3].wait()
     put(1, dot(acts_v[...], a_half))
-    last = pltpu.make_async_copy(parts, pay, sems.at[first + 1])
+    last = pltpu.make_async_copy(parts, pay, sems.at[first + 2])
     last.start()
-    store.wait()
+    for c in stores:
+        c.wait()
     last.wait()
 
 
-def prompts_kernel(place, prompts, frozen, down_w, acts, proj_out, keep, send, base):
-    del acts
+def base_part(place, prompts, frozen, i, cols):
+    owner = place[0] ^ owner_mask(i)
+    return dot(prompts[...], frozen[:, pl.ds(pl.multiple_of(owner * cols, cols), cols)])
+
+
+def prompts_kernel(place, prompts, frozen, down_w, proj_out, send):
     rows = prompts.shape[0]
-    cols = keep.shape[1]
-    count = keep.shape[0] // rows
+    cols = send.shape[1]
+    count = send.shape[0] // rows
+    for i in range(count):
+        send[i * rows : (i + 1) * rows, :] = base_part(
+            place, prompts, frozen, count + i, cols
+        ).astype(bf16)
     proj_out[...] = dot(prompts[...], down_w[...].astype(bf16)).astype(bf16)
-    base[...] = dot(prompts[...], frozen[...])
+
+
+def own_half_kernel(place, prompts, frozen, got, keep, send):
+    rows = prompts.shape[0]
+    cols = send.shape[1]
+    count = send.shape[0] // rows
     for i in range(2 * count):
-        owner = place[0] ^ owner_mask(i)
-        part = base[:, pl.ds(pl.multiple_of(owner * cols, cols), cols)]
-        here = pl.ds((i % count) * rows, rows)
+        part = base_part(place, prompts, frozen, i, cols)
+        part += got[i * rows : (i + 1) * rows, :].astype(f32)
         if i < count:
-            keep[here, :] = part
+            keep[i * rows : (i + 1) * rows, :] = part
         else:
-            send[here, :] = part.astype(bf16)
+            send[(i - count) * rows : (i - count + 1) * rows, :] = part.astype(bf16)
 
 
 def halve_kernel(held, got, keep, send):
@@ -221,42 +238,68 @@
     ]
 
 
-def project_kernel(got_ref, prompts, pa_rows, pay_ref):
-    rank = pay_ref.shape[2]
-    rows = prompts.shape[0]
-    blocks = whole_gradient(got_ref, rank)
-    squares = sum(b * b for b in blocks)
-    total = jnp.sum(squares, keepdims=True)
+def pieces(total):
     high = total.astype(bf16)
     rest = total - high.astype(f32)
     middle = rest.astype(bf16)
     low = (rest - middle.astype(f32)).astype(bf16)
+    return high.astype(f32), middle.astype(f32), low.astype(f32)
+
+
+def make_tail(total, rank):
     lane = lax.broadcasted_iota(jnp.int32, (TAIL, rank), 1)
-    tail = jnp.where(
-        lane == 0,
-        high.astype(f32),
-        jnp.where(lane == 1, middle.astype(f32), jnp.where(lane == 2, low.astype(f32), 0.0)),
+    high, middle, low = pieces(total)
+    return jnp.where(
+        lane == 0, high, jnp.where(lane == 1, middle, jnp.where(lane == 2, low, 0.0))
     ).astype(bf16)
+
+
+def read_tail(tail):
+    lane = lax.broadcasted_iota(jnp.int32, tail.shape, 1)
+    row = lax.broadcasted_iota(jnp.int32, tail.shape, 0)
+    return jnp.sum(jnp.where((row == 0) & (lane < 3), tail, 0.0), keepdims=True)
+
+
+def project_kernel(got_ref, prompts, pa_rows, out):
+    rank = out.shape[1]
+    rows = prompts.shape[0]
+    blocks = whole_gradient(got_ref, rank)
+    total = jnp.sum(sum(b * b for b in blocks), keepdims=True)
+    out[rows : rows + TAIL, :] = make_tail(total, rank)
+    out[rows + TAIL :, :] = pa_rows[...]
     g_down = jnp.concatenate(blocks[:-1], axis=1).astype(bf16)
-    proj = dot(prompts[...], g_down, NT).astype(bf16)
-    for j in range(pay_ref.shape[0]):
-        pay_ref[j, :rows, :] = proj
-        pay_ref[j, rows : rows + TAIL, :] = tail
-        pay_ref[j, rows + TAIL :, :] = pa_rows[...]
+    out[:rows, :] = dot(prompts[...], g_down, NT).astype(bf16)
+
+
+def pair_kernel(place, mine, got, pay):
+    peers, long, rank = pay.shape
+    piece = long - mine.shape[0]
+    rows = mine.shape[0] - TAIL - piece
+    proj = (mine[:rows, :].astype(f32) + got[:rows, :].astype(f32)).astype(bf16)
+    here = slice(rows, rows + TAIL)
+    total = read_tail(mine[here, :].astype(f32) + got[here, :].astype(f32))
+    tail = make_tail(total, rank)
+    first = rows + TAIL
+    side = place[0] & 1
+    own = pl.ds(pl.multiple_of(first + side * piece, 16), piece)
+    theirs = pl.ds(pl.multiple_of(first + (1 - side) * piece, 16), piece)
+    for j in range(peers):
+        pay[j, :rows, :] = proj
+        pay[j, here, :] = tail
+        pay[j, own, :] = mine[first:, :]
+        pay[j, theirs, :] = got[first:, :]
 
 
 def finish_kernel(got, base, base_got, got_g, down_w, up_w, next_down, next_up, keys):
     rows = keys.shape[0]
     rank = down_w.shape[1]
     peers = got.shape[0]
-    lane = lax.broadcasted_iota(jnp.int32, (TAIL, rank), 1)
-    place = lax.broadcasted_iota(jnp.int32, (TAIL, rank), 0)
     p_g = got[0, :rows, :].astype(f32)
     tail = got[0, rows : rows + TAIL, :].astype(f32)
     for j in range(1, peers):
         p_g += got[j, :rows, :].astype(f32)
         tail += got[j, rows : rows + TAIL, :].astype(f32)
-    squares = jnp.sum(jnp.where((place == 0) & (lane < 3), tail, 0.0), keepdims=True)
+    squares = read_tail(tail)
     factor = step_rate * jnp.minimum(1.0, clip_norm / jnp.sqrt(squares + 1e-12))
     blocks = whole_gradient(got_g, rank)
     for c, block in enumerate(blocks[:-1]):
@@ -308,13 +351,13 @@
     piece = rows // n_f
     slab = (width + cols) // n_near
 
-    gk, pay = call(
+    gk, two, pay = call(
         parts_kernel,
-        [shape((rows, cols), bf16), shape((n_f, 2 * piece, rank), bf16)],
+        [shape((rows, cols), bf16), shape((2 * rows, cols), bf16), shape((n_f, 2 * piece, rank), bf16)],
         [SMEM, SMEM] + [ANY] * 4,
         (lengths, buckets, acts, output_gradient, down_w, up_w),
         flops=2 * rows * rank * (width + cols),
-        out_specs=(HBM, HBM),
+        out_specs=(HBM, HBM, HBM),
         limit=60,
         scratch_shapes=[
             pltpu.VMEM((rows, width), bf16),
@@ -323,25 +366,20 @@
             pltpu.VMEM((rank, cols), f32),
             pltpu.VMEM((rows, cols), bf16),
             pltpu.VMEM((n_f, 2 * piece, rank), bf16),
-            pltpu.SemaphoreType.DMA((6,)),
+            pltpu.SemaphoreType.DMA((7,)),
         ],
     )
     got = swap(pay, FSDP)
     other = lax.ppermute(gk, "zlo", Z_PAIRS)
     place = lax.axis_index(FSDP).reshape(1)
-    proj, held, send = call(
+    proj, send = call(
         prompts_kernel,
-        [
-            shape((rows, rank), bf16),
-            shape((n_f // 2 * rows, cols), f32),
-            shape((n_f // 2 * rows, cols), bf16),
-        ],
-        [SMEM] + [VMEM] * 4,
-        (place, prompts, frozen, down_w, acts),
-        flops=2 * rows * width * (cols * n_f + rank),
-        scratch_shapes=[pltpu.VMEM((rows, cols * n_f), f32)],
-    )
-    got, proj, held, send, other = lax.optimization_barrier((got, proj, held, send, other))
+        [shape((rows, rank), bf16), shape((n_f // 2 * rows, cols), bf16)],
+        [SMEM] + [VMEM] * 3,
+        (place, prompts, frozen, down_w),
+        flops=rows * width * (cols * n_f + 2 * rank),
+    )
+    got, proj, send, other = lax.optimization_barrier((got, proj, send, other))
     (pay,) = call(
         sums_kernel,
         [shape((n_f, 3 * piece, rank), bf16)],
@@ -351,7 +389,7 @@
         scratch_shapes=[pltpu.VMEM((n_f, 3 * piece, rank), bf16), pltpu.SemaphoreType.DMA],
     )
     got = swap(pay, FSDP)
-    two = jnp.concatenate([gk, other], axis=0)
+    two = lax.dynamic_update_slice(two, other, (rows, 0))
     other = lax.ppermute(two, "x", X_NEAR)
     base_got = lax.ppermute(send, "x", X_FAR)
     got, two = lax.optimization_barrier((got, two))
@@ -377,7 +415,13 @@
         (got, two, other),
     )
     other = lax.ppermute(four, "x", X_FAR)
-    held, send = halve(held, base_got)
+    held, send = call(
+        own_half_kernel,
+        [shape((n_f // 4 * rows, cols), f32), shape((n_f // 4 * rows, cols), bf16)],
+        [SMEM] + [VMEM] * 3,
+        (place, prompts, frozen, base_got),
+        flops=rows * width * cols * n_f,
+    )
     got_g, pa_rows, up, held, send = lax.optimization_barrier((got_g, pa_rows, up, held, send))
     base_got = lax.ppermute(send, "x", X_NEAR)
     got = swap(add(got_g, n_far), FAR)
@@ -395,14 +439,22 @@
     got_g, input_gradient, base, base_got = lax.optimization_barrier(
         (got_g, input_gradient, base, base_got)
     )
-    (pay,) = call(
+    (mine,) = call(
         project_kernel,
-        [shape((n_f, rows + TAIL + piece, rank), bf16)],
+        [shape((rows + TAIL + piece, rank), bf16)],
         [VMEM] * 3,
         (got_g, prompts, pa_rows),
         flops=2 * rows * width * rank,
     )
-    got = swap(pay, FSDP)
+    got = lax.ppermute(mine, "zlo", Z_PAIRS)
+    n_x = lax.axis_size("x")
+    (pay,) = call(
+        pair_kernel,
+        [shape((n_x, rows + TAIL + 2 * piece, rank), bf16)],
+        [SMEM] + [VMEM] * 2,
+        (place, mine, got),
+    )
+    got = swap(pay, "x")
     next_down, next_up, keys = call(
         finish_kernel,
         [shape((width, rank), f32), shape((rank, cols), f32), shape((rows, cols), bf16)],

time: 111 us -> 110 us (level)
  blocking collectives: 22 us -> 13.5 us
  waiting for transfers between devices: 7.78 us -> 13.8 us
  local copies, waits for them, and re-layouts: 7.14 us -> 4.12 us
  starting transfers between devices: 56.2 us -> 59.2 us
  Pallas kernels: 15.9 us -> 17.1 us
    all_to_all x1, blocking collectives: 22 us -> 13.5 us  [swap(): return lax.all_to_all(v, axis, 0, 0, tiled=True)]
    ppermute x0 -> x1, waiting for transfers between devices: none -> 4.7 us  [per_device(): got = lax.ppermute(mine, 'zlo', Z_PAIRS)]
    ppermute x0 -> x1, starting transfers between devices: none -> 3.09 us  [per_device(): got = lax.ppermute(mine, 'zlo', Z_PAIRS)]
    unnamed x29 -> x20, local copies, waits for them, and re-layouts: 6.22 us -> 3.45 us
    pallas_call x12 -> x13, Pallas kernels: 15.9 us -> 17.1 us  [call(): pl.pallas_call(kernel, grid=(1,), in_specs=[spec or block(a) for spec, a...]
  transfers between devices with their start and end apart: 11 -> 12, of which waited for: 3 -> 6; matrix products, arithmetic and copies ran while one was open for 1% -> 1% of each run, Pallas kernels for 9% -> 11%
where the time goes in v8:
time: 110 us; the launch traced here: 109 us
  starting transfers between devices  59.2 us (54%)
  Pallas kernels  17.1 us (16%)
  waiting for transfers between devices  13.8 us (13%)
  blocking collectives  13.5 us (12%)
  local copies, waits for them, and re-layouts  4.12 us (4%)
    all_to_all x5, starting transfers between devices, swap(): return lax.all_to_all(v, axis, 0, 0, tiled=True)  36.9 us
    pallas_call x13, Pallas kernels, call(): pl.pallas_call(kernel, grid=(1,), in_specs=[spec or block(a) for spec, a...  17.1 us
    all_to_all x1, blocking collectives, swap(): return lax.all_to_all(v, axis, 0, 0, tiled=True)  13.5 us
    all_to_all x5, waiting for transfers between devices, swap(): return lax.all_to_all(v, axis, 0, 0, tiled=True)  8.13 us
    ppermute x1, waiting for transfers between devices, per_device(): got = lax.ppermute(mine, 'zlo', Z_PAIRS)  4.7 us
    ppermute x1, starting transfers between devices, per_device(): base_got = lax.ppermute(send, 'x', X_FAR)  4.57 us
    unnamed x20, local copies, waits for them, and re-layouts  3.45 us
    ppermute x1, starting transfers between devices, per_device(): base_got = lax.ppermute(send, 'x', X_NEAR)  3.39 us
  transfers between devices with their start and end apart: 12, of which 6 were waited for; matrix products, arithmetic and copies ran while one was open for 1% of the time, Pallas kernels for 11%

profile of v8, /device:TPU:1, one launch (start us, length us, event | category | flops | bytes accessed | tf_op | source)
XLA Modules:
  0.0 108.5 jit_solution(3226860923589462626)
XLA Ops:
  0.7 3.2 %shard_map.111 = (bf16[512,128]{1,0:T(8,128)(2,1)}, bf16[1024,128]{1,0:T(8,128)(2,1)}, bf16[8,128,128]{2,1,0:T(8,128)(2,1)}) custom-call(s32[2]{0:T(128)} %lens.1, s32[2]{0:T(128)} %buckets.1, bf16[512,640]{1,0:T(8,128)(2,1)} %acts.3, bf16[512,128]{1,0:T(8,128)(2,1)} %og.1, f32[640,128]{1,0:T(8,128)} %down_w.7, f32[128,128]{1,0:T(8,128)} %up_w.3), custom_call_target="tpu_custom_call" | custom-call | flops 100663296 | bytes 1835024 | tf_op jit(solution)/shard_map/pallas_call | solution.py:58
  3.9 6.7 %all-to-all-start = ((bf16[8,128,128]{2,1,0:T(8,128)(2,1)}), bf16[8,128,128]{2,1,0:T(8,128)(2,1)S(1)}, u32[]{:S(2)}, u32[]{:S(2)}) async-start(bf16[8,128,128]{2,1,0:T(8,128)(2,1)} %get-tuple-element.34), calls=%async_computation | async-start | bytes 524288 | tf_op jit(solution)/shard_map/all_to_all | solution.py:40
  10.6 3.4 %collective-permute-start = (bf16[512,128]{1,0:T(8,128)(2,1)}, bf16[512,128]{1,0:T(8,128)(2,1)S(1)}, u32[]{:S(2)}, u32[]{:S(2)}) collective-permute-start(bf16[512,128]{1,0:T(8,128)(2,1)} %get-tuple-element.37.gk), channel_id=1, source_target_pairs={{0,2},{2,0},{1,3},{3,1},{4,6},{6,4},{5,7},{7,5},{8,10},{10,8},{9,1... | collective-permute-start | bytes 393224 | tf_op jit(solution)/shard_map/ppermute | solution.py:373
  14.0 1.1 copy-done.1
  15.0 1.7 %shard_map.112 = (bf16[512,128]{1,0:T(8,128)(2,1)S(1)}, bf16[2048,128]{1,0:T(8,128)(2,1)}) custom-call(s32[1]{0:T(128)} %bitcast.place, bf16[512,640]{1,0:T(8,128)(2,1)S(1)} %copy-done.1, bf16[640,1024]{1,0:T(8,128)(2,1)S(1)} %copy-done, f32[640,128]{1,0:T(8,128)S(1)} %copy-done.3), custom_call_target="tpu_custom_call" | custom-call | flops 419430400 | bytes 2949124 | tf_op jit(solution)/shard_map/pallas_call | solution.py:58
  17.2 0.8 shard_map.113
  18.0 5.2 %all-to-all-start.1 = ((bf16[8,192,128]{2,1,0:T(8,128)(2,1)}), bf16[8,192,128]{2,1,0:T(8,128)(2,1)S(1)}, u32[]{:S(2)}, u32[]{:S(2)}) async-start(bf16[8,192,128]{2,1,0:T(8,128)(2,1)} %shard_map.113), calls=%async_computation.1 | async-start | bytes 786432 | tf_op jit(solution)/shard_map/all_to_all | solution.py:40
  23.2 4.6 %collective-permute-start.2 = (bf16[2048,128]{1,0:T(8,128)(2,1)}, bf16[2048,128]{1,0:T(8,128)(2,1)}, u32[]{:S(2)}, u32[]{:S(2)}) collective-permute-start(bf16[2048,128]{1,0:T(8,128)(2,1)} %get-tuple-element.46), channel_id=1, source_target_pairs={{0,12},{12,0},{4,8},{8,4},{1,13},{13,1},{5,9},{9,5},{2,14},{14,2},... | collective-permute-start | bytes 1572872 | tf_op jit(solution)/shard_map/ppermute | solution.py:394
  27.8 0.7 constant_dynamic-update-slice_fusion.two
  28.5 2.0 %collective-permute-start.1 = (bf16[1024,128]{1,0:T(8,128)(2,1)}, bf16[1024,128]{1,0:T(8,128)(2,1)}, u32[]{:S(2)}, u32[]{:S(2)}) collective-permute-start(bf16[1024,128]{1,0:T(8,128)(2,1)} %constant_dynamic-update-slice_fusion.two), channel_id=1, source_target_pairs={{0,4},{4,0},{8,12},{12,8},{1,5},{5,1},{9,13},{13,9},{2,6},{6,2},{1... | collective-permute-start | bytes 786440 | tf_op jit(solution)/shard_map/ppermute | solution.py:393
  30.5 1.0 shard_map.114
  31.6 9.8 %all-to-all-start.2 = ((bf16[16,48,128]{2,1,0:T(8,128)(2,1)}), bf16[16,48,128]{2,1,0:T(8,128)(2,1)S(1)}, u32[]{:S(2)}, u32[]{:S(2)}) async-start(bf16[16,48,128]{2,1,0:T(8,128)(2,1)} %shard_map.114), calls=%async_computation.2 | async-start | bytes 393216 | tf_op jit(solution)/shard_map/all_to_all | solution.py:40
  41.4 1.9 %shard_map.115 = (bf16[64,128]{1,0:T(8,128)(2,1)S(1)}, bf16[512,128]{1,0:T(8,128)(2,1)S(1)}, bf16[2048,128]{1,0:T(8,128)(2,1)}) custom-call(bf16[8,192,128]{2,1,0:T(8,128)(2,1)S(1)} %all-to-all-done.1.got_ref.got, bf16[1024,128]{1,0:T(8,128)(2,1)} %constant_dynamic-update-slice_fusion.two, bf16[1024,128]{1,0:T(8,128)(2,1)} %collective-permute-done.1.other), custom_call_target="tpu_custom_call" | custom-call | bytes 1589248 | tf_op jit(solution)/shard_map/pallas_call | solution.py:58
  43.3 2.8 %collective-permute-start.3 = (bf16[2048,128]{1,0:T(8,128)(2,1)}, bf16[2048,128]{1,0:T(8,128)(2,1)}, u32[]{:S(2)}, u32[]{:S(2)}) collective-permute-start(bf16[2048,128]{1,0:T(8,128)(2,1)} %get-tuple-element.50.near), channel_id=1, source_target_pairs={{0,12},{12,0},{4,8},{8,4},{1,13},{13,1},{5,9},{9,5},{2,14},{14,2},... | collective-permute-start | bytes 1572872 | tf_op jit(solution)/shard_map/ppermute | solution.py:417
  46.2 1.9 %shard_map.116 = (f32[1024,128]{1,0:T(8,128)S(1)}, bf16[1024,128]{1,0:T(8,128)(2,1)S(1)}) custom-call(s32[1]{0:T(128)} %bitcast.place, bf16[512,640]{1,0:T(8,128)(2,1)S(1)} %copy-done.2, bf16[640,1024]{1,0:T(8,128)(2,1)S(1)} %copy-done, bf16[2048,128]{1,0:T(8,128)(2,1)} %collective-permute-done.2.got), custom_call_target="tpu_custom_call" | custom-call | flops 335544320 | bytes 3276804 | tf_op jit(solution)/shard_map/pallas_call | solution.py:58
  48.1 0.7 copy-done.9
  48.8 3.0 %all-to-all-done.2.got_ref = bf16[16,48,128]{2,1,0:T(8,128)(2,1)S(1)} async-done(((bf16[16,48,128]{2,1,0:T(8,128)(2,1)}), bf16[16,48,128]{2,1,0:T(8,128)(2,1)S(1)}, u32[]{:S(2)}, u32[]{:S(2)}) %all-to-all-start.2) | async-done | bytes 196640 | tf_op jit(solution)/shard_map/all_to_all | solution.py:40
  51.7 0.7 shard_map.117
  52.4 9.1 %all-to-all-start.3 = ((bf16[4,48,128]{2,1,0:T(8,128)(2,1)}), bf16[4,48,128]{2,1,0:T(8,128)(2,1)S(1)}, u32[]{:S(2)}, u32[]{:S(2)}) async-start(bf16[4,48,128]{2,1,0:T(8,128)(2,1)} %shard_map.117), calls=%async_computation.3 | async-start | bytes 98304 | tf_op jit(solution)/shard_map/all_to_all | solution.py:40
  61.6 3.4 %collective-permute-start.4 = (bf16[1024,128]{1,0:T(8,128)(2,1)}, bf16[1024,128]{1,0:T(8,128)(2,1)S(1)}, u32[]{:S(2)}, u32[]{:S(2)}) collective-permute-start(bf16[1024,128]{1,0:T(8,128)(2,1)} %copy-done.9), channel_id=1, source_target_pairs={{0,4},{4,0},{8,12},{12,8},{1,5},{5,1},{9,13},{13,9},{2,6},{6,2},{1... | collective-permute-start | bytes 786440 | tf_op jit(solution)/shard_map/ppermute | solution.py:426
  65.0 3.5 %all-to-all-done.3.got_ref = bf16[4,48,128]{2,1,0:T(8,128)(2,1)S(1)} async-done(((bf16[4,48,128]{2,1,0:T(8,128)(2,1)}), bf16[4,48,128]{2,1,0:T(8,128)(2,1)S(1)}, u32[]{:S(2)}, u32[]{:S(2)}) %all-to-all-start.3) | async-done | bytes 49184 | tf_op jit(solution)/shard_map/all_to_all | solution.py:40
  68.5 0.8 shard_map.118
  69.3 6.1 %all-to-all-start.4 = ((bf16[16,48,128]{2,1,0:T(8,128)(2,1)}), bf16[16,48,128]{2,1,0:T(8,128)(2,1)S(1)}, u32[]{:S(2)}, u32[]{:S(2)}) async-start(bf16[16,48,128]{2,1,0:T(8,128)(2,1)} %shard_map.118), calls=%async_computation.4 | async-start | bytes 393216 | tf_op jit(solution)/shard_map/all_to_all | solution.py:40
  75.4 0.7 copy-done.5
  76.1 0.9 copy-done.6
  77.1 3.0 %collective-permute-start.5 = (bf16[512,128]{1,0:T(8,128)(2,1)S(1)}, bf16[512,128]{1,0:T(8,128)(2,1)S(1)}, u32[]{:S(2)}, u32[]{:S(2)}) collective-permute-start(bf16[512,128]{1,0:T(8,128)(2,1)S(1)} %get-tuple-element.55), channel_id=1, source_target_pairs={{0,2},{2,0},{1,3},{3,1},{4,6},{6,4},{5,7},{7,5},{8,10},{10,8},{9,1... | collective-permute-start | bytes 393224 | tf_op jit(solution)/shard_map/ppermute | solution.py:438
  80.1 3.4 %shard_map.119 = bf16[512,640]{1,0:T(8,128)(2,1)} custom-call(s32[1]{0:T(128)} %bitcast.place, bf16[2048,128]{1,0:T(8,128)(2,1)} %get-tuple-element.50.near, bf16[2048,128]{1,0:T(8,128)(2,1)} %collective-permute-done.3.far, bf16[512,128]{1,0:T(8,128)(2,1)S(1)} %get-tuple-element.51.up, f32[640,128]{1,0:T(8,128)S(1)} %copy-done.3, bf16[640,1024]{1,0:T(8,128)(2,1)S(1)} %copy-done), custom_call_target="tpu_custom_call" | custom-call | flops 754974720 | bytes 3473412 | tf_op jit(solution)/shard_map/pallas_call | solution.py:58
  84.1 1.7 %all-to-all-done.4.got_ref.got_g = bf16[16,48,128]{2,1,0:T(8,128)(2,1)S(1)} async-done(((bf16[16,48,128]{2,1,0:T(8,128)(2,1)}), bf16[16,48,128]{2,1,0:T(8,128)(2,1)S(1)}, u32[]{:S(2)}, u32[]{:S(2)}) %all-to-all-start.4) | async-done | bytes 196640 | tf_op jit(solution)/shard_map/all_to_all | solution.py:40
  86.1 3.1 %collective-permute-start.6 = (bf16[592,128]{1,0:T(8,128)(2,1)S(1)}, bf16[592,128]{1,0:T(8,128)(2,1)S(1)}, u32[]{:S(2)}, u32[]{:S(2)}) collective-permute-start(bf16[592,128]{1,0:T(8,128)(2,1)S(1)} %shard_map.121.mine), channel_id=1, source_target_pairs={{0,2},{2,0},{1,3},{3,1},{4,6},{6,4},{5,7},{7,5},{8,10},{10,8},{9,1... | collective-permute-start | bytes 454664 | tf_op jit(solution)/shard_map/ppermute | solution.py:449
  89.2 4.7 %collective-permute-done.6.got = bf16[592,128]{1,0:T(8,128)(2,1)S(1)} collective-permute-done((bf16[592,128]{1,0:T(8,128)(2,1)S(1)}, bf16[592,128]{1,0:T(8,128)(2,1)S(1)}, u32[]{:S(2)}, u32[]{:S(2)}) %collective-permute-start.6) | collective-permute-done | bytes 151584 | tf_op jit(solution)/shard_map/ppermute | solution.py:449
  94.0 13.5 %all_to_all.30.got = bf16[4,656,128]{2,1,0:T(8,128)(2,1)S(1)} all-to-all(bf16[4,656,128]{2,1,0:T(8,128)(2,1)S(1)} %shard_map.122), channel_id=1, replica_groups=mesh['zhi'=4,'y'=8,'x'=4,'zlo'=2,'core'=2] {'x'}, dimensions={0} | all-to-all | bytes 1343488 | tf_op jit(solution)/shard_map/all_to_all | solution.py:40
  107.5 1.0 shard_map.123
  (27 shorter events, 1.5 us)
Async XLA Ops:
  0.6 13.3 %copy-start.3 = (f32[640,128]{1,0:T(8,128)S(1)}, f32[640,128]{1,0:T(8,128)}, u32[]{:S(2)}) copy-start(f32[640,128]{1,0:T(8,128)} %down_w.7) | copy-start | bytes 983044
  0.6 13.3 %copy-start = (bf16[640,1024]{1,0:T(8,128)(2,1)S(1)}, bf16[640,1024]{1,0:T(8,128)(2,1)}, u32[]{:S(2)}) copy-start(bf16[640,1024]{1,0:T(8,128)(2,1)} %frozen.5) | copy-start | bytes 3932164
  3.9 13.3 %all-to-all-start = ((bf16[8,128,128]{2,1,0:T(8,128)(2,1)}), bf16[8,128,128]{2,1,0:T(8,128)(2,1)S(1)}, u32[]{:S(2)}, u32[]{:S(2)}) async-start(bf16[8,128,128]{2,1,0:T(8,128)(2,1)} %get-tuple-element.34), calls=%async_computation | async-start | bytes 524288 | tf_op jit(solution)/shard_map/all_to_all | solution.py:40
  10.6 6.6 %collective-permute-start = (bf16[512,128]{1,0:T(8,128)(2,1)}, bf16[512,128]{1,0:T(8,128)(2,1)S(1)}, u32[]{:S(2)}, u32[]{:S(2)}) collective-permute-start(bf16[512,128]{1,0:T(8,128)(2,1)} %get-tuple-element.37.gk), channel_id=1, source_target_pairs={{0,2},{2,0},{1,3},{3,1},{4,6},{6,4},{5,7},{7,5},{8,10},{10,8},{9,1... | collective-permute-start | bytes 393224 | tf_op jit(solution)/shard_map/ppermute | solution.py:373
  14.0 1.1 %copy-start.1 = (bf16[512,640]{1,0:T(8,128)(2,1)S(1)}, bf16[512,640]{1,0:T(8,128)(2,1)}, u32[]{:S(2)}) copy-start(bf16[512,640]{1,0:T(8,128)(2,1)} %prompts.5) | copy-start | bytes 1966084
  16.8 13.7 %copy-start.4 = (bf16[512,640]{1,0:T(8,128)(2,1)S(1)}, bf16[512,640]{1,0:T(8,128)(2,1)}, u32[]{:S(2)}) copy-start(bf16[512,640]{1,0:T(8,128)(2,1)} %acts.3) | copy-start | bytes 1966084
  16.8 13.8 %copy-start.8 = (bf16[512,128]{1,0:T(8,128)(2,1)S(1)}, bf16[512,128]{1,0:T(8,128)(2,1)}, u32[]{:S(2)}) copy-start(bf16[512,128]{1,0:T(8,128)(2,1)} %get-tuple-element.37.gk) | copy-start | bytes 393220
  18.0 12.5 %all-to-all-start.1 = ((bf16[8,192,128]{2,1,0:T(8,128)(2,1)}), bf16[8,192,128]{2,1,0:T(8,128)(2,1)S(1)}, u32[]{:S(2)}, u32[]{:S(2)}) async-start(bf16[8,192,128]{2,1,0:T(8,128)(2,1)} %shard_map.113), calls=%async_computation.1 | async-start | bytes 786432 | tf_op jit(solution)/shard_map/all_to_all | solution.py:40
  23.2 22.9 %collective-permute-start.2 = (bf16[2048,128]{1,0:T(8,128)(2,1)}, bf16[2048,128]{1,0:T(8,128)(2,1)}, u32[]{:S(2)}, u32[]{:S(2)}) collective-permute-start(bf16[2048,128]{1,0:T(8,128)(2,1)} %get-tuple-element.46), channel_id=1, source_target_pairs={{0,12},{12,0},{4,8},{8,4},{1,13},{13,1},{5,9},{9,5},{2,14},{14,2},... | collective-permute-start | bytes 1572872 | tf_op jit(solution)/shard_map/ppermute | solution.py:394
  28.5 17.7 %copy-start.2 = (bf16[512,640]{1,0:T(8,128)(2,1)S(1)}, bf16[512,640]{1,0:T(8,128)(2,1)}, u32[]{:S(2)}) copy-start(bf16[512,640]{1,0:T(8,128)(2,1)} %prompts.5) | copy-start | bytes 1966084
  28.5 13.0 %collective-permute-start.1 = (bf16[1024,128]{1,0:T(8,128)(2,1)}, bf16[1024,128]{1,0:T(8,128)(2,1)}, u32[]{:S(2)}, u32[]{:S(2)}) collective-permute-start(bf16[1024,128]{1,0:T(8,128)(2,1)} %constant_dynamic-update-slice_fusion.two), channel_id=1, source_target_pairs={{0,4},{4,0},{8,12},{12,8},{1,5},{5,1},{9,13},{13,9},{2,6},{6,2},{1... | collective-permute-start | bytes 786440 | tf_op jit(solution)/shard_map/ppermute | solution.py:393
  31.6 20.2 %all-to-all-start.2 = ((bf16[16,48,128]{2,1,0:T(8,128)(2,1)}), bf16[16,48,128]{2,1,0:T(8,128)(2,1)S(1)}, u32[]{:S(2)}, u32[]{:S(2)}) async-start(bf16[16,48,128]{2,1,0:T(8,128)(2,1)} %shard_map.114), calls=%async_computation.2 | async-start | bytes 393216 | tf_op jit(solution)/shard_map/all_to_all | solution.py:40
  43.3 36.8 %collective-permute-start.3 = (bf16[2048,128]{1,0:T(8,128)(2,1)}, bf16[2048,128]{1,0:T(8,128)(2,1)}, u32[]{:S(2)}, u32[]{:S(2)}) collective-permute-start(bf16[2048,128]{1,0:T(8,128)(2,1)} %get-tuple-element.50.near), channel_id=1, source_target_pairs={{0,12},{12,0},{4,8},{8,4},{1,13},{13,1},{5,9},{9,5},{2,14},{14,2},... | collective-permute-start | bytes 1572872 | tf_op jit(solution)/shard_map/ppermute | solution.py:417
  48.1 0.7 copy-start.9
  52.4 16.0 %all-to-all-start.3 = ((bf16[4,48,128]{2,1,0:T(8,128)(2,1)}), bf16[4,48,128]{2,1,0:T(8,128)(2,1)S(1)}, u32[]{:S(2)}, u32[]{:S(2)}) async-start(bf16[4,48,128]{2,1,0:T(8,128)(2,1)} %shard_map.117), calls=%async_computation.3 | async-start | bytes 98304 | tf_op jit(solution)/shard_map/all_to_all | solution.py:40
  61.6 13.8 %collective-permute-start.4 = (bf16[1024,128]{1,0:T(8,128)(2,1)}, bf16[1024,128]{1,0:T(8,128)(2,1)S(1)}, u32[]{:S(2)}, u32[]{:S(2)}) collective-permute-start(bf16[1024,128]{1,0:T(8,128)(2,1)} %copy-done.9), channel_id=1, source_target_pairs={{0,4},{4,0},{8,12},{12,8},{1,5},{5,1},{9,13},{13,9},{2,6},{6,2},{1... | collective-permute-start | bytes 786440 | tf_op jit(solution)/shard_map/ppermute | solution.py:426
  69.3 16.4 %all-to-all-start.4 = ((bf16[16,48,128]{2,1,0:T(8,128)(2,1)}), bf16[16,48,128]{2,1,0:T(8,128)(2,1)S(1)}, u32[]{:S(2)}, u32[]{:S(2)}) async-start(bf16[16,48,128]{2,1,0:T(8,128)(2,1)} %shard_map.118), calls=%async_computation.4 | async-start | bytes 393216 | tf_op jit(solution)/shard_map/all_to_all | solution.py:40
  75.4 0.7 copy-start.5
  76.1 0.9 copy-start.6
  77.1 7.0 %collective-permute-start.5 = (bf16[512,128]{1,0:T(8,128)(2,1)S(1)}, bf16[512,128]{1,0:T(8,128)(2,1)S(1)}, u32[]{:S(2)}, u32[]{:S(2)}) collective-permute-start(bf16[512,128]{1,0:T(8,128)(2,1)S(1)} %get-tuple-element.55), channel_id=1, source_target_pairs={{0,2},{2,0},{1,3},{3,1},{4,6},{6,4},{5,7},{7,5},{8,10},{10,8},{9,1... | collective-permute-start | bytes 393224 | tf_op jit(solution)/shard_map/ppermute | solution.py:438
  86.1 21.4 %copy-start.7 = (f32[128,128]{1,0:T(8,128)S(1)}, f32[128,128]{1,0:T(8,128)}, u32[]{:S(2)}) copy-start(f32[128,128]{1,0:T(8,128)} %up_w.3) | copy-start | bytes 196612
  86.1 7.8 %collective-permute-start.6 = (bf16[592,128]{1,0:T(8,128)(2,1)S(1)}, bf16[592,128]{1,0:T(8,128)(2,1)S(1)}, u32[]{:S(2)}, u32[]{:S(2)}) collective-permute-start(bf16[592,128]{1,0:T(8,128)(2,1)S(1)} %shard_map.121.mine), channel_id=1, source_target_pairs={{0,2},{2,0},{1,3},{3,1},{4,6},{6,4},{5,7},{7,5},{8,10},{10,8},{9,1... | collective-permute-start | bytes 454664 | tf_op jit(solution)/shard_map/ppermute | solution.py:449

commit v9 on v8

--- a/solution.py
+++ b/solution.py
@@ -238,79 +238,64 @@
     ]
 
 
-def pieces(total):
-    high = total.astype(bf16)
-    rest = total - high.astype(f32)
-    middle = rest.astype(bf16)
-    low = (rest - middle.astype(f32)).astype(bf16)
-    return high.astype(f32), middle.astype(f32), low.astype(f32)
-
-
 def make_tail(total, rank):
     lane = lax.broadcasted_iota(jnp.int32, (TAIL, rank), 1)
-    high, middle, low = pieces(total)
+    high = total.astype(bf16).astype(f32)
+    middle = (total - high).astype(bf16).astype(f32)
+    low = total - high - middle
     return jnp.where(
         lane == 0, high, jnp.where(lane == 1, middle, jnp.where(lane == 2, low, 0.0))
     ).astype(bf16)
 
 
-def read_tail(tail):
-    lane = lax.broadcasted_iota(jnp.int32, tail.shape, 1)
-    row = lax.broadcasted_iota(jnp.int32, tail.shape, 0)
-    return jnp.sum(jnp.where((row == 0) & (lane < 3), tail, 0.0), keepdims=True)
-
-
-def project_kernel(got_ref, prompts, pa_rows, out):
-    rank = out.shape[1]
-    rows = prompts.shape[0]
+def step_factor(got):
+    peers, long, rank = got.shape
+    piece = long - TAIL
+    lane = lax.broadcasted_iota(jnp.int32, (TAIL, rank), 1)
+    row = lax.broadcasted_iota(jnp.int32, (TAIL, rank), 0)
+    tail = got[0, piece:, :].astype(f32)
+    for j in range(1, peers):
+        tail += got[j, piece:, :].astype(f32)
+    squares = jnp.sum(jnp.where((row == 0) & (lane < 3), tail, 0.0), keepdims=True)
+    return step_rate * jnp.minimum(1.0, clip_norm / jnp.sqrt(squares + 1e-12))
+
+
+def project_kernel(got_ref, prompts, pay):
+    peers, long, rank = pay.shape
+    piece = long - TAIL
     blocks = whole_gradient(got_ref, rank)
-    total = jnp.sum(sum(b * b for b in blocks), keepdims=True)
-    out[rows : rows + TAIL, :] = make_tail(total, rank)
-    out[rows + TAIL :, :] = pa_rows[...]
+    tail = make_tail(jnp.sum(sum(b * b for b in blocks), keepdims=True), rank)
     g_down = jnp.concatenate(blocks[:-1], axis=1).astype(bf16)
-    out[:rows, :] = dot(prompts[...], g_down, NT).astype(bf16)
-
-
-def pair_kernel(place, mine, got, pay):
-    peers, long, rank = pay.shape
-    piece = long - mine.shape[0]
-    rows = mine.shape[0] - TAIL - piece
-    proj = (mine[:rows, :].astype(f32) + got[:rows, :].astype(f32)).astype(bf16)
-    here = slice(rows, rows + TAIL)
-    total = read_tail(mine[here, :].astype(f32) + got[here, :].astype(f32))
-    tail = make_tail(total, rank)
-    first = rows + TAIL
-    side = place[0] & 1
-    own = pl.ds(pl.multiple_of(first + side * piece, 16), piece)
-    theirs = pl.ds(pl.multiple_of(first + (1 - side) * piece, 16), piece)
+    proj = dot(prompts[...], g_down, NT).astype(bf16)
     for j in range(peers):
-        pay[j, :rows, :] = proj
-        pay[j, here, :] = tail
-        pay[j, own, :] = mine[first:, :]
-        pay[j, theirs, :] = got[first:, :]
-
-
-def finish_kernel(got, base, base_got, got_g, down_w, up_w, next_down, next_up, keys):
-    rows = keys.shape[0]
+        pay[j, :piece, :] = proj[j * piece : (j + 1) * piece]
+        pay[j, piece:, :] = tail
+
+
+def rows_kernel(got, pa_rows, pay):
+    peers, piece, _ = pay.shape
+    p_g = got[0, :piece, :].astype(f32)
+    for j in range(1, peers):
+        p_g += got[j, :piece, :].astype(f32)
+    rows = (pa_rows[...].astype(f32) - step_factor(got) * p_g).astype(bf16)
+    for j in range(peers):
+        pay[j] = rows
+
+
+def finish_kernel(got, sums, base, base_got, got_g, down_w, up_w, next_down, next_up, keys):
     rank = down_w.shape[1]
-    peers = got.shape[0]
-    p_g = got[0, :rows, :].astype(f32)
-    tail = got[0, rows : rows + TAIL, :].astype(f32)
-    for j in range(1, peers):
-        p_g += got[j, :rows, :].astype(f32)
-        tail += got[j, rows : rows + TAIL, :].astype(f32)
-    squares = read_tail(tail)
-    factor = step_rate * jnp.minimum(1.0, clip_norm / jnp.sqrt(squares + 1e-12))
+    factor = step_factor(sums)
     blocks = whole_gradient(got_g, rank)
-    for c, block in enumerate(blocks[:-1]):
-        here = pl.ds(c * rank, rank)
-        next_down[here, :] = down_w[here, :] - factor * block.T
     new_up = up_w[...] - factor * blocks[-1]
     next_up[...] = new_up
-    proj = rejoin(got, rows + TAIL, rows // peers).astype(f32) - factor * p_g
     keys[...] = (
-        base[...] + base_got[...].astype(f32) + adapter_scale * dot(proj.astype(bf16), new_up.astype(bf16))
+        base[...]
+        + base_got[...].astype(f32)
+        + adapter_scale * dot(rejoin(got, 0, got.shape[1]), new_up.astype(bf16))
     ).astype(bf16)
+    for c, part in enumerate(blocks[:-1]):
+        here = pl.ds(c * rank, rank)
+        next_down[here, :] = down_w[here, :] - factor * part.T
 
 
 def input_kernel(place, near, far, up, down_w, frozen, out, gk):
@@ -439,27 +424,23 @@
     got_g, input_gradient, base, base_got = lax.optimization_barrier(
         (got_g, input_gradient, base, base_got)
     )
-    (mine,) = call(
+    (pay,) = call(
         project_kernel,
-        [shape((rows + TAIL + piece, rank), bf16)],
-        [VMEM] * 3,
-        (got_g, prompts, pa_rows),
+        [shape((n_f, piece + TAIL, rank), bf16)],
+        [VMEM] * 2,
+        (got_g, prompts),
         flops=2 * rows * width * rank,
     )
-    got = lax.ppermute(mine, "zlo", Z_PAIRS)
-    n_x = lax.axis_size("x")
+    sums = swap(pay, FSDP)
     (pay,) = call(
-        pair_kernel,
-        [shape((n_x, rows + TAIL + 2 * piece, rank), bf16)],
-        [SMEM] + [VMEM] * 2,
-        (place, mine, got),
-    )
-    got = swap(pay, "x")
+        rows_kernel, [shape((n_f, piece, rank), bf16)], [VMEM] * 2, (sums, pa_rows)
+    )
+    got = swap(pay, FSDP)
     next_down, next_up, keys = call(
         finish_kernel,
         [shape((width, rank), f32), shape((rank, cols), f32), shape((rows, cols), bf16)],
-        [VMEM] * 6,
-        (got, base, base_got, got_g, down_w, up_w),
+        [VMEM] * 7,
+        (got, sums, base, base_got, got_g, down_w, up_w),
         flops=2 * rows * rank * cols,
     )
     return input_gradient, next_down, next_up, keys

time: 110 us -> 107 us (0.973)
  blocking collectives: 13.5 us -> 18.6 us
  waiting for transfers between devices: 13.8 us -> 9.08 us
  starting transfers between devices: 59.2 us -> 56.1 us
    all_to_all x1 -> x2, blocking collectives: 13.5 us -> 18.6 us  [swap(): return lax.all_to_all(v, axis, 0, 0, tiled=True)]
    ppermute x1 -> x0, waiting for transfers between devices: 4.7 us -> none  [per_device(): got = lax.ppermute(mine, 'zlo', Z_PAIRS)]
    ppermute x1 -> x0, starting transfers between devices: 3.09 us -> none  [per_device(): got = lax.ppermute(mine, 'zlo', Z_PAIRS)]
  transfers between devices with their start and end apart: 12 -> 11, of which waited for: 6 -> 5; matrix products, arithmetic and copies ran while one was open for 1% -> 1% of each run, Pallas kernels for 11% -> 11%
where the time goes in v9:
time: 107 us; the launch traced here: 106 us
  starting transfers between devices  56.1 us (52%)
  blocking collectives  18.6 us (17%)
  Pallas kernels  17.1 us (16%)
  waiting for transfers between devices  9.08 us (8%)
  local copies, waits for them, and re-layouts  4.12 us (4%)
    all_to_all x5, starting transfers between devices, swap(): return lax.all_to_all(v, axis, 0, 0, tiled=True)  36.9 us
    all_to_all x2, blocking collectives, swap(): return lax.all_to_all(v, axis, 0, 0, tiled=True)  18.6 us
    pallas_call x13, Pallas kernels, call(): pl.pallas_call(kernel, grid=(1,), in_specs=[spec or block(a) for spec, a...  17.1 us
    all_to_all x5, waiting for transfers between devices, swap(): return lax.all_to_all(v, axis, 0, 0, tiled=True)  8.14 us
    ppermute x1, starting transfers between devices, per_device(): base_got = lax.ppermute(send, 'x', X_FAR)  4.57 us
    unnamed x20, local copies, waits for them, and re-layouts  3.45 us
    ppermute x1, starting transfers between devices, per_device(): base_got = lax.ppermute(send, 'x', X_NEAR)  3.39 us
    ppermute x1, starting transfers between devices, per_device(): other = lax.ppermute(gk, 'zlo', Z_PAIRS)  3.36 us
  transfers between devices with their start and end apart: 11, of which 5 were waited for; matrix products, arithmetic and copies ran while one was open for 1% of the time, Pallas kernels for 11%

profile of v9, /device:TPU:1, one launch (start us, length us, event | category | flops | bytes accessed | tf_op | source)
XLA Modules:
  0.0 105.8 jit_solution(2168569056790822564)
XLA Ops:
  0.7 3.2 %shard_map.111 = (bf16[512,128]{1,0:T(8,128)(2,1)}, bf16[1024,128]{1,0:T(8,128)(2,1)}, bf16[8,128,128]{2,1,0:T(8,128)(2,1)}) custom-call(s32[2]{0:T(128)} %lens.1, s32[2]{0:T(128)} %buckets.1, bf16[512,640]{1,0:T(8,128)(2,1)} %acts.3, bf16[512,128]{1,0:T(8,128)(2,1)} %og.1, f32[640,128]{1,0:T(8,128)} %down_w.7, f32[128,128]{1,0:T(8,128)} %up_w.3), custom_call_target="tpu_custom_call" | custom-call | flops 100663296 | bytes 1835024 | tf_op jit(solution)/shard_map/pallas_call | solution.py:58
  3.9 6.7 %all-to-all-start = ((bf16[8,128,128]{2,1,0:T(8,128)(2,1)}), bf16[8,128,128]{2,1,0:T(8,128)(2,1)S(1)}, u32[]{:S(2)}, u32[]{:S(2)}) async-start(bf16[8,128,128]{2,1,0:T(8,128)(2,1)} %get-tuple-element.34), calls=%async_computation | async-start | bytes 524288 | tf_op jit(solution)/shard_map/all_to_all | solution.py:40
  10.6 3.4 %collective-permute-start = (bf16[512,128]{1,0:T(8,128)(2,1)}, bf16[512,128]{1,0:T(8,128)(2,1)S(1)}, u32[]{:S(2)}, u32[]{:S(2)}) collective-permute-start(bf16[512,128]{1,0:T(8,128)(2,1)} %get-tuple-element.37.gk), channel_id=1, source_target_pairs={{0,2},{2,0},{1,3},{3,1},{4,6},{6,4},{5,7},{7,5},{8,10},{10,8},{9,1... | collective-permute-start | bytes 393224 | tf_op jit(solution)/shard_map/ppermute | solution.py:358
  14.0 1.1 %copy-done.1 = bf16[512,640]{1,0:T(8,128)(2,1)S(1)} copy-done((bf16[512,640]{1,0:T(8,128)(2,1)S(1)}, bf16[512,640]{1,0:T(8,128)(2,1)}, u32[]{:S(2)}) %copy-start.1) | copy-done | bytes 655384
  15.0 1.7 %shard_map.112 = (bf16[512,128]{1,0:T(8,128)(2,1)S(1)}, bf16[2048,128]{1,0:T(8,128)(2,1)}) custom-call(s32[1]{0:T(128)} %bitcast.place, bf16[512,640]{1,0:T(8,128)(2,1)S(1)} %copy-done.1, bf16[640,1024]{1,0:T(8,128)(2,1)S(1)} %copy-done, f32[640,128]{1,0:T(8,128)S(1)} %copy-done.3), custom_call_target="tpu_custom_call" | custom-call | flops 419430400 | bytes 2949124 | tf_op jit(solution)/shard_map/pallas_call | solution.py:58
  17.2 0.8 shard_map.113
  18.0 5.2 %all-to-all-start.1 = ((bf16[8,192,128]{2,1,0:T(8,128)(2,1)}), bf16[8,192,128]{2,1,0:T(8,128)(2,1)S(1)}, u32[]{:S(2)}, u32[]{:S(2)}) async-start(bf16[8,192,128]{2,1,0:T(8,128)(2,1)} %shard_map.113), calls=%async_computation.1 | async-start | bytes 786432 | tf_op jit(solution)/shard_map/all_to_all | solution.py:40
  23.2 4.6 %collective-permute-start.2 = (bf16[2048,128]{1,0:T(8,128)(2,1)}, bf16[2048,128]{1,0:T(8,128)(2,1)}, u32[]{:S(2)}, u32[]{:S(2)}) collective-permute-start(bf16[2048,128]{1,0:T(8,128)(2,1)} %get-tuple-element.46), channel_id=1, source_target_pairs={{0,12},{12,0},{4,8},{8,4},{1,13},{13,1},{5,9},{9,5},{2,14},{14,2},... | collective-permute-start | bytes 1572872 | tf_op jit(solution)/shard_map/ppermute | solution.py:379
  27.8 0.7 constant_dynamic-update-slice_fusion.two
  28.5 2.0 %collective-permute-start.1 = (bf16[1024,128]{1,0:T(8,128)(2,1)}, bf16[1024,128]{1,0:T(8,128)(2,1)}, u32[]{:S(2)}, u32[]{:S(2)}) collective-permute-start(bf16[1024,128]{1,0:T(8,128)(2,1)} %constant_dynamic-update-slice_fusion.two), channel_id=1, source_target_pairs={{0,4},{4,0},{8,12},{12,8},{1,5},{5,1},{9,13},{13,9},{2,6},{6,2},{1... | collective-permute-start | bytes 786440 | tf_op jit(solution)/shard_map/ppermute | solution.py:378
  30.5 1.0 shard_map.114
  31.6 9.8 %all-to-all-start.2 = ((bf16[16,48,128]{2,1,0:T(8,128)(2,1)}), bf16[16,48,128]{2,1,0:T(8,128)(2,1)S(1)}, u32[]{:S(2)}, u32[]{:S(2)}) async-start(bf16[16,48,128]{2,1,0:T(8,128)(2,1)} %shard_map.114), calls=%async_computation.2 | async-start | bytes 393216 | tf_op jit(solution)/shard_map/all_to_all | solution.py:40
  41.4 1.9 %shard_map.115 = (bf16[64,128]{1,0:T(8,128)(2,1)S(1)}, bf16[512,128]{1,0:T(8,128)(2,1)S(1)}, bf16[2048,128]{1,0:T(8,128)(2,1)}) custom-call(bf16[8,192,128]{2,1,0:T(8,128)(2,1)S(1)} %all-to-all-done.1.got_ref.got, bf16[1024,128]{1,0:T(8,128)(2,1)} %constant_dynamic-update-slice_fusion.two, bf16[1024,128]{1,0:T(8,128)(2,1)} %collective-permute-done.1.other), custom_call_target="tpu_custom_call" | custom-call | bytes 1589248 | tf_op jit(solution)/shard_map/pallas_call | solution.py:58
  43.3 2.8 %collective-permute-start.3 = (bf16[2048,128]{1,0:T(8,128)(2,1)}, bf16[2048,128]{1,0:T(8,128)(2,1)}, u32[]{:S(2)}, u32[]{:S(2)}) collective-permute-start(bf16[2048,128]{1,0:T(8,128)(2,1)} %get-tuple-element.50.near), channel_id=1, source_target_pairs={{0,12},{12,0},{4,8},{8,4},{1,13},{13,1},{5,9},{9,5},{2,14},{14,2},... | collective-permute-start | bytes 1572872 | tf_op jit(solution)/shard_map/ppermute | solution.py:402
  46.2 1.9 %shard_map.116 = (f32[1024,128]{1,0:T(8,128)S(1)}, bf16[1024,128]{1,0:T(8,128)(2,1)S(1)}) custom-call(s32[1]{0:T(128)} %bitcast.place, bf16[512,640]{1,0:T(8,128)(2,1)S(1)} %copy-done.2, bf16[640,1024]{1,0:T(8,128)(2,1)S(1)} %copy-done, bf16[2048,128]{1,0:T(8,128)(2,1)} %collective-permute-done.2.got), custom_call_target="tpu_custom_call" | custom-call | flops 335544320 | bytes 3276804 | tf_op jit(solution)/shard_map/pallas_call | solution.py:58
  48.1 0.7 copy-done.9
  48.8 3.0 %all-to-all-done.2.got_ref = bf16[16,48,128]{2,1,0:T(8,128)(2,1)S(1)} async-done(((bf16[16,48,128]{2,1,0:T(8,128)(2,1)}), bf16[16,48,128]{2,1,0:T(8,128)(2,1)S(1)}, u32[]{:S(2)}, u32[]{:S(2)}) %all-to-all-start.2) | async-done | bytes 196640 | tf_op jit(solution)/shard_map/all_to_all | solution.py:40
  51.7 0.7 shard_map.117
  52.4 9.1 %all-to-all-start.3 = ((bf16[4,48,128]{2,1,0:T(8,128)(2,1)}), bf16[4,48,128]{2,1,0:T(8,128)(2,1)S(1)}, u32[]{:S(2)}, u32[]{:S(2)}) async-start(bf16[4,48,128]{2,1,0:T(8,128)(2,1)} %shard_map.117), calls=%async_computation.3 | async-start | bytes 98304 | tf_op jit(solution)/shard_map/all_to_all | solution.py:40
  61.5 3.4 %collective-permute-start.4 = (bf16[1024,128]{1,0:T(8,128)(2,1)}, bf16[1024,128]{1,0:T(8,128)(2,1)S(1)}, u32[]{:S(2)}, u32[]{:S(2)}) collective-permute-start(bf16[1024,128]{1,0:T(8,128)(2,1)} %copy-done.9), channel_id=1, source_target_pairs={{0,4},{4,0},{8,12},{12,8},{1,5},{5,1},{9,13},{13,9},{2,6},{6,2},{1... | collective-permute-start | bytes 786440 | tf_op jit(solution)/shard_map/ppermute | solution.py:411
  64.9 3.5 %all-to-all-done.3.got_ref = bf16[4,48,128]{2,1,0:T(8,128)(2,1)S(1)} async-done(((bf16[4,48,128]{2,1,0:T(8,128)(2,1)}), bf16[4,48,128]{2,1,0:T(8,128)(2,1)S(1)}, u32[]{:S(2)}, u32[]{:S(2)}) %all-to-all-start.3) | async-done | bytes 49184 | tf_op jit(solution)/shard_map/all_to_all | solution.py:40
  68.4 0.8 shard_map.118
  69.3 6.1 %all-to-all-start.4 = ((bf16[16,48,128]{2,1,0:T(8,128)(2,1)}), bf16[16,48,128]{2,1,0:T(8,128)(2,1)S(1)}, u32[]{:S(2)}, u32[]{:S(2)}) async-start(bf16[16,48,128]{2,1,0:T(8,128)(2,1)} %shard_map.118), calls=%async_computation.4 | async-start | bytes 393216 | tf_op jit(solution)/shard_map/all_to_all | solution.py:40
  75.4 0.7 copy-done.5
  76.1 0.9 copy-done.6
  77.1 3.0 %collective-permute-start.5 = (bf16[512,128]{1,0:T(8,128)(2,1)S(1)}, bf16[512,128]{1,0:T(8,128)(2,1)S(1)}, u32[]{:S(2)}, u32[]{:S(2)}) collective-permute-start(bf16[512,128]{1,0:T(8,128)(2,1)S(1)} %get-tuple-element.55), channel_id=1, source_target_pairs={{0,2},{2,0},{1,3},{3,1},{4,6},{6,4},{5,7},{7,5},{8,10},{10,8},{9,1... | collective-permute-start | bytes 393224 | tf_op jit(solution)/shard_map/ppermute | solution.py:423
  80.1 3.4 %shard_map.119 = bf16[512,640]{1,0:T(8,128)(2,1)} custom-call(s32[1]{0:T(128)} %bitcast.place, bf16[2048,128]{1,0:T(8,128)(2,1)} %get-tuple-element.50.near, bf16[2048,128]{1,0:T(8,128)(2,1)} %collective-permute-done.3.far, bf16[512,128]{1,0:T(8,128)(2,1)S(1)} %get-tuple-element.51.up, f32[640,128]{1,0:T(8,128)S(1)} %copy-done.3, bf16[640,1024]{1,0:T(8,128)(2,1)S(1)} %copy-done), custom_call_target="tpu_custom_call" | custom-call | flops 754974720 | bytes 3473412 | tf_op jit(solution)/shard_map/pallas_call | solution.py:58
  83.5 0.5 collective-permute-done.5.base_got
  84.1 1.7 %all-to-all-done.4.got_ref.got_g = bf16[16,48,128]{2,1,0:T(8,128)(2,1)S(1)} async-done(((bf16[16,48,128]{2,1,0:T(8,128)(2,1)}), bf16[16,48,128]{2,1,0:T(8,128)(2,1)S(1)}, u32[]{:S(2)}, u32[]{:S(2)}) %all-to-all-start.4) | async-done | bytes 196640 | tf_op jit(solution)/shard_map/all_to_all | solution.py:40
  86.1 10.6 %all_to_all.35.got.sums = bf16[8,80,128]{2,1,0:T(8,128)(2,1)S(1)} all-to-all(bf16[8,80,128]{2,1,0:T(8,128)(2,1)S(1)} %shard_map.121), channel_id=1, replica_groups=mesh['zhi'=4,'y'=8,'x'=4,'zlo'=2,'core'=2] {'x','zlo'}, dimensions={0} | all-to-all | bytes 327680 | tf_op jit(solution)/shard_map/all_to_all | solution.py:40
  96.8 8.0 %all_to_all.36.got = bf16[8,64,128]{2,1,0:T(8,128)(2,1)S(1)} all-to-all(bf16[8,64,128]{2,1,0:T(8,128)(2,1)S(1)} %shard_map.122), channel_id=1, replica_groups=mesh['zhi'=4,'y'=8,'x'=4,'zlo'=2,'core'=2] {'x','zlo'}, dimensions={0} | all-to-all | bytes 262144 | tf_op jit(solution)/shard_map/all_to_all | solution.py:40
  104.8 1.0 shard_map.123
  (26 shorter events, 1.0 us)
Async XLA Ops:
  0.6 13.3 %copy-start.3 = (f32[640,128]{1,0:T(8,128)S(1)}, f32[640,128]{1,0:T(8,128)}, u32[]{:S(2)}) copy-start(f32[640,128]{1,0:T(8,128)} %down_w.7) | copy-start | bytes 983044
  0.6 13.3 %copy-start = (bf16[640,1024]{1,0:T(8,128)(2,1)S(1)}, bf16[640,1024]{1,0:T(8,128)(2,1)}, u32[]{:S(2)}) copy-start(bf16[640,1024]{1,0:T(8,128)(2,1)} %frozen.5) | copy-start | bytes 3932164
  3.9 13.3 %all-to-all-start = ((bf16[8,128,128]{2,1,0:T(8,128)(2,1)}), bf16[8,128,128]{2,1,0:T(8,128)(2,1)S(1)}, u32[]{:S(2)}, u32[]{:S(2)}) async-start(bf16[8,128,128]{2,1,0:T(8,128)(2,1)} %get-tuple-element.34), calls=%async_computation | async-start | bytes 524288 | tf_op jit(solution)/shard_map/all_to_all | solution.py:40
  10.6 6.6 %collective-permute-start = (bf16[512,128]{1,0:T(8,128)(2,1)}, bf16[512,128]{1,0:T(8,128)(2,1)S(1)}, u32[]{:S(2)}, u32[]{:S(2)}) collective-permute-start(bf16[512,128]{1,0:T(8,128)(2,1)} %get-tuple-element.37.gk), channel_id=1, source_target_pairs={{0,2},{2,0},{1,3},{3,1},{4,6},{6,4},{5,7},{7,5},{8,10},{10,8},{9,1... | collective-permute-start | bytes 393224 | tf_op jit(solution)/shard_map/ppermute | solution.py:358
  14.0 1.1 %copy-start.1 = (bf16[512,640]{1,0:T(8,128)(2,1)S(1)}, bf16[512,640]{1,0:T(8,128)(2,1)}, u32[]{:S(2)}) copy-start(bf16[512,640]{1,0:T(8,128)(2,1)} %prompts.5) | copy-start | bytes 1966084
  16.8 13.7 %copy-start.4 = (bf16[512,640]{1,0:T(8,128)(2,1)S(1)}, bf16[512,640]{1,0:T(8,128)(2,1)}, u32[]{:S(2)}) copy-start(bf16[512,640]{1,0:T(8,128)(2,1)} %acts.3) | copy-start | bytes 1966084
  16.8 13.7 %copy-start.8 = (bf16[512,128]{1,0:T(8,128)(2,1)S(1)}, bf16[512,128]{1,0:T(8,128)(2,1)}, u32[]{:S(2)}) copy-start(bf16[512,128]{1,0:T(8,128)(2,1)} %get-tuple-element.37.gk) | copy-start | bytes 393220
  18.0 12.5 %all-to-all-start.1 = ((bf16[8,192,128]{2,1,0:T(8,128)(2,1)}), bf16[8,192,128]{2,1,0:T(8,128)(2,1)S(1)}, u32[]{:S(2)}, u32[]{:S(2)}) async-start(bf16[8,192,128]{2,1,0:T(8,128)(2,1)} %shard_map.113), calls=%async_computation.1 | async-start | bytes 786432 | tf_op jit(solution)/shard_map/all_to_all | solution.py:40
  23.2 22.9 %collective-permute-start.2 = (bf16[2048,128]{1,0:T(8,128)(2,1)}, bf16[2048,128]{1,0:T(8,128)(2,1)}, u32[]{:S(2)}, u32[]{:S(2)}) collective-permute-start(bf16[2048,128]{1,0:T(8,128)(2,1)} %get-tuple-element.46), channel_id=1, source_target_pairs={{0,12},{12,0},{4,8},{8,4},{1,13},{13,1},{5,9},{9,5},{2,14},{14,2},... | collective-permute-start | bytes 1572872 | tf_op jit(solution)/shard_map/ppermute | solution.py:379
  28.5 17.7 %copy-start.2 = (bf16[512,640]{1,0:T(8,128)(2,1)S(1)}, bf16[512,640]{1,0:T(8,128)(2,1)}, u32[]{:S(2)}) copy-start(bf16[512,640]{1,0:T(8,128)(2,1)} %prompts.5) | copy-start | bytes 1966084
  28.5 12.9 %collective-permute-start.1 = (bf16[1024,128]{1,0:T(8,128)(2,1)}, bf16[1024,128]{1,0:T(8,128)(2,1)}, u32[]{:S(2)}, u32[]{:S(2)}) collective-permute-start(bf16[1024,128]{1,0:T(8,128)(2,1)} %constant_dynamic-update-slice_fusion.two), channel_id=1, source_target_pairs={{0,4},{4,0},{8,12},{12,8},{1,5},{5,1},{9,13},{13,9},{2,6},{6,2},{1... | collective-permute-start | bytes 786440 | tf_op jit(solution)/shard_map/ppermute | solution.py:378
  31.6 20.1 %all-to-all-start.2 = ((bf16[16,48,128]{2,1,0:T(8,128)(2,1)}), bf16[16,48,128]{2,1,0:T(8,128)(2,1)S(1)}, u32[]{:S(2)}, u32[]{:S(2)}) async-start(bf16[16,48,128]{2,1,0:T(8,128)(2,1)} %shard_map.114), calls=%async_computation.2 | async-start | bytes 393216 | tf_op jit(solution)/shard_map/all_to_all | solution.py:40
  43.3 36.8 %collective-permute-start.3 = (bf16[2048,128]{1,0:T(8,128)(2,1)}, bf16[2048,128]{1,0:T(8,128)(2,1)}, u32[]{:S(2)}, u32[]{:S(2)}) collective-permute-start(bf16[2048,128]{1,0:T(8,128)(2,1)} %get-tuple-element.50.near), channel_id=1, source_target_pairs={{0,12},{12,0},{4,8},{8,4},{1,13},{13,1},{5,9},{9,5},{2,14},{14,2},... | collective-permute-start | bytes 1572872 | tf_op jit(solution)/shard_map/ppermute | solution.py:402
  48.0 0.7 copy-start.9
  52.4 16.0 %all-to-all-start.3 = ((bf16[4,48,128]{2,1,0:T(8,128)(2,1)}), bf16[4,48,128]{2,1,0:T(8,128)(2,1)S(1)}, u32[]{:S(2)}, u32[]{:S(2)}) async-start(bf16[4,48,128]{2,1,0:T(8,128)(2,1)} %shard_map.117), calls=%async_computation.3 | async-start | bytes 98304 | tf_op jit(solution)/shard_map/all_to_all | solution.py:40
  61.5 13.8 %collective-permute-start.4 = (bf16[1024,128]{1,0:T(8,128)(2,1)}, bf16[1024,128]{1,0:T(8,128)(2,1)S(1)}, u32[]{:S(2)}, u32[]{:S(2)}) collective-permute-start(bf16[1024,128]{1,0:T(8,128)(2,1)} %copy-done.9), channel_id=1, source_target_pairs={{0,4},{4,0},{8,12},{12,8},{1,5},{5,1},{9,13},{13,9},{2,6},{6,2},{1... | collective-permute-start | bytes 786440 | tf_op jit(solution)/shard_map/ppermute | solution.py:411
  69.3 16.4 %all-to-all-start.4 = ((bf16[16,48,128]{2,1,0:T(8,128)(2,1)}), bf16[16,48,128]{2,1,0:T(8,128)(2,1)S(1)}, u32[]{:S(2)}, u32[]{:S(2)}) async-start(bf16[16,48,128]{2,1,0:T(8,128)(2,1)} %shard_map.118), calls=%async_computation.4 | async-start | bytes 393216 | tf_op jit(solution)/shard_map/all_to_all | solution.py:40
  75.4 0.7 copy-start.5
  76.1 0.9 copy-start.6
  77.1 7.0 %collective-permute-start.5 = (bf16[512,128]{1,0:T(8,128)(2,1)S(1)}, bf16[512,128]{1,0:T(8,128)(2,1)S(1)}, u32[]{:S(2)}, u32[]{:S(2)}) collective-permute-start(bf16[512,128]{1,0:T(8,128)(2,1)S(1)} %get-tuple-element.55), channel_id=1, source_target_pairs={{0,2},{2,0},{1,3},{3,1},{4,6},{6,4},{5,7},{7,5},{8,10},{10,8},{9,1... | collective-permute-start | bytes 393224 | tf_op jit(solution)/shard_map/ppermute | solution.py:423
  83.5 21.3 %copy-start.7 = (f32[128,128]{1,0:T(8,128)S(1)}, f32[128,128]{1,0:T(8,128)}, u32[]{:S(2)}) copy-start(f32[128,128]{1,0:T(8,128)} %up_w.3) | copy-start | bytes 196612

commit v10 on v9

--- a/solution.py
+++ b/solution.py
@@ -12,8 +12,9 @@
 
 AXES = ("zhi", "y", "x", "zlo", "core")
 FSDP = ("x", "zlo")
+PEERS = ("zlo", "x")
 ROWS = ("zhi", "y", "core")
-NEAR = ("y", "core")
+NEAR = ("core", "y")
 FAR = "zhi"
 TAIL = 16
 bf16 = jnp.bfloat16
@@ -354,7 +355,7 @@
             pltpu.SemaphoreType.DMA((7,)),
         ],
     )
-    got = swap(pay, FSDP)
+    got = swap(pay, PEERS)
     other = lax.ppermute(gk, "zlo", Z_PAIRS)
     place = lax.axis_index(FSDP).reshape(1)
     proj, send = call(
@@ -373,7 +374,7 @@
         out_specs=(HBM,),
         scratch_shapes=[pltpu.VMEM((n_f, 3 * piece, rank), bf16), pltpu.SemaphoreType.DMA],
     )
-    got = swap(pay, FSDP)
+    got = swap(pay, PEERS)
     two = lax.dynamic_update_slice(two, other, (rows, 0))
     other = lax.ppermute(two, "x", X_NEAR)
     base_got = lax.ppermute(send, "x", X_FAR)
@@ -431,11 +432,11 @@
         (got_g, prompts),
         flops=2 * rows * width * rank,
     )
-    sums = swap(pay, FSDP)
+    sums = swap(pay, PEERS)
     (pay,) = call(
         rows_kernel, [shape((n_f, piece, rank), bf16)], [VMEM] * 2, (sums, pa_rows)
     )
-    got = swap(pay, FSDP)
+    got = swap(pay, PEERS)
     next_down, next_up, keys = call(
         finish_kernel,
         [shape((width, rank), f32), shape((rank, cols), f32), shape((rows, cols), bf16)],

time: 107 us -> 107 us (level)
  the two profiles are of different devices: /device:TPU:1 before, /device:TPU:8 now
where the time goes in v10:
time: 107 us; the launch traced here: 106 us
  starting transfers between devices  54.4 us (51%)
  blocking collectives  20.4 us (19%)
  Pallas kernels  17.1 us (16%)
  waiting for transfers between devices  8.94 us (8%)
  local copies, waits for them, and re-layouts  4.12 us (4%)
    all_to_all x5, starting transfers between devices, swap(): return lax.all_to_all(v, axis, 0, 0, tiled=True)  33.1 us
    all_to_all x2, blocking collectives, swap(): return lax.all_to_all(v, axis, 0, 0, tiled=True)  20.4 us
    pallas_call x13, Pallas kernels, call(): pl.pallas_call(kernel, grid=(1,), in_specs=[spec or block(a) for spec, a...  17.1 us
    all_to_all x5, waiting for transfers between devices, swap(): return lax.all_to_all(v, axis, 0, 0, tiled=True)  6.98 us
    ppermute x1, starting transfers between devices, per_device(): base_got = lax.ppermute(send, 'x', X_FAR)  5.13 us
    ppermute x1, starting transfers between devices, per_device(): other = lax.ppermute(gk, 'zlo', Z_PAIRS)  3.92 us
    ppermute x1, starting transfers between devices, per_device(): base_got = lax.ppermute(send, 'x', X_NEAR)  3.67 us
    unnamed x20, local copies, waits for them, and re-layouts  3.45 us
  transfers between devices with their start and end apart: 11, of which 5 were waited for; matrix products, arithmetic and copies ran while one was open for 1% of the time, Pallas kernels for 11%

profile of v10, /device:TPU:8, one launch (start us, length us, event | category | flops | bytes accessed | tf_op | source)
XLA Modules:
  0.0 105.8 jit_solution(17554246984939679536)
XLA Ops:
  0.7 3.2 %shard_map.111 = (bf16[512,128]{1,0:T(8,128)(2,1)}, bf16[1024,128]{1,0:T(8,128)(2,1)}, bf16[8,128,128]{2,1,0:T(8,128)(2,1)}) custom-call(s32[2]{0:T(128)} %lens.1, s32[2]{0:T(128)} %buckets.1, bf16[512,640]{1,0:T(8,128)(2,1)} %acts.3, bf16[512,128]{1,0:T(8,128)(2,1)} %og.1, f32[640,128]{1,0:T(8,128)} %down_w.7, f32[128,128]{1,0:T(8,128)} %up_w.3), custom_call_target="tpu_custom_call" | custom-call | flops 100663296 | bytes 1835024 | tf_op jit(solution)/shard_map/pallas_call | solution.py:59
  3.9 6.1 %all-to-all-start = ((bf16[8,128,128]{2,1,0:T(8,128)(2,1)}), bf16[8,128,128]{2,1,0:T(8,128)(2,1)S(1)}, u32[]{:S(2)}, u32[]{:S(2)}) async-start(bf16[8,128,128]{2,1,0:T(8,128)(2,1)} %get-tuple-element.34), calls=%async_computation | async-start | bytes 524288 | tf_op jit(solution)/shard_map/all_to_all | solution.py:41
  10.0 3.9 %collective-permute-start = (bf16[512,128]{1,0:T(8,128)(2,1)}, bf16[512,128]{1,0:T(8,128)(2,1)S(1)}, u32[]{:S(2)}, u32[]{:S(2)}) collective-permute-start(bf16[512,128]{1,0:T(8,128)(2,1)} %get-tuple-element.37.gk), channel_id=1, source_target_pairs={{0,2},{2,0},{1,3},{3,1},{4,6},{6,4},{5,7},{7,5},{8,10},{10,8},{9,1... | collective-permute-start | bytes 393224 | tf_op jit(solution)/shard_map/ppermute | solution.py:359
  14.0 1.1 %copy-done.1 = bf16[512,640]{1,0:T(8,128)(2,1)S(1)} copy-done((bf16[512,640]{1,0:T(8,128)(2,1)S(1)}, bf16[512,640]{1,0:T(8,128)(2,1)}, u32[]{:S(2)}) %copy-start.1) | copy-done | bytes 655384
  15.1 1.7 %shard_map.112 = (bf16[512,128]{1,0:T(8,128)(2,1)S(1)}, bf16[2048,128]{1,0:T(8,128)(2,1)}) custom-call(s32[1]{0:T(128)} %bitcast.place, bf16[512,640]{1,0:T(8,128)(2,1)S(1)} %copy-done.1, bf16[640,1024]{1,0:T(8,128)(2,1)S(1)} %copy-done, f32[640,128]{1,0:T(8,128)S(1)} %copy-done.3), custom_call_target="tpu_custom_call" | custom-call | flops 419430400 | bytes 2949124 | tf_op jit(solution)/shard_map/pallas_call | solution.py:59
  16.8 1.2 %collective-permute-done = bf16[512,128]{1,0:T(8,128)(2,1)S(1)} collective-permute-done((bf16[512,128]{1,0:T(8,128)(2,1)}, bf16[512,128]{1,0:T(8,128)(2,1)S(1)}, u32[]{:S(2)}, u32[]{:S(2)}) %collective-permute-start) | collective-permute-done | bytes 131104 | tf_op jit(solution)/shard_map/ppermute | solution.py:359
  18.0 0.8 shard_map.113
  18.8 4.8 %all-to-all-start.1 = ((bf16[8,192,128]{2,1,0:T(8,128)(2,1)}), bf16[8,192,128]{2,1,0:T(8,128)(2,1)S(1)}, u32[]{:S(2)}, u32[]{:S(2)}) async-start(bf16[8,192,128]{2,1,0:T(8,128)(2,1)} %shard_map.113), calls=%async_computation.1 | async-start | bytes 786432 | tf_op jit(solution)/shard_map/all_to_all | solution.py:41
  23.6 5.1 %collective-permute-start.2 = (bf16[2048,128]{1,0:T(8,128)(2,1)}, bf16[2048,128]{1,0:T(8,128)(2,1)}, u32[]{:S(2)}, u32[]{:S(2)}) collective-permute-start(bf16[2048,128]{1,0:T(8,128)(2,1)} %get-tuple-element.46), channel_id=1, source_target_pairs={{0,12},{12,0},{4,8},{8,4},{1,13},{13,1},{5,9},{9,5},{2,14},{14,2},... | collective-permute-start | bytes 1572872 | tf_op jit(solution)/shard_map/ppermute | solution.py:380
  28.8 0.7 constant_dynamic-update-slice_fusion.two
  29.4 2.3 %collective-permute-start.1 = (bf16[1024,128]{1,0:T(8,128)(2,1)}, bf16[1024,128]{1,0:T(8,128)(2,1)}, u32[]{:S(2)}, u32[]{:S(2)}) collective-permute-start(bf16[1024,128]{1,0:T(8,128)(2,1)} %constant_dynamic-update-slice_fusion.two), channel_id=1, source_target_pairs={{0,4},{4,0},{8,12},{12,8},{1,5},{5,1},{9,13},{13,9},{2,6},{6,2},{1... | collective-permute-start | bytes 786440 | tf_op jit(solution)/shard_map/ppermute | solution.py:379
  31.7 1.0 shard_map.114
  32.8 7.6 %all-to-all-start.2 = ((bf16[16,48,128]{2,1,0:T(8,128)(2,1)}), bf16[16,48,128]{2,1,0:T(8,128)(2,1)S(1)}, u32[]{:S(2)}, u32[]{:S(2)}) async-start(bf16[16,48,128]{2,1,0:T(8,128)(2,1)} %shard_map.114), calls=%async_computation.2 | async-start | bytes 393216 | tf_op jit(solution)/shard_map/all_to_all | solution.py:41
  40.4 1.9 %shard_map.115 = (bf16[64,128]{1,0:T(8,128)(2,1)S(1)}, bf16[512,128]{1,0:T(8,128)(2,1)S(1)}, bf16[2048,128]{1,0:T(8,128)(2,1)}) custom-call(bf16[8,192,128]{2,1,0:T(8,128)(2,1)S(1)} %all-to-all-done.1.got_ref.got, bf16[1024,128]{1,0:T(8,128)(2,1)} %constant_dynamic-update-slice_fusion.two, bf16[1024,128]{1,0:T(8,128)(2,1)} %collective-permute-done.1.other), custom_call_target="tpu_custom_call" | custom-call | bytes 1589248 | tf_op jit(solution)/shard_map/pallas_call | solution.py:59
  42.3 3.1 %collective-permute-start.3 = (bf16[2048,128]{1,0:T(8,128)(2,1)}, bf16[2048,128]{1,0:T(8,128)(2,1)}, u32[]{:S(2)}, u32[]{:S(2)}) collective-permute-start(bf16[2048,128]{1,0:T(8,128)(2,1)} %get-tuple-element.50.near), channel_id=1, source_target_pairs={{0,12},{12,0},{4,8},{8,4},{1,13},{13,1},{5,9},{9,5},{2,14},{14,2},... | collective-permute-start | bytes 1572872 | tf_op jit(solution)/shard_map/ppermute | solution.py:403
  45.4 1.9 %shard_map.116 = (f32[1024,128]{1,0:T(8,128)S(1)}, bf16[1024,128]{1,0:T(8,128)(2,1)S(1)}) custom-call(s32[1]{0:T(128)} %bitcast.place, bf16[512,640]{1,0:T(8,128)(2,1)S(1)} %copy-done.2, bf16[640,1024]{1,0:T(8,128)(2,1)S(1)} %copy-done, bf16[2048,128]{1,0:T(8,128)(2,1)} %collective-permute-done.2.got), custom_call_target="tpu_custom_call" | custom-call | flops 335544320 | bytes 3276804 | tf_op jit(solution)/shard_map/pallas_call | solution.py:59
  47.3 0.7 copy-done.9
  48.0 2.0 %all-to-all-done.2.got_ref = bf16[16,48,128]{2,1,0:T(8,128)(2,1)S(1)} async-done(((bf16[16,48,128]{2,1,0:T(8,128)(2,1)}), bf16[16,48,128]{2,1,0:T(8,128)(2,1)S(1)}, u32[]{:S(2)}, u32[]{:S(2)}) %all-to-all-start.2) | async-done | bytes 196640 | tf_op jit(solution)/shard_map/all_to_all | solution.py:41
  50.0 0.7 shard_map.117
  50.6 9.4 %all-to-all-start.3 = ((bf16[4,48,128]{2,1,0:T(8,128)(2,1)}), bf16[4,48,128]{2,1,0:T(8,128)(2,1)S(1)}, u32[]{:S(2)}, u32[]{:S(2)}) async-start(bf16[4,48,128]{2,1,0:T(8,128)(2,1)} %shard_map.117), calls=%async_computation.3 | async-start | bytes 98304 | tf_op jit(solution)/shard_map/all_to_all | solution.py:41
  60.1 3.7 %collective-permute-start.4 = (bf16[1024,128]{1,0:T(8,128)(2,1)}, bf16[1024,128]{1,0:T(8,128)(2,1)S(1)}, u32[]{:S(2)}, u32[]{:S(2)}) collective-permute-start(bf16[1024,128]{1,0:T(8,128)(2,1)} %copy-done.9), channel_id=1, source_target_pairs={{0,4},{4,0},{8,12},{12,8},{1,5},{5,1},{9,13},{13,9},{2,6},{6,2},{1... | collective-permute-start | bytes 786440 | tf_op jit(solution)/shard_map/ppermute | solution.py:412
  63.7 4.5 %all-to-all-done.3.got_ref = bf16[4,48,128]{2,1,0:T(8,128)(2,1)S(1)} async-done(((bf16[4,48,128]{2,1,0:T(8,128)(2,1)}), bf16[4,48,128]{2,1,0:T(8,128)(2,1)S(1)}, u32[]{:S(2)}, u32[]{:S(2)}) %all-to-all-start.3) | async-done | bytes 49184 | tf_op jit(solution)/shard_map/all_to_all | solution.py:41
  68.3 0.8 shard_map.118
  69.1 5.2 %all-to-all-start.4 = ((bf16[16,48,128]{2,1,0:T(8,128)(2,1)}), bf16[16,48,128]{2,1,0:T(8,128)(2,1)S(1)}, u32[]{:S(2)}, u32[]{:S(2)}) async-start(bf16[16,48,128]{2,1,0:T(8,128)(2,1)} %shard_map.118), calls=%async_computation.4 | async-start | bytes 393216 | tf_op jit(solution)/shard_map/all_to_all | solution.py:41
  74.4 0.7 copy-done.5
  75.0 0.9 copy-done.6
  76.0 3.2 %collective-permute-start.5 = (bf16[512,128]{1,0:T(8,128)(2,1)S(1)}, bf16[512,128]{1,0:T(8,128)(2,1)S(1)}, u32[]{:S(2)}, u32[]{:S(2)}) collective-permute-start(bf16[512,128]{1,0:T(8,128)(2,1)S(1)} %get-tuple-element.55), channel_id=1, source_target_pairs={{0,2},{2,0},{1,3},{3,1},{4,6},{6,4},{5,7},{7,5},{8,10},{10,8},{9,1... | collective-permute-start | bytes 393224 | tf_op jit(solution)/shard_map/ppermute | solution.py:424
  79.3 3.4 %shard_map.119 = bf16[512,640]{1,0:T(8,128)(2,1)} custom-call(s32[1]{0:T(128)} %bitcast.place, bf16[2048,128]{1,0:T(8,128)(2,1)} %get-tuple-element.50.near, bf16[2048,128]{1,0:T(8,128)(2,1)} %collective-permute-done.3.far, bf16[512,128]{1,0:T(8,128)(2,1)S(1)} %get-tuple-element.51.up, f32[640,128]{1,0:T(8,128)S(1)} %copy-done.3, bf16[640,1024]{1,0:T(8,128)(2,1)S(1)} %copy-done), custom_call_target="tpu_custom_call" | custom-call | flops 754974720 | bytes 3473412 | tf_op jit(solution)/shard_map/pallas_call | solution.py:59
  82.7 0.8 collective-permute-done.5.base_got
  84.3 11.3 %all_to_all.35.got.sums = bf16[8,80,128]{2,1,0:T(8,128)(2,1)S(1)} all-to-all(bf16[8,80,128]{2,1,0:T(8,128)(2,1)S(1)} %shard_map.121), channel_id=1, replica_groups=mesh['zhi'=4,'y'=8,'x'=4,'zlo'=2,'core'=2] {'zlo','x'}, dimensions={0} | all-to-all | bytes 327680 | tf_op jit(solution)/shard_map/all_to_all | solution.py:41
  95.7 9.1 %all_to_all.36.got = bf16[8,64,128]{2,1,0:T(8,128)(2,1)S(1)} all-to-all(bf16[8,64,128]{2,1,0:T(8,128)(2,1)S(1)} %shard_map.122), channel_id=1, replica_groups=mesh['zhi'=4,'y'=8,'x'=4,'zlo'=2,'core'=2] {'zlo','x'}, dimensions={0} | all-to-all | bytes 262144 | tf_op jit(solution)/shard_map/all_to_all | solution.py:41
  104.8 1.0 shard_map.123
  (26 shorter events, 1.0 us)
Async XLA Ops:
  0.6 13.3 %copy-start.3 = (f32[640,128]{1,0:T(8,128)S(1)}, f32[640,128]{1,0:T(8,128)}, u32[]{:S(2)}) copy-start(f32[640,128]{1,0:T(8,128)} %down_w.7) | copy-start | bytes 983044
  0.6 13.3 %copy-start = (bf16[640,1024]{1,0:T(8,128)(2,1)S(1)}, bf16[640,1024]{1,0:T(8,128)(2,1)}, u32[]{:S(2)}) copy-start(bf16[640,1024]{1,0:T(8,128)(2,1)} %frozen.5) | copy-start | bytes 3932164
  3.9 14.1 %all-to-all-start = ((bf16[8,128,128]{2,1,0:T(8,128)(2,1)}), bf16[8,128,128]{2,1,0:T(8,128)(2,1)S(1)}, u32[]{:S(2)}, u32[]{:S(2)}) async-start(bf16[8,128,128]{2,1,0:T(8,128)(2,1)} %get-tuple-element.34), calls=%async_computation | async-start | bytes 524288 | tf_op jit(solution)/shard_map/all_to_all | solution.py:41
  10.0 8.0 %collective-permute-start = (bf16[512,128]{1,0:T(8,128)(2,1)}, bf16[512,128]{1,0:T(8,128)(2,1)S(1)}, u32[]{:S(2)}, u32[]{:S(2)}) collective-permute-start(bf16[512,128]{1,0:T(8,128)(2,1)} %get-tuple-element.37.gk), channel_id=1, source_target_pairs={{0,2},{2,0},{1,3},{3,1},{4,6},{6,4},{5,7},{7,5},{8,10},{10,8},{9,1... | collective-permute-start | bytes 393224 | tf_op jit(solution)/shard_map/ppermute | solution.py:359
  14.0 1.1 %copy-start.1 = (bf16[512,640]{1,0:T(8,128)(2,1)S(1)}, bf16[512,640]{1,0:T(8,128)(2,1)}, u32[]{:S(2)}) copy-start(bf16[512,640]{1,0:T(8,128)(2,1)} %prompts.5) | copy-start | bytes 1966084
  16.8 14.9 %copy-start.4 = (bf16[512,640]{1,0:T(8,128)(2,1)S(1)}, bf16[512,640]{1,0:T(8,128)(2,1)}, u32[]{:S(2)}) copy-start(bf16[512,640]{1,0:T(8,128)(2,1)} %acts.3) | copy-start | bytes 1966084
  16.8 14.9 %copy-start.8 = (bf16[512,128]{1,0:T(8,128)(2,1)S(1)}, bf16[512,128]{1,0:T(8,128)(2,1)}, u32[]{:S(2)}) copy-start(bf16[512,128]{1,0:T(8,128)(2,1)} %get-tuple-element.37.gk) | copy-start | bytes 393220
  18.8 12.9 %all-to-all-start.1 = ((bf16[8,192,128]{2,1,0:T(8,128)(2,1)}), bf16[8,192,128]{2,1,0:T(8,128)(2,1)S(1)}, u32[]{:S(2)}, u32[]{:S(2)}) async-start(bf16[8,192,128]{2,1,0:T(8,128)(2,1)} %shard_map.113), calls=%async_computation.1 | async-start | bytes 786432 | tf_op jit(solution)/shard_map/all_to_all | solution.py:41
  23.6 21.7 %collective-permute-start.2 = (bf16[2048,128]{1,0:T(8,128)(2,1)}, bf16[2048,128]{1,0:T(8,128)(2,1)}, u32[]{:S(2)}, u32[]{:S(2)}) collective-permute-start(bf16[2048,128]{1,0:T(8,128)(2,1)} %get-tuple-element.46), channel_id=1, source_target_pairs={{0,12},{12,0},{4,8},{8,4},{1,13},{13,1},{5,9},{9,5},{2,14},{14,2},... | collective-permute-start | bytes 1572872 | tf_op jit(solution)/shard_map/ppermute | solution.py:380
  29.4 15.9 %copy-start.2 = (bf16[512,640]{1,0:T(8,128)(2,1)S(1)}, bf16[512,640]{1,0:T(8,128)(2,1)}, u32[]{:S(2)}) copy-start(bf16[512,640]{1,0:T(8,128)(2,1)} %prompts.5) | copy-start | bytes 1966084
  29.4 10.9 %collective-permute-start.1 = (bf16[1024,128]{1,0:T(8,128)(2,1)}, bf16[1024,128]{1,0:T(8,128)(2,1)}, u32[]{:S(2)}, u32[]{:S(2)}) collective-permute-start(bf16[1024,128]{1,0:T(8,128)(2,1)} %constant_dynamic-update-slice_fusion.two), channel_id=1, source_target_pairs={{0,4},{4,0},{8,12},{12,8},{1,5},{5,1},{9,13},{13,9},{2,6},{6,2},{1... | collective-permute-start | bytes 786440 | tf_op jit(solution)/shard_map/ppermute | solution.py:379
  32.8 17.2 %all-to-all-start.2 = ((bf16[16,48,128]{2,1,0:T(8,128)(2,1)}), bf16[16,48,128]{2,1,0:T(8,128)(2,1)S(1)}, u32[]{:S(2)}, u32[]{:S(2)}) async-start(bf16[16,48,128]{2,1,0:T(8,128)(2,1)} %shard_map.114), calls=%async_computation.2 | async-start | bytes 393216 | tf_op jit(solution)/shard_map/all_to_all | solution.py:41
  42.3 37.0 %collective-permute-start.3 = (bf16[2048,128]{1,0:T(8,128)(2,1)}, bf16[2048,128]{1,0:T(8,128)(2,1)}, u32[]{:S(2)}, u32[]{:S(2)}) collective-permute-start(bf16[2048,128]{1,0:T(8,128)(2,1)} %get-tuple-element.50.near), channel_id=1, source_target_pairs={{0,12},{12,0},{4,8},{8,4},{1,13},{13,1},{5,9},{9,5},{2,14},{14,2},... | collective-permute-start | bytes 1572872 | tf_op jit(solution)/shard_map/ppermute | solution.py:403
  47.2 0.7 copy-start.9
  50.6 17.6 %all-to-all-start.3 = ((bf16[4,48,128]{2,1,0:T(8,128)(2,1)}), bf16[4,48,128]{2,1,0:T(8,128)(2,1)S(1)}, u32[]{:S(2)}, u32[]{:S(2)}) async-start(bf16[4,48,128]{2,1,0:T(8,128)(2,1)} %shard_map.117), calls=%async_computation.3 | async-start | bytes 98304 | tf_op jit(solution)/shard_map/all_to_all | solution.py:41
  60.1 14.3 %collective-permute-start.4 = (bf16[1024,128]{1,0:T(8,128)(2,1)}, bf16[1024,128]{1,0:T(8,128)(2,1)S(1)}, u32[]{:S(2)}, u32[]{:S(2)}) collective-permute-start(bf16[1024,128]{1,0:T(8,128)(2,1)} %copy-done.9), channel_id=1, source_target_pairs={{0,4},{4,0},{8,12},{12,8},{1,5},{5,1},{9,13},{13,9},{2,6},{6,2},{1... | collective-permute-start | bytes 786440 | tf_op jit(solution)/shard_map/ppermute | solution.py:412
  69.1 14.8 %all-to-all-start.4 = ((bf16[16,48,128]{2,1,0:T(8,128)(2,1)}), bf16[16,48,128]{2,1,0:T(8,128)(2,1)S(1)}, u32[]{:S(2)}, u32[]{:S(2)}) async-start(bf16[16,48,128]{2,1,0:T(8,128)(2,1)} %shard_map.118), calls=%async_computation.4 | async-start | bytes 393216 | tf_op jit(solution)/shard_map/all_to_all | solution.py:41
  74.3 0.7 copy-start.5
  75.0 0.9 copy-start.6
  76.0 7.4 %collective-permute-start.5 = (bf16[512,128]{1,0:T(8,128)(2,1)S(1)}, bf16[512,128]{1,0:T(8,128)(2,1)S(1)}, u32[]{:S(2)}, u32[]{:S(2)}) collective-permute-start(bf16[512,128]{1,0:T(8,128)(2,1)S(1)} %get-tuple-element.55), channel_id=1, source_target_pairs={{0,2},{2,0},{1,3},{3,1},{4,6},{6,4},{5,7},{7,5},{8,10},{10,8},{9,1... | collective-permute-start | bytes 393224 | tf_op jit(solution)/shard_map/ppermute | solution.py:424
  82.7 22.1 %copy-start.7 = (f32[128,128]{1,0:T(8,128)S(1)}, f32[128,128]{1,0:T(8,128)}, u32[]{:S(2)}) copy-start(f32[128,128]{1,0:T(8,128)} %up_w.3) | copy-start | bytes 196612

commit v11 on v10

--- a/solution.py
+++ b/solution.py
@@ -14,8 +14,7 @@
 FSDP = ("x", "zlo")
 PEERS = ("zlo", "x")
 ROWS = ("zhi", "y", "core")
-NEAR = ("core", "y")
-FAR = "zhi"
+SUMMED = ("y", "zhi")
 TAIL = 16
 bf16 = jnp.bfloat16
 f32 = jnp.float32
@@ -28,6 +27,7 @@
     return lax.dot_general(a, b, dims, preferred_element_type=f32)
 
 
+CORES = ((0, 1), (1, 0))
 Z_PAIRS = ((0, 1), (1, 0))
 X_NEAR = ((0, 1), (1, 0), (2, 3), (3, 2))
 X_FAR = ((0, 3), (3, 0), (1, 2), (2, 1))
@@ -180,7 +180,7 @@
     )
 
 
-def grads_kernel(got_ref, acts, gk, pay, pay_v, sem):
+def grads_kernel(got_ref, acts, gk, pay):
     rows = acts.shape[0]
     piece = rows // got_ref.shape[0]
     lanes = gk.shape[1]
@@ -190,43 +190,29 @@
     peers = pay.shape[0]
     step = g.shape[0] // peers
     for j in range(peers):
-        pay_v[j] = jnp.concatenate(
+        pay[j] = jnp.concatenate(
             [
                 g[j * step : (j + 1) * step, c * lanes : (c + 1) * lanes]
                 for c in range(g.shape[1] // lanes)
             ],
             axis=0,
         ).astype(pay.dtype)
-    copy = pltpu.make_async_copy(pay_v, pay, sem)
-    copy.start()
-    copy.wait()
-
-
-def add_kernel(got_ref, pay, total_v, sems):
+
+
+def add_kernel(got_ref, out):
     total = got_ref[0].astype(f32)
     for j in range(1, got_ref.shape[0]):
         total += got_ref[j].astype(f32)
-    total_v[...] = total.astype(pay.dtype)
-    copies = [
-        pltpu.make_async_copy(total_v, pay.at[j], sems.at[j]) for j in range(pay.shape[0])
-    ]
-    for c in copies:
-        c.start()
-    for c in copies:
-        c.wait()
-
-
-def add(got, peers):
-    dims = got.shape[1:]
-    (pay,) = call(
-        add_kernel,
-        [shape((peers,) + dims, bf16)],
-        [VMEM],
-        (got,),
-        out_specs=(HBM,),
-        scratch_shapes=[pltpu.VMEM(dims, bf16), pltpu.SemaphoreType.DMA((peers,))],
-    )
-    return pay
+    out[...] = total
+
+
+def spread_kernel(mine, got, out, pay, sem):
+    total = (mine[...] + got[...]).astype(bf16)
+    for j in range(pay.shape[0]):
+        pay[j] = total
+    copy = pltpu.make_async_copy(pay, out, sem)
+    copy.start()
+    copy.wait()
 
 
 def whole_gradient(got_ref, rank):
@@ -314,10 +300,13 @@
     ).astype(bf16)
 
 
-def beside_kernel(got, two, other, pa_out, up_out, four):
+def join_kernel(two, other, four):
     count = two.shape[0]
     four[:count, :] = two[...]
     four[count:, :] = other[...]
+
+
+def beside_kernel(got, pa_out, up_out):
     peers = got.shape[0]
     piece = pa_out.shape[0]
     up_out[...] = rejoin(got, 0, piece)
@@ -332,10 +321,9 @@
     width, rank = down_w.shape
     cols = up_w.shape[1]
     n_f = lax.axis_size(FSDP)
-    n_near = lax.axis_size(NEAR)
-    n_far = lax.axis_size(FAR)
+    n_d = lax.axis_size(SUMMED)
     piece = rows // n_f
-    slab = (width + cols) // n_near
+    slab = (width + cols) // n_d
 
     gk, two, pay = call(
         parts_kernel,
@@ -382,25 +370,20 @@
 
     (pay,) = call(
         grads_kernel,
-        [shape((n_near, slab, rank), bf16)],
+        [shape((n_d, slab, rank), bf16)],
         [VMEM] * 3,
         (got, acts, gk),
         flops=2 * rows * rank * (width + cols),
-        out_specs=(HBM,),
-        scratch_shapes=[pltpu.VMEM((n_near, slab, rank), bf16), pltpu.SemaphoreType.DMA],
-    )
-    got_g = swap(pay, NEAR)
-    pa_rows, up, four = call(
+    )
+    got_g = swap(pay, SUMMED)
+    pa_rows, up = call(
         beside_kernel,
-        [
-            shape((piece, rank), bf16),
-            shape((rows, rank), bf16),
-            shape((n_f // 2 * rows, cols), bf16),
-        ],
-        [VMEM] * 3,
-        (got, two, other),
-    )
-    other = lax.ppermute(four, "x", X_FAR)
+        [shape((piece, rank), bf16), shape((rows, rank), bf16)],
+        [VMEM],
+        (got,),
+    )
+    (four,) = call(join_kernel, [shape((n_f // 2 * rows, cols), bf16)], [VMEM] * 2, (two, other))
+    far = lax.ppermute(four, "x", X_FAR)
     held, send = call(
         own_half_kernel,
         [shape((n_f // 4 * rows, cols), f32), shape((n_f // 4 * rows, cols), bf16)],
@@ -408,15 +391,25 @@
         (place, prompts, frozen, base_got),
         flops=rows * width * cols * n_f,
     )
-    got_g, pa_rows, up, held, send = lax.optimization_barrier((got_g, pa_rows, up, held, send))
     base_got = lax.ppermute(send, "x", X_NEAR)
-    got = swap(add(got_g, n_far), FAR)
-    got_g = swap(add(got, n_near), NEAR)
+    got_g, pa_rows, up, held = lax.optimization_barrier((got_g, pa_rows, up, held))
+    (mine,) = call(add_kernel, [shape((slab, rank), f32)], [VMEM], (got_g,))
+    other = lax.ppermute(mine, "core", CORES)
+    dims = (n_d, slab, rank)
+    (pay,) = call(
+        spread_kernel,
+        [shape(dims, bf16)],
+        [VMEM] * 2,
+        (mine, other),
+        out_specs=(HBM,),
+        scratch_shapes=[pltpu.VMEM(dims, bf16), pltpu.SemaphoreType.DMA],
+    )
+    got_g = swap(pay, SUMMED)
     (input_gradient,) = call(
         input_kernel,
         [shape((rows, width), bf16)],
         [SMEM] + [VMEM] * 5,
-        (place, four, other, up, down_w, frozen),
+        (place, four, far, up, down_w, frozen),
         flops=2 * rows * width * (cols * n_f + rank),
         scratch_shapes=[pltpu.VMEM((rows, cols * n_f), bf16)],
     )

time: 107 us -> 112 us (1.047)
  starting transfers between devices: 54.4 us -> 58.9 us
  local copies, waits for them, and re-layouts: 4.12 us -> 5.6 us
    all_to_all x5 -> x4, starting transfers between devices: 33.1 us -> 36.6 us  [swap(): return lax.all_to_all(v, axis, 0, 0, tiled=True)]
    all_to_all x5 -> x4, waiting for transfers between devices: 6.98 us -> 4.07 us  [swap(): return lax.all_to_all(v, axis, 0, 0, tiled=True)]
    ppermute x1 -> x2, starting transfers between devices: 3.06 us -> 5.13 us  [the longest x1 3.08 us: per_device(): far = lax.ppermute(four, 'x', X_FAR)]
    unnamed x20 -> x28, local copies, waits for them, and re-layouts: 3.45 us -> 4.93 us
    ppermute x1, waiting for transfers between devices: 0.75 us -> 2.07 us  [per_device(): base_got = lax.ppermute(send, 'zlo', Z_PAIRS)]
    ppermute x1, starting transfers between devices: 3.67 us -> 2.51 us  [per_device(): base_got = lax.ppermute(send, 'x', X_NEAR)]
    ppermute x1 -> x2, waiting for transfers between devices: 0.01 us -> 1.15 us  [the longest x1 1.14 us: per_device(): other = lax.ppermute(mine, 'core', CORES)]
    pallas_call x13 -> x14, Pallas kernels: 17.1 us -> 16.3 us  [call(): pl.pallas_call(kernel, grid=(1,), in_specs=[spec or block(a) for spec, a...]
  transfers between devices with their start and end apart: 11 -> 11, of which waited for: 5 -> 5; matrix products, arithmetic and copies ran while one was open for 1% -> 1% of each run, Pallas kernels for 11% -> 10%
where the time goes in v11:
time: 112 us; the launch traced here: 111 us
  starting transfers between devices  58.9 us (53%)
  blocking collectives  20.6 us (18%)
  Pallas kernels  16.3 us (15%)
  waiting for transfers between devices  8.48 us (8%)
  local copies, waits for them, and re-layouts  5.6 us (5%)
    all_to_all x4, starting transfers between devices, swap(): return lax.all_to_all(v, axis, 0, 0, tiled=True)  36.6 us
    all_to_all x2, blocking collectives, swap(): return lax.all_to_all(v, axis, 0, 0, tiled=True)  20.6 us
    pallas_call x14, Pallas kernels, call(): pl.pallas_call(kernel, grid=(1,), in_specs=[spec or block(a) for spec, a...  16.3 us
    ppermute x1, starting transfers between devices, per_device(): base_got = lax.ppermute(send, 'x', X_FAR)  5.13 us
    unnamed x28, local copies, waits for them, and re-layouts  4.93 us
    all_to_all x4, waiting for transfers between devices, swap(): return lax.all_to_all(v, axis, 0, 0, tiled=True)  4.07 us
    ppermute x1, starting transfers between devices, per_device(): other = lax.ppermute(gk, 'zlo', Z_PAIRS)  3.92 us
    ppermute x1, starting transfers between devices, per_device(): base_got = lax.ppermute(send, 'zlo', Z_PAIRS)  3.37 us
  transfers between devices with their start and end apart: 11, of which 5 were waited for; matrix products, arithmetic and copies ran while one was open for 1% of the time, Pallas kernels for 10%

profile of v11, /device:TPU:8, one launch (start us, length us, event | category | flops | bytes accessed | tf_op | source)
XLA Modules:
  0.0 110.9 jit_solution(15770240059147724567)
XLA Ops:
  0.7 3.2 %shard_map.111 = (bf16[512,128]{1,0:T(8,128)(2,1)}, bf16[1024,128]{1,0:T(8,128)(2,1)}, bf16[8,128,128]{2,1,0:T(8,128)(2,1)}) custom-call(s32[2]{0:T(128)} %lens.1, s32[2]{0:T(128)} %buckets.1, bf16[512,640]{1,0:T(8,128)(2,1)} %acts.3, bf16[512,128]{1,0:T(8,128)(2,1)} %og.1, f32[640,128]{1,0:T(8,128)} %down_w.7, f32[128,128]{1,0:T(8,128)} %up_w.3), custom_call_target="tpu_custom_call" | custom-call | flops 100663296 | bytes 1835024 | tf_op jit(solution)/shard_map/pallas_call | solution.py:59
  3.9 6.1 %all-to-all-start = ((bf16[8,128,128]{2,1,0:T(8,128)(2,1)}), bf16[8,128,128]{2,1,0:T(8,128)(2,1)S(1)}, u32[]{:S(2)}, u32[]{:S(2)}) async-start(bf16[8,128,128]{2,1,0:T(8,128)(2,1)} %get-tuple-element.32), calls=%async_computation | async-start | bytes 524288 | tf_op jit(solution)/shard_map/all_to_all | solution.py:41
  10.0 3.9 %collective-permute-start = (bf16[512,128]{1,0:T(8,128)(2,1)}, bf16[512,128]{1,0:T(8,128)(2,1)S(1)}, u32[]{:S(2)}, u32[]{:S(2)}) collective-permute-start(bf16[512,128]{1,0:T(8,128)(2,1)} %get-tuple-element.35.gk), channel_id=1, source_target_pairs={{0,2},{2,0},{1,3},{3,1},{4,6},{6,4},{5,7},{7,5},{8,10},{10,8},{9,1... | collective-permute-start | bytes 393224 | tf_op jit(solution)/shard_map/ppermute | solution.py:347
  14.0 1.1 copy-done.1
  15.1 1.8 %shard_map.112 = (bf16[512,128]{1,0:T(8,128)(2,1)S(1)}, bf16[2048,128]{1,0:T(8,128)(2,1)}) custom-call(s32[1]{0:T(128)} %bitcast.place, bf16[512,640]{1,0:T(8,128)(2,1)S(1)} %copy-done.1, bf16[640,1024]{1,0:T(8,128)(2,1)S(1)} %copy-done, f32[640,128]{1,0:T(8,128)S(1)} %copy-done.3), custom_call_target="tpu_custom_call" | custom-call | flops 419430400 | bytes 2949124 | tf_op jit(solution)/shard_map/pallas_call | solution.py:59
  16.8 1.2 %collective-permute-done = bf16[512,128]{1,0:T(8,128)(2,1)S(1)} collective-permute-done((bf16[512,128]{1,0:T(8,128)(2,1)}, bf16[512,128]{1,0:T(8,128)(2,1)S(1)}, u32[]{:S(2)}, u32[]{:S(2)}) %collective-permute-start) | collective-permute-done | bytes 131104 | tf_op jit(solution)/shard_map/ppermute | solution.py:347
  18.0 0.8 shard_map.113
  18.8 4.8 %all-to-all-start.1 = ((bf16[8,192,128]{2,1,0:T(8,128)(2,1)}), bf16[8,192,128]{2,1,0:T(8,128)(2,1)S(1)}, u32[]{:S(2)}, u32[]{:S(2)}) async-start(bf16[8,192,128]{2,1,0:T(8,128)(2,1)} %shard_map.113), calls=%async_computation.1 | async-start | bytes 786432 | tf_op jit(solution)/shard_map/all_to_all | solution.py:41
  23.6 5.1 %collective-permute-start.1 = (bf16[2048,128]{1,0:T(8,128)(2,1)}, bf16[2048,128]{1,0:T(8,128)(2,1)}, u32[]{:S(2)}, u32[]{:S(2)}) collective-permute-start(bf16[2048,128]{1,0:T(8,128)(2,1)} %get-tuple-element.43), channel_id=1, source_target_pairs={{0,12},{12,0},{4,8},{8,4},{1,13},{13,1},{5,9},{9,5},{2,14},{14,2},... | collective-permute-start | bytes 1572872 | tf_op jit(solution)/shard_map/ppermute | solution.py:368
  28.7 0.7 constant_dynamic-update-slice_fusion.two
  29.4 2.3 %collective-permute-start.3 = (bf16[1024,128]{1,0:T(8,128)(2,1)}, bf16[1024,128]{1,0:T(8,128)(2,1)}, u32[]{:S(2)}, u32[]{:S(2)}) collective-permute-start(bf16[1024,128]{1,0:T(8,128)(2,1)} %constant_dynamic-update-slice_fusion.two), channel_id=1, source_target_pairs={{0,4},{4,0},{8,12},{12,8},{1,5},{5,1},{9,13},{13,9},{2,6},{6,2},{1... | collective-permute-start | bytes 786440 | tf_op jit(solution)/shard_map/ppermute | solution.py:367
  32.1 0.7 copy-done.5
  32.7 15.3 %all-to-all-start.2 = ((bf16[32,24,128]{2,1,0:T(8,128)(2,1)}), bf16[32,24,128]{2,1,0:T(8,128)(2,1)S(1)}, u32[]{:S(2)}, u32[]{:S(2)}) async-start(bf16[32,24,128]{2,1,0:T(8,128)(2,1)} %copy-done.5), calls=%async_computation.2 | async-start | bytes 393216 | tf_op jit(solution)/shard_map/all_to_all | solution.py:41
  48.0 1.1 shard_map.119.near
  49.1 3.1 %collective-permute-start.4 = (bf16[2048,128]{1,0:T(8,128)(2,1)S(1)}, bf16[2048,128]{1,0:T(8,128)(2,1)}, u32[]{:S(2)}, u32[]{:S(2)}) collective-permute-start(bf16[2048,128]{1,0:T(8,128)(2,1)S(1)} %shard_map.119.near), channel_id=1, source_target_pairs={{0,12},{12,0},{4,8},{8,4},{1,13},{13,1},{5,9},{9,5},{2,14},{14,2},... | collective-permute-start | bytes 1572872 | tf_op jit(solution)/shard_map/ppermute | solution.py:386
  52.2 2.6 %shard_map.116 = (f32[1024,128]{1,0:T(8,128)S(1)}, bf16[1024,128]{1,0:T(8,128)(2,1)}) custom-call(s32[1]{0:T(128)} %bitcast.place, bf16[512,640]{1,0:T(8,128)(2,1)S(1)} %copy-done.2, bf16[640,1024]{1,0:T(8,128)(2,1)S(1)} %copy-done, bf16[2048,128]{1,0:T(8,128)(2,1)} %collective-permute-done.1.got), custom_call_target="tpu_custom_call" | custom-call | flops 335544320 | bytes 3276804 | tf_op jit(solution)/shard_map/pallas_call | solution.py:59
  54.8 0.8 copy-done.6
  55.6 2.5 %collective-permute-start.5 = (bf16[1024,128]{1,0:T(8,128)(2,1)}, bf16[1024,128]{1,0:T(8,128)(2,1)}, u32[]{:S(2)}, u32[]{:S(2)}) collective-permute-start(bf16[1024,128]{1,0:T(8,128)(2,1)} %get-tuple-element.49), channel_id=1, source_target_pairs={{0,4},{4,0},{8,12},{12,8},{1,5},{5,1},{9,13},{13,9},{2,6},{6,2},{1... | collective-permute-start | bytes 786440 | tf_op jit(solution)/shard_map/ppermute | solution.py:394
  58.8 1.8 %all-to-all-done.2.got_ref = bf16[32,24,128]{2,1,0:T(8,128)(2,1)S(1)} async-done(((bf16[32,24,128]{2,1,0:T(8,128)(2,1)}), bf16[32,24,128]{2,1,0:T(8,128)(2,1)S(1)}, u32[]{:S(2)}, u32[]{:S(2)}) %all-to-all-start.2) | async-done | bytes 196640 | tf_op jit(solution)/shard_map/all_to_all | solution.py:41
  60.7 2.1 %collective-permute-start.2 = (f32[24,128]{1,0:T(8,128)S(1)}, f32[24,128]{1,0:T(8,128)S(1)}, u32[]{:S(2)}, u32[]{:S(2)}) collective-permute-start(f32[24,128]{1,0:T(8,128)S(1)} %shard_map.117.mine), channel_id=1, source_target_pairs={{0,1},{1,0},{2,3},{3,2},{4,5},{5,4},{6,7},{7,6},{8,9},{9,8},{10,11... | collective-permute-start | bytes 36872 | tf_op jit(solution)/shard_map/ppermute | solution.py:397
  62.7 1.1 %collective-permute-done.2.got = f32[24,128]{1,0:T(8,128)S(1)} collective-permute-done((f32[24,128]{1,0:T(8,128)S(1)}, f32[24,128]{1,0:T(8,128)S(1)}, u32[]{:S(2)}, u32[]{:S(2)}) %collective-permute-start.2) | collective-permute-done | bytes 12320 | tf_op jit(solution)/shard_map/ppermute | solution.py:397
  63.9 0.7 shard_map.118
  64.6 10.4 %all-to-all-start.3 = ((bf16[32,24,128]{2,1,0:T(8,128)(2,1)}), bf16[32,24,128]{2,1,0:T(8,128)(2,1)S(1)}, u32[]{:S(2)}, u32[]{:S(2)}) async-start(bf16[32,24,128]{2,1,0:T(8,128)(2,1)} %shard_map.118), calls=%async_computation.3 | async-start | bytes 393216 | tf_op jit(solution)/shard_map/all_to_all | solution.py:41
  75.0 1.0 copy-done.7
  76.1 1.0 shard_map.121
  77.1 3.4 %collective-permute-start.6 = (bf16[512,128]{1,0:T(8,128)(2,1)S(1)}, bf16[512,128]{1,0:T(8,128)(2,1)S(1)}, u32[]{:S(2)}, u32[]{:S(2)}) collective-permute-start(bf16[512,128]{1,0:T(8,128)(2,1)S(1)} %get-tuple-element.51), channel_id=1, source_target_pairs={{0,2},{2,0},{1,3},{3,1},{4,6},{6,4},{5,7},{7,5},{8,10},{10,8},{9,1... | collective-permute-start | bytes 393224 | tf_op jit(solution)/shard_map/ppermute | solution.py:417
  80.5 3.3 %shard_map.120 = bf16[512,640]{1,0:T(8,128)(2,1)} custom-call(s32[1]{0:T(128)} %bitcast.place, bf16[2048,128]{1,0:T(8,128)(2,1)S(1)} %shard_map.119.near, bf16[2048,128]{1,0:T(8,128)(2,1)} %collective-permute-done.4.far, bf16[512,128]{1,0:T(8,128)(2,1)S(1)} %copy-done.10, f32[640,128]{1,0:T(8,128)S(1)} %copy-done.3, bf16[640,1024]{1,0:T(8,128)(2,1)S(1)} %copy-done), custom_call_target="tpu_custom_call" | custom-call | flops 754974720 | bytes 3473412 | tf_op jit(solution)/shard_map/pallas_call | solution.py:59
  83.7 2.1 %collective-permute-done.6.base_got = bf16[512,128]{1,0:T(8,128)(2,1)S(1)} collective-permute-done((bf16[512,128]{1,0:T(8,128)(2,1)S(1)}, bf16[512,128]{1,0:T(8,128)(2,1)S(1)}, u32[]{:S(2)}, u32[]{:S(2)}) %collective-permute-start.6) | collective-permute-done | bytes 131104 | tf_op jit(solution)/shard_map/ppermute | solution.py:417
  86.5 2.3 %all-to-all-done.3.got_ref.got_g = bf16[32,24,128]{2,1,0:T(8,128)(2,1)S(1)} async-done(((bf16[32,24,128]{2,1,0:T(8,128)(2,1)}), bf16[32,24,128]{2,1,0:T(8,128)(2,1)S(1)}, u32[]{:S(2)}, u32[]{:S(2)}) %all-to-all-start.3) | async-done | bytes 196640 | tf_op jit(solution)/shard_map/all_to_all | solution.py:41
  89.1 11.5 %all_to_all.30.got.sums = bf16[8,80,128]{2,1,0:T(8,128)(2,1)S(1)} all-to-all(bf16[8,80,128]{2,1,0:T(8,128)(2,1)S(1)} %shard_map.122), channel_id=1, replica_groups=mesh['zhi'=4,'y'=8,'x'=4,'zlo'=2,'core'=2] {'zlo','x'}, dimensions={0} | all-to-all | bytes 327680 | tf_op jit(solution)/shard_map/all_to_all | solution.py:41
  100.8 9.1 %all_to_all.31.got = bf16[8,64,128]{2,1,0:T(8,128)(2,1)S(1)} all-to-all(bf16[8,64,128]{2,1,0:T(8,128)(2,1)S(1)} %shard_map.123), channel_id=1, replica_groups=mesh['zhi'=4,'y'=8,'x'=4,'zlo'=2,'core'=2] {'zlo','x'}, dimensions={0} | all-to-all | bytes 262144 | tf_op jit(solution)/shard_map/all_to_all | solution.py:41
  109.9 1.0 shard_map.124
  (35 shorter events, 2.3 us)
Async XLA Ops:
  0.6 13.3 %copy-start.3 = (f32[640,128]{1,0:T(8,128)S(1)}, f32[640,128]{1,0:T(8,128)}, u32[]{:S(2)}) copy-start(f32[640,128]{1,0:T(8,128)} %down_w.7) | copy-start | bytes 983044
  0.6 13.3 %copy-start = (bf16[640,1024]{1,0:T(8,128)(2,1)S(1)}, bf16[640,1024]{1,0:T(8,128)(2,1)}, u32[]{:S(2)}) copy-start(bf16[640,1024]{1,0:T(8,128)(2,1)} %frozen.5) | copy-start | bytes 3932164
  3.9 14.1 %all-to-all-start = ((bf16[8,128,128]{2,1,0:T(8,128)(2,1)}), bf16[8,128,128]{2,1,0:T(8,128)(2,1)S(1)}, u32[]{:S(2)}, u32[]{:S(2)}) async-start(bf16[8,128,128]{2,1,0:T(8,128)(2,1)} %get-tuple-element.32), calls=%async_computation | async-start | bytes 524288 | tf_op jit(solution)/shard_map/all_to_all | solution.py:41
  10.0 8.0 %collective-permute-start = (bf16[512,128]{1,0:T(8,128)(2,1)}, bf16[512,128]{1,0:T(8,128)(2,1)S(1)}, u32[]{:S(2)}, u32[]{:S(2)}) collective-permute-start(bf16[512,128]{1,0:T(8,128)(2,1)} %get-tuple-element.35.gk), channel_id=1, source_target_pairs={{0,2},{2,0},{1,3},{3,1},{4,6},{6,4},{5,7},{7,5},{8,10},{10,8},{9,1... | collective-permute-start | bytes 393224 | tf_op jit(solution)/shard_map/ppermute | solution.py:347
  14.0 1.1 copy-start.1
  16.8 14.9 %copy-start.4 = (bf16[512,640]{1,0:T(8,128)(2,1)S(1)}, bf16[512,640]{1,0:T(8,128)(2,1)}, u32[]{:S(2)}) copy-start(bf16[512,640]{1,0:T(8,128)(2,1)} %acts.3) | copy-start | bytes 1966084
  16.8 14.9 %copy-start.13 = (bf16[512,128]{1,0:T(8,128)(2,1)S(1)}, bf16[512,128]{1,0:T(8,128)(2,1)}, u32[]{:S(2)}) copy-start(bf16[512,128]{1,0:T(8,128)(2,1)} %get-tuple-element.35.gk) | copy-start | bytes 393220
  18.8 12.9 %all-to-all-start.1 = ((bf16[8,192,128]{2,1,0:T(8,128)(2,1)}), bf16[8,192,128]{2,1,0:T(8,128)(2,1)S(1)}, u32[]{:S(2)}, u32[]{:S(2)}) async-start(bf16[8,192,128]{2,1,0:T(8,128)(2,1)} %shard_map.113), calls=%async_computation.1 | async-start | bytes 786432 | tf_op jit(solution)/shard_map/all_to_all | solution.py:41
  23.6 28.6 %collective-permute-start.1 = (bf16[2048,128]{1,0:T(8,128)(2,1)}, bf16[2048,128]{1,0:T(8,128)(2,1)}, u32[]{:S(2)}, u32[]{:S(2)}) collective-permute-start(bf16[2048,128]{1,0:T(8,128)(2,1)} %get-tuple-element.43), channel_id=1, source_target_pairs={{0,12},{12,0},{4,8},{8,4},{1,13},{13,1},{5,9},{9,5},{2,14},{14,2},... | collective-permute-start | bytes 1572872 | tf_op jit(solution)/shard_map/ppermute | solution.py:368
  29.4 22.8 %copy-start.2 = (bf16[512,640]{1,0:T(8,128)(2,1)S(1)}, bf16[512,640]{1,0:T(8,128)(2,1)}, u32[]{:S(2)}) copy-start(bf16[512,640]{1,0:T(8,128)(2,1)} %prompts.5) | copy-start | bytes 1966084
  29.4 18.6 %collective-permute-start.3 = (bf16[1024,128]{1,0:T(8,128)(2,1)}, bf16[1024,128]{1,0:T(8,128)(2,1)}, u32[]{:S(2)}, u32[]{:S(2)}) collective-permute-start(bf16[1024,128]{1,0:T(8,128)(2,1)} %constant_dynamic-update-slice_fusion.two), channel_id=1, source_target_pairs={{0,4},{4,0},{8,12},{12,8},{1,5},{5,1},{9,13},{13,9},{2,6},{6,2},{1... | collective-permute-start | bytes 786440 | tf_op jit(solution)/shard_map/ppermute | solution.py:367
  32.1 0.7 copy-start.5
  32.7 27.9 %all-to-all-start.2 = ((bf16[32,24,128]{2,1,0:T(8,128)(2,1)}), bf16[32,24,128]{2,1,0:T(8,128)(2,1)S(1)}, u32[]{:S(2)}, u32[]{:S(2)}) async-start(bf16[32,24,128]{2,1,0:T(8,128)(2,1)} %copy-done.5), calls=%async_computation.2 | async-start | bytes 393216 | tf_op jit(solution)/shard_map/all_to_all | solution.py:41
  49.1 31.3 %collective-permute-start.4 = (bf16[2048,128]{1,0:T(8,128)(2,1)S(1)}, bf16[2048,128]{1,0:T(8,128)(2,1)}, u32[]{:S(2)}, u32[]{:S(2)}) collective-permute-start(bf16[2048,128]{1,0:T(8,128)(2,1)S(1)} %shard_map.119.near), channel_id=1, source_target_pairs={{0,12},{12,0},{4,8},{8,4},{1,13},{13,1},{5,9},{9,5},{2,14},{14,2},... | collective-permute-start | bytes 1572872 | tf_op jit(solution)/shard_map/ppermute | solution.py:386
  54.8 0.8 copy-start.6
  55.6 19.4 %collective-permute-start.5 = (bf16[1024,128]{1,0:T(8,128)(2,1)}, bf16[1024,128]{1,0:T(8,128)(2,1)}, u32[]{:S(2)}, u32[]{:S(2)}) collective-permute-start(bf16[1024,128]{1,0:T(8,128)(2,1)} %get-tuple-element.49), channel_id=1, source_target_pairs={{0,4},{4,0},{8,12},{12,8},{1,5},{5,1},{9,13},{13,9},{2,6},{6,2},{1... | collective-permute-start | bytes 786440 | tf_op jit(solution)/shard_map/ppermute | solution.py:394
  58.2 0.7 copy-start.9
  60.6 19.8 %copy-start.10 = (bf16[512,128]{1,0:T(8,128)(2,1)S(1)}, bf16[512,128]{1,0:T(8,128)(2,1)}, u32[]{:S(2)}) copy-start(bf16[512,128]{1,0:T(8,128)(2,1)} %copy-done.9) | copy-start | bytes 393220
  60.7 3.2 %collective-permute-start.2 = (f32[24,128]{1,0:T(8,128)S(1)}, f32[24,128]{1,0:T(8,128)S(1)}, u32[]{:S(2)}, u32[]{:S(2)}) collective-permute-start(f32[24,128]{1,0:T(8,128)S(1)} %shard_map.117.mine), channel_id=1, source_target_pairs={{0,1},{1,0},{2,3},{3,2},{4,5},{5,4},{6,7},{7,6},{8,9},{9,8},{10,11... | collective-permute-start | bytes 36872 | tf_op jit(solution)/shard_map/ppermute | solution.py:397
  64.6 24.1 %all-to-all-start.3 = ((bf16[32,24,128]{2,1,0:T(8,128)(2,1)}), bf16[32,24,128]{2,1,0:T(8,128)(2,1)S(1)}, u32[]{:S(2)}, u32[]{:S(2)}) async-start(bf16[32,24,128]{2,1,0:T(8,128)(2,1)} %shard_map.118), calls=%async_computation.3 | async-start | bytes 393216 | tf_op jit(solution)/shard_map/all_to_all | solution.py:41
  75.0 1.0 copy-start.7
  77.1 8.7 %collective-permute-start.6 = (bf16[512,128]{1,0:T(8,128)(2,1)S(1)}, bf16[512,128]{1,0:T(8,128)(2,1)S(1)}, u32[]{:S(2)}, u32[]{:S(2)}) collective-permute-start(bf16[512,128]{1,0:T(8,128)(2,1)S(1)} %get-tuple-element.51), channel_id=1, source_target_pairs={{0,2},{2,0},{1,3},{3,1},{4,6},{6,4},{5,7},{7,5},{8,10},{10,8},{9,1... | collective-permute-start | bytes 393224 | tf_op jit(solution)/shard_map/ppermute | solution.py:417
  83.7 26.1 %copy-start.8 = (f32[128,128]{1,0:T(8,128)S(1)}, f32[128,128]{1,0:T(8,128)}, u32[]{:S(2)}) copy-start(f32[128,128]{1,0:T(8,128)} %up_w.3) | copy-start | bytes 196612
  85.8 0.7 copy-start.11
  88.7 21.1 %copy-start.12 = (bf16[512,128]{1,0:T(8,128)(2,1)S(1)}, bf16[512,128]{1,0:T(8,128)(2,1)}, u32[]{:S(2)}) copy-start(bf16[512,128]{1,0:T(8,128)(2,1)} %copy-done.11) | copy-start | bytes 393220

commit v12 on v10

--- a/solution.py
+++ b/solution.py
@@ -74,14 +74,17 @@
 
 def parts_kernel(
     lens, buckets, acts, og, down_w, up_w, gk_out, two_out, pay,
-    acts_v, og_v, down_v, up_v, gk, parts, sems,
+    acts_v, og_v, down_v, up_v, gk, ups, downs, sems,
 ):
     rows = acts.shape[0]
     seqs = lens.shape[0]
     slot = rows // seqs
     peers = pay.shape[0]
     piece = rows // peers
-    pairs = ((og, og_v), (up_w, up_v), (down_w, down_v), (acts, acts_v))
+    half = rows // 2
+    pairs = [(og, og_v), (up_w, up_v), (down_w, down_v)] + [
+        (acts.at[pl.ds(h * half, half), :], acts_v.at[pl.ds(h * half, half), :]) for h in range(2)
+    ]
     loads = [pltpu.make_async_copy(a, b, sems.at[i]) for i, (a, b) in enumerate(pairs)]
     for c in loads:
         c.start()
@@ -99,22 +102,29 @@
     for c in stores:
         c.start()
 
-    def put(k, v):
-        v = v.astype(bf16)
-        for j in range(peers):
-            parts[j, k * piece : (k + 1) * piece, :] = v[j * piece : (j + 1) * piece]
-
     loads[1].wait()
-    put(0, dot(gk[...], up_v[...].astype(bf16), NT))
+    up = dot(gk[...], up_v[...].astype(bf16), NT).astype(bf16)
+    for j in range(peers):
+        ups[j] = up[j * piece : (j + 1) * piece]
+    stores.append(pltpu.make_async_copy(ups, pay.at[:, pl.ds(0, piece), :], sems.at[first + 2]))
+    stores[-1].start()
     loads[2].wait()
     a_half = down_v[...].astype(bf16)
-    loads[3].wait()
-    put(1, dot(acts_v[...], a_half))
-    last = pltpu.make_async_copy(parts, pay, sems.at[first + 2])
-    last.start()
+    count = peers // 2
+    for h in range(2):
+        loads[3 + h].wait()
+        down = dot(acts_v[h * half : (h + 1) * half, :], a_half).astype(bf16)
+        for j in range(count):
+            downs[h * count + j] = down[j * piece : (j + 1) * piece]
+        mine = pl.ds(h * count, count)
+        stores.append(
+            pltpu.make_async_copy(
+                downs.at[mine], pay.at[mine, pl.ds(piece, piece), :], sems.at[first + 3 + h]
+            )
+        )
+        stores[-1].start()
     for c in stores:
         c.wait()
-    last.wait()
 
 
 def base_part(place, prompts, frozen, i, cols):
@@ -146,16 +156,34 @@
             send[(i - count) * rows : (i - count + 1) * rows, :] = part.astype(bf16)
 
 
-def halve_kernel(held, got, keep, send):
+def halve_kernel(held, got, keep, send, held_v, got_v, sems):
+    loads = [
+        pltpu.make_async_copy(held, held_v, sems.at[0]),
+        pltpu.make_async_copy(got, got_v, sems.at[1]),
+    ]
+    for c in loads:
+        c.start()
+    for c in loads:
+        c.wait()
     half = keep.shape[0]
-    keep[...] = held[:half, :] + got[:half, :].astype(f32)
-    send[...] = (held[half:, :] + got[half:, :].astype(f32)).astype(bf16)
+    keep[...] = held_v[:half, :] + got_v[:half, :].astype(f32)
+    send[...] = (held_v[half:, :] + got_v[half:, :].astype(f32)).astype(bf16)
 
 
 def halve(held, got):
-    half = held.shape[0] // 2
-    dims = (half, held.shape[1])
-    return call(halve_kernel, [shape(dims, f32), shape(dims, bf16)], [VMEM] * 2, (held, got))
+    dims = (held.shape[0] // 2, held.shape[1])
+    return call(
+        halve_kernel,
+        [shape(dims, f32), shape(dims, bf16)],
+        [HBM] * 2,
+        (held, got),
+        limit=60,
+        scratch_shapes=[
+            pltpu.VMEM(held.shape, f32),
+            pltpu.VMEM(got.shape, bf16),
+            pltpu.SemaphoreType.DMA((2,)),
+        ],
+    )
 
 
 def sums_kernel(got_ref, proj, pay, pay_v, sem):
@@ -283,20 +311,31 @@
         pay[j] = rows
 
 
-def finish_kernel(got, sums, base, base_got, got_g, down_w, up_w, next_down, next_up, keys):
+def finish_kernel(
+    got, sums, base, base_got, got_g, down_w, up_w, next_down, next_up, keys,
+    down_v, up_v, keys_v, sems,
+):
     rank = down_w.shape[1]
     factor = step_factor(sums)
     blocks = whole_gradient(got_g, rank)
     new_up = up_w[...] - factor * blocks[-1]
-    next_up[...] = new_up
-    keys[...] = (
+    up_v[...] = new_up
+    copies = [pltpu.make_async_copy(up_v, next_up, sems.at[0])]
+    copies[-1].start()
+    for c, part in enumerate(blocks[:-1]):
+        here = pl.ds(c * rank, rank)
+        down_v[here, :] = down_w[here, :] - factor * part.T
+        copies.append(pltpu.make_async_copy(down_v.at[here], next_down.at[here], sems.at[2 + c]))
+        copies[-1].start()
+    keys_v[...] = (
         base[...]
         + base_got[...].astype(f32)
         + adapter_scale * dot(rejoin(got, 0, got.shape[1]), new_up.astype(bf16))
     ).astype(bf16)
-    for c, part in enumerate(blocks[:-1]):
-        here = pl.ds(c * rank, rank)
-        next_down[here, :] = down_w[here, :] - factor * part.T
+    copies.append(pltpu.make_async_copy(keys_v, keys, sems.at[1]))
+    copies[-1].start()
+    for c in copies:
+        c.wait()
 
 
 def input_kernel(place, near, far, up, down_w, frozen, out, gk):
@@ -351,8 +390,9 @@
             pltpu.VMEM((width, rank), f32),
             pltpu.VMEM((rank, cols), f32),
             pltpu.VMEM((rows, cols), bf16),
-            pltpu.VMEM((n_f, 2 * piece, rank), bf16),
-            pltpu.SemaphoreType.DMA((7,)),
+            pltpu.VMEM((n_f, piece, rank), bf16),
+            pltpu.VMEM((n_f, piece, rank), bf16),
+            pltpu.SemaphoreType.DMA((10,)),
         ],
     )
     got = swap(pay, PEERS)
@@ -377,6 +417,7 @@
     got = swap(pay, PEERS)
     two = lax.dynamic_update_slice(two, other, (rows, 0))
     other = lax.ppermute(two, "x", X_NEAR)
+    _, send = lax.optimization_barrier((two, send))
     base_got = lax.ppermute(send, "x", X_FAR)
     got, two = lax.optimization_barrier((got, two))
 
@@ -443,6 +484,13 @@
         [VMEM] * 7,
         (got, sums, base, base_got, got_g, down_w, up_w),
         flops=2 * rows * rank * cols,
+        out_specs=(HBM, HBM, HBM),
+        scratch_shapes=[
+            pltpu.VMEM((width, rank), f32),
+            pltpu.VMEM((rank, cols), f32),
+            pltpu.VMEM((rows, cols), bf16),
+            pltpu.SemaphoreType.DMA((2 + width // rank,)),
+        ],
     )
     return input_gradient, next_down, next_up, keys
 

time: 107 us -> 106 us (level)
  transfers between devices with their start and end apart: 11 -> 11, of which waited for: 5 -> 4; matrix products, arithmetic and copies ran while one was open for 1% -> 1% of each run, Pallas kernels for 11% -> 11%
where the time goes in v12:
time: 106 us; the launch traced here: 105 us
  starting transfers between devices  53.8 us (51%)
  blocking collectives  20.4 us (19%)
  Pallas kernels  17.3 us (16%)
  waiting for transfers between devices  9.52 us (9%)
  local copies, waits for them, and re-layouts  3.35 us (3%)
    all_to_all x5, starting transfers between devices, swap(): return lax.all_to_all(v, axis, 0, 0, tiled=True)  32.4 us
    all_to_all x2, blocking collectives, swap(): return lax.all_to_all(v, axis, 0, 0, tiled=True)  20.4 us
    pallas_call x13, Pallas kernels, call(): pl.pallas_call(kernel, grid=(1,), in_specs=[spec or block(a) for spec, a...  17.3 us
    all_to_all x5, waiting for transfers between devices, swap(): return lax.all_to_all(v, axis, 0, 0, tiled=True)  7.27 us
    ppermute x1, starting transfers between devices, per_device(): base_got = lax.ppermute(send, 'x', X_FAR)  5.26 us
    ppermute x1, starting transfers between devices, per_device(): other = lax.ppermute(gk, 'zlo', Z_PAIRS)  3.92 us
    ppermute x1, starting transfers between devices, per_device(): base_got = lax.ppermute(send, 'x', X_NEAR)  3.67 us
    ppermute x1, starting transfers between devices, per_device(): base_got = lax.ppermute(send, 'zlo', Z_PAIRS)  3.24 us
  transfers between devices with their start and end apart: 11, of which 4 were waited for; matrix products, arithmetic and copies ran while one was open for 1% of the time, Pallas kernels for 11%

profile of v12, /device:TPU:8, one launch (start us, length us, event | category | flops | bytes accessed | tf_op | source)
XLA Modules:
  0.0 105.2 jit_solution(13701710543443533883)
XLA Ops:
  0.7 3.2 %shard_map.111 = (bf16[512,128]{1,0:T(8,128)(2,1)}, bf16[1024,128]{1,0:T(8,128)(2,1)}, bf16[8,128,128]{2,1,0:T(8,128)(2,1)}) custom-call(s32[2]{0:T(128)} %lens.1, s32[2]{0:T(128)} %buckets.1, bf16[512,640]{1,0:T(8,128)(2,1)} %acts.3, bf16[512,128]{1,0:T(8,128)(2,1)} %og.1, f32[640,128]{1,0:T(8,128)} %down_w.7, f32[128,128]{1,0:T(8,128)} %up_w.3), custom_call_target="tpu_custom_call" | custom-call | flops 100663296 | bytes 1835024 | tf_op jit(solution)/shard_map/pallas_call | solution.py:59
  3.9 6.1 %all-to-all-start = ((bf16[8,128,128]{2,1,0:T(8,128)(2,1)}), bf16[8,128,128]{2,1,0:T(8,128)(2,1)S(1)}, u32[]{:S(2)}, u32[]{:S(2)}) async-start(bf16[8,128,128]{2,1,0:T(8,128)(2,1)} %get-tuple-element.35), calls=%async_computation | async-start | bytes 524288 | tf_op jit(solution)/shard_map/all_to_all | solution.py:41
  10.0 3.9 %collective-permute-start = (bf16[512,128]{1,0:T(8,128)(2,1)}, bf16[512,128]{1,0:T(8,128)(2,1)S(1)}, u32[]{:S(2)}, u32[]{:S(2)}) collective-permute-start(bf16[512,128]{1,0:T(8,128)(2,1)} %get-tuple-element.38.gk), channel_id=1, source_target_pairs={{0,2},{2,0},{1,3},{3,1},{4,6},{6,4},{5,7},{7,5},{8,10},{10,8},{9,1... | collective-permute-start | bytes 393224 | tf_op jit(solution)/shard_map/ppermute | solution.py:399
  14.0 1.1 %copy-done.1 = bf16[512,640]{1,0:T(8,128)(2,1)S(1)} copy-done((bf16[512,640]{1,0:T(8,128)(2,1)S(1)}, bf16[512,640]{1,0:T(8,128)(2,1)}, u32[]{:S(2)}) %copy-start.1) | copy-done | bytes 655384
  15.1 1.0 shard_map.112
  16.1 0.8 copy-done.9
  16.9 1.1 %collective-permute-done = bf16[512,128]{1,0:T(8,128)(2,1)S(1)} collective-permute-done((bf16[512,128]{1,0:T(8,128)(2,1)}, bf16[512,128]{1,0:T(8,128)(2,1)S(1)}, u32[]{:S(2)}, u32[]{:S(2)}) %collective-permute-start) | collective-permute-done | bytes 131104 | tf_op jit(solution)/shard_map/ppermute | solution.py:399
  18.0 0.8 shard_map.113
  18.8 4.8 %all-to-all-start.1 = ((bf16[8,192,128]{2,1,0:T(8,128)(2,1)}), bf16[8,192,128]{2,1,0:T(8,128)(2,1)S(1)}, u32[]{:S(2)}, u32[]{:S(2)}) async-start(bf16[8,192,128]{2,1,0:T(8,128)(2,1)} %shard_map.113), calls=%async_computation.1 | async-start | bytes 786432 | tf_op jit(solution)/shard_map/all_to_all | solution.py:41
  23.6 0.7 constant_dynamic-update-slice_fusion.two
  24.3 5.3 %collective-permute-start.2 = (bf16[2048,128]{1,0:T(8,128)(2,1)}, bf16[2048,128]{1,0:T(8,128)(2,1)}, u32[]{:S(2)}, u32[]{:S(2)}) collective-permute-start(bf16[2048,128]{1,0:T(8,128)(2,1)} %copy-done.9), channel_id=1, source_target_pairs={{0,12},{12,0},{4,8},{8,4},{1,13},{13,1},{5,9},{9,5},{2,14},{14,2},... | collective-permute-start | bytes 1572872 | tf_op jit(solution)/shard_map/ppermute | solution.py:421
  29.6 2.2 %collective-permute-start.1 = (bf16[1024,128]{1,0:T(8,128)(2,1)}, bf16[1024,128]{1,0:T(8,128)(2,1)}, u32[]{:S(2)}, u32[]{:S(2)}) collective-permute-start(bf16[1024,128]{1,0:T(8,128)(2,1)} %constant_dynamic-update-slice_fusion.two), channel_id=1, source_target_pairs={{0,4},{4,0},{8,12},{12,8},{1,5},{5,1},{9,13},{13,9},{2,6},{6,2},{1... | collective-permute-start | bytes 786440 | tf_op jit(solution)/shard_map/ppermute | solution.py:419
  31.8 1.0 shard_map.114
  32.8 7.6 %all-to-all-start.2 = ((bf16[16,48,128]{2,1,0:T(8,128)(2,1)}), bf16[16,48,128]{2,1,0:T(8,128)(2,1)S(1)}, u32[]{:S(2)}, u32[]{:S(2)}) async-start(bf16[16,48,128]{2,1,0:T(8,128)(2,1)} %shard_map.114), calls=%async_computation.2 | async-start | bytes 393216 | tf_op jit(solution)/shard_map/all_to_all | solution.py:41
  40.4 1.1 %shard_map.115 = (bf16[64,128]{1,0:T(8,128)(2,1)S(1)}, bf16[512,128]{1,0:T(8,128)(2,1)S(1)}, bf16[2048,128]{1,0:T(8,128)(2,1)S(1)}) custom-call(bf16[8,192,128]{2,1,0:T(8,128)(2,1)S(1)} %all-to-all-done.1.got_ref.got, bf16[1024,128]{1,0:T(8,128)(2,1)} %constant_dynamic-update-slice_fusion.two, bf16[1024,128]{1,0:T(8,128)(2,1)} %collective-permute-done.1.other), custom_call_target="tpu_custom_call" | custom-call | bytes 1589248 | tf_op jit(solution)/shard_map/pallas_call | solution.py:59
  41.5 3.1 %collective-permute-start.3 = (bf16[2048,128]{1,0:T(8,128)(2,1)S(1)}, bf16[2048,128]{1,0:T(8,128)(2,1)}, u32[]{:S(2)}, u32[]{:S(2)}) collective-permute-start(bf16[2048,128]{1,0:T(8,128)(2,1)S(1)} %get-tuple-element.52.near), channel_id=1, source_target_pairs={{0,12},{12,0},{4,8},{8,4},{1,13},{13,1},{5,9},{9,5},{2,14},{14,2},... | collective-permute-start | bytes 1572872 | tf_op jit(solution)/shard_map/ppermute | solution.py:444
  44.6 1.9 %shard_map.116 = (f32[1024,128]{1,0:T(8,128)S(1)}, bf16[1024,128]{1,0:T(8,128)(2,1)S(1)}) custom-call(s32[1]{0:T(128)} %bitcast.place, bf16[512,640]{1,0:T(8,128)(2,1)S(1)} %copy-done.2, bf16[640,1024]{1,0:T(8,128)(2,1)S(1)} %copy-done, bf16[2048,128]{1,0:T(8,128)(2,1)} %collective-permute-done.2.got), custom_call_target="tpu_custom_call" | custom-call | flops 335544320 | bytes 3276804 | tf_op jit(solution)/shard_map/pallas_call | solution.py:59
  46.5 0.8 copy-done.5
  47.3 2.7 %all-to-all-done.2.got_ref = bf16[16,48,128]{2,1,0:T(8,128)(2,1)S(1)} async-done(((bf16[16,48,128]{2,1,0:T(8,128)(2,1)}), bf16[16,48,128]{2,1,0:T(8,128)(2,1)S(1)}, u32[]{:S(2)}, u32[]{:S(2)}) %all-to-all-start.2) | async-done | bytes 196640 | tf_op jit(solution)/shard_map/all_to_all | solution.py:41
  50.0 0.7 shard_map.117
  50.6 9.4 %all-to-all-start.3 = ((bf16[4,48,128]{2,1,0:T(8,128)(2,1)}), bf16[4,48,128]{2,1,0:T(8,128)(2,1)S(1)}, u32[]{:S(2)}, u32[]{:S(2)}) async-start(bf16[4,48,128]{2,1,0:T(8,128)(2,1)} %shard_map.117), calls=%async_computation.3 | async-start | bytes 98304 | tf_op jit(solution)/shard_map/all_to_all | solution.py:41
  60.1 3.7 %collective-permute-start.4 = (bf16[1024,128]{1,0:T(8,128)(2,1)S(1)}, bf16[1024,128]{1,0:T(8,128)(2,1)}, u32[]{:S(2)}, u32[]{:S(2)}) collective-permute-start(bf16[1024,128]{1,0:T(8,128)(2,1)S(1)} %get-tuple-element.55), channel_id=1, source_target_pairs={{0,4},{4,0},{8,12},{12,8},{1,5},{5,1},{9,13},{13,9},{2,6},{6,2},{1... | collective-permute-start | bytes 786440 | tf_op jit(solution)/shard_map/ppermute | solution.py:453
  63.7 4.5 %all-to-all-done.3.got_ref = bf16[4,48,128]{2,1,0:T(8,128)(2,1)S(1)} async-done(((bf16[4,48,128]{2,1,0:T(8,128)(2,1)}), bf16[4,48,128]{2,1,0:T(8,128)(2,1)S(1)}, u32[]{:S(2)}, u32[]{:S(2)}) %all-to-all-start.3) | async-done | bytes 49184 | tf_op jit(solution)/shard_map/all_to_all | solution.py:41
  68.3 0.8 shard_map.118
  69.1 4.5 %all-to-all-start.4 = ((bf16[16,48,128]{2,1,0:T(8,128)(2,1)}), bf16[16,48,128]{2,1,0:T(8,128)(2,1)S(1)}, u32[]{:S(2)}, u32[]{:S(2)}) async-start(bf16[16,48,128]{2,1,0:T(8,128)(2,1)} %shard_map.118), calls=%async_computation.4 | async-start | bytes 393216 | tf_op jit(solution)/shard_map/all_to_all | solution.py:41
  73.7 1.9 %shard_map.120 = (f32[512,128]{1,0:T(8,128)}, bf16[512,128]{1,0:T(8,128)(2,1)}) custom-call(f32[1024,128]{1,0:T(8,128)} %copy-done.5, bf16[1024,128]{1,0:T(8,128)(2,1)} %collective-permute-done.4.got), custom_call_target="tpu_custom_call" | custom-call | bytes 1179648 | tf_op jit(solution)/shard_map/pallas_call | solution.py:59
  75.6 3.2 %collective-permute-start.5 = (bf16[512,128]{1,0:T(8,128)(2,1)}, bf16[512,128]{1,0:T(8,128)(2,1)S(1)}, u32[]{:S(2)}, u32[]{:S(2)}) collective-permute-start(bf16[512,128]{1,0:T(8,128)(2,1)} %get-tuple-element.57), channel_id=1, source_target_pairs={{0,2},{2,0},{1,3},{3,1},{4,6},{6,4},{5,7},{7,5},{8,10},{10,8},{9,1... | collective-permute-start | bytes 393224 | tf_op jit(solution)/shard_map/ppermute | solution.py:465
  78.8 3.3 %shard_map.119 = bf16[512,640]{1,0:T(8,128)(2,1)} custom-call(s32[1]{0:T(128)} %bitcast.place, bf16[2048,128]{1,0:T(8,128)(2,1)S(1)} %get-tuple-element.52.near, bf16[2048,128]{1,0:T(8,128)(2,1)} %collective-permute-done.3.far, bf16[512,128]{1,0:T(8,128)(2,1)S(1)} %get-tuple-element.53.up, f32[640,128]{1,0:T(8,128)S(1)} %copy-done.3, ...), custom_call_target="tpu_custom_call" | custom-call | flops 754974720 | bytes 3473412 | tf_op jit(solution)/shard_map/pallas_call | solution.py:59
  82.1 1.1 %collective-permute-done.5.base_got = bf16[512,128]{1,0:T(8,128)(2,1)S(1)} collective-permute-done((bf16[512,128]{1,0:T(8,128)(2,1)}, bf16[512,128]{1,0:T(8,128)(2,1)S(1)}, u32[]{:S(2)}, u32[]{:S(2)}) %collective-permute-start.5) | collective-permute-done | bytes 131104 | tf_op jit(solution)/shard_map/ppermute | solution.py:465
  83.6 11.3 %all_to_all.35.got.sums = bf16[8,80,128]{2,1,0:T(8,128)(2,1)S(1)} all-to-all(bf16[8,80,128]{2,1,0:T(8,128)(2,1)S(1)} %shard_map.121), channel_id=1, replica_groups=mesh['zhi'=4,'y'=8,'x'=4,'zlo'=2,'core'=2] {'zlo','x'}, dimensions={0} | all-to-all | bytes 327680 | tf_op jit(solution)/shard_map/all_to_all | solution.py:41
  95.0 9.1 %all_to_all.36.got = bf16[8,64,128]{2,1,0:T(8,128)(2,1)S(1)} all-to-all(bf16[8,64,128]{2,1,0:T(8,128)(2,1)S(1)} %shard_map.122), channel_id=1, replica_groups=mesh['zhi'=4,'y'=8,'x'=4,'zlo'=2,'core'=2] {'zlo','x'}, dimensions={0} | all-to-all | bytes 262144 | tf_op jit(solution)/shard_map/all_to_all | solution.py:41
  104.1 1.1 %shard_map.123 = (f32[640,128]{1,0:T(8,128)}, f32[128,128]{1,0:T(8,128)}, bf16[512,128]{1,0:T(8,128)(2,1)}) custom-call(bf16[8,64,128]{2,1,0:T(8,128)(2,1)S(1)} %all_to_all.36.got, bf16[8,80,128]{2,1,0:T(8,128)(2,1)S(1)} %all_to_all.35.got.sums, f32[512,128]{1,0:T(8,128)S(1)} %copy-done.6, bf16[512,128]{1,0:T(8,128)(2,1)S(1)} %collective-permute-done.5.base_got, ...), custom_call_target="tpu_custom_call" | custom-call | flops 16777216 | bytes 1802240 | tf_op jit(solution)/shard_map/pallas_call | solution.py:59
  (26 shorter events, 0.6 us)
Async XLA Ops:
  0.6 13.3 %copy-start.3 = (f32[640,128]{1,0:T(8,128)S(1)}, f32[640,128]{1,0:T(8,128)}, u32[]{:S(2)}) copy-start(f32[640,128]{1,0:T(8,128)} %down_w.7) | copy-start | bytes 983044
  0.6 13.3 %copy-start = (bf16[640,1024]{1,0:T(8,128)(2,1)S(1)}, bf16[640,1024]{1,0:T(8,128)(2,1)}, u32[]{:S(2)}) copy-start(bf16[640,1024]{1,0:T(8,128)(2,1)} %frozen.5) | copy-start | bytes 3932164
  3.9 14.1 %all-to-all-start = ((bf16[8,128,128]{2,1,0:T(8,128)(2,1)}), bf16[8,128,128]{2,1,0:T(8,128)(2,1)S(1)}, u32[]{:S(2)}, u32[]{:S(2)}) async-start(bf16[8,128,128]{2,1,0:T(8,128)(2,1)} %get-tuple-element.35), calls=%async_computation | async-start | bytes 524288 | tf_op jit(solution)/shard_map/all_to_all | solution.py:41
  10.0 8.0 %collective-permute-start = (bf16[512,128]{1,0:T(8,128)(2,1)}, bf16[512,128]{1,0:T(8,128)(2,1)S(1)}, u32[]{:S(2)}, u32[]{:S(2)}) collective-permute-start(bf16[512,128]{1,0:T(8,128)(2,1)} %get-tuple-element.38.gk), channel_id=1, source_target_pairs={{0,2},{2,0},{1,3},{3,1},{4,6},{6,4},{5,7},{7,5},{8,10},{10,8},{9,1... | collective-permute-start | bytes 393224 | tf_op jit(solution)/shard_map/ppermute | solution.py:399
  14.0 1.1 %copy-start.1 = (bf16[512,640]{1,0:T(8,128)(2,1)S(1)}, bf16[512,640]{1,0:T(8,128)(2,1)}, u32[]{:S(2)}) copy-start(bf16[512,640]{1,0:T(8,128)(2,1)} %prompts.5) | copy-start | bytes 1966084
  16.1 0.8 copy-start.9
  16.9 14.9 %copy-start.4 = (bf16[512,640]{1,0:T(8,128)(2,1)S(1)}, bf16[512,640]{1,0:T(8,128)(2,1)}, u32[]{:S(2)}) copy-start(bf16[512,640]{1,0:T(8,128)(2,1)} %acts.3) | copy-start | bytes 1966084
  16.9 14.9 %copy-start.8 = (bf16[512,128]{1,0:T(8,128)(2,1)S(1)}, bf16[512,128]{1,0:T(8,128)(2,1)}, u32[]{:S(2)}) copy-start(bf16[512,128]{1,0:T(8,128)(2,1)} %get-tuple-element.38.gk) | copy-start | bytes 393220
  18.8 12.9 %all-to-all-start.1 = ((bf16[8,192,128]{2,1,0:T(8,128)(2,1)}), bf16[8,192,128]{2,1,0:T(8,128)(2,1)S(1)}, u32[]{:S(2)}, u32[]{:S(2)}) async-start(bf16[8,192,128]{2,1,0:T(8,128)(2,1)} %shard_map.113), calls=%async_computation.1 | async-start | bytes 786432 | tf_op jit(solution)/shard_map/all_to_all | solution.py:41
  24.3 20.3 %copy-start.2 = (bf16[512,640]{1,0:T(8,128)(2,1)S(1)}, bf16[512,640]{1,0:T(8,128)(2,1)}, u32[]{:S(2)}) copy-start(bf16[512,640]{1,0:T(8,128)(2,1)} %prompts.5) | copy-start | bytes 1966084
  24.3 20.3 %collective-permute-start.2 = (bf16[2048,128]{1,0:T(8,128)(2,1)}, bf16[2048,128]{1,0:T(8,128)(2,1)}, u32[]{:S(2)}, u32[]{:S(2)}) collective-permute-start(bf16[2048,128]{1,0:T(8,128)(2,1)} %copy-done.9), channel_id=1, source_target_pairs={{0,12},{12,0},{4,8},{8,4},{1,13},{13,1},{5,9},{9,5},{2,14},{14,2},... | collective-permute-start | bytes 1572872 | tf_op jit(solution)/shard_map/ppermute | solution.py:421
  29.6 10.8 %collective-permute-start.1 = (bf16[1024,128]{1,0:T(8,128)(2,1)}, bf16[1024,128]{1,0:T(8,128)(2,1)}, u32[]{:S(2)}, u32[]{:S(2)}) collective-permute-start(bf16[1024,128]{1,0:T(8,128)(2,1)} %constant_dynamic-update-slice_fusion.two), channel_id=1, source_target_pairs={{0,4},{4,0},{8,12},{12,8},{1,5},{5,1},{9,13},{13,9},{2,6},{6,2},{1... | collective-permute-start | bytes 786440 | tf_op jit(solution)/shard_map/ppermute | solution.py:419
  32.8 17.2 %all-to-all-start.2 = ((bf16[16,48,128]{2,1,0:T(8,128)(2,1)}), bf16[16,48,128]{2,1,0:T(8,128)(2,1)S(1)}, u32[]{:S(2)}, u32[]{:S(2)}) async-start(bf16[16,48,128]{2,1,0:T(8,128)(2,1)} %shard_map.114), calls=%async_computation.2 | async-start | bytes 393216 | tf_op jit(solution)/shard_map/all_to_all | solution.py:41
  41.5 37.3 %collective-permute-start.3 = (bf16[2048,128]{1,0:T(8,128)(2,1)S(1)}, bf16[2048,128]{1,0:T(8,128)(2,1)}, u32[]{:S(2)}, u32[]{:S(2)}) collective-permute-start(bf16[2048,128]{1,0:T(8,128)(2,1)S(1)} %get-tuple-element.52.near), channel_id=1, source_target_pairs={{0,12},{12,0},{4,8},{8,4},{1,13},{13,1},{5,9},{9,5},{2,14},{14,2},... | collective-permute-start | bytes 1572872 | tf_op jit(solution)/shard_map/ppermute | solution.py:444
  46.5 0.8 copy-start.5
  50.6 17.6 %all-to-all-start.3 = ((bf16[4,48,128]{2,1,0:T(8,128)(2,1)}), bf16[4,48,128]{2,1,0:T(8,128)(2,1)S(1)}, u32[]{:S(2)}, u32[]{:S(2)}) async-start(bf16[4,48,128]{2,1,0:T(8,128)(2,1)} %shard_map.117), calls=%async_computation.3 | async-start | bytes 98304 | tf_op jit(solution)/shard_map/all_to_all | solution.py:41
  60.1 13.6 %collective-permute-start.4 = (bf16[1024,128]{1,0:T(8,128)(2,1)S(1)}, bf16[1024,128]{1,0:T(8,128)(2,1)}, u32[]{:S(2)}, u32[]{:S(2)}) collective-permute-start(bf16[1024,128]{1,0:T(8,128)(2,1)S(1)} %get-tuple-element.55), channel_id=1, source_target_pairs={{0,4},{4,0},{8,12},{12,8},{1,5},{5,1},{9,13},{13,9},{2,6},{6,2},{1... | collective-permute-start | bytes 786440 | tf_op jit(solution)/shard_map/ppermute | solution.py:453
  69.1 14.2 %all-to-all-start.4 = ((bf16[16,48,128]{2,1,0:T(8,128)(2,1)}), bf16[16,48,128]{2,1,0:T(8,128)(2,1)S(1)}, u32[]{:S(2)}, u32[]{:S(2)}) async-start(bf16[16,48,128]{2,1,0:T(8,128)(2,1)} %shard_map.118), calls=%async_computation.4 | async-start | bytes 393216 | tf_op jit(solution)/shard_map/all_to_all | solution.py:41
  75.6 7.7 %collective-permute-start.5 = (bf16[512,128]{1,0:T(8,128)(2,1)}, bf16[512,128]{1,0:T(8,128)(2,1)S(1)}, u32[]{:S(2)}, u32[]{:S(2)}) collective-permute-start(bf16[512,128]{1,0:T(8,128)(2,1)} %get-tuple-element.57), channel_id=1, source_target_pairs={{0,2},{2,0},{1,3},{3,1},{4,6},{6,4},{5,7},{7,5},{8,10},{10,8},{9,1... | collective-permute-start | bytes 393224 | tf_op jit(solution)/shard_map/ppermute | solution.py:465
  82.1 22.1 %copy-start.6 = (f32[512,128]{1,0:T(8,128)S(1)}, f32[512,128]{1,0:T(8,128)}, u32[]{:S(2)}) copy-start(f32[512,128]{1,0:T(8,128)} %get-tuple-element.61.base) | copy-start | bytes 786436
  82.1 22.1 %copy-start.7 = (f32[128,128]{1,0:T(8,128)S(1)}, f32[128,128]{1,0:T(8,128)}, u32[]{:S(2)}) copy-start(f32[128,128]{1,0:T(8,128)} %up_w.3) | copy-start | bytes 196612

commit v13 on v12

--- a/solution.py
+++ b/solution.py
@@ -34,7 +34,7 @@
 
 
 def owner_mask(i):
-    return (i & 1) ^ (2 if i & 2 else 0) ^ (6 if i & 4 else 0)
+    return (i & 1) ^ (6 if i & 2 else 0) ^ (2 if i & 4 else 0)
 
 
 def swap(v, axis):
@@ -416,9 +416,9 @@
     )
     got = swap(pay, PEERS)
     two = lax.dynamic_update_slice(two, other, (rows, 0))
-    other = lax.ppermute(two, "x", X_NEAR)
+    other = lax.ppermute(two, "x", X_FAR)
     _, send = lax.optimization_barrier((two, send))
-    base_got = lax.ppermute(send, "x", X_FAR)
+    base_got = lax.ppermute(send, "x", X_NEAR)
     got, two = lax.optimization_barrier((got, two))
 
     (pay,) = call(
@@ -441,7 +441,7 @@
         [VMEM] * 3,
         (got, two, other),
     )
-    other = lax.ppermute(four, "x", X_FAR)
+    other = lax.ppermute(four, "x", X_NEAR)
     held, send = call(
         own_half_kernel,
         [shape((n_f // 4 * rows, cols), f32), shape((n_f // 4 * rows, cols), bf16)],
@@ -450,7 +450,7 @@
         flops=rows * width * cols * n_f,
     )
     got_g, pa_rows, up, held, send = lax.optimization_barrier((got_g, pa_rows, up, held, send))
-    base_got = lax.ppermute(send, "x", X_NEAR)
+    base_got = lax.ppermute(send, "x", X_FAR)
     got = swap(add(got_g, n_far), FAR)
     got_g = swap(add(got, n_near), NEAR)
     (input_gradient,) = call(

time: 106 us -> 106 us (level)
  starting transfers between devices: 53.8 us -> 52.6 us
  waiting for transfers between devices: 9.52 us -> 10.7 us
    ppermute x1, starting transfers between devices: 5.26 us -> 3.07 us  [per_device(): base_got = lax.ppermute(send, 'x', X_FAR)]
    ppermute x2, starting transfers between devices: 5.24 us -> 6.45 us  [the longest x1 3.98 us: per_device(): other = lax.ppermute(two, 'x', X_FAR)]
    all_to_all x5, waiting for transfers between devices: 7.27 us -> 8.48 us  [swap(): return lax.all_to_all(v, axis, 0, 0, tiled=True)]
where the time goes in v13:
time: 106 us; the launch traced here: 105 us
  starting transfers between devices  52.6 us (50%)
  blocking collectives  19.8 us (19%)
  Pallas kernels  17.3 us (16%)
  waiting for transfers between devices  10.7 us (10%)
  local copies, waits for them, and re-layouts  3.35 us (3%)
    all_to_all x5, starting transfers between devices, swap(): return lax.all_to_all(v, axis, 0, 0, tiled=True)  31.8 us
    all_to_all x2, blocking collectives, swap(): return lax.all_to_all(v, axis, 0, 0, tiled=True)  19.8 us
    pallas_call x13, Pallas kernels, call(): pl.pallas_call(kernel, grid=(1,), in_specs=[spec or block(a) for spec, a...  17.3 us
    all_to_all x5, waiting for transfers between devices, swap(): return lax.all_to_all(v, axis, 0, 0, tiled=True)  8.48 us
    ppermute x1, starting transfers between devices, per_device(): base_got = lax.ppermute(send, 'x', X_NEAR)  4.05 us
    ppermute x1, starting transfers between devices, per_device(): other = lax.ppermute(two, 'x', X_FAR)  3.98 us
    ppermute x1, starting transfers between devices, per_device(): other = lax.ppermute(gk, 'zlo', Z_PAIRS)  3.92 us
    ppermute x1, starting transfers between devices, per_device(): base_got = lax.ppermute(send, 'zlo', Z_PAIRS)  3.25 us
  transfers between devices with their start and end apart: 11, of which 4 were waited for; matrix products, arithmetic and copies ran while one was open for 1% of the time, Pallas kernels for 11%

profile of v13, /device:TPU:8, one launch (start us, length us, event | category | flops | bytes accessed | tf_op | source)
XLA Modules:
  0.0 104.6 jit_solution(1782220697197979362)
XLA Ops:
  0.7 3.2 %shard_map.111 = (bf16[512,128]{1,0:T(8,128)(2,1)}, bf16[1024,128]{1,0:T(8,128)(2,1)}, bf16[8,128,128]{2,1,0:T(8,128)(2,1)}) custom-call(s32[2]{0:T(128)} %lens.1, s32[2]{0:T(128)} %buckets.1, bf16[512,640]{1,0:T(8,128)(2,1)} %acts.3, bf16[512,128]{1,0:T(8,128)(2,1)} %og.1, f32[640,128]{1,0:T(8,128)} %down_w.7, f32[128,128]{1,0:T(8,128)} %up_w.3), custom_call_target="tpu_custom_call" | custom-call | flops 100663296 | bytes 1835024 | tf_op jit(solution)/shard_map/pallas_call | solution.py:59
  3.9 6.1 %all-to-all-start = ((bf16[8,128,128]{2,1,0:T(8,128)(2,1)}), bf16[8,128,128]{2,1,0:T(8,128)(2,1)S(1)}, u32[]{:S(2)}, u32[]{:S(2)}) async-start(bf16[8,128,128]{2,1,0:T(8,128)(2,1)} %get-tuple-element.35), calls=%async_computation | async-start | bytes 524288 | tf_op jit(solution)/shard_map/all_to_all | solution.py:41
  10.0 3.9 %collective-permute-start = (bf16[512,128]{1,0:T(8,128)(2,1)}, bf16[512,128]{1,0:T(8,128)(2,1)S(1)}, u32[]{:S(2)}, u32[]{:S(2)}) collective-permute-start(bf16[512,128]{1,0:T(8,128)(2,1)} %get-tuple-element.38.gk), channel_id=1, source_target_pairs={{0,2},{2,0},{1,3},{3,1},{4,6},{6,4},{5,7},{7,5},{8,10},{10,8},{9,1... | collective-permute-start | bytes 393224 | tf_op jit(solution)/shard_map/ppermute | solution.py:399
  14.0 1.1 %copy-done.1 = bf16[512,640]{1,0:T(8,128)(2,1)S(1)} copy-done((bf16[512,640]{1,0:T(8,128)(2,1)S(1)}, bf16[512,640]{1,0:T(8,128)(2,1)}, u32[]{:S(2)}) %copy-start.1) | copy-done | bytes 655384
  15.1 1.0 shard_map.112
  16.1 0.8 copy-done.9
  16.9 1.1 %collective-permute-done = bf16[512,128]{1,0:T(8,128)(2,1)S(1)} collective-permute-done((bf16[512,128]{1,0:T(8,128)(2,1)}, bf16[512,128]{1,0:T(8,128)(2,1)S(1)}, u32[]{:S(2)}, u32[]{:S(2)}) %collective-permute-start) | collective-permute-done | bytes 131104 | tf_op jit(solution)/shard_map/ppermute | solution.py:399
  18.0 0.8 shard_map.113
  18.8 4.8 %all-to-all-start.1 = ((bf16[8,192,128]{2,1,0:T(8,128)(2,1)}), bf16[8,192,128]{2,1,0:T(8,128)(2,1)S(1)}, u32[]{:S(2)}, u32[]{:S(2)}) async-start(bf16[8,192,128]{2,1,0:T(8,128)(2,1)} %shard_map.113), calls=%async_computation.1 | async-start | bytes 786432 | tf_op jit(solution)/shard_map/all_to_all | solution.py:41
  23.6 0.7 constant_dynamic-update-slice_fusion.two
  24.3 4.1 %collective-permute-start.2 = (bf16[2048,128]{1,0:T(8,128)(2,1)}, bf16[2048,128]{1,0:T(8,128)(2,1)}, u32[]{:S(2)}, u32[]{:S(2)}) collective-permute-start(bf16[2048,128]{1,0:T(8,128)(2,1)} %copy-done.9), channel_id=1, source_target_pairs={{0,4},{4,0},{8,12},{12,8},{1,5},{5,1},{9,13},{13,9},{2,6},{6,2},{1... | collective-permute-start | bytes 1572872 | tf_op jit(solution)/shard_map/ppermute | solution.py:421
  28.3 4.0 %collective-permute-start.1 = (bf16[1024,128]{1,0:T(8,128)(2,1)}, bf16[1024,128]{1,0:T(8,128)(2,1)}, u32[]{:S(2)}, u32[]{:S(2)}) collective-permute-start(bf16[1024,128]{1,0:T(8,128)(2,1)} %constant_dynamic-update-slice_fusion.two), channel_id=1, source_target_pairs={{0,12},{12,0},{4,8},{8,4},{1,13},{13,1},{5,9},{9,5},{2,14},{14,2},... | collective-permute-start | bytes 786440 | tf_op jit(solution)/shard_map/ppermute | solution.py:419
  32.4 1.0 shard_map.114
  33.4 7.6 %all-to-all-start.2 = ((bf16[16,48,128]{2,1,0:T(8,128)(2,1)}), bf16[16,48,128]{2,1,0:T(8,128)(2,1)S(1)}, u32[]{:S(2)}, u32[]{:S(2)}) async-start(bf16[16,48,128]{2,1,0:T(8,128)(2,1)} %shard_map.114), calls=%async_computation.2 | async-start | bytes 393216 | tf_op jit(solution)/shard_map/all_to_all | solution.py:41
  41.0 1.1 %shard_map.115 = (bf16[64,128]{1,0:T(8,128)(2,1)S(1)}, bf16[512,128]{1,0:T(8,128)(2,1)S(1)}, bf16[2048,128]{1,0:T(8,128)(2,1)S(1)}) custom-call(bf16[8,192,128]{2,1,0:T(8,128)(2,1)S(1)} %all-to-all-done.1.got_ref.got, bf16[1024,128]{1,0:T(8,128)(2,1)} %constant_dynamic-update-slice_fusion.two, bf16[1024,128]{1,0:T(8,128)(2,1)} %collective-permute-done.1.other), custom_call_target="tpu_custom_call" | custom-call | bytes 1589248 | tf_op jit(solution)/shard_map/pallas_call | solution.py:59
  42.1 2.5 %collective-permute-start.3 = (bf16[2048,128]{1,0:T(8,128)(2,1)S(1)}, bf16[2048,128]{1,0:T(8,128)(2,1)}, u32[]{:S(2)}, u32[]{:S(2)}) collective-permute-start(bf16[2048,128]{1,0:T(8,128)(2,1)S(1)} %get-tuple-element.52.near), channel_id=1, source_target_pairs={{0,4},{4,0},{8,12},{12,8},{1,5},{5,1},{9,13},{13,9},{2,6},{6,2},{1... | collective-permute-start | bytes 1572872 | tf_op jit(solution)/shard_map/ppermute | solution.py:444
  44.6 1.9 %shard_map.116 = (f32[1024,128]{1,0:T(8,128)S(1)}, bf16[1024,128]{1,0:T(8,128)(2,1)S(1)}) custom-call(s32[1]{0:T(128)} %bitcast.place, bf16[512,640]{1,0:T(8,128)(2,1)S(1)} %copy-done.2, bf16[640,1024]{1,0:T(8,128)(2,1)S(1)} %copy-done, bf16[2048,128]{1,0:T(8,128)(2,1)} %collective-permute-done.2.got), custom_call_target="tpu_custom_call" | custom-call | flops 335544320 | bytes 3276804 | tf_op jit(solution)/shard_map/pallas_call | solution.py:59
  46.5 0.8 copy-done.5
  47.3 3.3 %all-to-all-done.2.got_ref = bf16[16,48,128]{2,1,0:T(8,128)(2,1)S(1)} async-done(((bf16[16,48,128]{2,1,0:T(8,128)(2,1)}), bf16[16,48,128]{2,1,0:T(8,128)(2,1)S(1)}, u32[]{:S(2)}, u32[]{:S(2)}) %all-to-all-start.2) | async-done | bytes 196640 | tf_op jit(solution)/shard_map/all_to_all | solution.py:41
  50.6 0.7 shard_map.117
  51.2 9.4 %all-to-all-start.3 = ((bf16[4,48,128]{2,1,0:T(8,128)(2,1)}), bf16[4,48,128]{2,1,0:T(8,128)(2,1)S(1)}, u32[]{:S(2)}, u32[]{:S(2)}) async-start(bf16[4,48,128]{2,1,0:T(8,128)(2,1)} %shard_map.117), calls=%async_computation.3 | async-start | bytes 98304 | tf_op jit(solution)/shard_map/all_to_all | solution.py:41
  60.7 3.1 %collective-permute-start.4 = (bf16[1024,128]{1,0:T(8,128)(2,1)S(1)}, bf16[1024,128]{1,0:T(8,128)(2,1)}, u32[]{:S(2)}, u32[]{:S(2)}) collective-permute-start(bf16[1024,128]{1,0:T(8,128)(2,1)S(1)} %get-tuple-element.55), channel_id=1, source_target_pairs={{0,12},{12,0},{4,8},{8,4},{1,13},{13,1},{5,9},{9,5},{2,14},{14,2},... | collective-permute-start | bytes 786440 | tf_op jit(solution)/shard_map/ppermute | solution.py:453
  63.7 5.1 %all-to-all-done.3.got_ref = bf16[4,48,128]{2,1,0:T(8,128)(2,1)S(1)} async-done(((bf16[4,48,128]{2,1,0:T(8,128)(2,1)}), bf16[4,48,128]{2,1,0:T(8,128)(2,1)S(1)}, u32[]{:S(2)}, u32[]{:S(2)}) %all-to-all-start.3) | async-done | bytes 49184 | tf_op jit(solution)/shard_map/all_to_all | solution.py:41
  68.9 0.8 shard_map.118
  69.7 3.9 %all-to-all-start.4 = ((bf16[16,48,128]{2,1,0:T(8,128)(2,1)}), bf16[16,48,128]{2,1,0:T(8,128)(2,1)S(1)}, u32[]{:S(2)}, u32[]{:S(2)}) async-start(bf16[16,48,128]{2,1,0:T(8,128)(2,1)} %shard_map.118), calls=%async_computation.4 | async-start | bytes 393216 | tf_op jit(solution)/shard_map/all_to_all | solution.py:41
  73.7 1.9 %shard_map.120 = (f32[512,128]{1,0:T(8,128)}, bf16[512,128]{1,0:T(8,128)(2,1)}) custom-call(f32[1024,128]{1,0:T(8,128)} %copy-done.5, bf16[1024,128]{1,0:T(8,128)(2,1)} %collective-permute-done.4.got), custom_call_target="tpu_custom_call" | custom-call | bytes 1179648 | tf_op jit(solution)/shard_map/pallas_call | solution.py:59
  75.6 3.2 %collective-permute-start.5 = (bf16[512,128]{1,0:T(8,128)(2,1)}, bf16[512,128]{1,0:T(8,128)(2,1)S(1)}, u32[]{:S(2)}, u32[]{:S(2)}) collective-permute-start(bf16[512,128]{1,0:T(8,128)(2,1)} %get-tuple-element.57), channel_id=1, source_target_pairs={{0,2},{2,0},{1,3},{3,1},{4,6},{6,4},{5,7},{7,5},{8,10},{10,8},{9,1... | collective-permute-start | bytes 393224 | tf_op jit(solution)/shard_map/ppermute | solution.py:465
  78.8 3.3 %shard_map.119 = bf16[512,640]{1,0:T(8,128)(2,1)} custom-call(s32[1]{0:T(128)} %bitcast.place, bf16[2048,128]{1,0:T(8,128)(2,1)S(1)} %get-tuple-element.52.near, bf16[2048,128]{1,0:T(8,128)(2,1)} %collective-permute-done.3.far, bf16[512,128]{1,0:T(8,128)(2,1)S(1)} %get-tuple-element.53.up, f32[640,128]{1,0:T(8,128)S(1)} %copy-done.3, ...), custom_call_target="tpu_custom_call" | custom-call | flops 754974720 | bytes 3473412 | tf_op jit(solution)/shard_map/pallas_call | solution.py:59
  82.1 1.1 %collective-permute-done.5.base_got = bf16[512,128]{1,0:T(8,128)(2,1)S(1)} collective-permute-done((bf16[512,128]{1,0:T(8,128)(2,1)}, bf16[512,128]{1,0:T(8,128)(2,1)S(1)}, u32[]{:S(2)}, u32[]{:S(2)}) %collective-permute-start.5) | collective-permute-done | bytes 131104 | tf_op jit(solution)/shard_map/ppermute | solution.py:465
  83.6 10.7 %all_to_all.35.got.sums = bf16[8,80,128]{2,1,0:T(8,128)(2,1)S(1)} all-to-all(bf16[8,80,128]{2,1,0:T(8,128)(2,1)S(1)} %shard_map.121), channel_id=1, replica_groups=mesh['zhi'=4,'y'=8,'x'=4,'zlo'=2,'core'=2] {'zlo','x'}, dimensions={0} | all-to-all | bytes 327680 | tf_op jit(solution)/shard_map/all_to_all | solution.py:41
  94.4 9.1 %all_to_all.36.got = bf16[8,64,128]{2,1,0:T(8,128)(2,1)S(1)} all-to-all(bf16[8,64,128]{2,1,0:T(8,128)(2,1)S(1)} %shard_map.122), channel_id=1, replica_groups=mesh['zhi'=4,'y'=8,'x'=4,'zlo'=2,'core'=2] {'zlo','x'}, dimensions={0} | all-to-all | bytes 262144 | tf_op jit(solution)/shard_map/all_to_all | solution.py:41
  103.5 1.1 %shard_map.123 = (f32[640,128]{1,0:T(8,128)}, f32[128,128]{1,0:T(8,128)}, bf16[512,128]{1,0:T(8,128)(2,1)}) custom-call(bf16[8,64,128]{2,1,0:T(8,128)(2,1)S(1)} %all_to_all.36.got, bf16[8,80,128]{2,1,0:T(8,128)(2,1)S(1)} %all_to_all.35.got.sums, f32[512,128]{1,0:T(8,128)S(1)} %copy-done.6, bf16[512,128]{1,0:T(8,128)(2,1)S(1)} %collective-permute-done.5.base_got, ...), custom_call_target="tpu_custom_call" | custom-call | flops 16777216 | bytes 1802240 | tf_op jit(solution)/shard_map/pallas_call | solution.py:59
  (26 shorter events, 0.6 us)
Async XLA Ops:
  0.6 13.3 %copy-start.3 = (f32[640,128]{1,0:T(8,128)S(1)}, f32[640,128]{1,0:T(8,128)}, u32[]{:S(2)}) copy-start(f32[640,128]{1,0:T(8,128)} %down_w.7) | copy-start | bytes 983044
  0.6 13.3 %copy-start = (bf16[640,1024]{1,0:T(8,128)(2,1)S(1)}, bf16[640,1024]{1,0:T(8,128)(2,1)}, u32[]{:S(2)}) copy-start(bf16[640,1024]{1,0:T(8,128)(2,1)} %frozen.5) | copy-start | bytes 3932164
  3.9 14.1 %all-to-all-start = ((bf16[8,128,128]{2,1,0:T(8,128)(2,1)}), bf16[8,128,128]{2,1,0:T(8,128)(2,1)S(1)}, u32[]{:S(2)}, u32[]{:S(2)}) async-start(bf16[8,128,128]{2,1,0:T(8,128)(2,1)} %get-tuple-element.35), calls=%async_computation | async-start | bytes 524288 | tf_op jit(solution)/shard_map/all_to_all | solution.py:41
  10.0 8.0 %collective-permute-start = (bf16[512,128]{1,0:T(8,128)(2,1)}, bf16[512,128]{1,0:T(8,128)(2,1)S(1)}, u32[]{:S(2)}, u32[]{:S(2)}) collective-permute-start(bf16[512,128]{1,0:T(8,128)(2,1)} %get-tuple-element.38.gk), channel_id=1, source_target_pairs={{0,2},{2,0},{1,3},{3,1},{4,6},{6,4},{5,7},{7,5},{8,10},{10,8},{9,1... | collective-permute-start | bytes 393224 | tf_op jit(solution)/shard_map/ppermute | solution.py:399
  14.0 1.1 %copy-start.1 = (bf16[512,640]{1,0:T(8,128)(2,1)S(1)}, bf16[512,640]{1,0:T(8,128)(2,1)}, u32[]{:S(2)}) copy-start(bf16[512,640]{1,0:T(8,128)(2,1)} %prompts.5) | copy-start | bytes 1966084
  16.1 0.8 copy-start.9
  16.9 15.5 %copy-start.4 = (bf16[512,640]{1,0:T(8,128)(2,1)S(1)}, bf16[512,640]{1,0:T(8,128)(2,1)}, u32[]{:S(2)}) copy-start(bf16[512,640]{1,0:T(8,128)(2,1)} %acts.3) | copy-start | bytes 1966084
  16.9 15.5 %copy-start.8 = (bf16[512,128]{1,0:T(8,128)(2,1)S(1)}, bf16[512,128]{1,0:T(8,128)(2,1)}, u32[]{:S(2)}) copy-start(bf16[512,128]{1,0:T(8,128)(2,1)} %get-tuple-element.38.gk) | copy-start | bytes 393220
  18.8 13.5 %all-to-all-start.1 = ((bf16[8,192,128]{2,1,0:T(8,128)(2,1)}), bf16[8,192,128]{2,1,0:T(8,128)(2,1)S(1)}, u32[]{:S(2)}, u32[]{:S(2)}) async-start(bf16[8,192,128]{2,1,0:T(8,128)(2,1)} %shard_map.113), calls=%async_computation.1 | async-start | bytes 786432 | tf_op jit(solution)/shard_map/all_to_all | solution.py:41
  24.3 20.3 %copy-start.2 = (bf16[512,640]{1,0:T(8,128)(2,1)S(1)}, bf16[512,640]{1,0:T(8,128)(2,1)}, u32[]{:S(2)}) copy-start(bf16[512,640]{1,0:T(8,128)(2,1)} %prompts.5) | copy-start | bytes 1966084
  24.3 20.3 %collective-permute-start.2 = (bf16[2048,128]{1,0:T(8,128)(2,1)}, bf16[2048,128]{1,0:T(8,128)(2,1)}, u32[]{:S(2)}, u32[]{:S(2)}) collective-permute-start(bf16[2048,128]{1,0:T(8,128)(2,1)} %copy-done.9), channel_id=1, source_target_pairs={{0,4},{4,0},{8,12},{12,8},{1,5},{5,1},{9,13},{13,9},{2,6},{6,2},{1... | collective-permute-start | bytes 1572872 | tf_op jit(solution)/shard_map/ppermute | solution.py:421
  28.3 12.6 %collective-permute-start.1 = (bf16[1024,128]{1,0:T(8,128)(2,1)}, bf16[1024,128]{1,0:T(8,128)(2,1)}, u32[]{:S(2)}, u32[]{:S(2)}) collective-permute-start(bf16[1024,128]{1,0:T(8,128)(2,1)} %constant_dynamic-update-slice_fusion.two), channel_id=1, source_target_pairs={{0,12},{12,0},{4,8},{8,4},{1,13},{13,1},{5,9},{9,5},{2,14},{14,2},... | collective-permute-start | bytes 786440 | tf_op jit(solution)/shard_map/ppermute | solution.py:419
  33.4 17.2 %all-to-all-start.2 = ((bf16[16,48,128]{2,1,0:T(8,128)(2,1)}), bf16[16,48,128]{2,1,0:T(8,128)(2,1)S(1)}, u32[]{:S(2)}, u32[]{:S(2)}) async-start(bf16[16,48,128]{2,1,0:T(8,128)(2,1)} %shard_map.114), calls=%async_computation.2 | async-start | bytes 393216 | tf_op jit(solution)/shard_map/all_to_all | solution.py:41
  42.1 36.7 %collective-permute-start.3 = (bf16[2048,128]{1,0:T(8,128)(2,1)S(1)}, bf16[2048,128]{1,0:T(8,128)(2,1)}, u32[]{:S(2)}, u32[]{:S(2)}) collective-permute-start(bf16[2048,128]{1,0:T(8,128)(2,1)S(1)} %get-tuple-element.52.near), channel_id=1, source_target_pairs={{0,4},{4,0},{8,12},{12,8},{1,5},{5,1},{9,13},{13,9},{2,6},{6,2},{1... | collective-permute-start | bytes 1572872 | tf_op jit(solution)/shard_map/ppermute | solution.py:444
  46.5 0.8 copy-start.5
  51.2 17.6 %all-to-all-start.3 = ((bf16[4,48,128]{2,1,0:T(8,128)(2,1)}), bf16[4,48,128]{2,1,0:T(8,128)(2,1)S(1)}, u32[]{:S(2)}, u32[]{:S(2)}) async-start(bf16[4,48,128]{2,1,0:T(8,128)(2,1)} %shard_map.117), calls=%async_computation.3 | async-start | bytes 98304 | tf_op jit(solution)/shard_map/all_to_all | solution.py:41
  60.7 13.0 %collective-permute-start.4 = (bf16[1024,128]{1,0:T(8,128)(2,1)S(1)}, bf16[1024,128]{1,0:T(8,128)(2,1)}, u32[]{:S(2)}, u32[]{:S(2)}) collective-permute-start(bf16[1024,128]{1,0:T(8,128)(2,1)S(1)} %get-tuple-element.55), channel_id=1, source_target_pairs={{0,12},{12,0},{4,8},{8,4},{1,13},{13,1},{5,9},{9,5},{2,14},{14,2},... | collective-permute-start | bytes 786440 | tf_op jit(solution)/shard_map/ppermute | solution.py:453
  69.7 13.5 %all-to-all-start.4 = ((bf16[16,48,128]{2,1,0:T(8,128)(2,1)}), bf16[16,48,128]{2,1,0:T(8,128)(2,1)S(1)}, u32[]{:S(2)}, u32[]{:S(2)}) async-start(bf16[16,48,128]{2,1,0:T(8,128)(2,1)} %shard_map.118), calls=%async_computation.4 | async-start | bytes 393216 | tf_op jit(solution)/shard_map/all_to_all | solution.py:41
  75.6 7.7 %collective-permute-start.5 = (bf16[512,128]{1,0:T(8,128)(2,1)}, bf16[512,128]{1,0:T(8,128)(2,1)S(1)}, u32[]{:S(2)}, u32[]{:S(2)}) collective-permute-start(bf16[512,128]{1,0:T(8,128)(2,1)} %get-tuple-element.57), channel_id=1, source_target_pairs={{0,2},{2,0},{1,3},{3,1},{4,6},{6,4},{5,7},{7,5},{8,10},{10,8},{9,1... | collective-permute-start | bytes 393224 | tf_op jit(solution)/shard_map/ppermute | solution.py:465
  82.1 21.4 %copy-start.6 = (f32[512,128]{1,0:T(8,128)S(1)}, f32[512,128]{1,0:T(8,128)}, u32[]{:S(2)}) copy-start(f32[512,128]{1,0:T(8,128)} %get-tuple-element.61.base) | copy-start | bytes 786436
  82.1 21.4 %copy-start.7 = (f32[128,128]{1,0:T(8,128)S(1)}, f32[128,128]{1,0:T(8,128)}, u32[]{:S(2)}) copy-start(f32[128,128]{1,0:T(8,128)} %up_w.3) | copy-start | bytes 196612

commit v14 on v13

--- a/solution.py
+++ b/solution.py
@@ -417,7 +417,6 @@
     got = swap(pay, PEERS)
     two = lax.dynamic_update_slice(two, other, (rows, 0))
     other = lax.ppermute(two, "x", X_FAR)
-    _, send = lax.optimization_barrier((two, send))
     base_got = lax.ppermute(send, "x", X_NEAR)
     got, two = lax.optimization_barrier((got, two))
 

time: 106 us -> 107 us (level)
  Pallas kernels: 17.3 us -> 18.7 us
    pallas_call x13, Pallas kernels: 17.3 us -> 18.7 us  [call(): pl.pallas_call(kernel, grid=(1,), in_specs=[spec or block(a) for spec, a...]
  transfers between devices with their start and end apart: 11 -> 11, of which waited for: 4 -> 4; matrix products, arithmetic and copies ran while one was open for 1% -> 1% of each run, Pallas kernels for 11% -> 12%
where the time goes in v14:
time: 107 us; the launch traced here: 106 us
  starting transfers between devices  53.3 us (50%)
  blocking collectives  19.8 us (19%)
  Pallas kernels  18.7 us (17%)
  waiting for transfers between devices  10.1 us (9%)
  local copies, waits for them, and re-layouts  3.27 us (3%)
    all_to_all x5, starting transfers between devices, swap(): return lax.all_to_all(v, axis, 0, 0, tiled=True)  32.5 us
    all_to_all x2, blocking collectives, swap(): return lax.all_to_all(v, axis, 0, 0, tiled=True)  19.8 us
    pallas_call x13, Pallas kernels, call(): pl.pallas_call(kernel, grid=(1,), in_specs=[spec or block(a) for spec, a...  18.7 us
    all_to_all x5, waiting for transfers between devices, swap(): return lax.all_to_all(v, axis, 0, 0, tiled=True)  7.74 us
    ppermute x1, starting transfers between devices, per_device(): other = lax.ppermute(two, 'x', X_FAR)  4.1 us
    ppermute x1, starting transfers between devices, per_device(): base_got = lax.ppermute(send, 'x', X_NEAR)  3.92 us
    ppermute x1, starting transfers between devices, per_device(): other = lax.ppermute(gk, 'zlo', Z_PAIRS)  3.92 us
    ppermute x1, starting transfers between devices, per_device(): base_got = lax.ppermute(send, 'zlo', Z_PAIRS)  3.25 us
  transfers between devices with their start and end apart: 11, of which 4 were waited for; matrix products, arithmetic and copies ran while one was open for 1% of the time, Pallas kernels for 12%

profile of v14, /device:TPU:8, one launch (start us, length us, event | category | flops | bytes accessed | tf_op | source)
XLA Modules:
  0.0 106.0 jit_solution(5410547691039635110)
XLA Ops:
  0.7 3.2 %shard_map.111 = (bf16[512,128]{1,0:T(8,128)(2,1)}, bf16[1024,128]{1,0:T(8,128)(2,1)}, bf16[8,128,128]{2,1,0:T(8,128)(2,1)}) custom-call(s32[2]{0:T(128)} %lens.1, s32[2]{0:T(128)} %buckets.1, bf16[512,640]{1,0:T(8,128)(2,1)} %acts.3, bf16[512,128]{1,0:T(8,128)(2,1)} %og.1, f32[640,128]{1,0:T(8,128)} %down_w.7, f32[128,128]{1,0:T(8,128)} %up_w.3), custom_call_target="tpu_custom_call" | custom-call | flops 100663296 | bytes 1835024 | tf_op jit(solution)/shard_map/pallas_call | solution.py:59
  3.9 6.1 %all-to-all-start = ((bf16[8,128,128]{2,1,0:T(8,128)(2,1)}), bf16[8,128,128]{2,1,0:T(8,128)(2,1)S(1)}, u32[]{:S(2)}, u32[]{:S(2)}) async-start(bf16[8,128,128]{2,1,0:T(8,128)(2,1)} %get-tuple-element.34), calls=%async_computation | async-start | bytes 524288 | tf_op jit(solution)/shard_map/all_to_all | solution.py:41
  10.0 3.9 %collective-permute-start = (bf16[512,128]{1,0:T(8,128)(2,1)}, bf16[512,128]{1,0:T(8,128)(2,1)S(1)}, u32[]{:S(2)}, u32[]{:S(2)}) collective-permute-start(bf16[512,128]{1,0:T(8,128)(2,1)} %get-tuple-element.37.gk), channel_id=1, source_target_pairs={{0,2},{2,0},{1,3},{3,1},{4,6},{6,4},{5,7},{7,5},{8,10},{10,8},{9,1... | collective-permute-start | bytes 393224 | tf_op jit(solution)/shard_map/ppermute | solution.py:399
  14.0 1.1 %copy-done.1 = bf16[512,640]{1,0:T(8,128)(2,1)S(1)} copy-done((bf16[512,640]{1,0:T(8,128)(2,1)S(1)}, bf16[512,640]{1,0:T(8,128)(2,1)}, u32[]{:S(2)}) %copy-start.1) | copy-done | bytes 655384
  15.1 1.7 %shard_map.112 = (bf16[512,128]{1,0:T(8,128)(2,1)S(1)}, bf16[2048,128]{1,0:T(8,128)(2,1)}) custom-call(s32[1]{0:T(128)} %bitcast.place, bf16[512,640]{1,0:T(8,128)(2,1)S(1)} %copy-done.1, bf16[640,1024]{1,0:T(8,128)(2,1)S(1)} %copy-done, f32[640,128]{1,0:T(8,128)S(1)} %copy-done.3), custom_call_target="tpu_custom_call" | custom-call | flops 419430400 | bytes 2949124 | tf_op jit(solution)/shard_map/pallas_call | solution.py:59
  16.8 1.2 %collective-permute-done = bf16[512,128]{1,0:T(8,128)(2,1)S(1)} collective-permute-done((bf16[512,128]{1,0:T(8,128)(2,1)}, bf16[512,128]{1,0:T(8,128)(2,1)S(1)}, u32[]{:S(2)}, u32[]{:S(2)}) %collective-permute-start) | collective-permute-done | bytes 131104 | tf_op jit(solution)/shard_map/ppermute | solution.py:399
  18.0 0.8 shard_map.113
  18.8 4.8 %all-to-all-start.1 = ((bf16[8,192,128]{2,1,0:T(8,128)(2,1)}), bf16[8,192,128]{2,1,0:T(8,128)(2,1)S(1)}, u32[]{:S(2)}, u32[]{:S(2)}) async-start(bf16[8,192,128]{2,1,0:T(8,128)(2,1)} %shard_map.113), calls=%async_computation.1 | async-start | bytes 786432 | tf_op jit(solution)/shard_map/all_to_all | solution.py:41
  23.6 3.9 %collective-permute-start.2 = (bf16[2048,128]{1,0:T(8,128)(2,1)}, bf16[2048,128]{1,0:T(8,128)(2,1)}, u32[]{:S(2)}, u32[]{:S(2)}) collective-permute-start(bf16[2048,128]{1,0:T(8,128)(2,1)} %get-tuple-element.46), channel_id=1, source_target_pairs={{0,4},{4,0},{8,12},{12,8},{1,5},{5,1},{9,13},{13,9},{2,6},{6,2},{1... | collective-permute-start | bytes 1572872 | tf_op jit(solution)/shard_map/ppermute | solution.py:420
  27.5 0.7 constant_dynamic-update-slice_fusion.two
  28.2 4.1 %collective-permute-start.1 = (bf16[1024,128]{1,0:T(8,128)(2,1)}, bf16[1024,128]{1,0:T(8,128)(2,1)}, u32[]{:S(2)}, u32[]{:S(2)}) collective-permute-start(bf16[1024,128]{1,0:T(8,128)(2,1)} %constant_dynamic-update-slice_fusion.two), channel_id=1, source_target_pairs={{0,12},{12,0},{4,8},{8,4},{1,13},{13,1},{5,9},{9,5},{2,14},{14,2},... | collective-permute-start | bytes 786440 | tf_op jit(solution)/shard_map/ppermute | solution.py:419
  32.3 1.0 shard_map.114
  33.4 7.6 %all-to-all-start.2 = ((bf16[16,48,128]{2,1,0:T(8,128)(2,1)}), bf16[16,48,128]{2,1,0:T(8,128)(2,1)S(1)}, u32[]{:S(2)}, u32[]{:S(2)}) async-start(bf16[16,48,128]{2,1,0:T(8,128)(2,1)} %shard_map.114), calls=%async_computation.2 | async-start | bytes 393216 | tf_op jit(solution)/shard_map/all_to_all | solution.py:41
  41.0 1.1 %shard_map.115 = (bf16[64,128]{1,0:T(8,128)(2,1)S(1)}, bf16[512,128]{1,0:T(8,128)(2,1)S(1)}, bf16[2048,128]{1,0:T(8,128)(2,1)S(1)}) custom-call(bf16[8,192,128]{2,1,0:T(8,128)(2,1)S(1)} %all-to-all-done.1.got_ref.got, bf16[1024,128]{1,0:T(8,128)(2,1)} %constant_dynamic-update-slice_fusion.two, bf16[1024,128]{1,0:T(8,128)(2,1)} %collective-permute-done.1.other), custom_call_target="tpu_custom_call" | custom-call | bytes 1589248 | tf_op jit(solution)/shard_map/pallas_call | solution.py:59
  42.1 2.5 %collective-permute-start.3 = (bf16[2048,128]{1,0:T(8,128)(2,1)S(1)}, bf16[2048,128]{1,0:T(8,128)(2,1)}, u32[]{:S(2)}, u32[]{:S(2)}) collective-permute-start(bf16[2048,128]{1,0:T(8,128)(2,1)S(1)} %get-tuple-element.50.near), channel_id=1, source_target_pairs={{0,4},{4,0},{8,12},{12,8},{1,5},{5,1},{9,13},{13,9},{2,6},{6,2},{1... | collective-permute-start | bytes 1572872 | tf_op jit(solution)/shard_map/ppermute | solution.py:443
  44.6 2.6 %shard_map.116 = (f32[1024,128]{1,0:T(8,128)S(1)}, bf16[1024,128]{1,0:T(8,128)(2,1)}) custom-call(s32[1]{0:T(128)} %bitcast.place, bf16[512,640]{1,0:T(8,128)(2,1)S(1)} %copy-done.2, bf16[640,1024]{1,0:T(8,128)(2,1)S(1)} %copy-done, bf16[2048,128]{1,0:T(8,128)(2,1)} %collective-permute-done.2.got), custom_call_target="tpu_custom_call" | custom-call | flops 335544320 | bytes 3276804 | tf_op jit(solution)/shard_map/pallas_call | solution.py:59
  47.2 0.8 copy-done.5
  48.0 2.6 %all-to-all-done.2.got_ref = bf16[16,48,128]{2,1,0:T(8,128)(2,1)S(1)} async-done(((bf16[16,48,128]{2,1,0:T(8,128)(2,1)}), bf16[16,48,128]{2,1,0:T(8,128)(2,1)S(1)}, u32[]{:S(2)}, u32[]{:S(2)}) %all-to-all-start.2) | async-done | bytes 196640 | tf_op jit(solution)/shard_map/all_to_all | solution.py:41
  50.6 0.7 shard_map.117
  51.2 9.4 %all-to-all-start.3 = ((bf16[4,48,128]{2,1,0:T(8,128)(2,1)}), bf16[4,48,128]{2,1,0:T(8,128)(2,1)S(1)}, u32[]{:S(2)}, u32[]{:S(2)}) async-start(bf16[4,48,128]{2,1,0:T(8,128)(2,1)} %shard_map.117), calls=%async_computation.3 | async-start | bytes 98304 | tf_op jit(solution)/shard_map/all_to_all | solution.py:41
  60.6 3.1 %collective-permute-start.4 = (bf16[1024,128]{1,0:T(8,128)(2,1)}, bf16[1024,128]{1,0:T(8,128)(2,1)S(1)}, u32[]{:S(2)}, u32[]{:S(2)}) collective-permute-start(bf16[1024,128]{1,0:T(8,128)(2,1)} %get-tuple-element.53), channel_id=1, source_target_pairs={{0,12},{12,0},{4,8},{8,4},{1,13},{13,1},{5,9},{9,5},{2,14},{14,2},... | collective-permute-start | bytes 786440 | tf_op jit(solution)/shard_map/ppermute | solution.py:452
  63.7 5.1 %all-to-all-done.3.got_ref = bf16[4,48,128]{2,1,0:T(8,128)(2,1)S(1)} async-done(((bf16[4,48,128]{2,1,0:T(8,128)(2,1)}), bf16[4,48,128]{2,1,0:T(8,128)(2,1)S(1)}, u32[]{:S(2)}, u32[]{:S(2)}) %all-to-all-start.3) | async-done | bytes 49184 | tf_op jit(solution)/shard_map/all_to_all | solution.py:41
  68.9 0.8 shard_map.118
  69.7 4.6 %all-to-all-start.4 = ((bf16[16,48,128]{2,1,0:T(8,128)(2,1)}), bf16[16,48,128]{2,1,0:T(8,128)(2,1)S(1)}, u32[]{:S(2)}, u32[]{:S(2)}) async-start(bf16[16,48,128]{2,1,0:T(8,128)(2,1)} %shard_map.118), calls=%async_computation.4 | async-start | bytes 393216 | tf_op jit(solution)/shard_map/all_to_all | solution.py:41
  74.4 0.7 copy-done.9
  75.0 1.9 %shard_map.120 = (f32[512,128]{1,0:T(8,128)}, bf16[512,128]{1,0:T(8,128)(2,1)}) custom-call(f32[1024,128]{1,0:T(8,128)} %copy-done.5, bf16[1024,128]{1,0:T(8,128)(2,1)} %copy-done.9), custom_call_target="tpu_custom_call" | custom-call | bytes 1179648 | tf_op jit(solution)/shard_map/pallas_call | solution.py:59
  76.9 3.2 %collective-permute-start.5 = (bf16[512,128]{1,0:T(8,128)(2,1)}, bf16[512,128]{1,0:T(8,128)(2,1)S(1)}, u32[]{:S(2)}, u32[]{:S(2)}) collective-permute-start(bf16[512,128]{1,0:T(8,128)(2,1)} %get-tuple-element.55), channel_id=1, source_target_pairs={{0,2},{2,0},{1,3},{3,1},{4,6},{6,4},{5,7},{7,5},{8,10},{10,8},{9,1... | collective-permute-start | bytes 393224 | tf_op jit(solution)/shard_map/ppermute | solution.py:464
  80.2 3.3 %shard_map.119 = bf16[512,640]{1,0:T(8,128)(2,1)} custom-call(s32[1]{0:T(128)} %bitcast.place, bf16[2048,128]{1,0:T(8,128)(2,1)S(1)} %get-tuple-element.50.near, bf16[2048,128]{1,0:T(8,128)(2,1)} %collective-permute-done.3.far, bf16[512,128]{1,0:T(8,128)(2,1)S(1)} %get-tuple-element.51.up, f32[640,128]{1,0:T(8,128)S(1)} %copy-done.3, ...), custom_call_target="tpu_custom_call" | custom-call | flops 754974720 | bytes 3473412 | tf_op jit(solution)/shard_map/pallas_call | solution.py:59
  83.5 1.1 %collective-permute-done.5.base_got = bf16[512,128]{1,0:T(8,128)(2,1)S(1)} collective-permute-done((bf16[512,128]{1,0:T(8,128)(2,1)}, bf16[512,128]{1,0:T(8,128)(2,1)S(1)}, u32[]{:S(2)}, u32[]{:S(2)}) %collective-permute-start.5) | collective-permute-done | bytes 131104 | tf_op jit(solution)/shard_map/ppermute | solution.py:464
  84.9 10.7 %all_to_all.35.got.sums = bf16[8,80,128]{2,1,0:T(8,128)(2,1)S(1)} all-to-all(bf16[8,80,128]{2,1,0:T(8,128)(2,1)S(1)} %shard_map.121), channel_id=1, replica_groups=mesh['zhi'=4,'y'=8,'x'=4,'zlo'=2,'core'=2] {'zlo','x'}, dimensions={0} | all-to-all | bytes 327680 | tf_op jit(solution)/shard_map/all_to_all | solution.py:41
  95.8 9.1 %all_to_all.36.got = bf16[8,64,128]{2,1,0:T(8,128)(2,1)S(1)} all-to-all(bf16[8,64,128]{2,1,0:T(8,128)(2,1)S(1)} %shard_map.122), channel_id=1, replica_groups=mesh['zhi'=4,'y'=8,'x'=4,'zlo'=2,'core'=2] {'zlo','x'}, dimensions={0} | all-to-all | bytes 262144 | tf_op jit(solution)/shard_map/all_to_all | solution.py:41
  104.9 1.1 %shard_map.123 = (f32[640,128]{1,0:T(8,128)}, f32[128,128]{1,0:T(8,128)}, bf16[512,128]{1,0:T(8,128)(2,1)}) custom-call(bf16[8,64,128]{2,1,0:T(8,128)(2,1)S(1)} %all_to_all.36.got, bf16[8,80,128]{2,1,0:T(8,128)(2,1)S(1)} %all_to_all.35.got.sums, f32[512,128]{1,0:T(8,128)S(1)} %copy-done.6, bf16[512,128]{1,0:T(8,128)(2,1)S(1)} %collective-permute-done.5.base_got, ...), custom_call_target="tpu_custom_call" | custom-call | flops 16777216 | bytes 1802240 | tf_op jit(solution)/shard_map/pallas_call | solution.py:59
  (26 shorter events, 0.5 us)
Async XLA Ops:
  0.6 13.3 %copy-start.3 = (f32[640,128]{1,0:T(8,128)S(1)}, f32[640,128]{1,0:T(8,128)}, u32[]{:S(2)}) copy-start(f32[640,128]{1,0:T(8,128)} %down_w.7) | copy-start | bytes 983044
  0.6 13.3 %copy-start = (bf16[640,1024]{1,0:T(8,128)(2,1)S(1)}, bf16[640,1024]{1,0:T(8,128)(2,1)}, u32[]{:S(2)}) copy-start(bf16[640,1024]{1,0:T(8,128)(2,1)} %frozen.5) | copy-start | bytes 3932164
  3.9 14.1 %all-to-all-start = ((bf16[8,128,128]{2,1,0:T(8,128)(2,1)}), bf16[8,128,128]{2,1,0:T(8,128)(2,1)S(1)}, u32[]{:S(2)}, u32[]{:S(2)}) async-start(bf16[8,128,128]{2,1,0:T(8,128)(2,1)} %get-tuple-element.34), calls=%async_computation | async-start | bytes 524288 | tf_op jit(solution)/shard_map/all_to_all | solution.py:41
  10.0 8.0 %collective-permute-start = (bf16[512,128]{1,0:T(8,128)(2,1)}, bf16[512,128]{1,0:T(8,128)(2,1)S(1)}, u32[]{:S(2)}, u32[]{:S(2)}) collective-permute-start(bf16[512,128]{1,0:T(8,128)(2,1)} %get-tuple-element.37.gk), channel_id=1, source_target_pairs={{0,2},{2,0},{1,3},{3,1},{4,6},{6,4},{5,7},{7,5},{8,10},{10,8},{9,1... | collective-permute-start | bytes 393224 | tf_op jit(solution)/shard_map/ppermute | solution.py:399
  14.0 1.1 %copy-start.1 = (bf16[512,640]{1,0:T(8,128)(2,1)S(1)}, bf16[512,640]{1,0:T(8,128)(2,1)}, u32[]{:S(2)}) copy-start(bf16[512,640]{1,0:T(8,128)(2,1)} %prompts.5) | copy-start | bytes 1966084
  16.8 15.5 %copy-start.4 = (bf16[512,640]{1,0:T(8,128)(2,1)S(1)}, bf16[512,640]{1,0:T(8,128)(2,1)}, u32[]{:S(2)}) copy-start(bf16[512,640]{1,0:T(8,128)(2,1)} %acts.3) | copy-start | bytes 1966084
  16.8 15.5 %copy-start.8 = (bf16[512,128]{1,0:T(8,128)(2,1)S(1)}, bf16[512,128]{1,0:T(8,128)(2,1)}, u32[]{:S(2)}) copy-start(bf16[512,128]{1,0:T(8,128)(2,1)} %get-tuple-element.37.gk) | copy-start | bytes 393220
  18.8 13.5 %all-to-all-start.1 = ((bf16[8,192,128]{2,1,0:T(8,128)(2,1)}), bf16[8,192,128]{2,1,0:T(8,128)(2,1)S(1)}, u32[]{:S(2)}, u32[]{:S(2)}) async-start(bf16[8,192,128]{2,1,0:T(8,128)(2,1)} %shard_map.113), calls=%async_computation.1 | async-start | bytes 786432 | tf_op jit(solution)/shard_map/all_to_all | solution.py:41
  23.6 20.9 %collective-permute-start.2 = (bf16[2048,128]{1,0:T(8,128)(2,1)}, bf16[2048,128]{1,0:T(8,128)(2,1)}, u32[]{:S(2)}, u32[]{:S(2)}) collective-permute-start(bf16[2048,128]{1,0:T(8,128)(2,1)} %get-tuple-element.46), channel_id=1, source_target_pairs={{0,4},{4,0},{8,12},{12,8},{1,5},{5,1},{9,13},{13,9},{2,6},{6,2},{1... | collective-permute-start | bytes 1572872 | tf_op jit(solution)/shard_map/ppermute | solution.py:420
  28.2 16.3 %copy-start.2 = (bf16[512,640]{1,0:T(8,128)(2,1)S(1)}, bf16[512,640]{1,0:T(8,128)(2,1)}, u32[]{:S(2)}) copy-start(bf16[512,640]{1,0:T(8,128)(2,1)} %prompts.5) | copy-start | bytes 1966084
  28.2 12.7 %collective-permute-start.1 = (bf16[1024,128]{1,0:T(8,128)(2,1)}, bf16[1024,128]{1,0:T(8,128)(2,1)}, u32[]{:S(2)}, u32[]{:S(2)}) collective-permute-start(bf16[1024,128]{1,0:T(8,128)(2,1)} %constant_dynamic-update-slice_fusion.two), channel_id=1, source_target_pairs={{0,12},{12,0},{4,8},{8,4},{1,13},{13,1},{5,9},{9,5},{2,14},{14,2},... | collective-permute-start | bytes 786440 | tf_op jit(solution)/shard_map/ppermute | solution.py:419
  33.4 17.2 %all-to-all-start.2 = ((bf16[16,48,128]{2,1,0:T(8,128)(2,1)}), bf16[16,48,128]{2,1,0:T(8,128)(2,1)S(1)}, u32[]{:S(2)}, u32[]{:S(2)}) async-start(bf16[16,48,128]{2,1,0:T(8,128)(2,1)} %shard_map.114), calls=%async_computation.2 | async-start | bytes 393216 | tf_op jit(solution)/shard_map/all_to_all | solution.py:41
  42.1 38.1 %collective-permute-start.3 = (bf16[2048,128]{1,0:T(8,128)(2,1)S(1)}, bf16[2048,128]{1,0:T(8,128)(2,1)}, u32[]{:S(2)}, u32[]{:S(2)}) collective-permute-start(bf16[2048,128]{1,0:T(8,128)(2,1)S(1)} %get-tuple-element.50.near), channel_id=1, source_target_pairs={{0,4},{4,0},{8,12},{12,8},{1,5},{5,1},{9,13},{13,9},{2,6},{6,2},{1... | collective-permute-start | bytes 1572872 | tf_op jit(solution)/shard_map/ppermute | solution.py:443
  47.2 0.8 copy-start.5
  51.2 17.6 %all-to-all-start.3 = ((bf16[4,48,128]{2,1,0:T(8,128)(2,1)}), bf16[4,48,128]{2,1,0:T(8,128)(2,1)S(1)}, u32[]{:S(2)}, u32[]{:S(2)}) async-start(bf16[4,48,128]{2,1,0:T(8,128)(2,1)} %shard_map.117), calls=%async_computation.3 | async-start | bytes 98304 | tf_op jit(solution)/shard_map/all_to_all | solution.py:41
  60.6 13.7 %collective-permute-start.4 = (bf16[1024,128]{1,0:T(8,128)(2,1)}, bf16[1024,128]{1,0:T(8,128)(2,1)S(1)}, u32[]{:S(2)}, u32[]{:S(2)}) collective-permute-start(bf16[1024,128]{1,0:T(8,128)(2,1)} %get-tuple-element.53), channel_id=1, source_target_pairs={{0,12},{12,0},{4,8},{8,4},{1,13},{13,1},{5,9},{9,5},{2,14},{14,2},... | collective-permute-start | bytes 786440 | tf_op jit(solution)/shard_map/ppermute | solution.py:452
  69.7 14.9 %all-to-all-start.4 = ((bf16[16,48,128]{2,1,0:T(8,128)(2,1)}), bf16[16,48,128]{2,1,0:T(8,128)(2,1)S(1)}, u32[]{:S(2)}, u32[]{:S(2)}) async-start(bf16[16,48,128]{2,1,0:T(8,128)(2,1)} %shard_map.118), calls=%async_computation.4 | async-start | bytes 393216 | tf_op jit(solution)/shard_map/all_to_all | solution.py:41
  74.3 0.7 copy-start.9
  76.9 7.7 %collective-permute-start.5 = (bf16[512,128]{1,0:T(8,128)(2,1)}, bf16[512,128]{1,0:T(8,128)(2,1)S(1)}, u32[]{:S(2)}, u32[]{:S(2)}) collective-permute-start(bf16[512,128]{1,0:T(8,128)(2,1)} %get-tuple-element.55), channel_id=1, source_target_pairs={{0,2},{2,0},{1,3},{3,1},{4,6},{6,4},{5,7},{7,5},{8,10},{10,8},{9,1... | collective-permute-start | bytes 393224 | tf_op jit(solution)/shard_map/ppermute | solution.py:464
  83.5 21.4 %copy-start.6 = (f32[512,128]{1,0:T(8,128)S(1)}, f32[512,128]{1,0:T(8,128)}, u32[]{:S(2)}) copy-start(f32[512,128]{1,0:T(8,128)} %get-tuple-element.59.base) | copy-start | bytes 786436
  83.5 21.4 %copy-start.7 = (f32[128,128]{1,0:T(8,128)S(1)}, f32[128,128]{1,0:T(8,128)}, u32[]{:S(2)}) copy-start(f32[128,128]{1,0:T(8,128)} %up_w.3) | copy-start | bytes 196612
